TPU v7x, 32 devices: a whole 2x2x4 slice. The times are simulated.
32 devices in a mesh: row: 8 (over z, x), col: 4 (over y, core).
Axes of the slice: x: 2, y: 2, z: 4, core: 2. Of those that a mesh axis runs over, the one named last changes fastest.
Arguments:
- amplitudes: bfloat16 [8192, 8192], P('row', 'col'), may hold values from -6 to 6
- integrals: bfloat16 [8192, 2048], P('col', 'row'), may hold values from -0.0625 to 0.0625
- amp_mask: int32 [64, 64], P('row', 'col'), may hold values 0 or 1
- int_mask: int32 [64, 16], P('col', 'row'), may hold values 0 or 1
Outputs:
- ladder: bfloat16 [8192, 2048], P('row', 'col')
All inputs are finite; a program needn't handle non-finite values. No bound on the sum of `amp_mask` or of `int_mask` on one device may be relied on, other than what follows from the above.
Results may differ from a plain program's by a relative error of at most 0.001.
Values may be sent and summed in bfloat16 or wider, within the bound.
No kernel may reach another device: no remote copies, remote signals or barrier semaphores. Data moves between devices by JAX's collectives and lax.ppermute only.
A program may use at most 128 MiB of HBM per device.

v0:
```python
import jax
import jax.numpy as jnp
from jax import lax
from jax.sharding import PartitionSpec as P

TILE = 128


def expand(mask):
    spread = jnp.repeat(jnp.repeat(mask, TILE, axis=0), TILE, axis=1)
    return spread.astype(jnp.bfloat16)


def per_device(amplitudes, integrals, amp_mask, int_mask):
    sparse_amp = amplitudes * expand(amp_mask)
    sparse_int = integrals * expand(int_mask)
    partial_value = jnp.dot(
        sparse_amp,
        lax.all_gather(sparse_int, "row", axis=1, tiled=True),
        preferred_element_type=jnp.float32,
    )
    ladder = lax.psum_scatter(partial_value, "col", scatter_dimension=1, tiled=True)
    return ladder.astype(jnp.bfloat16)


def solution(mesh):
    in_specs = (P("row", "col"), P("col", "row"), P("row", "col"), P("col", "row"))
    out_specs = P("row", "col")
    return jax.shard_map(
        per_device, mesh=mesh, in_specs=in_specs, out_specs=out_specs, check_vma=False
    )
```

profile of v0, /device:TPU:24, one launch (start us, length us, event | category | flops | bytes accessed | tf_op | source)
XLA Modules:
  0.0 239.5 jit_solution(14581913447136909084)
XLA Ops:
  6.5 0.0 copy-start
  6.5 0.0 all-gather.2.cloned.1.call-start
  6.5 0.7 convert_element_type.28
  7.2 0.1 copy.5
  7.3 0.1 broadcast_in_dim.14
  7.4 5.8 %broadcast_in_dim.15 = bf16[2048,2,128]{2,1,0:T(2,128)(2,1)S(1)} broadcast(bf16[2048,2]{1,0:T(8,128)(2,1)S(1)} %bitcast.12), dimensions={0,1} | broadcast | bytes 1056768 | tf_op jit(solution)/shard_map/broadcast_in_dim | solution.py:10
  13.2 2.4 bitcast_multiply_fusion.2
  15.6 0.0 all-gather.2.cloned.1.call-update
  15.6 0.0 reduce-scatter.2.cloned.1.call-start
  15.6 0.0 copy-done
  15.7 124.6 %all-gather.2.cloned.1.call-done = bf16[2048,2048]{1,0:T(8,128)(2,1)} async-done(((bf16[2048,256]{1,0:T(8,128)(2,1)}), bf16[2048,2048]{1,0:T(8,128)(2,1)}) %all-gather.2.cloned.1.call-update) | async-done | bytes 8388624 | tf_op jit(solution)/shard_map/all_gather | solution.py:19
  140.2 0.0 copy-start.1
  140.3 4.5 %broadcast_in_dim.13 = bf16[1024,16,128]{2,1,0:T(8,128)(2,1)S(1)} broadcast(bf16[1024,16]{1,0:T(8,128)(2,1)S(1)} %bitcast.13), dimensions={0,1} | broadcast | bytes 4227072 | tf_op jit(solution)/shard_map/broadcast_in_dim | solution.py:10
  144.7 0.0 copy-done.1
  144.8 13.2 %fusion = f32[1024,2048]{1,0:T(8,128)} fusion(bf16[2048,2048]{1,0:T(8,128)(2,1)} %all-gather.2.cloned.1.call-done, bf16[1024,2048]{1,0:T(8,128)(2,1)S(1)} %copy-done.1, bf16[128,8,16,128]{3,2,1,0:T(8,128)(2,1)S(1)} %bitcast.11), kind=kOutput, calls=%fused_computation.1 | convolution fusion | flops 8592031744 | bytes 25165824 | tf_op jit(solution)/shard_map/dot_general | solution.py:17
  158.0 0.0 reduce-scatter.2.cloned.1.call-update
  158.0 71.9 %reduce-scatter.2.cloned.1.call-done = f32[1024,512]{1,0:T(8,128)} async-done(((f32[1024,2048]{1,0:T(8,128)}), f32[1024,512]{1,0:T(8,128)}) %reduce-scatter.2.cloned.1.call-update) | async-done | bytes 2097168 | tf_op jit(solution)/shard_map/reduce_scatter | solution.py:22
  229.9 2.7 %convert_element_type.31 = bf16[1024,512]{1,0:T(8,128)(2,1)} convert(f32[1024,512]{1,0:T(8,128)} %reduce-scatter.2.cloned.1.call-done) | non-fusion elementwise | flops 524288 | bytes 3145728 | tf_op jit(solution)/shard_map/convert_element_type | solution.py:23
  (2 shorter events, 0.0 us)
Async XLA Ops:
  6.5 9.1 %copy-start = (s32[8,16]{1,0:T(8,128)S(1)}, s32[8,16]{1,0:T(8,128)}, u32[]{:S(2)}) copy-start(s32[8,16]{1,0:T(8,128)} %param.6) | copy-start | bytes 1540
  6.5 133.7 %all-gather.2.cloned.1.call-start = ((), (), s32[]{:S(2)}) async-start(), calls=%async_computation.1 | async-start | bytes 9437184 | tf_op jit(solution)/shard_map/all_gather | solution.py:19
  15.6 214.3 %reduce-scatter.2.cloned.1.call-start = ((), (), s32[]{:S(2)}) async-start(), calls=%async_computation.2 | async-start | bytes 10485760 | tf_op jit(solution)/shard_map/reduce_scatter | solution.py:22
  140.2 4.5 %copy-start.1 = (bf16[1024,2048]{1,0:T(8,128)(2,1)S(1)}, bf16[1024,2048]{1,0:T(8,128)(2,1)}, u32[]{:S(2)}) copy-start(bf16[1024,2048]{1,0:T(8,128)(2,1)} %param.4) | copy-start | bytes 12582916
Sparse Core Ops, SparseCore 0:
  15.7 124.4 all-gather.1
  158.1 71.7 reduce-scatter.1
where the time goes:
time: 241 us; the launch traced here: 239 us
  waiting for transfers between devices  197 us (82%)
  between operations  13.4 us (6%)
  matrix products  13.2 us (5%)
  local copies, waits for them, and re-layouts  10.5 us (4%)
  other arithmetic  5.77 us (2%)
    all_gather x1, waiting for transfers between devices, per_device(): lax.all_gather(sparse_int, 'row', axis=1, tiled=True)  125 us
    reduce_scatter x1, waiting for transfers between devices, per_device(): lax.psum_scatter(partial_value, 'col', scatter_dimension=1, tiled=True)  71.9 us
    dot_general x1, matrix products, per_device(): jnp.dot(sparse_amp, lax.all_gather(sparse_int, 'row', axis=1, tiled=True)...  13.2 us
    broadcast_in_dim x4, local copies, waits for them, and re-layouts, expand(): spread = jnp.repeat(jnp.repeat(mask, TILE, axis=0), TILE, axis=1)  10.4 us
  transfers between devices with their start and end apart: 2, of which 2 were waited for; matrix products, arithmetic and copies ran while one was open for 0% of the time, Pallas kernels for 0%

commit v1 on v0

v1 whole, which is shorter than its diff:
```python
import functools

import jax
import jax.numpy as jnp
from jax import lax
from jax.experimental import pallas as pl
from jax.experimental.pallas import tpu as pltpu
from jax.sharding import PartitionSpec as P

TILE = 128
VMEM_LIMIT = 48 * 1024 * 1024


def expand(mask):
    spread = jnp.repeat(jnp.repeat(mask, TILE, axis=0), TILE, axis=1)
    return spread.astype(jnp.bfloat16)


def dense_ladder(amplitudes, integrals, amp_mask, int_mask):
    sparse_amp = amplitudes * expand(amp_mask)
    sparse_int = integrals * expand(int_mask)
    partial_value = jnp.dot(
        sparse_amp,
        lax.all_gather(sparse_int, "row", axis=1, tiled=True),
        preferred_element_type=jnp.float32,
    )
    ladder = lax.psum_scatter(partial_value, "col", scatter_dimension=1, tiled=True)
    return ladder.astype(jnp.bfloat16)


def pack_tiles(integrals, flat_mask, cap):
    wide = integrals.shape[1] // TILE
    tiles = flat_mask.shape[1]

    def kernel(mask_ref, b_ref, out_ref):
        place = jnp.int32(0)
        for t in range(tiles):
            k, n = divmod(t, wide)
            keep = mask_ref[0, t] != 0

            @pl.when(keep & (place < cap))
            def _(k=k, n=n, place=place):
                at = pl.multiple_of(place * TILE, TILE)
                out_ref[pl.ds(at, TILE), :] = b_ref[k * TILE:(k + 1) * TILE, n * TILE:(n + 1) * TILE]

            place = place + keep.astype(jnp.int32)

    return pl.pallas_call(
        kernel,
        out_shape=jax.ShapeDtypeStruct((cap * TILE, TILE), integrals.dtype),
        in_specs=[pl.BlockSpec(memory_space=pltpu.SMEM), pl.BlockSpec(memory_space=pltpu.VMEM)],
        out_specs=pl.BlockSpec(memory_space=pltpu.VMEM),
        compiler_params=pltpu.CompilerParams(vmem_limit_bytes=VMEM_LIMIT),
        cost_estimate=pl.CostEstimate(flops=0, bytes_accessed=2 << 20, transcendentals=0),
        name="pack_tiles",
    )(flat_mask, integrals)


def mask_tiles(amplitudes, mask):
    rows, cols = amplitudes.shape

    def kernel(mask_ref, a_ref, out_ref):
        i = pl.program_id(0)
        for t in range(cols // TILE):
            at = slice(t * TILE, (t + 1) * TILE)
            tile = a_ref[:, at]
            out_ref[:, at] = jnp.where(mask_ref[i, t] != 0, tile, jnp.zeros_like(tile))

    block = pl.BlockSpec((TILE, cols), lambda i: (i, 0))
    return pl.pallas_call(
        kernel,
        grid=(rows // TILE,),
        out_shape=jax.ShapeDtypeStruct(amplitudes.shape, amplitudes.dtype),
        in_specs=[pl.BlockSpec(memory_space=pltpu.SMEM), block],
        out_specs=block,
        compiler_params=pltpu.CompilerParams(vmem_limit_bytes=VMEM_LIMIT),
        cost_estimate=pl.CostEstimate(flops=0, bytes_accessed=2 * amplitudes.size * 2, transcendentals=0),
        name="mask_tiles",
    )(mask, amplitudes)


def shard_product(amps, masks, pick, shard, choices):
    rows, depth = amps.shape
    tiles = masks.shape[1]
    wide = tiles * TILE // depth
    cap = sum(part.shape[0] for part in choices[0])
    parts = []
    for choice in choices:
        for part in choice:
            if not any(part is p for p in parts):
                parts.append(part)
    step = 256

    def kernel(pick_ref, masks_ref, a_ref, *rest):
        refs = rest[:len(parts)]
        out_ref, packed, wide_ref, sem = rest[len(parts):]

        @pl.when(pl.program_id(0) == 0)
        def _():
            for number, choice in enumerate(choices):
                @pl.when(pick_ref[0] == number)
                def _(choice=choice):
                    at = 0
                    copies = []
                    for part in choice:
                        index = [part is p for p in parts].index(True)
                        copies.append(pltpu.make_async_copy(
                            refs[index], packed.at[pl.ds(at, part.shape[0])], sem.at[len(copies)]))
                        at += part.shape[0]
                    for copy in copies:
                        copy.start()
                    for copy in copies:
                        copy.wait()

            place = jnp.int32(0)
            for t in range(tiles):
                k, n = divmod(t, wide)
                rows_at = slice(k * TILE, (k + 1) * TILE)
                cols_at = slice(n * TILE, (n + 1) * TILE)
                keep = masks_ref[pick_ref[1], t] != 0
                at = pl.multiple_of(jnp.minimum(place * TILE, cap - TILE), TILE)
                tile = packed[pl.ds(at, TILE), :]
                wide_ref[rows_at, cols_at] = jnp.where(keep, tile, jnp.zeros_like(tile))
                place = place + keep.astype(jnp.int32)

        out_ref[...] = jnp.dot(a_ref[...], wide_ref[...], preferred_element_type=jnp.float32)

    return pl.pallas_call(
        kernel,
        out_shape=jax.ShapeDtypeStruct((rows, wide * TILE), jnp.float32),
        grid_spec=pltpu.PrefetchScalarGridSpec(
            num_scalar_prefetch=2,
            grid=(rows // step,),
            in_specs=[pl.BlockSpec((step, depth), lambda i, *_: (i, 0))]
            + [pl.BlockSpec(memory_space=pl.ANY)] * len(parts),
            out_specs=pl.BlockSpec((step, wide * TILE), lambda i, *_: (i, 0)),
            scratch_shapes=[
                pltpu.VMEM((cap, TILE), amps.dtype),
                pltpu.VMEM((depth, wide * TILE), amps.dtype),
                pltpu.SemaphoreType.DMA((2,)),
            ],
        ),
        compiler_params=pltpu.CompilerParams(vmem_limit_bytes=VMEM_LIMIT),
        cost_estimate=pl.CostEstimate(
            flops=2 * rows * depth * wide * TILE, bytes_accessed=amps.size * 2 + (2 << 20), transcendentals=0),
        name="shard_product",
    )(jnp.stack([pick, shard]).astype(jnp.int32), masks, amps, *parts)


Z, X, Y = 4, 2, 2


def row_moves(to):
    return [(z * 2 + x, to(z, x)[0] * 2 + to(z, x)[1]) for z in range(Z) for x in range(X) if to(z, x) is not None]


ENDS, MIDDLE = (0, 3), (1, 2)
ACROSS_X = row_moves(lambda z, x: (z, 1 - x))
ACROSS_X_ENDS = row_moves(lambda z, x: (z, 1 - x) if z in ENDS else None)
ACROSS_X_MIDDLE = row_moves(lambda z, x: (z, 1 - x) if z in MIDDLE else None)
PAIR = row_moves(lambda z, x: (z ^ 1, x))
CENTRE = row_moves(lambda z, x: (3 - z, x) if z in MIDDLE else None)
OUTWARD = row_moves(lambda z, x: (z ^ 1, x) if z in MIDDLE else None)
CORES = [(0, 1), (1, 0), (2, 3), (3, 2)]


def across_y(far):
    pairs = []
    for z in range(Z):
        home = (z // 2) ^ int(far)
        for x in range(X):
            for c in range(2):
                row = z * 2 + x
                pairs.append((row * 4 + (1 - home) * 2 + c, row * 4 + home * 2 + c))
    return pairs


def sparse_ladder(amplitudes, integrals, amp_mask, int_mask):
    barrier = lax.optimization_barrier
    tiles = int_mask.size
    cap = tiles * 3 // 4
    row, col = lax.axis_index("row"), lax.axis_index("col")
    z, x = row // 2, row % 2
    y, c = col // 2, col % 2
    end = (z == 0) | (z == 3)

    flat_mask = int_mask.reshape(1, tiles)
    masks = lax.all_gather(flat_mask, "row", axis=0, tiled=True)
    most = jnp.max(jnp.sum((masks != 0).astype(jnp.int32), axis=1))
    too_many = jnp.max(lax.all_gather(most, "col", axis=0)) > cap

    own = pack_tiles(integrals, flat_mask, cap)
    amps = mask_tiles(amplitudes, amp_mask)

    move = lambda value, pairs: lax.ppermute(value, "row", pairs)
    half = cap * TILE // 2
    pair, centre, own_x = barrier((move(own, PAIR), move(own, CENTRE), move(own, ACROSS_X)))
    two_end, two_mid, pair_x = barrier((move(centre, OUTWARD), move(pair, CENTRE), move(pair, ACROSS_X)))
    three_end, three_mid_x, two_x_end, two_x_mid = barrier((
        move(two_mid, OUTWARD), move(own_x, CENTRE), move(two_end, ACROSS_X_ENDS), move(two_mid, ACROSS_X_MIDDLE)))
    three_x_end = (move(three_end[:half], ACROSS_X_ENDS), move(two_x_mid[half:], OUTWARD))

    product = functools.partial(shard_product, amps, masks)
    is_end = end.astype(jnp.int32)

    def stage(first, second, first_z, second_z, at_x, far):
        choices = first[0] + second[0]
        first_pick, second_pick = first[1], second[1] + len(first[0])
        keep_first = first_z % 2 == c
        send = product(
            jnp.where(keep_first, second_pick, first_pick), jnp.where(keep_first, second_z, first_z) * 2 + at_x, choices)
        got = lax.ppermute(send, "col", CORES)
        keep = product(
            jnp.where(keep_first, first_pick, second_pick), jnp.where(keep_first, first_z, second_z) * 2 + at_x, choices)
        total = keep + got
        return total, lax.ppermute(total, ("row", "col"), across_y(far))

    zero = jnp.int32(0)
    near_own = stage(([[own]], zero), ([[pair]], zero), z, z ^ 1, x, False)
    near_x = stage(([[own_x]], zero), ([[pair_x]], zero), z, z ^ 1, 1 - x, False)
    far_own = stage(
        ([[two_mid], [two_end]], is_end), ([[centre], [three_end]], is_end), z ^ 2, z ^ 3, x, True)
    far_x = stage(
        ([[two_x_mid], [two_x_end]], is_end), ([[three_mid_x], list(three_x_end)], is_end), z ^ 2, z ^ 3, 1 - x, True)

    near = z // 2 == y
    mine = jnp.where(near, near_own[0] + near_own[1], far_own[0] + far_own[1]).astype(jnp.bfloat16)
    other = jnp.where(near, near_x[0] + near_x[1], far_x[0] + far_x[1]).astype(jnp.bfloat16)
    ladder = jnp.concatenate([jnp.where(x == 0, mine, other), jnp.where(x == 0, other, mine)], axis=1)
    return lax.cond(
        too_many, lambda: dense_ladder(amplitudes, integrals, amp_mask, int_mask), lambda: ladder)


def solution(mesh):
    in_specs = (P("row", "col"), P("col", "row"), P("row", "col"), P("col", "row"))
    out_specs = P("row", "col")
    here = dict(mesh.shape)
    per_device = sparse_ladder if here == {"row": Z * X, "col": Y * 2} else dense_ladder
    return jax.shard_map(
        per_device, mesh=mesh, in_specs=in_specs, out_specs=out_specs, check_vma=False
    )
```

time: 241 us -> 218 us (0.905)
  the two profiles are of different devices: /device:TPU:24 before, /device:TPU:12 now
where the time goes in v1:
time: 218 us; the launch traced here: 217 us
  blocking collectives  57.4 us (26%)
  Pallas kernels  51.7 us (24%)
  starting transfers between devices  36.8 us (17%)
  waiting for transfers between devices  33.6 us (15%)
  between operations  14.6 us (7%)
  other arithmetic  13 us (6%)
  local copies, waits for them, and re-layouts  9.83 us (5%)
    pallas_call x8, Pallas kernels, shard_product(): pl.pallas_call(kernel, out_shape=jax.ShapeDtypeStruct((rows, wide * TILE)...  44.9 us
    unnamed x1, blocking collectives  42.6 us
    ppermute x12, waiting for transfers between devices, sparse_ladder(): move = lambda value, pairs: lax.ppermute(value, 'row', pairs)  33.5 us
    ppermute x12, starting transfers between devices, sparse_ladder(): move = lambda value, pairs: lax.ppermute(value, 'row', pairs)  26 us
    all_gather x1, blocking collectives, sparse_ladder(): masks = lax.all_gather(flat_mask, 'row', axis=0, tiled=True)  14.8 us
    unnamed x39, local copies, waits for them, and re-layouts  9.68 us
    ppermute x4, starting transfers between devices, stage(): return (total, lax.ppermute(total, ('row', 'col'), across_y(far)))  8.49 us
    add x4, other arithmetic, stage(): total = keep + got  7.46 us
  transfers between devices with their start and end apart: 20, of which 6 were waited for; matrix products, arithmetic and copies ran while one was open for 5% of the time, Pallas kernels for 23%

profile of v1, /device:TPU:12, one launch (start us, length us, event | category | flops | bytes accessed | tf_op | source)
XLA Modules:
  0.0 217.2 jit_solution(13957284003776561445)
XLA Ops:
  6.5 0.8 copy.16
  7.3 0.1 reshape.11.mask_ref
  7.4 1.6 pack_tiles.1.rest_0_
  9.0 1.6 collective-permute-start.2
  10.5 3.5 %collective-permute-start.1 = (bf16[3072,128]{1,0:T(8,128)(2,1)S(1)}, bf16[3072,128]{1,0:T(8,128)(2,1)S(1)}, u32[]{:S(2)}, u32[]{:S(2)}) collective-permute-start(bf16[3072,128]{1,0:T(8,128)(2,1)S(1)} %pack_tiles.1.rest_0_), channel_id=1, source_target_pairs={{8,16},{12,20},{16,8},{20,12},{9,17},{13,21},{17,9},{21,13},{10,18... | collective-permute-start | bytes 2359304 | tf_op jit(solution)/shard_map/ppermute | solution.py:195
  14.1 14.2 %collective-permute-done.2.rest_0_ = bf16[3072,128]{1,0:T(8,128)(2,1)S(1)} collective-permute-done((bf16[3072,128]{1,0:T(8,128)(2,1)S(1)}, bf16[3072,128]{1,0:T(8,128)(2,1)S(1)}, u32[]{:S(2)}, u32[]{:S(2)}) %collective-permute-start.2) | collective-permute-done | bytes 786464 | tf_op jit(solution)/shard_map/ppermute | solution.py:195
  28.3 3.1 %collective-permute-done.1.rest_2_ = bf16[3072,128]{1,0:T(8,128)(2,1)S(1)} collective-permute-done((bf16[3072,128]{1,0:T(8,128)(2,1)S(1)}, bf16[3072,128]{1,0:T(8,128)(2,1)S(1)}, u32[]{:S(2)}, u32[]{:S(2)}) %collective-permute-start.1) | collective-permute-done | bytes 786464 | tf_op jit(solution)/shard_map/ppermute | solution.py:195
  31.4 1.4 collective-permute-done.rest_1_
  32.8 3.1 %collective-permute-start.5 = (bf16[3072,128]{1,0:T(8,128)(2,1)S(1)}, bf16[3072,128]{1,0:T(8,128)(2,1)}, u32[]{:S(2)}, u32[]{:S(2)}) collective-permute-start(bf16[3072,128]{1,0:T(8,128)(2,1)S(1)} %collective-permute-done.1.rest_2_), channel_id=1, source_target_pairs={{8,0},{12,4},{16,24},{20,28},{9,1},{13,5},{17,25},{21,29},{10,2},{... | collective-permute-start | bytes 2359304 | tf_op jit(solution)/shard_map/ppermute | solution.py:195
  35.8 0.9 copy-done.7
  36.7 0.5 collective-permute-start.7
  37.3 2.4 %collective-permute-start.6 = (bf16[3072,128]{1,0:T(8,128)(2,1)S(1)}, bf16[3072,128]{1,0:T(8,128)(2,1)}, u32[]{:S(2)}, u32[]{:S(2)}) collective-permute-start(bf16[3072,128]{1,0:T(8,128)(2,1)S(1)} %collective-permute-done.rest_1_), channel_id=1, source_target_pairs={{8,16},{12,20},{16,8},{20,12},{9,17},{13,21},{17,9},{21,13},{10,18... | collective-permute-start | bytes 2359304 | tf_op jit(solution)/shard_map/ppermute | solution.py:195
  39.6 0.9 copy-done.1
  40.5 3.5 %collective-permute-start.9 = (bf16[3072,128]{1,0:T(8,128)(2,1)S(1)}, bf16[3072,128]{1,0:T(8,128)(2,1)}, u32[]{:S(2)}, u32[]{:S(2)}) collective-permute-start(bf16[3072,128]{1,0:T(8,128)(2,1)S(1)} %collective-permute-done.2.rest_0_), channel_id=1, source_target_pairs={{8,16},{12,20},{16,8},{20,12},{9,17},{13,21},{17,9},{21,13},{10,18... | collective-permute-start | bytes 2359304 | tf_op jit(solution)/shard_map/ppermute | solution.py:195
  44.0 6.5 %collective-permute-done.5.rest_1_ = bf16[3072,128]{1,0:T(8,128)(2,1)} collective-permute-done((bf16[3072,128]{1,0:T(8,128)(2,1)S(1)}, bf16[3072,128]{1,0:T(8,128)(2,1)}, u32[]{:S(2)}, u32[]{:S(2)}) %collective-permute-start.5) | collective-permute-done | bytes 786464 | tf_op jit(solution)/shard_map/ppermute | solution.py:195
  50.6 4.0 %collective-permute-done.7.rest_1_ = bf16[3072,128]{1,0:T(8,128)(2,1)S(1)} collective-permute-done((bf16[3072,128]{1,0:T(8,128)(2,1)S(1)}, bf16[3072,128]{1,0:T(8,128)(2,1)S(1)}, u32[]{:S(2)}, u32[]{:S(2)}) %collective-permute-start.7) | collective-permute-done | bytes 786464 | tf_op jit(solution)/shard_map/ppermute | solution.py:195
  54.6 0.9 copy-done.4
  55.4 4.3 %collective-permute-done.6.rest_0_ = bf16[3072,128]{1,0:T(8,128)(2,1)} collective-permute-done((bf16[3072,128]{1,0:T(8,128)(2,1)S(1)}, bf16[3072,128]{1,0:T(8,128)(2,1)}, u32[]{:S(2)}, u32[]{:S(2)}) %collective-permute-start.6) | collective-permute-done | bytes 786464 | tf_op jit(solution)/shard_map/ppermute | solution.py:195
  59.7 1.6 collective-permute-start.10
  61.3 3.4 %collective-permute-start.11 = (bf16[3072,128]{1,0:T(8,128)(2,1)}, bf16[3072,128]{1,0:T(8,128)(2,1)S(1)}, u32[]{:S(2)}, u32[]{:S(2)}) collective-permute-start(bf16[3072,128]{1,0:T(8,128)(2,1)} %collective-permute-done.6.rest_0_), channel_id=1, source_target_pairs={{8,12},{12,8},{16,20},{20,16},{9,13},{13,9},{17,21},{21,17},{10,14... | collective-permute-start | bytes 2359304 | tf_op jit(solution)/shard_map/ppermute | solution.py:195
  64.7 1.3 collective-permute-start.8
  66.2 0.1 reshape.15
  66.3 5.2 %mask_tiles.1.a_ref = bf16[1024,2048]{1,0:T(8,128)(2,1)S(1)} custom-call(s32[8,16]{1,0:T(8,128)} %mask_ref.1, bf16[1024,2048]{1,0:T(8,128)(2,1)} %a_ref.1), custom_call_target="tpu_custom_call" | custom-call | bytes 8388608 | tf_op jit(solution)/shard_map/mask_tiles/pallas_call | solution.py:70
  71.5 2.0 copy-done
  73.5 14.8 %all-gather = s32[8,1,32]{2,1,0:T(1,128)S(1)} all-gather(s32[1,1,32]{2,1,0:T(1,128)S(1)} %reshape.15), channel_id=1, replica_groups=mesh['row'=8,'col'=4] {'row'}, dimensions={0}, use_global_device_ids=true | all-gather | bytes 1152 | tf_op jit(solution)/shard_map/all_gather | solution.py:188
  88.3 0.1 pad_add_fusion.1.pick_ref
  88.3 0.1 pad_add_fusion.5.pick_ref
  88.4 0.1 pad_add_fusion.3.pick_ref
  88.6 4.4 %collective-permute-start.17 = (bf16[1536,128]{1,0:T(8,128)(2,1)S(1)}, bf16[1536,128]{1,0:T(8,128)(2,1)S(1)}, u32[]{:S(2)}, u32[]{:S(2)}) collective-permute-start(bf16[1536,128]{1,0:T(8,128)(2,1)S(1)} %slice.7), channel_id=1, source_target_pairs={{8,0},{12,4},{16,24},{20,28},{9,1},{13,5},{17,25},{21,29},{10,2},{... | collective-permute-start | bytes 1179656 | tf_op jit(solution)/shard_map/ppermute | solution.py:195
  93.0 0.7 collective-permute-start.16
  93.7 0.1 pad_add_fusion.7.pick_ref
  93.8 5.8 %shard_product.9 = f32[1024,256]{1,0:T(8,128)} custom-call(s32[2]{0:T(128)S(1)} %pad_add_fusion.1.pick_ref, s32[8,32]{1,0:T(8,128)S(1)} %bitcast.25, bf16[1024,2048]{1,0:T(8,128)(2,1)} %copy-done, bf16[3072,128]{1,0:T(8,128)(2,1)S(1)} %pack_tiles.1.rest_0_, bf16[3072,128]{1,0:T(8,128)(2,1)S(1)} %copy-done.2), custom_call_target="tpu_custom_call" | custom-call | flops 1073741824 | bytes 6291456 | tf_op jit(solution)/shard_map/shard_product/pallas_call | solution.py:128
  99.7 5.8 %shard_product.13 = f32[1024,256]{1,0:T(8,128)} custom-call(s32[2]{0:T(128)S(1)} %pad_add_fusion.5.pick_ref, s32[8,32]{1,0:T(8,128)S(1)} %bitcast.26, bf16[1024,2048]{1,0:T(8,128)(2,1)} %copy-done, bf16[3072,128]{1,0:T(8,128)(2,1)S(1)} %collective-permute-done.2.rest_0_, bf16[3072,128]{1,0:T(8,128)(2,1)S(1)} %copy-done.5), custom_call_target="tpu_custom_call" | custom-call | flops 1073741824 | bytes 6291456 | tf_op jit(solution)/shard_map/shard_product/pallas_call | solution.py:128
  105.5 0.5 collective-permute-start.14
  106.1 6.9 %shard_product.11 = f32[1024,256]{1,0:T(8,128)} custom-call(s32[2]{0:T(128)S(1)} %pad_add_fusion.3.pick_ref, s32[8,32]{1,0:T(8,128)S(1)} %bitcast.27, bf16[1024,2048]{1,0:T(8,128)(2,1)} %copy-done, bf16[3072,128]{1,0:T(8,128)(2,1)} %collective-permute-done.6.rest_0_, bf16[3072,128]{1,0:T(8,128)(2,1)} %collective-permute-done.5.rest_1_, ...), custom_call_target="tpu_custom_call" | custom-call | flops 1073741824 | bytes 6291456 | tf_op jit(solution)/shard_map/shard_product/pallas_call | solution.py:128
  113.1 5.8 %shard_product.15 = f32[1024,256]{1,0:T(8,128)} custom-call(s32[2]{0:T(128)S(1)} %pad_add_fusion.7.pick_ref, s32[8,32]{1,0:T(8,128)S(1)} %bitcast.28, bf16[1024,2048]{1,0:T(8,128)(2,1)} %copy-done, bf16[3072,128]{1,0:T(8,128)(2,1)S(1)} %collective-permute-done.11.rest_0_, bf16[3072,128]{1,0:T(8,128)(2,1)} %collective-permute-done.10.rest_1_, ...), custom_call_target="tpu_custom_call" | custom-call | flops 1073741824 | bytes 6291456 | tf_op jit(solution)/shard_map/shard_product/pallas_call | solution.py:128
  119.0 1.7 collective-permute-start.18
  120.6 0.1 pad_add_fusion.pick_ref
  120.7 0.1 pad_add_fusion.4.pick_ref
  120.8 0.1 pad_add_fusion.2.pick_ref
  120.9 0.1 pad_add_fusion.6.pick_ref
  120.9 1.1 copy-done.3
  122.1 4.8 %shard_product.8 = f32[1024,256]{1,0:T(8,128)S(1)} custom-call(s32[2]{0:T(128)S(1)} %pad_add_fusion.pick_ref, s32[8,32]{1,0:T(8,128)S(1)} %bitcast.29, bf16[1024,2048]{1,0:T(8,128)(2,1)} %copy-done, bf16[3072,128]{1,0:T(8,128)(2,1)S(1)} %pack_tiles.1.rest_0_, bf16[3072,128]{1,0:T(8,128)(2,1)S(1)} %copy-done.3), custom_call_target="tpu_custom_call" | custom-call | flops 1073741824 | bytes 6291456 | tf_op jit(solution)/shard_map/shard_product/pallas_call | solution.py:128
  126.9 4.9 %shard_product.12 = f32[1024,256]{1,0:T(8,128)S(1)} custom-call(s32[2]{0:T(128)S(1)} %pad_add_fusion.4.pick_ref, s32[8,32]{1,0:T(8,128)S(1)} %bitcast.30, bf16[1024,2048]{1,0:T(8,128)(2,1)} %copy-done, bf16[3072,128]{1,0:T(8,128)(2,1)S(1)} %collective-permute-done.2.rest_0_, bf16[3072,128]{1,0:T(8,128)(2,1)S(1)} %copy-done.6), custom_call_target="tpu_custom_call" | custom-call | flops 1073741824 | bytes 6291456 | tf_op jit(solution)/shard_map/shard_product/pallas_call | solution.py:128
  131.8 2.3 %add.77 = f32[1024,256]{1,0:T(8,128)} add(f32[1024,256]{1,0:T(8,128)S(1)} %shard_product.8, f32[1024,256]{1,0:T(8,128)} %collective-permute-done.3) | non-fusion elementwise | flops 262144 | bytes 3145728 | tf_op jit(solution)/shard_map/add | solution.py:215
  134.2 3.5 %collective-permute-start.4 = (f32[1024,256]{1,0:T(8,128)}, f32[1024,256]{1,0:T(8,128)}, u32[]{:S(2)}, u32[]{:S(2)}) collective-permute-start(f32[1024,256]{1,0:T(8,128)} %add.77), channel_id=1, source_target_pairs={{2,0},{3,1},{6,4},{7,5},{10,8},{11,9},{14,12},{15,13},{16,18},{17,... | collective-permute-start | bytes 3145736 | tf_op jit(solution)/shard_map/ppermute | solution.py:216
  137.7 4.9 %shard_product.10 = f32[1024,256]{1,0:T(8,128)S(1)} custom-call(s32[2]{0:T(128)S(1)} %pad_add_fusion.2.pick_ref, s32[8,32]{1,0:T(8,128)S(1)} %bitcast.31, bf16[1024,2048]{1,0:T(8,128)(2,1)} %copy-done, bf16[3072,128]{1,0:T(8,128)(2,1)} %collective-permute-done.6.rest_0_, bf16[3072,128]{1,0:T(8,128)(2,1)} %collective-permute-done.5.rest_1_, ...), custom_call_target="tpu_custom_call" | custom-call | flops 1073741824 | bytes 6291456 | tf_op jit(solution)/shard_map/shard_product/pallas_call | solution.py:128
  142.6 2.4 %add.87 = f32[1024,256]{1,0:T(8,128)} add(f32[1024,256]{1,0:T(8,128)S(1)} %shard_product.12, f32[1024,256]{1,0:T(8,128)} %collective-permute-done.14) | non-fusion elementwise | flops 262144 | bytes 3145728 | tf_op jit(solution)/shard_map/add | solution.py:215
  145.0 2.4 %collective-permute-start.15 = (f32[1024,256]{1,0:T(8,128)}, f32[1024,256]{1,0:T(8,128)}, u32[]{:S(2)}, u32[]{:S(2)}) collective-permute-start(f32[1024,256]{1,0:T(8,128)} %add.87), channel_id=1, source_target_pairs={{2,0},{3,1},{6,4},{7,5},{10,8},{11,9},{14,12},{15,13},{16,18},{17,... | collective-permute-start | bytes 3145736 | tf_op jit(solution)/shard_map/ppermute | solution.py:216
  147.3 6.0 %shard_product.14 = f32[1024,256]{1,0:T(8,128)S(1)} custom-call(s32[2]{0:T(128)S(1)} %pad_add_fusion.6.pick_ref, s32[8,32]{1,0:T(8,128)S(1)} %bitcast.32, bf16[1024,2048]{1,0:T(8,128)(2,1)} %copy-done, bf16[3072,128]{1,0:T(8,128)(2,1)S(1)} %collective-permute-done.11.rest_0_, bf16[3072,128]{1,0:T(8,128)(2,1)} %collective-permute-done.10.rest_1_, ...), custom_call_target="tpu_custom_call" | custom-call | flops 1073741824 | bytes 6291456 | tf_op jit(solution)/shard_map/shard_product/pallas_call | solution.py:128
  153.4 1.4 add.83
  154.7 1.3 collective-permute-start.13
  156.0 1.4 add.91
  157.4 1.3 collective-permute-start.19
  158.7 0.7 dynamic-slice
  159.4 0.1 convert_reduce_fusion
  159.5 0.6 reduce_max.18
  160.1 1.4 dynamic-update-slice
  161.5 42.6 %all-reduce = s32[4]{0:T(128)S(1)} all-reduce(s32[4]{0:T(128)S(1)} %dynamic-update-slice), channel_id=1, replica_groups=mesh['row'=8,'col'=4] {'col'}, use_global_device_ids=true, to_apply=%add | all-reduce | flops 4 | bytes 32
  204.1 0.6 reduce_max.19
  205.5 3.5 %broadcast_select_fusion.1 = (bf16[1024,256]{1,0:T(8,128)(2,1)S(1)}, bf16[1024,256]{1,0:T(8,128)(2,1)S(1)}, bf16[1024,256]{1,0:T(8,128)(2,1)S(1)}) fusion(pred[]{:T(512)S(6)} %eq.28, f32[1024,256]{1,0:T(8,128)S(1)} %add.83, f32[1024,256]{1,0:T(8,128)} %collective-permute-done.13, f32[1024,256]{1,0:T(8,128)} %add.77, f32[1024,256]{1,0:T(8,128)} %collective-permute-done.4, ...), kind=kLoop, calls=%fused_computation.8 | loop fusion | flops 2359296 | bytes 9961474 | tf_op jit(solution)/shard_map/jit(_where)/select_n | solution.py:229
  209.1 0.1 pad_maximum_fusion
  209.1 0.2 conditional.1
  209.4 1.0 copy-done.14
  (49 shorter events, 0.4 us)
Async XLA Ops:
  9.0 19.3 %collective-permute-start.2 = (bf16[3072,128]{1,0:T(8,128)(2,1)S(1)}, bf16[3072,128]{1,0:T(8,128)(2,1)S(1)}, u32[]{:S(2)}, u32[]{:S(2)}) collective-permute-start(bf16[3072,128]{1,0:T(8,128)(2,1)S(1)} %pack_tiles.1.rest_0_), channel_id=1, source_target_pairs={{0,4},{4,0},{8,12},{12,8},{16,20},{20,16},{24,28},{28,24},{1,5},{5... | collective-permute-start | bytes 2359304 | tf_op jit(solution)/shard_map/ppermute | solution.py:195
  10.5 20.9 %collective-permute-start.1 = (bf16[3072,128]{1,0:T(8,128)(2,1)S(1)}, bf16[3072,128]{1,0:T(8,128)(2,1)S(1)}, u32[]{:S(2)}, u32[]{:S(2)}) collective-permute-start(bf16[3072,128]{1,0:T(8,128)(2,1)S(1)} %pack_tiles.1.rest_0_), channel_id=1, source_target_pairs={{8,16},{12,20},{16,8},{20,12},{9,17},{13,21},{17,9},{21,13},{10,18... | collective-permute-start | bytes 2359304 | tf_op jit(solution)/shard_map/ppermute | solution.py:195
  14.0 18.8 %collective-permute-start = (bf16[3072,128]{1,0:T(8,128)(2,1)S(1)}, bf16[3072,128]{1,0:T(8,128)(2,1)S(1)}, u32[]{:S(2)}, u32[]{:S(2)}) collective-permute-start(bf16[3072,128]{1,0:T(8,128)(2,1)S(1)} %pack_tiles.1.rest_0_), channel_id=1, source_target_pairs={{0,8},{4,12},{8,0},{12,4},{16,24},{20,28},{24,16},{28,20},{1,9},{5... | collective-permute-start | bytes 2359304 | tf_op jit(solution)/shard_map/ppermute | solution.py:195
  32.8 17.8 %collective-permute-start.5 = (bf16[3072,128]{1,0:T(8,128)(2,1)S(1)}, bf16[3072,128]{1,0:T(8,128)(2,1)}, u32[]{:S(2)}, u32[]{:S(2)}) collective-permute-start(bf16[3072,128]{1,0:T(8,128)(2,1)S(1)} %collective-permute-done.1.rest_2_), channel_id=1, source_target_pairs={{8,0},{12,4},{16,24},{20,28},{9,1},{13,5},{17,25},{21,29},{10,2},{... | collective-permute-start | bytes 2359304 | tf_op jit(solution)/shard_map/ppermute | solution.py:195
  35.8 0.9 copy-start.7
  36.7 17.8 %collective-permute-start.7 = (bf16[3072,128]{1,0:T(8,128)(2,1)S(1)}, bf16[3072,128]{1,0:T(8,128)(2,1)S(1)}, u32[]{:S(2)}, u32[]{:S(2)}) collective-permute-start(bf16[3072,128]{1,0:T(8,128)(2,1)S(1)} %collective-permute-done.rest_1_), channel_id=1, source_target_pairs={{0,4},{4,0},{8,12},{12,8},{16,20},{20,16},{24,28},{28,24},{1,5},{5... | collective-permute-start | bytes 2359304 | tf_op jit(solution)/shard_map/ppermute | solution.py:195
  37.3 22.5 %collective-permute-start.6 = (bf16[3072,128]{1,0:T(8,128)(2,1)S(1)}, bf16[3072,128]{1,0:T(8,128)(2,1)}, u32[]{:S(2)}, u32[]{:S(2)}) collective-permute-start(bf16[3072,128]{1,0:T(8,128)(2,1)S(1)} %collective-permute-done.rest_1_), channel_id=1, source_target_pairs={{8,16},{12,20},{16,8},{20,12},{9,17},{13,21},{17,9},{21,13},{10,18... | collective-permute-start | bytes 2359304 | tf_op jit(solution)/shard_map/ppermute | solution.py:195
  39.6 0.9 copy-start.1
  40.5 47.9 %collective-permute-start.9 = (bf16[3072,128]{1,0:T(8,128)(2,1)S(1)}, bf16[3072,128]{1,0:T(8,128)(2,1)}, u32[]{:S(2)}, u32[]{:S(2)}) collective-permute-start(bf16[3072,128]{1,0:T(8,128)(2,1)S(1)} %collective-permute-done.2.rest_0_), channel_id=1, source_target_pairs={{8,16},{12,20},{16,8},{20,12},{9,17},{13,21},{17,9},{21,13},{10,18... | collective-permute-start | bytes 2359304 | tf_op jit(solution)/shard_map/ppermute | solution.py:195
  54.6 0.9 copy-start.4
  59.7 28.8 %collective-permute-start.10 = (bf16[3072,128]{1,0:T(8,128)(2,1)}, bf16[3072,128]{1,0:T(8,128)(2,1)}, u32[]{:S(2)}, u32[]{:S(2)}) collective-permute-start(bf16[3072,128]{1,0:T(8,128)(2,1)} %collective-permute-done.5.rest_1_), channel_id=1, source_target_pairs={{0,4},{4,0},{24,28},{28,24},{1,5},{5,1},{25,29},{29,25},{2,6},{6,2... | collective-permute-start | bytes 2359304 | tf_op jit(solution)/shard_map/ppermute | solution.py:195
  61.3 27.2 %collective-permute-start.11 = (bf16[3072,128]{1,0:T(8,128)(2,1)}, bf16[3072,128]{1,0:T(8,128)(2,1)S(1)}, u32[]{:S(2)}, u32[]{:S(2)}) collective-permute-start(bf16[3072,128]{1,0:T(8,128)(2,1)} %collective-permute-done.6.rest_0_), channel_id=1, source_target_pairs={{8,12},{12,8},{16,20},{20,16},{9,13},{13,9},{17,21},{21,17},{10,14... | collective-permute-start | bytes 2359304 | tf_op jit(solution)/shard_map/ppermute | solution.py:195
  64.7 23.8 %collective-permute-start.8 = (bf16[3072,128]{1,0:T(8,128)(2,1)}, bf16[3072,128]{1,0:T(8,128)(2,1)S(1)}, u32[]{:S(2)}, u32[]{:S(2)}) collective-permute-start(bf16[3072,128]{1,0:T(8,128)(2,1)} %collective-permute-done.6.rest_0_), channel_id=1, source_target_pairs={{8,0},{12,4},{16,24},{20,28},{9,1},{13,5},{17,25},{21,29},{10,2},{... | collective-permute-start | bytes 2359304 | tf_op jit(solution)/shard_map/ppermute | solution.py:195
  66.3 27.5 %copy-start.2 = (bf16[3072,128]{1,0:T(8,128)(2,1)S(1)}, bf16[3072,128]{1,0:T(8,128)(2,1)}, u32[]{:S(2)}) copy-start(bf16[3072,128]{1,0:T(8,128)(2,1)} %copy-done.1) | copy-start | bytes 2359300
  71.5 2.0 copy-start
  88.5 11.2 %copy-start.5 = (bf16[3072,128]{1,0:T(8,128)(2,1)S(1)}, bf16[3072,128]{1,0:T(8,128)(2,1)}, u32[]{:S(2)}) copy-start(bf16[3072,128]{1,0:T(8,128)(2,1)} %copy-done.4) | copy-start | bytes 2359300
  88.6 24.5 %collective-permute-start.17 = (bf16[1536,128]{1,0:T(8,128)(2,1)S(1)}, bf16[1536,128]{1,0:T(8,128)(2,1)S(1)}, u32[]{:S(2)}, u32[]{:S(2)}) collective-permute-start(bf16[1536,128]{1,0:T(8,128)(2,1)S(1)} %slice.7), channel_id=1, source_target_pairs={{8,0},{12,4},{16,24},{20,28},{9,1},{13,5},{17,25},{21,29},{10,2},{... | collective-permute-start | bytes 1179656 | tf_op jit(solution)/shard_map/ppermute | solution.py:195
  93.0 20.1 %collective-permute-start.16 = (bf16[1536,128]{1,0:T(8,128)(2,1)S(1)}, bf16[1536,128]{1,0:T(8,128)(2,1)S(1)}, u32[]{:S(2)}, u32[]{:S(2)}) collective-permute-start(bf16[1536,128]{1,0:T(8,128)(2,1)S(1)} %slice.6), channel_id=1, source_target_pairs={{0,4},{4,0},{24,28},{28,24},{1,5},{5,1},{25,29},{29,25},{2,6},{6,2... | collective-permute-start | bytes 1179656 | tf_op jit(solution)/shard_map/ppermute | solution.py:195
  99.6 6.5 %copy-start.8 = (bf16[3072,128]{1,0:T(8,128)(2,1)S(1)}, bf16[3072,128]{1,0:T(8,128)(2,1)}, u32[]{:S(2)}) copy-start(bf16[3072,128]{1,0:T(8,128)(2,1)} %copy-done.7) | copy-start | bytes 2359300
  99.6 32.2 %collective-permute-start.3 = (f32[1024,256]{1,0:T(8,128)}, f32[1024,256]{1,0:T(8,128)}, u32[]{:S(2)}, u32[]{:S(2)}) collective-permute-start(f32[1024,256]{1,0:T(8,128)} %shard_product.9), channel_id=1, source_target_pairs={{0,1},{1,0},{2,3},{3,2},{4,5},{5,4},{6,7},{7,6},{8,9},{9,8},{10,11... | collective-permute-start | bytes 3145736 | tf_op jit(solution)/shard_map/ppermute | solution.py:212
  105.5 37.1 %collective-permute-start.14 = (f32[1024,256]{1,0:T(8,128)}, f32[1024,256]{1,0:T(8,128)}, u32[]{:S(2)}, u32[]{:S(2)}) collective-permute-start(f32[1024,256]{1,0:T(8,128)} %shard_product.13), channel_id=1, source_target_pairs={{0,1},{1,0},{2,3},{3,2},{4,5},{5,4},{6,7},{7,6},{8,9},{9,8},{10,11... | collective-permute-start | bytes 3145736 | tf_op jit(solution)/shard_map/ppermute | solution.py:212
  113.0 40.4 %collective-permute-start.12 = (f32[1024,256]{1,0:T(8,128)}, f32[1024,256]{1,0:T(8,128)}, u32[]{:S(2)}, u32[]{:S(2)}) collective-permute-start(f32[1024,256]{1,0:T(8,128)} %shard_product.11), channel_id=1, source_target_pairs={{0,1},{1,0},{2,3},{3,2},{4,5},{5,4},{6,7},{7,6},{8,9},{9,8},{10,11... | collective-permute-start | bytes 3145736 | tf_op jit(solution)/shard_map/ppermute | solution.py:212
  113.1 5.8 %copy-start.10 = (bf16[1536,128]{1,0:T(8,128)(2,1)}, bf16[1536,128]{1,0:T(8,128)(2,1)S(1)}, u32[]{:S(2)}) copy-start(bf16[1536,128]{1,0:T(8,128)(2,1)S(1)} %collective-permute-done.16.rest_3_) | copy-start | bytes 1179652
  119.0 37.1 %collective-permute-start.18 = (f32[1024,256]{1,0:T(8,128)}, f32[1024,256]{1,0:T(8,128)}, u32[]{:S(2)}, u32[]{:S(2)}) collective-permute-start(f32[1024,256]{1,0:T(8,128)} %shard_product.15), channel_id=1, source_target_pairs={{0,1},{1,0},{2,3},{3,2},{4,5},{5,4},{6,7},{7,6},{8,9},{9,8},{10,11... | collective-permute-start | bytes 3145736 | tf_op jit(solution)/shard_map/ppermute | solution.py:212
  120.9 1.1 copy-start.3
  122.1 4.9 %copy-start.6 = (bf16[3072,128]{1,0:T(8,128)(2,1)S(1)}, bf16[3072,128]{1,0:T(8,128)(2,1)}, u32[]{:S(2)}) copy-start(bf16[3072,128]{1,0:T(8,128)(2,1)} %copy-done.4) | copy-start | bytes 2359300
  126.9 10.8 %copy-start.9 = (bf16[3072,128]{1,0:T(8,128)(2,1)S(1)}, bf16[3072,128]{1,0:T(8,128)(2,1)}, u32[]{:S(2)}) copy-start(bf16[3072,128]{1,0:T(8,128)(2,1)} %copy-done.7) | copy-start | bytes 2359300
  134.2 13.2 %copy-start.11 = (bf16[1536,128]{1,0:T(8,128)(2,1)S(1)}, bf16[1536,128]{1,0:T(8,128)(2,1)}, u32[]{:S(2)}) copy-start(bf16[1536,128]{1,0:T(8,128)(2,1)} %copy-done.10) | copy-start | bytes 1179652
  134.2 71.3 %collective-permute-start.4 = (f32[1024,256]{1,0:T(8,128)}, f32[1024,256]{1,0:T(8,128)}, u32[]{:S(2)}, u32[]{:S(2)}) collective-permute-start(f32[1024,256]{1,0:T(8,128)} %add.77), channel_id=1, source_target_pairs={{2,0},{3,1},{6,4},{7,5},{10,8},{11,9},{14,12},{15,13},{16,18},{17,... | collective-permute-start | bytes 3145736 | tf_op jit(solution)/shard_map/ppermute | solution.py:216
  145.0 60.5 %collective-permute-start.15 = (f32[1024,256]{1,0:T(8,128)}, f32[1024,256]{1,0:T(8,128)}, u32[]{:S(2)}, u32[]{:S(2)}) collective-permute-start(f32[1024,256]{1,0:T(8,128)} %add.87), channel_id=1, source_target_pairs={{2,0},{3,1},{6,4},{7,5},{10,8},{11,9},{14,12},{15,13},{16,18},{17,... | collective-permute-start | bytes 3145736 | tf_op jit(solution)/shard_map/ppermute | solution.py:216
  153.4 5.4 %copy-start.17 = (u32[32]{0:T(128)S(1)}, u32[32]{0:T(128)}, u32[]{:S(2)}) copy-start(u32[32]{0:T(128)} %constant.75) | copy-start | bytes 388
  154.7 50.7 %collective-permute-start.13 = (f32[1024,256]{1,0:T(8,128)S(1)}, f32[1024,256]{1,0:T(8,128)}, u32[]{:S(2)}, u32[]{:S(2)}) collective-permute-start(f32[1024,256]{1,0:T(8,128)S(1)} %add.83), channel_id=1, source_target_pairs={{0,2},{1,3},{4,6},{5,7},{8,10},{9,11},{12,14},{13,15},{18,16},{19,... | collective-permute-start | bytes 3145736 | tf_op jit(solution)/shard_map/ppermute | solution.py:216
  157.4 48.1 %collective-permute-start.19 = (f32[1024,256]{1,0:T(8,128)S(1)}, f32[1024,256]{1,0:T(8,128)}, u32[]{:S(2)}, u32[]{:S(2)}) collective-permute-start(f32[1024,256]{1,0:T(8,128)S(1)} %add.91), channel_id=1, source_target_pairs={{0,2},{1,3},{4,6},{5,7},{8,10},{9,11},{12,14},{13,15},{18,16},{19,... | collective-permute-start | bytes 3145736 | tf_op jit(solution)/shard_map/ppermute | solution.py:216
  205.4 3.6 %copy-start.12 = (bf16[2048,256]{1,0:T(8,128)(2,1)S(1)}, bf16[2048,256]{1,0:T(8,128)(2,1)}, u32[]{:S(2)}) copy-start(bf16[2048,256]{1,0:T(8,128)(2,1)} %b_ref.1) | copy-start | bytes 3145732
  205.4 3.6 %copy-start.15 = (s32[8,16]{1,0:T(8,128)S(1)}, s32[8,16]{1,0:T(8,128)}, u32[]{:S(2)}) copy-start(s32[8,16]{1,0:T(8,128)} %mask_ref.1) | copy-start | bytes 1540
  205.4 3.6 %copy-start.16 = (s32[16,2]{0,1:T(2,128)S(1)}, s32[16,2]{0,1:T(2,128)}, u32[]{:S(2)}) copy-start(s32[16,2]{0,1:T(2,128)} %param.9) | copy-start | bytes 388
  209.4 1.0 copy-start.14

commit v2 on v0

v2 whole, which is shorter than its diff:
```python
import jax
import jax.numpy as jnp
from jax import lax
from jax.experimental import pallas as pl
from jax.experimental.pallas import tpu as pltpu
from jax.sharding import PartitionSpec as P

TILE = 128
VMEM_LIMIT = 12 * 1024 * 1024


def expand(mask):
    spread = jnp.repeat(jnp.repeat(mask, TILE, axis=0), TILE, axis=1)
    return spread.astype(jnp.bfloat16)


def dense_ladder(amplitudes, integrals, amp_mask, int_mask):
    rows, cols = lax.axis_size("row"), lax.axis_size("col")
    row, col = lax.axis_index("row"), lax.axis_index("col")
    sparse_amp = amplitudes * expand(amp_mask)
    sparse_int = integrals * expand(int_mask)
    width = integrals.shape[1]
    share = rows * width // cols
    sums = jnp.zeros((amplitudes.shape[0], rows * width), jnp.float32)
    for step in range(rows):
        shard = lax.ppermute(sparse_int, "row", [((r + step) % rows, r) for r in range(rows)]) if step else sparse_int
        part = jnp.dot(sparse_amp, shard, preferred_element_type=jnp.float32)
        sums = lax.dynamic_update_slice(sums, part, (0, (row + step) % rows * width))
    ladder = lax.dynamic_slice(sums, (0, col * share), (sums.shape[0], share))
    for step in range(1, cols):
        part = lax.dynamic_slice(sums, (0, (col + step) % cols * share), (sums.shape[0], share))
        ladder = ladder + lax.ppermute(part, "col", [(c, (c + step) % cols) for c in range(cols)])
    return ladder.astype(jnp.bfloat16)


TOKEN = jax.ShapeDtypeStruct((8, TILE), jnp.float32)
LIGHT = pl.CostEstimate(flops=1, bytes_accessed=1, transcendentals=0)
META = 16


def in_hbm(array):
    return pltpu.with_memory_space_constraint(array, pltpu.HBM)


def call(kernel, name, **kwargs):
    return pl.pallas_call(
        kernel,
        compiler_params=pltpu.CompilerParams(vmem_limit_bytes=VMEM_LIMIT),
        cost_estimate=LIGHT,
        name=name,
        **kwargs,
    )


VMEM = pl.BlockSpec(memory_space=pltpu.VMEM)
SMEM = pl.BlockSpec(memory_space=pltpu.SMEM)
ANY = pl.BlockSpec(memory_space=pl.ANY)


def pack_tiles(shards, masks, across_masks, cap):
    wide = shards[0].shape[1] // TILE
    tiles = masks[0].shape[0]
    count = len(shards)

    def kernel(*refs):
        mask_refs, across_refs, b_refs, out_ref = refs[:count], refs[count:2 * count], refs[2 * count:-1], refs[-1]
        place = across = jnp.int32(0)
        lane = lax.broadcasted_iota(jnp.int32, (META, TILE), 1)
        sub = lax.broadcasted_iota(jnp.int32, (META, TILE), 0)
        meta = jnp.zeros((META, TILE), jnp.float32)
        for s in range(count):
            for t in range(tiles):
                k, n = divmod(t, wide)
                keep = mask_refs[s][t] != 0

                @pl.when(keep & (place < cap))
                def _(s=s, k=k, n=n, place=place):
                    at = pl.multiple_of(place * TILE, TILE)
                    out_ref[pl.ds(at, TILE), :] = b_refs[s][k * TILE:(k + 1) * TILE, n * TILE:(n + 1) * TILE]

                place = place + keep.astype(jnp.int32)
                across = across + (across_refs[s][t] != 0).astype(jnp.int32)
                meta = jnp.where((lane == s * tiles + t) & keep, 1.0, meta)
        more = jnp.maximum(place, across) > cap
        meta = jnp.where(sub == 0, meta, jnp.where((sub == 1) & more, 1.0, 0.0))
        out_ref[cap * TILE:, :] = meta.astype(out_ref.dtype)

    return call(
        kernel, "pack_tiles",
        out_shape=jax.ShapeDtypeStruct((cap * TILE + META, TILE), shards[0].dtype),
        in_specs=[SMEM] * (2 * count) + [VMEM] * count,
        out_specs=VMEM,
    )(*masks, *across_masks, *shards)


def mask_tiles(amplitudes, mask):
    rows, cols = amplitudes.shape
    step = 2

    def kernel(mask_ref, a_ref, out_ref, token_ref):
        i = pl.program_id(0)
        token_ref[...] = jnp.zeros_like(token_ref)
        for r in range(step):
            for t in range(cols // TILE):
                spot = (slice(r * TILE, (r + 1) * TILE), slice(t * TILE, (t + 1) * TILE))
                keep = mask_ref[i * step + r, t] != 0

                @pl.when(keep)
                def _(spot=spot):
                    out_ref[spot] = a_ref[spot]

                @pl.when(jnp.logical_not(keep))
                def _(spot=spot):
                    out_ref[spot] = jnp.zeros((TILE, TILE), out_ref.dtype)

    block = pl.BlockSpec((step * TILE, cols), lambda i: (i, 0))
    return call(
        kernel, "mask_tiles",
        grid=(rows // TILE // step,),
        out_shape=(jax.ShapeDtypeStruct(amplitudes.shape, amplitudes.dtype), TOKEN),
        in_specs=[SMEM, block],
        out_specs=(block, pl.BlockSpec(TOKEN.shape, lambda i: (0, 0))),
    )(mask, amplitudes)


def shard_product(amps, picks, step, choices, tokens):
    rows, depth = amps[0].shape
    count = len(amps)
    height = sum(part.shape[0] for part in choices[0])
    cap = height - META
    wide = 2
    tiles = count * wide * depth // TILE
    word = 16
    parts = []
    for choice in choices:
        for part in choice:
            if not any(part is p for p in parts):
                parts.append(part)

    def kernel(picks_ref, *refs):
        token_refs, refs = refs[:len(tokens)], refs[len(tokens):]
        a_refs, refs = refs[:count], refs[count:]
        p_any, refs = refs[:len(parts)], refs[len(parts):]
        out_ref, token_ref, packed, wide_ref, sem = refs
        pick = picks_ref[step]
        token_ref[...] = sum(ref[...] for ref in token_refs)
        for number, choice in enumerate(choices):
            @pl.when(pick == number)
            def _(choice=choice):
                at = 0
                copies = []
                for part in choice:
                    index = [part is p for p in parts].index(True)
                    copies.append(pltpu.make_async_copy(
                        p_any[index], packed.at[pl.ds(at, part.shape[0])], sem.at[len(copies)]))
                    at += part.shape[0]
                for copy in copies:
                    copy.start()
                for copy in copies:
                    copy.wait()

        @pl.when(pick >= 0)
        def _():
            meta = packed[cap:, :].astype(jnp.float32)
            lane = lax.broadcasted_iota(jnp.int32, meta.shape, 1)
            sub = lax.broadcasted_iota(jnp.int32, meta.shape, 0)
            first = (sub == 0) & (meta != 0)
            bits = [
                jnp.sum(jnp.where(
                    first & (lane >= lo) & (lane < lo + word), jnp.left_shift(1, (lane - lo) & (word - 1)), 0))
                for lo in range(0, tiles, word)]
            token_ref[...] += jnp.where(sub == 1, meta, 0.0)[:token_ref.shape[0]]
            place = jnp.int32(0)
            for s in range(count):
                for t in range(s * tiles // count, (s + 1) * tiles // count):
                    k, n = divmod(t, wide)
                    keep = ((bits[t // word] >> (t % word)) & 1) != 0
                    at = pl.multiple_of(jnp.minimum(place * TILE, cap - TILE), TILE)
                    tile = packed[pl.ds(at, TILE), :]
                    wide_ref[k * TILE:(k + 1) * TILE, n * TILE:(n + 1) * TILE] = jnp.where(
                        keep, tile, jnp.zeros_like(tile))
                    place = place + keep.astype(jnp.int32)
                term = jnp.dot(
                    a_refs[s][...], wide_ref[s * depth:(s + 1) * depth, :], preferred_element_type=jnp.float32)
                if s:
                    out_ref[...] += term
                else:
                    out_ref[...] = term

    return call(
        kernel, "shard_product",
        out_shape=(jax.ShapeDtypeStruct((rows, wide * TILE), jnp.float32), TOKEN),
        in_specs=[SMEM] + [VMEM] * (len(tokens) + count) + [ANY] * len(parts),
        out_specs=(VMEM, VMEM),
        scratch_shapes=[
            pltpu.VMEM((height, TILE), amps[0].dtype),
            pltpu.VMEM((count * depth, wide * TILE), amps[0].dtype),
            pltpu.SemaphoreType.DMA((2,)),
        ],
    )(picks, *tokens, *amps, *map(in_hbm, parts))


def add_sums(one, two):
    def kernel(one_ref, two_ref, out_ref, token_ref):
        token_ref[...] = jnp.zeros_like(token_ref)
        out_ref[...] = one_ref[...] + two_ref[...]

    return call(
        kernel, "add_sums",
        out_shape=(jax.ShapeDtypeStruct(one.shape, one.dtype), TOKEN),
        in_specs=[VMEM, VMEM],
        out_specs=(VMEM, VMEM),
    )(one, two)


def top_and_rest(one, two, at):
    def kernel(one_ref, two_ref, top_ref, rest_ref, sem):
        copies = [
            pltpu.make_async_copy(one_ref.at[pl.ds(0, at)], top_ref, sem.at[0]),
            pltpu.make_async_copy(two_ref.at[pl.ds(at, two.shape[0] - at)], rest_ref, sem.at[1])]
        for copy in copies:
            copy.start()
        for copy in copies:
            copy.wait()

    return call(
        kernel, "top_and_rest",
        out_shape=(
            jax.ShapeDtypeStruct((at, one.shape[1]), one.dtype),
            jax.ShapeDtypeStruct((two.shape[0] - at, two.shape[1]), two.dtype)),
        in_specs=[ANY, ANY],
        out_specs=(VMEM, VMEM),
        scratch_shapes=[pltpu.SemaphoreType.DMA((2,))],
    )(in_hbm(one), in_hbm(two))


Z, X, Y = 4, 2, 2
AXES = ("row", "col")


def device(z, x, y, c):
    return (z * X + x) * Y * 2 + y * 2 + c


def moves(to, home=True):
    pairs = []
    for z in range(Z):
        for x in range(X):
            for y in range(Y):
                if to(z, x) is not None:
                    c = z % 2 if home else 1 - z % 2
                    pairs.append((device(z, x, y, c), device(*to(z, x), y, c)))
    return pairs


def across_x(z, x):
    return z, 1 - x


def across_x_ends(z, x):
    return (z, 1 - x) if z in (0, 3) else None


def across_x_middle(z, x):
    return (z, 1 - x) if z in (1, 2) else None


def to_pair(z, x):
    return z ^ 1, x


def over_centre(z, x):
    return (3 - z, x) if z in (1, 2) else None


def outward(z, x):
    return (z ^ 1, x) if z in (1, 2) else None


def to_y(far, cores):
    pairs = []
    for z in range(Z):
        end = (z // 2) ^ int(far)
        for x in range(X):
            for c in cores(z):
                pairs.append((device(z, x, 1 - end, c), device(z, x, end, c)))
    return pairs


def both(z):
    return 0, 1


def home_core(z):
    return (z % 2,)


def other_core(z):
    return (1 - z % 2,)


FROM_OTHER_CORE = [
    (device(z, x, y, 1 - z % 2), device(z, x, y, z % 2)) for z in range(Z) for x in range(X) for y in range(Y)]
CORES = [(0, 1), (1, 0), (2, 3), (3, 2)]
CHIPS_Y = [(0, 2), (2, 0), (1, 3), (3, 1)]
CROSSWISE = [(0, 3), (3, 0), (1, 2), (2, 1)]


def sparse_ladder(amplitudes, integrals, amp_mask, int_mask):
    barrier = lax.optimization_barrier
    tiles = int_mask.size
    cap = 2 * tiles * 11 // 16
    half = cap * TILE // 2
    row, col = lax.axis_index("row"), lax.axis_index("col")
    z, x = row // X, row % X
    y, c = col // 2, col % 2
    is_end = ((z == 0) | (z == Z - 1)).astype(jnp.int32)
    home = z % 2 == c

    def move(value, pairs):
        return lax.ppermute(value, AXES, pairs)

    def after(*tokens):
        return lambda *shards: barrier((*shards, tokens))

    picks = jnp.stack([
        jnp.where(home, 0, 1),
        jnp.where(home, is_end, -1),
        jnp.where(home, 0, 1),
        jnp.where(home, is_end, 2 + is_end),
        jnp.where(home, -1, is_end),
    ]).astype(jnp.int32)

    flat_mask = int_mask.reshape(tiles)
    other = move(integrals, FROM_OTHER_CORE)
    other_mask, across, other_across = [lax.ppermute(flat_mask, "col", p) for p in (CORES, CHIPS_Y, CROSSWISE)]
    other_mask, amplitudes_now, picks = barrier((other_mask, amplitudes, picks))
    masked, masked_token = mask_tiles(amplitudes_now, amp_mask)
    own = pack_tiles((integrals, other), (flat_mask, other_mask), (across, other_across), cap)

    amps = (masked, lax.ppermute(masked, "col", CORES))
    one, centre, own_x, tokens = after(masked_token)(
        move(own, moves(to_pair)), move(own, moves(over_centre)), move(own, moves(across_x)))

    a_sum, token = shard_product(amps, picks, 0, [[own], [one]], tokens)
    a_far = move(a_sum, to_y(False, both))
    two_end, two_mid, one_x, tokens = after(token)(
        move(centre, moves(outward, False)), move(one, moves(over_centre, False)), move(one, moves(across_x, False)))

    c_sum, token = shard_product(amps, picks, 1, [[two_mid], [two_end]], tokens)
    c_far = move(c_sum, to_y(True, home_core))
    b_sum, token = shard_product(amps, picks, 2, [[own_x], [one_x]], (token,))
    b_far = move(b_sum, to_y(False, both))
    a_both, a_token = add_sums(a_sum, a_far)
    three_end, three_mid_x, two_x_end, two_x_mid, tokens = after(token, a_token)(
        move(two_mid, moves(outward)), move(own_x, moves(over_centre)),
        move(two_end, moves(across_x_ends)), move(two_mid, moves(across_x_middle)))

    d_sum, token = shard_product(
        amps, picks, 3, [[two_x_mid], [two_x_end], [centre], [three_end]], tokens)
    top, rest = top_and_rest(three_end, two_x_mid, half)
    three_x, three_x_rest, tokens = after(token)(
        move(top, moves(across_x_ends, False)), move(rest, moves(outward)))

    d_far = move(d_sum, to_y(True, both))
    e_sum, token = shard_product(amps, picks, 4, [[three_mid_x], [three_x, three_x_rest]], tokens)
    e_far = move(e_sum, to_y(True, other_core))
    excess = token + lax.ppermute(token, "col", CORES)

    def finish():
        near = z // 2 == y
        d_both = d_sum + d_far
        mine = jnp.where(near, a_both, jnp.where(home, c_sum + c_far, d_both)).astype(jnp.bfloat16)
        rest = jnp.where(near, b_sum + b_far, jnp.where(home, d_both, e_sum + e_far)).astype(jnp.bfloat16)
        return jnp.concatenate([jnp.where(x == 0, mine, rest), jnp.where(x == 0, rest, mine)], axis=1)

    return lax.cond(
        jnp.max(excess) > 0, lambda: dense_ladder(amplitudes, integrals, amp_mask, int_mask), finish)


def solution(mesh):
    in_specs = (P("row", "col"), P("col", "row"), P("row", "col"), P("col", "row"))
    out_specs = P("row", "col")
    here = dict(mesh.shape)
    per_device = sparse_ladder if here == {"row": Z * X, "col": Y * 2} else dense_ladder
    return jax.shard_map(
        per_device, mesh=mesh, in_specs=in_specs, out_specs=out_specs, check_vma=False
    )
```

time: 241 us -> 161 us (0.67)
  the two profiles are of different devices: /device:TPU:24 before, /device:TPU:12 now
where the time goes in v2:
time: 161 us; the launch traced here: 160 us
  waiting for transfers between devices  87.2 us (54%)
  starting transfers between devices  34 us (21%)
  Pallas kernels  28.9 us (18%)
  other arithmetic  5.51 us (3%)
  local copies, waits for them, and re-layouts  3.69 us (2%)
    ppermute x18, waiting for transfers between devices, move(): return lax.ppermute(value, AXES, pairs)  82.2 us
    ppermute x18, starting transfers between devices, move(): return lax.ppermute(value, AXES, pairs)  32.9 us
    pallas_call x5, Pallas kernels, shard_product(): call(kernel, 'shard_product', out_shape=(jax.ShapeDtypeStruct((rows, wide...  21.7 us
    pallas_call x1, Pallas kernels, mask_tiles(): call(kernel, 'mask_tiles', grid=(rows // TILE // step,), out_shape=(jax.S...  4.14 us
    ppermute x3, waiting for transfers between devices, sparse_ladder(): lax.ppermute(flat_mask, 'col', p)  3.84 us
    select_n x1, other arithmetic, finish(): jnp.where(x == 0, mine, rest)  3.79 us
    unnamed x33, local copies, waits for them, and re-layouts  3.52 us
  transfers between devices with their start and end apart: 23, of which 11 were waited for; matrix products, arithmetic and copies ran while one was open for 0% of the time, Pallas kernels for 14%

profile of v2, /device:TPU:12, one launch (start us, length us, event | category | flops | bytes accessed | tf_op | source)
XLA Modules:
  0.0 160.5 jit_solution(5713519850312168501)
XLA Ops:
  0.0 0.8 copy.10
  0.8 0.1 reshape.11.refs_0_
  0.9 0.1 collective-permute-start.10
  1.1 0.1 stack.20.picks_ref
  1.2 1.0 collective-permute-done.10.refs_1_
  2.1 4.1 %mask_tiles.1 = (bf16[1024,2048]{1,0:T(8,128)(2,1)S(1)}, f32[8,128]{1,0:T(8,128)S(1)}) custom-call(s32[8,16]{1,0:T(8,128)} %mask_ref.1, bf16[1024,2048]{1,0:T(8,128)(2,1)} %a_ref), custom_call_target="tpu_custom_call" | custom-call | flops 1 | bytes 1 | tf_op jit(solution)/shard_map/mask_tiles/pallas_call | solution.py:117
  6.3 0.3 collective-permute-start.20
  6.5 2.3 %collective-permute-start.13 = (bf16[2048,256]{1,0:T(8,128)(2,1)S(1)}, bf16[2048,256]{1,0:T(8,128)(2,1)S(1)}, u32[]{:S(2)}, u32[]{:S(2)}) collective-permute-start(bf16[2048,256]{1,0:T(8,128)(2,1)S(1)} %copy-done.6), channel_id=1, source_target_pairs={{1,0},{3,2},{5,4},{7,6},{8,9},{10,11},{12,13},{14,15},{17,16},{19,... | collective-permute-start | bytes 3145736 | tf_op jit(solution)/shard_map/ppermute | solution.py:321
  8.8 0.6 collective-permute-start.11
  9.4 0.2 collective-permute-start.12
  9.5 2.9 %collective-permute-done.11.refs_2_ = s32[32]{0:T(128)S(1)} collective-permute-done((s32[32]{0:T(128)S(1)}, s32[32]{0:T(128)S(1)}, u32[]{:S(2)}, u32[]{:S(2)}) %collective-permute-start.11) | collective-permute-done | bytes 160 | tf_op jit(solution)/shard_map/ppermute | solution.py:336
  12.4 0.0 collective-permute-done.12.refs_3_
  12.4 2.4 %collective-permute-done.13.refs_5_ = bf16[2048,256]{1,0:T(8,128)(2,1)S(1)} collective-permute-done((bf16[2048,256]{1,0:T(8,128)(2,1)S(1)}, bf16[2048,256]{1,0:T(8,128)(2,1)S(1)}, u32[]{:S(2)}, u32[]{:S(2)}) %collective-permute-start.13) | collective-permute-done | bytes 1048608 | tf_op jit(solution)/shard_map/ppermute | solution.py:321
  14.8 1.3 pack_tiles.1.refs_3_
  16.1 1.3 collective-permute-start.14
  17.4 1.3 collective-permute-start.15
  18.7 0.8 collective-permute-start.16
  19.5 17.6 %collective-permute-done.14.refs_4_ = bf16[5648,128]{1,0:T(8,128)(2,1)S(1)} collective-permute-done((bf16[5648,128]{1,0:T(8,128)(2,1)S(1)}, bf16[5648,128]{1,0:T(8,128)(2,1)S(1)}, u32[]{:S(2)}, u32[]{:S(2)}) %collective-permute-start.14) | collective-permute-done | bytes 1445920 | tf_op jit(solution)/shard_map/ppermute | solution.py:321
  37.1 2.5 %collective-permute-done.15.refs_6_ = bf16[5648,128]{1,0:T(8,128)(2,1)S(1)} collective-permute-done((bf16[5648,128]{1,0:T(8,128)(2,1)S(1)}, bf16[5648,128]{1,0:T(8,128)(2,1)S(1)}, u32[]{:S(2)}, u32[]{:S(2)}) %collective-permute-start.15) | collective-permute-done | bytes 1445920 | tf_op jit(solution)/shard_map/ppermute | solution.py:321
  39.5 0.0 collective-permute-done.16.refs_3_
  39.5 4.3 %collective-permute-start.17 = (bf16[5648,128]{1,0:T(8,128)(2,1)S(1)}, bf16[5648,128]{1,0:T(8,128)(2,1)S(1)}, u32[]{:S(2)}, u32[]{:S(2)}) collective-permute-start(bf16[5648,128]{1,0:T(8,128)(2,1)S(1)} %collective-permute-done.15.refs_6_), channel_id=1, source_target_pairs={{8,0},{10,2},{12,4},{14,6},{17,25},{19,27},{21,29},{23,31}} | collective-permute-start | bytes 4337672 | tf_op jit(solution)/shard_map/ppermute | solution.py:321
  43.8 2.5 %collective-permute-start.18 = (bf16[5648,128]{1,0:T(8,128)(2,1)S(1)}, bf16[5648,128]{1,0:T(8,128)(2,1)S(1)}, u32[]{:S(2)}, u32[]{:S(2)}) collective-permute-start(bf16[5648,128]{1,0:T(8,128)(2,1)S(1)} %collective-permute-done.14.refs_4_), channel_id=1, source_target_pairs={{8,16},{10,18},{12,20},{14,22},{17,9},{19,11},{21,13},{23,15}} | collective-permute-start | bytes 4337672 | tf_op jit(solution)/shard_map/ppermute | solution.py:321
  46.3 3.4 %collective-permute-start.19 = (bf16[5648,128]{1,0:T(8,128)(2,1)S(1)}, bf16[5648,128]{1,0:T(8,128)(2,1)S(1)}, u32[]{:S(2)}, u32[]{:S(2)}) collective-permute-start(bf16[5648,128]{1,0:T(8,128)(2,1)S(1)} %collective-permute-done.14.refs_4_), channel_id=1, source_target_pairs={{1,5},{3,7},{5,1},{7,3},{8,12},{10,14},{12,8},{14,10},{17,21},{19,... | collective-permute-start | bytes 4337672 | tf_op jit(solution)/shard_map/ppermute | solution.py:321
  49.8 1.3 collective-permute-start.22
  51.1 0.0 collective-permute-done.20.refs_2_.refs_3_
  51.1 4.5 %shard_product.5 = (f32[1024,256]{1,0:T(8,128)S(1)}, f32[8,128]{1,0:T(8,128)S(1)}) custom-call(s32[5]{0:T(128)S(1)} %stack.20.picks_ref, f32[8,128]{1,0:T(8,128)S(1)} %get-tuple-element.140.refs_0_, bf16[1024,2048]{1,0:T(8,128)(2,1)S(1)} %get-tuple-element.141.refs_1_.refs_2_, bf16[1024,2048]{1,0:T(8,128)(2,1)S(1)} %collective-permute-done.20.refs_2_.refs_3_, ...), custom_call_target="tpu_custom_call" | custom-call | flops 1 | bytes 1 | tf_op jit(solution)/shard_map/shard_product/pallas_call | solution.py:190
  55.7 4.6 %collective-permute-done.17.refs_4_ = bf16[5648,128]{1,0:T(8,128)(2,1)S(1)} collective-permute-done((bf16[5648,128]{1,0:T(8,128)(2,1)S(1)}, bf16[5648,128]{1,0:T(8,128)(2,1)S(1)}, u32[]{:S(2)}, u32[]{:S(2)}) %collective-permute-start.17) | collective-permute-done | bytes 1445920 | tf_op jit(solution)/shard_map/ppermute | solution.py:321
  60.3 14.7 %collective-permute-done.18.refs_3_ = bf16[5648,128]{1,0:T(8,128)(2,1)S(1)} collective-permute-done((bf16[5648,128]{1,0:T(8,128)(2,1)S(1)}, bf16[5648,128]{1,0:T(8,128)(2,1)S(1)}, u32[]{:S(2)}, u32[]{:S(2)}) %collective-permute-start.18) | collective-permute-done | bytes 1445920 | tf_op jit(solution)/shard_map/ppermute | solution.py:321
  75.0 0.0 collective-permute-done.19.refs_4_
  75.0 0.7 collective-permute-start.21
  75.7 0.8 collective-permute-start.23
  76.5 0.8 collective-permute-start.24
  77.3 2.5 %collective-permute-start.25 = (f32[1024,256]{1,0:T(8,128)S(1)}, f32[1024,256]{1,0:T(8,128)S(1)}, u32[]{:S(2)}, u32[]{:S(2)}) collective-permute-start(f32[1024,256]{1,0:T(8,128)S(1)} %get-tuple-element.150.one_ref), channel_id=1, source_target_pairs={{2,0},{3,1},{6,4},{7,5},{10,8},{11,9},{14,12},{15,13},{16,18},{17,... | collective-permute-start | bytes 3145736 | tf_op jit(solution)/shard_map/ppermute | solution.py:321
  79.8 0.6 shard_product.6
  80.4 5.5 %shard_product.7 = (f32[1024,256]{1,0:T(8,128)}, f32[8,128]{1,0:T(8,128)S(1)}) custom-call(s32[5]{0:T(128)S(1)} %stack.20.picks_ref, f32[8,128]{1,0:T(8,128)S(1)} %get-tuple-element.147.refs_0_, bf16[1024,2048]{1,0:T(8,128)(2,1)S(1)} %get-tuple-element.141.refs_1_.refs_2_, bf16[1024,2048]{1,0:T(8,128)(2,1)S(1)} %collective-permute-done.20.refs_2_.refs_3_, ...), custom_call_target="tpu_custom_call" | custom-call | flops 1 | bytes 1 | tf_op jit(solution)/shard_map/shard_product/pallas_call | solution.py:190
  85.9 13.4 %collective-permute-done.25.two_ref = f32[1024,256]{1,0:T(8,128)S(1)} collective-permute-done((f32[1024,256]{1,0:T(8,128)S(1)}, f32[1024,256]{1,0:T(8,128)S(1)}, u32[]{:S(2)}, u32[]{:S(2)}) %collective-permute-start.25) | collective-permute-done | bytes 1048608 | tf_op jit(solution)/shard_map/ppermute | solution.py:321
  99.3 0.2 add_sums.1
  99.5 0.0 collective-permute-done.22.refs_3_
  99.5 0.0 collective-permute-done.21.one_ref.refs_7_
  99.5 0.0 collective-permute-done.23.refs_5_
  99.6 1.6 copy-done.2
  101.1 1.6 %top_and_rest.1 = (bf16[2816,128]{1,0:T(8,128)(2,1)S(1)}, bf16[2832,128]{1,0:T(8,128)(2,1)S(1)}) custom-call(bf16[5648,128]{1,0:T(8,128)(2,1)} %copy-done.2, bf16[5648,128]{1,0:T(8,128)(2,1)} %copy-done.3), custom_call_target="tpu_custom_call" | custom-call | flops 1 | bytes 1 | tf_op jit(solution)/shard_map/top_and_rest/pallas_call | solution.py:226
  102.7 0.7 collective-permute-start.27
  103.5 0.7 collective-permute-start.26
  104.2 5.4 %collective-permute-start.31 = (f32[1024,256]{1,0:T(8,128)}, f32[1024,256]{1,0:T(8,128)}, u32[]{:S(2)}, u32[]{:S(2)}) collective-permute-start(f32[1024,256]{1,0:T(8,128)} %get-tuple-element.168), channel_id=1, source_target_pairs={{2,0},{3,1},{6,4},{7,5},{10,8},{11,9},{14,12},{15,13},{16,18},{17,... | collective-permute-start | bytes 3145736 | tf_op jit(solution)/shard_map/ppermute | solution.py:321
  109.6 1.7 %collective-permute-start.29 = (f32[1024,256]{1,0:T(8,128)S(1)}, f32[1024,256]{1,0:T(8,128)}, u32[]{:S(2)}, u32[]{:S(2)}) collective-permute-start(f32[1024,256]{1,0:T(8,128)S(1)} %get-tuple-element.165), channel_id=1, source_target_pairs={{0,2},{4,6},{9,11},{13,15},{18,16},{22,20},{27,25},{31,29}} | collective-permute-start | bytes 3145736 | tf_op jit(solution)/shard_map/ppermute | solution.py:321
  111.2 5.5 %shard_product.8 = (f32[1024,256]{1,0:T(8,128)}, f32[8,128]{1,0:T(8,128)S(1)}) custom-call(s32[5]{0:T(128)S(1)} %stack.20.picks_ref, f32[8,128]{1,0:T(8,128)S(1)} %get-tuple-element.156.refs_0_, f32[8,128]{1,0:T(8,128)S(1)} %get-tuple-element.157.refs_1_, bf16[1024,2048]{1,0:T(8,128)(2,1)S(1)} %get-tuple-element.141.refs_1_.refs_2_, ...), custom_call_target="tpu_custom_call" | custom-call | flops 1 | bytes 1 | tf_op jit(solution)/shard_map/shard_product/pallas_call | solution.py:190
  116.7 1.3 collective-permute-start.30
  118.0 0.0 collective-permute-done.26.refs_4_
  118.1 0.0 copy-start.15
  118.1 0.9 copy-done.16
  119.0 0.2 copy-done.15
  119.2 5.6 %shard_product.9 = (f32[1024,256]{1,0:T(8,128)}, f32[8,128]{1,0:T(8,128)S(1)}) custom-call(s32[5]{0:T(128)S(1)} %stack.20.picks_ref, f32[8,128]{1,0:T(8,128)S(1)} %get-tuple-element.160.refs_0_, bf16[1024,2048]{1,0:T(8,128)(2,1)S(1)} %get-tuple-element.141.refs_1_.refs_2_, bf16[1024,2048]{1,0:T(8,128)(2,1)S(1)} %collective-permute-done.20.refs_2_.refs_3_, ...), custom_call_target="tpu_custom_call" | custom-call | flops 1 | bytes 1 | tf_op jit(solution)/shard_map/shard_product/pallas_call | solution.py:190
  124.8 1.3 collective-permute-start.32
  126.1 0.1 collective-permute-start.28
  126.1 1.2 collective-permute-done.28
  127.3 0.6 add_reduce_fusion
  128.6 0.0 collective-permute-done.31
  128.6 15.7 %collective-permute-done.30 = f32[1024,256]{1,0:T(8,128)} collective-permute-done((f32[1024,256]{1,0:T(8,128)}, f32[1024,256]{1,0:T(8,128)}, u32[]{:S(2)}, u32[]{:S(2)}) %collective-permute-start.30) | collective-permute-done | bytes 1048608 | tf_op jit(solution)/shard_map/ppermute | solution.py:321
  144.3 11.2 %collective-permute-done.32 = f32[1024,256]{1,0:T(8,128)} collective-permute-done((f32[1024,256]{1,0:T(8,128)}, f32[1024,256]{1,0:T(8,128)}, u32[]{:S(2)}, u32[]{:S(2)}) %collective-permute-start.32) | collective-permute-done | bytes 1048608 | tf_op jit(solution)/shard_map/ppermute | solution.py:321
  155.6 4.9 %conditional.1 = (bf16[1024,512]{1,0:T(8,128)(2,1)}) conditional(s32[]{:T(128)} %convert_element_type.38, (s32[]{:T(128)}, s32[]{:T(128)}, s32[]{:T(128)}, s32[]{:T(128)}, pred[]{:T(512)}, /*index=5*/s32[]{:T(128)}, pred[]{:T(512)}, f32[1024,256]{1,0:T(8,128)S(1)}, f32[1024,256]{1,0:T(8,128)}, f32[1024,256]{1,0:T(8,128)}, ...), branch_computations={%region_1.2_spmd, %region_2.3_spmd} | conditional | flops 8594653184 | bytes 206655584 | solution.py:377
  155.6 3.8 %broadcast_select_fusion.1 = (bf16[1024,256]{1,0:T(8,128)(2,1)S(1)}, bf16[1024,256]{1,0:T(8,128)(2,1)S(1)}, bf16[1024,256]{1,0:T(8,128)(2,1)S(1)}) fusion(pred[]{:T(512)S(6)} %eq.26, f32[1024,256]{1,0:T(8,128)S(1)} %get-tuple-element.84, f32[1024,256]{1,0:T(8,128)} %get-tuple-element.88, f32[1024,256]{1,0:T(8,128)} %get-tuple-element.89, ...), kind=kLoop, calls=%fused_computation.4 | loop fusion | flops 2621440 | bytes 11010051 | tf_op jit(solution)/shard_map/cond/branch_0_fun/jit(_where)/select_n | solution.py:375
  159.4 0.1 broadcast_select_fusion
  159.4 1.1 pad_maximum_fusion
  (31 shorter events, 0.1 us)
Async XLA Ops:
  0.0 6.5 %copy-start.6 = (bf16[2048,256]{1,0:T(8,128)(2,1)S(1)}, bf16[2048,256]{1,0:T(8,128)(2,1)}, u32[]{:S(2)}) copy-start(bf16[2048,256]{1,0:T(8,128)(2,1)} %refs_4_.1) | copy-start | bytes 3145732
  0.9 1.2 collective-permute-start.10
  6.3 44.8 %collective-permute-start.20 = (bf16[1024,2048]{1,0:T(8,128)(2,1)S(1)}, bf16[1024,2048]{1,0:T(8,128)(2,1)S(1)}, u32[]{:S(2)}, u32[]{:S(2)}) collective-permute-start(bf16[1024,2048]{1,0:T(8,128)(2,1)S(1)} %get-tuple-element.141.refs_1_.refs_2_), channel_id=1, source_target_pairs={{0,1},{1,0},{2,3},{3,2},{4,5},{5,4},{6,7},{7,6},{8,9},{9,8},{10,11... | collective-permute-start | bytes 12582920 | tf_op jit(solution)/shard_map/ppermute | solution.py:341
  6.5 8.3 %collective-permute-start.13 = (bf16[2048,256]{1,0:T(8,128)(2,1)S(1)}, bf16[2048,256]{1,0:T(8,128)(2,1)S(1)}, u32[]{:S(2)}, u32[]{:S(2)}) collective-permute-start(bf16[2048,256]{1,0:T(8,128)(2,1)S(1)} %copy-done.6), channel_id=1, source_target_pairs={{1,0},{3,2},{5,4},{7,6},{8,9},{10,11},{12,13},{14,15},{17,16},{19,... | collective-permute-start | bytes 3145736 | tf_op jit(solution)/shard_map/ppermute | solution.py:321
  8.8 3.6 %collective-permute-start.11 = (s32[32]{0:T(128)S(1)}, s32[32]{0:T(128)S(1)}, u32[]{:S(2)}, u32[]{:S(2)}) collective-permute-start(s32[32]{0:T(128)S(1)} %reshape.11.refs_0_), channel_id=1, source_target_pairs={{0,2},{2,0},{1,3},{3,1},{4,6},{6,4},{5,7},{7,5},{8,10},{10,8},{9,1... | collective-permute-start | bytes 392 | tf_op jit(solution)/shard_map/ppermute | solution.py:336
  9.4 3.0 %collective-permute-start.12 = (s32[32]{0:T(128)S(1)}, s32[32]{0:T(128)S(1)}, u32[]{:S(2)}, u32[]{:S(2)}) collective-permute-start(s32[32]{0:T(128)S(1)} %reshape.11.refs_0_), channel_id=1, source_target_pairs={{0,3},{3,0},{1,2},{2,1},{4,7},{7,4},{5,6},{6,5},{8,11},{11,8},{9,1... | collective-permute-start | bytes 392 | tf_op jit(solution)/shard_map/ppermute | solution.py:336
  16.1 35.0 %copy-start = (bf16[5648,128]{1,0:T(8,128)(2,1)}, bf16[5648,128]{1,0:T(8,128)(2,1)S(1)}, u32[]{:S(2)}) copy-start(bf16[5648,128]{1,0:T(8,128)(2,1)S(1)} %pack_tiles.1.refs_3_) | copy-start | bytes 4337668
  16.1 20.9 %collective-permute-start.14 = (bf16[5648,128]{1,0:T(8,128)(2,1)S(1)}, bf16[5648,128]{1,0:T(8,128)(2,1)S(1)}, u32[]{:S(2)}, u32[]{:S(2)}) collective-permute-start(bf16[5648,128]{1,0:T(8,128)(2,1)S(1)} %pack_tiles.1.refs_3_), channel_id=1, source_target_pairs={{0,8},{2,10},{4,12},{6,14},{9,1},{11,3},{13,5},{15,7},{16,24},{18,... | collective-permute-start | bytes 4337672 | tf_op jit(solution)/shard_map/ppermute | solution.py:321
  17.4 22.1 %collective-permute-start.15 = (bf16[5648,128]{1,0:T(8,128)(2,1)S(1)}, bf16[5648,128]{1,0:T(8,128)(2,1)S(1)}, u32[]{:S(2)}, u32[]{:S(2)}) collective-permute-start(bf16[5648,128]{1,0:T(8,128)(2,1)S(1)} %pack_tiles.1.refs_3_), channel_id=1, source_target_pairs={{9,17},{11,19},{13,21},{15,23},{16,8},{18,10},{20,12},{22,14}} | collective-permute-start | bytes 4337672 | tf_op jit(solution)/shard_map/ppermute | solution.py:321
  18.7 20.8 %collective-permute-start.16 = (bf16[5648,128]{1,0:T(8,128)(2,1)S(1)}, bf16[5648,128]{1,0:T(8,128)(2,1)S(1)}, u32[]{:S(2)}, u32[]{:S(2)}) collective-permute-start(bf16[5648,128]{1,0:T(8,128)(2,1)S(1)} %pack_tiles.1.refs_3_), channel_id=1, source_target_pairs={{0,4},{2,6},{4,0},{6,2},{9,13},{11,15},{13,9},{15,11},{16,20},{18,... | collective-permute-start | bytes 4337672 | tf_op jit(solution)/shard_map/ppermute | solution.py:321
  37.1 14.0 %copy-start.13 = (bf16[5648,128]{1,0:T(8,128)(2,1)}, bf16[5648,128]{1,0:T(8,128)(2,1)S(1)}, u32[]{:S(2)}) copy-start(bf16[5648,128]{1,0:T(8,128)(2,1)S(1)} %collective-permute-done.14.refs_4_) | copy-start | bytes 4337668
  39.5 16.1 %copy-start.7 = (bf16[5648,128]{1,0:T(8,128)(2,1)}, bf16[5648,128]{1,0:T(8,128)(2,1)S(1)}, u32[]{:S(2)}) copy-start(bf16[5648,128]{1,0:T(8,128)(2,1)S(1)} %collective-permute-done.15.refs_6_) | copy-start | bytes 4337668
  39.5 16.1 %copy-start.9 = (bf16[5648,128]{1,0:T(8,128)(2,1)}, bf16[5648,128]{1,0:T(8,128)(2,1)S(1)}, u32[]{:S(2)}) copy-start(bf16[5648,128]{1,0:T(8,128)(2,1)S(1)} %collective-permute-done.16.refs_3_) | copy-start | bytes 4337668
  39.5 20.8 %collective-permute-start.17 = (bf16[5648,128]{1,0:T(8,128)(2,1)S(1)}, bf16[5648,128]{1,0:T(8,128)(2,1)S(1)}, u32[]{:S(2)}, u32[]{:S(2)}) collective-permute-start(bf16[5648,128]{1,0:T(8,128)(2,1)S(1)} %collective-permute-done.15.refs_6_), channel_id=1, source_target_pairs={{8,0},{10,2},{12,4},{14,6},{17,25},{19,27},{21,29},{23,31}} | collective-permute-start | bytes 4337672 | tf_op jit(solution)/shard_map/ppermute | solution.py:321
  43.8 31.1 %collective-permute-start.18 = (bf16[5648,128]{1,0:T(8,128)(2,1)S(1)}, bf16[5648,128]{1,0:T(8,128)(2,1)S(1)}, u32[]{:S(2)}, u32[]{:S(2)}) collective-permute-start(bf16[5648,128]{1,0:T(8,128)(2,1)S(1)} %collective-permute-done.14.refs_4_), channel_id=1, source_target_pairs={{8,16},{10,18},{12,20},{14,22},{17,9},{19,11},{21,13},{23,15}} | collective-permute-start | bytes 4337672 | tf_op jit(solution)/shard_map/ppermute | solution.py:321
  46.3 28.7 %collective-permute-start.19 = (bf16[5648,128]{1,0:T(8,128)(2,1)S(1)}, bf16[5648,128]{1,0:T(8,128)(2,1)S(1)}, u32[]{:S(2)}, u32[]{:S(2)}) collective-permute-start(bf16[5648,128]{1,0:T(8,128)(2,1)S(1)} %collective-permute-done.14.refs_4_), channel_id=1, source_target_pairs={{1,5},{3,7},{5,1},{7,3},{8,12},{10,14},{12,8},{14,10},{17,21},{19,... | collective-permute-start | bytes 4337672 | tf_op jit(solution)/shard_map/ppermute | solution.py:321
  49.8 49.7 %collective-permute-start.22 = (bf16[5648,128]{1,0:T(8,128)(2,1)S(1)}, bf16[5648,128]{1,0:T(8,128)(2,1)S(1)}, u32[]{:S(2)}, u32[]{:S(2)}) collective-permute-start(bf16[5648,128]{1,0:T(8,128)(2,1)S(1)} %collective-permute-done.16.refs_3_), channel_id=1, source_target_pairs={{9,17},{11,19},{13,21},{15,23},{16,8},{18,10},{20,12},{22,14}} | collective-permute-start | bytes 4337672 | tf_op jit(solution)/shard_map/ppermute | solution.py:321
  60.3 19.5 %copy-start.10 = (bf16[5648,128]{1,0:T(8,128)(2,1)}, bf16[5648,128]{1,0:T(8,128)(2,1)S(1)}, u32[]{:S(2)}) copy-start(bf16[5648,128]{1,0:T(8,128)(2,1)S(1)} %collective-permute-done.17.refs_4_) | copy-start | bytes 4337668
  75.0 4.8 %copy-start.11 = (bf16[5648,128]{1,0:T(8,128)(2,1)}, bf16[5648,128]{1,0:T(8,128)(2,1)S(1)}, u32[]{:S(2)}) copy-start(bf16[5648,128]{1,0:T(8,128)(2,1)S(1)} %collective-permute-done.18.refs_3_) | copy-start | bytes 4337668
  75.0 5.4 %copy-start.14 = (bf16[5648,128]{1,0:T(8,128)(2,1)}, bf16[5648,128]{1,0:T(8,128)(2,1)S(1)}, u32[]{:S(2)}) copy-start(bf16[5648,128]{1,0:T(8,128)(2,1)S(1)} %collective-permute-done.19.refs_4_) | copy-start | bytes 4337668
  75.0 24.5 %collective-permute-start.21 = (bf16[5648,128]{1,0:T(8,128)(2,1)S(1)}, bf16[5648,128]{1,0:T(8,128)(2,1)S(1)}, u32[]{:S(2)}, u32[]{:S(2)}) collective-permute-start(bf16[5648,128]{1,0:T(8,128)(2,1)S(1)} %collective-permute-done.18.refs_3_), channel_id=1, source_target_pairs={{9,1},{11,3},{13,5},{15,7},{16,24},{18,26},{20,28},{22,30}} | collective-permute-start | bytes 4337672 | tf_op jit(solution)/shard_map/ppermute | solution.py:321
  75.7 23.8 %collective-permute-start.23 = (bf16[5648,128]{1,0:T(8,128)(2,1)S(1)}, bf16[5648,128]{1,0:T(8,128)(2,1)S(1)}, u32[]{:S(2)}, u32[]{:S(2)}) collective-permute-start(bf16[5648,128]{1,0:T(8,128)(2,1)S(1)} %collective-permute-done.17.refs_4_), channel_id=1, source_target_pairs={{0,4},{2,6},{4,0},{6,2},{25,29},{27,31},{29,25},{31,27}} | collective-permute-start | bytes 4337672 | tf_op jit(solution)/shard_map/ppermute | solution.py:321
  76.5 23.0 %collective-permute-start.24 = (bf16[5648,128]{1,0:T(8,128)(2,1)S(1)}, bf16[5648,128]{1,0:T(8,128)(2,1)S(1)}, u32[]{:S(2)}, u32[]{:S(2)}) collective-permute-start(bf16[5648,128]{1,0:T(8,128)(2,1)S(1)} %collective-permute-done.18.refs_3_), channel_id=1, source_target_pairs={{9,13},{11,15},{13,9},{15,11},{16,20},{18,22},{20,16},{22,18}} | collective-permute-start | bytes 4337672 | tf_op jit(solution)/shard_map/ppermute | solution.py:321
  77.3 22.1 %collective-permute-start.25 = (f32[1024,256]{1,0:T(8,128)S(1)}, f32[1024,256]{1,0:T(8,128)S(1)}, u32[]{:S(2)}, u32[]{:S(2)}) collective-permute-start(f32[1024,256]{1,0:T(8,128)S(1)} %get-tuple-element.150.one_ref), channel_id=1, source_target_pairs={{2,0},{3,1},{6,4},{7,5},{10,8},{11,9},{14,12},{15,13},{16,18},{17,... | collective-permute-start | bytes 3145736 | tf_op jit(solution)/shard_map/ppermute | solution.py:321
  99.5 18.6 %copy-start.8 = (bf16[5648,128]{1,0:T(8,128)(2,1)}, bf16[5648,128]{1,0:T(8,128)(2,1)S(1)}, u32[]{:S(2)}) copy-start(bf16[5648,128]{1,0:T(8,128)(2,1)S(1)} %collective-permute-done.22.refs_3_) | copy-start | bytes 4337668
  99.5 1.6 %copy-start.2 = (bf16[5648,128]{1,0:T(8,128)(2,1)}, bf16[5648,128]{1,0:T(8,128)(2,1)S(1)}, u32[]{:S(2)}) copy-start(bf16[5648,128]{1,0:T(8,128)(2,1)S(1)} %collective-permute-done.21.one_ref.refs_7_) | copy-start | bytes 4337668
  99.5 11.7 %copy-start.12 = (bf16[5648,128]{1,0:T(8,128)(2,1)}, bf16[5648,128]{1,0:T(8,128)(2,1)S(1)}, u32[]{:S(2)}) copy-start(bf16[5648,128]{1,0:T(8,128)(2,1)S(1)} %collective-permute-done.23.refs_5_) | copy-start | bytes 4337668
  99.5 1.6 copy-start.3
  102.7 15.3 %collective-permute-start.27 = (bf16[2832,128]{1,0:T(8,128)(2,1)S(1)}, bf16[2832,128]{1,0:T(8,128)(2,1)S(1)}, u32[]{:S(2)}, u32[]{:S(2)}) collective-permute-start(bf16[2832,128]{1,0:T(8,128)(2,1)S(1)} %get-tuple-element.155), channel_id=1, source_target_pairs={{9,1},{11,3},{13,5},{15,7},{16,24},{18,26},{20,28},{22,30}} | collective-permute-start | bytes 2174984 | tf_op jit(solution)/shard_map/ppermute | solution.py:321
  103.5 14.6 %collective-permute-start.26 = (bf16[2816,128]{1,0:T(8,128)(2,1)S(1)}, bf16[2816,128]{1,0:T(8,128)(2,1)S(1)}, u32[]{:S(2)}, u32[]{:S(2)}) collective-permute-start(bf16[2816,128]{1,0:T(8,128)(2,1)S(1)} %get-tuple-element.154), channel_id=1, source_target_pairs={{1,5},{3,7},{5,1},{7,3},{24,28},{26,30},{28,24},{30,26}} | collective-permute-start | bytes 2162696 | tf_op jit(solution)/shard_map/ppermute | solution.py:321
  104.2 24.4 %collective-permute-start.31 = (f32[1024,256]{1,0:T(8,128)}, f32[1024,256]{1,0:T(8,128)}, u32[]{:S(2)}, u32[]{:S(2)}) collective-permute-start(f32[1024,256]{1,0:T(8,128)} %get-tuple-element.168), channel_id=1, source_target_pairs={{2,0},{3,1},{6,4},{7,5},{10,8},{11,9},{14,12},{15,13},{16,18},{17,... | collective-permute-start | bytes 3145736 | tf_op jit(solution)/shard_map/ppermute | solution.py:321
  109.6 19.0 %collective-permute-start.29 = (f32[1024,256]{1,0:T(8,128)S(1)}, f32[1024,256]{1,0:T(8,128)}, u32[]{:S(2)}, u32[]{:S(2)}) collective-permute-start(f32[1024,256]{1,0:T(8,128)S(1)} %get-tuple-element.165), channel_id=1, source_target_pairs={{0,2},{4,6},{9,11},{13,15},{18,16},{22,20},{27,25},{31,29}} | collective-permute-start | bytes 3145736 | tf_op jit(solution)/shard_map/ppermute | solution.py:321
  116.7 27.6 %collective-permute-start.30 = (f32[1024,256]{1,0:T(8,128)}, f32[1024,256]{1,0:T(8,128)}, u32[]{:S(2)}, u32[]{:S(2)}) collective-permute-start(f32[1024,256]{1,0:T(8,128)} %get-tuple-element.166), channel_id=1, source_target_pairs={{0,2},{1,3},{4,6},{5,7},{8,10},{9,11},{12,14},{13,15},{18,16},{19,... | collective-permute-start | bytes 3145736 | tf_op jit(solution)/shard_map/ppermute | solution.py:321
  118.1 0.9 copy-start.16
  118.1 1.1 copy-start.15
  119.2 36.4 %copy-start.17 = (s32[8,16]{1,0:T(8,128)S(1)}, s32[8,16]{1,0:T(8,128)}, u32[]{:S(2)}) copy-start(s32[8,16]{1,0:T(8,128)} %mask_ref.1) | copy-start | bytes 1540
  119.2 36.4 %copy-start.18 = (s32[16,2]{0,1:T(2,128)S(1)}, s32[16,2]{0,1:T(2,128)}, u32[]{:S(2)}) copy-start(s32[16,2]{0,1:T(2,128)} %param.9) | copy-start | bytes 388
  124.8 30.8 %collective-permute-start.32 = (f32[1024,256]{1,0:T(8,128)}, f32[1024,256]{1,0:T(8,128)}, u32[]{:S(2)}, u32[]{:S(2)}) collective-permute-start(f32[1024,256]{1,0:T(8,128)} %get-tuple-element.169), channel_id=1, source_target_pairs={{1,3},{5,7},{8,10},{12,14},{19,17},{23,21},{26,24},{30,28}} | collective-permute-start | bytes 3145736 | tf_op jit(solution)/shard_map/ppermute | solution.py:321
  126.1 1.2 collective-permute-start.28

commit v3 on v2

--- a/solution.py
+++ b/solution.py
@@ -35,6 +35,11 @@
 
 TOKEN = jax.ShapeDtypeStruct((8, TILE), jnp.float32)
 LIGHT = pl.CostEstimate(flops=1, bytes_accessed=1, transcendentals=0)
+STEPS = 5
+TOP = 12
+LOW = 4
+BITS = 16 + LOW
+GROUP = 128
 META = 16
 
 
@@ -42,11 +47,11 @@
     return pltpu.with_memory_space_constraint(array, pltpu.HBM)
 
 
-def call(kernel, name, **kwargs):
+def call(kernel, name, cost=LIGHT, **kwargs):
     return pl.pallas_call(
         kernel,
         compiler_params=pltpu.CompilerParams(vmem_limit_bytes=VMEM_LIMIT),
-        cost_estimate=LIGHT,
+        cost_estimate=cost,
         name=name,
         **kwargs,
     )
@@ -59,7 +64,7 @@
 
 def pack_tiles(shards, masks, across_masks, cap):
     wide = shards[0].shape[1] // TILE
-    tiles = masks[0].shape[0]
+    tiles = masks[0].size
     count = len(shards)
 
     def kernel(*refs):
@@ -71,7 +76,7 @@
         for s in range(count):
             for t in range(tiles):
                 k, n = divmod(t, wide)
-                keep = mask_refs[s][t] != 0
+                keep = mask_refs[s][k, n] != 0
 
                 @pl.when(keep & (place < cap))
                 def _(s=s, k=k, n=n, place=place):
@@ -79,7 +84,7 @@
                     out_ref[pl.ds(at, TILE), :] = b_refs[s][k * TILE:(k + 1) * TILE, n * TILE:(n + 1) * TILE]
 
                 place = place + keep.astype(jnp.int32)
-                across = across + (across_refs[s][t] != 0).astype(jnp.int32)
+                across = across + (across_refs[s][k, n] != 0).astype(jnp.int32)
                 meta = jnp.where((lane == s * tiles + t) & keep, 1.0, meta)
         more = jnp.maximum(place, across) > cap
         meta = jnp.where(sub == 0, meta, jnp.where((sub == 1) & more, 1.0, 0.0))
@@ -115,7 +120,7 @@
 
     block = pl.BlockSpec((step * TILE, cols), lambda i: (i, 0))
     return call(
-        kernel, "mask_tiles",
+        kernel, "mask_tiles", pl.CostEstimate(flops=0, bytes_accessed=4 * amplitudes.size, transcendentals=0),
         grid=(rows // TILE // step,),
         out_shape=(jax.ShapeDtypeStruct(amplitudes.shape, amplitudes.dtype), TOKEN),
         in_specs=[SMEM, block],
@@ -141,7 +146,7 @@
         token_refs, refs = refs[:len(tokens)], refs[len(tokens):]
         a_refs, refs = refs[:count], refs[count:]
         p_any, refs = refs[:len(parts)], refs[len(parts):]
-        out_ref, token_ref, packed, wide_ref, sem = refs
+        out_ref, coded_ref, token_ref, packed, wide_ref, sem = refs
         pick = picks_ref[step]
         token_ref[...] = sum(ref[...] for ref in token_refs)
         for number, choice in enumerate(choices):
@@ -187,11 +192,18 @@
                 else:
                     out_ref[...] = term
 
+        @pl.when((pick >= 0) & (picks_ref[STEPS + step] != 0))
+        def _():
+            encode(out_ref, coded_ref)
+
     return call(
         kernel, "shard_product",
-        out_shape=(jax.ShapeDtypeStruct((rows, wide * TILE), jnp.float32), TOKEN),
+        out_shape=(
+            jax.ShapeDtypeStruct((rows, wide * TILE), jnp.float32),
+            jax.ShapeDtypeStruct((coded_rows(rows), wide * TILE), jnp.int16),
+            TOKEN),
         in_specs=[SMEM] + [VMEM] * (len(tokens) + count) + [ANY] * len(parts),
-        out_specs=(VMEM, VMEM),
+        out_specs=(VMEM, VMEM, VMEM),
         scratch_shapes=[
             pltpu.VMEM((height, TILE), amps[0].dtype),
             pltpu.VMEM((count * depth, wide * TILE), amps[0].dtype),
@@ -200,17 +212,74 @@
     )(picks, *tokens, *amps, *map(in_hbm, parts))
 
 
-def add_sums(one, two):
-    def kernel(one_ref, two_ref, out_ref, token_ref):
+def coded_rows(rows):
+    return rows + rows // (16 // LOW) + META
+
+
+def step_factors(exponent):
+    power = BITS - 1 - TOP - exponent
+    factors = []
+    for part in (power // 2, power - power // 2):
+        factor = jnp.ones(part.shape, jnp.float32)
+        for bit in range(7):
+            factor = factor * jnp.where((part >> bit) & 1 != 0, 2.0 ** (1 << bit), 1.0)
+        factors.append(factor)
+    return factors
+
+
+def encode(sums_ref, coded_ref):
+    rows, cols = sums_ref.shape
+    groups = rows // GROUP
+    largest = jnp.concatenate([
+        jnp.max(jnp.abs(sums_ref[g * GROUP:(g + 1) * GROUP, :]), axis=0, keepdims=True) for g in range(groups)])
+    rest = largest * 2.0 ** -TOP
+    exponent = jnp.zeros(rest.shape, jnp.int32)
+    for bit in (64, 32, 16, 8, 4, 2, 1):
+        small = rest < 2.0 ** -bit
+        rest = jnp.where(small, rest * 2.0 ** bit, rest)
+        exponent = jnp.where(small, exponent - bit, exponent)
+    one, two = step_factors(exponent)
+    share = 16 // LOW
+    block = rows // share
+    for start in range(0, block, GROUP):
+        low = jnp.zeros((GROUP, cols), jnp.int32)
+        for part in range(share):
+            at = part * block + start
+            g = at // GROUP
+            value = sums_ref[at:at + GROUP, :] * one[g:g + 1] * two[g:g + 1]
+            value = jnp.minimum(jnp.round(value).astype(jnp.int32), (1 << (BITS - 1)) - 1)
+            coded_ref[at:at + GROUP, :] = (value >> LOW).astype(jnp.int16)
+            low = low | ((value & ((1 << LOW) - 1)) << (LOW * part))
+        coded_ref[rows + start:rows + start + GROUP, :] = (low - 32768).astype(jnp.int16)
+    coded_ref[rows + block:, :] = jnp.concatenate([exponent] * (META // groups)).astype(jnp.int16)
+
+
+def add_coded(sums, coded):
+    rows, cols = sums.shape
+    groups = rows // GROUP
+    share = 16 // LOW
+    block = rows // share
+
+    def kernel(sums_ref, coded_ref, out_ref, token_ref):
         token_ref[...] = jnp.zeros_like(token_ref)
-        out_ref[...] = one_ref[...] + two_ref[...]
+        one, two = step_factors(coded_ref[rows + block:, :].astype(jnp.int32)[:groups])
+        one, two = 1.0 / one, 1.0 / two
+        for start in range(0, block, GROUP):
+            low = coded_ref[rows + start:rows + start + GROUP, :].astype(jnp.int32) + 32768
+            for part in range(share):
+                at = part * block + start
+                g = at // GROUP
+                high = coded_ref[at:at + GROUP, :].astype(jnp.int32)
+                value = (high << LOW) | ((low >> (LOW * part)) & ((1 << LOW) - 1))
+                far = value.astype(jnp.float32) * one[g:g + 1] * two[g:g + 1]
+                out_ref[at:at + GROUP, :] = (sums_ref[at:at + GROUP, :] + far).astype(out_ref.dtype)
 
     return call(
-        kernel, "add_sums",
-        out_shape=(jax.ShapeDtypeStruct(one.shape, one.dtype), TOKEN),
+        kernel, "add_coded",
+        out_shape=(jax.ShapeDtypeStruct(sums.shape, jnp.bfloat16), TOKEN),
         in_specs=[VMEM, VMEM],
         out_specs=(VMEM, VMEM),
-    )(one, two)
+    )(sums, coded)
 
 
 def top_and_rest(one, two, at):
@@ -231,7 +300,7 @@
         in_specs=[ANY, ANY],
         out_specs=(VMEM, VMEM),
         scratch_shapes=[pltpu.SemaphoreType.DMA((2,))],
-    )(in_hbm(one), in_hbm(two))
+    )(one, two)
 
 
 Z, X, Y = 4, 2, 2
@@ -323,55 +392,58 @@
     def after(*tokens):
         return lambda *shards: barrier((*shards, tokens))
 
+    near = z // 2 == y
     picks = jnp.stack([
         jnp.where(home, 0, 1),
         jnp.where(home, is_end, -1),
         jnp.where(home, 0, 1),
         jnp.where(home, is_end, 2 + is_end),
         jnp.where(home, -1, is_end),
-    ]).astype(jnp.int32)
-
-    flat_mask = int_mask.reshape(tiles)
+    ] + [jnp.where(near, s, 1 - s) for s in (0, 1, 0, 1, 1)]).astype(jnp.int32)
+
     other = move(integrals, FROM_OTHER_CORE)
-    other_mask, across, other_across = [lax.ppermute(flat_mask, "col", p) for p in (CORES, CHIPS_Y, CROSSWISE)]
-    other_mask, amplitudes_now, picks = barrier((other_mask, amplitudes, picks))
+    other_mask, across, other_across = [lax.ppermute(int_mask, "col", p) for p in (CORES, CHIPS_Y, CROSSWISE)]
+    own = pack_tiles((integrals, other), (int_mask, other_mask), (across, other_across), cap)
+    own, picks, amplitudes_now = barrier((own, picks, amplitudes))
+
     masked, masked_token = mask_tiles(amplitudes_now, amp_mask)
-    own = pack_tiles((integrals, other), (flat_mask, other_mask), (across, other_across), cap)
-
     amps = (masked, lax.ppermute(masked, "col", CORES))
     one, centre, own_x, tokens = after(masked_token)(
         move(own, moves(to_pair)), move(own, moves(over_centre)), move(own, moves(across_x)))
 
-    a_sum, token = shard_product(amps, picks, 0, [[own], [one]], tokens)
-    a_far = move(a_sum, to_y(False, both))
-    two_end, two_mid, one_x, tokens = after(token)(
-        move(centre, moves(outward, False)), move(one, moves(over_centre, False)), move(one, moves(across_x, False)))
-
-    c_sum, token = shard_product(amps, picks, 1, [[two_mid], [two_end]], tokens)
-    c_far = move(c_sum, to_y(True, home_core))
-    b_sum, token = shard_product(amps, picks, 2, [[own_x], [one_x]], (token,))
-    b_far = move(b_sum, to_y(False, both))
-    a_both, a_token = add_sums(a_sum, a_far)
+    a_sum, a_coded, token = shard_product(amps, picks, 0, [[own], [one]], tokens)
+    a_far = move(a_coded, to_y(False, both))
+    two_end, two_mid, one_x, own_x, tokens = after(token)(
+        move(centre, moves(outward, False)), move(one, moves(over_centre, False)), move(one, moves(across_x, False)),
+        own_x)
+
+    c_sum, c_coded, token = shard_product(amps, picks, 1, [[two_mid], [two_end]], tokens)
+    c_far = move(c_coded, to_y(True, home_core))
+    b_sum, b_coded, token = shard_product(amps, picks, 2, [[own_x], [one_x]], (token,))
+    b_far = move(b_coded, to_y(False, both))
+    a_both, a_token = add_coded(a_sum, a_far)
     three_end, three_mid_x, two_x_end, two_x_mid, tokens = after(token, a_token)(
         move(two_mid, moves(outward)), move(own_x, moves(over_centre)),
         move(two_end, moves(across_x_ends)), move(two_mid, moves(across_x_middle)))
 
-    d_sum, token = shard_product(
+    d_sum, d_coded, token = shard_product(
         amps, picks, 3, [[two_x_mid], [two_x_end], [centre], [three_end]], tokens)
     top, rest = top_and_rest(three_end, two_x_mid, half)
-    three_x, three_x_rest, tokens = after(token)(
+    c_both, c_token = add_coded(c_sum, c_far)
+    three_x, three_x_rest, tokens = after(token, c_token)(
         move(top, moves(across_x_ends, False)), move(rest, moves(outward)))
 
-    d_far = move(d_sum, to_y(True, both))
-    e_sum, token = shard_product(amps, picks, 4, [[three_mid_x], [three_x, three_x_rest]], tokens)
-    e_far = move(e_sum, to_y(True, other_core))
+    d_far = move(d_coded, to_y(True, both))
+    e_sum, e_coded, token = shard_product(amps, picks, 4, [[three_mid_x], [three_x, three_x_rest]], tokens)
+    e_far = move(e_coded, to_y(True, other_core))
     excess = token + lax.ppermute(token, "col", CORES)
+    b_both, _ = add_coded(b_sum, b_far)
+    d_both, _ = add_coded(d_sum, d_far)
+    e_both, _ = add_coded(e_sum, e_far)
 
     def finish():
-        near = z // 2 == y
-        d_both = d_sum + d_far
-        mine = jnp.where(near, a_both, jnp.where(home, c_sum + c_far, d_both)).astype(jnp.bfloat16)
-        rest = jnp.where(near, b_sum + b_far, jnp.where(home, d_both, e_sum + e_far)).astype(jnp.bfloat16)
+        mine = jnp.where(near, a_both, jnp.where(home, c_both, d_both))
+        rest = jnp.where(near, b_both, jnp.where(home, d_both, e_both))
         return jnp.concatenate([jnp.where(x == 0, mine, rest), jnp.where(x == 0, rest, mine)], axis=1)
 
     return lax.cond(

time: 161 us -> 132 us (0.82)
  the two profiles are of different devices: /device:TPU:12 before, /device:TPU:16 now
where the time goes in v3:
time: 132 us; the launch traced here: 131 us
  waiting for transfers between devices  54.5 us (41%)
  starting transfers between devices  38.3 us (29%)
  Pallas kernels  32.3 us (24%)
  other arithmetic  3.1 us (2%)
  local copies, waits for them, and re-layouts  1.98 us (2%)
    ppermute x18, waiting for transfers between devices, move(): return lax.ppermute(value, AXES, pairs)  51.5 us
    ppermute x18, starting transfers between devices, move(): return lax.ppermute(value, AXES, pairs)  35.4 us
    pallas_call x5, Pallas kernels, shard_product(): call(kernel, 'shard_product', out_shape=(jax.ShapeDtypeStruct((rows, wide...  19.8 us
    pallas_call x5, Pallas kernels, add_coded(): call(kernel, 'add_coded', out_shape=(jax.ShapeDtypeStruct(sums.shape, jnp...  5.29 us
    pallas_call x1, Pallas kernels, mask_tiles(): call(kernel, 'mask_tiles', pl.CostEstimate(flops=0, bytes_accessed=4 * am...  4.64 us
    ppermute x3, waiting for transfers between devices, sparse_ladder(): lax.ppermute(int_mask, 'col', p)  2.98 us
    ppermute x3, starting transfers between devices, sparse_ladder(): lax.ppermute(int_mask, 'col', p)  2.71 us
  transfers between devices with their start and end apart: 23, of which 9 were waited for; matrix products, arithmetic and copies ran while one was open for 1% of the time, Pallas kernels for 19%

profile of v3, /device:TPU:16, one launch (start us, length us, event | category | flops | bytes accessed | tf_op | source)
XLA Modules:
  0.0 131.3 jit_solution(3461175789198374844)
XLA Ops:
  0.0 1.3 collective-permute-start.13
  1.3 0.8 copy.11.refs_0_
  2.0 1.2 collective-permute-start.10
  3.2 1.5 %collective-permute-start.11 = (s32[16,2]{1,0:T(8,128)S(1)}, s32[16,2]{1,0:T(8,128)S(1)}, u32[]{:S(2)}, u32[]{:S(2)}) collective-permute-start(s32[16,2]{1,0:T(8,128)S(1)} %copy.11.refs_0_), channel_id=1, source_target_pairs={{0,2},{2,0},{1,3},{3,1},{4,6},{6,4},{5,7},{7,5},{8,10},{10,8},{9,1... | collective-permute-start | bytes 392 | tf_op jit(solution)/shard_map/ppermute | solution.py:405
  4.8 0.0 collective-permute-start.12
  4.8 0.1 stack.31.picks_ref
  4.8 0.0 collective-permute-done.10.refs_1_
  4.9 2.0 %collective-permute-done.11.refs_2_ = s32[16,2]{1,0:T(8,128)S(1)} collective-permute-done((s32[16,2]{1,0:T(8,128)S(1)}, s32[16,2]{1,0:T(8,128)S(1)}, u32[]{:S(2)}, u32[]{:S(2)}) %collective-permute-start.11) | collective-permute-done | bytes 160 | tf_op jit(solution)/shard_map/ppermute | solution.py:405
  6.9 0.9 collective-permute-done.12.refs_3_
  7.8 0.0 collective-permute-done.13.refs_5_
  7.8 1.9 %pack_tiles.1.refs_3_ = bf16[5648,128]{1,0:T(8,128)(2,1)S(1)} custom-call(s32[16,2]{1,0:T(8,128)S(1)} %copy.11.refs_0_, s32[16,2]{1,0:T(8,128)S(1)} %collective-permute-done.10.refs_1_, s32[16,2]{1,0:T(8,128)S(1)} %collective-permute-done.11.refs_2_, s32[16,2]{1,0:T(8,128)S(1)} %collective-permute-done.12.refs_3_, bf16[2048,256]{1,0:T(8,128)(2,1)} %refs_4_.1, ...), custom_call_target="tpu_custom_call" | custom-call | flops 1 | bytes 1 | tf_op jit(solution)/shard_map/pack_tiles/pallas_call | solution.py:93
  9.8 4.6 %mask_tiles.1 = (bf16[1024,2048]{1,0:T(8,128)(2,1)S(1)}, f32[8,128]{1,0:T(8,128)S(1)}) custom-call(s32[8,16]{1,0:T(8,128)} %mask_ref.1, bf16[1024,2048]{1,0:T(8,128)(2,1)} %a_ref), custom_call_target="tpu_custom_call" | custom-call | bytes 8388608 | tf_op jit(solution)/shard_map/mask_tiles/pallas_call | solution.py:122
  14.4 0.1 collective-permute-start.20
  14.5 3.1 %collective-permute-start.14 = (bf16[5648,128]{1,0:T(8,128)(2,1)S(1)}, bf16[5648,128]{1,0:T(8,128)(2,1)S(1)}, u32[]{:S(2)}, u32[]{:S(2)}) collective-permute-start(bf16[5648,128]{1,0:T(8,128)(2,1)S(1)} %pack_tiles.1.refs_3_), channel_id=1, source_target_pairs={{0,8},{2,10},{4,12},{6,14},{9,1},{11,3},{13,5},{15,7},{16,24},{18,... | collective-permute-start | bytes 4337672 | tf_op jit(solution)/shard_map/ppermute | solution.py:390
  17.6 1.4 %collective-permute-start.15 = (bf16[5648,128]{1,0:T(8,128)(2,1)S(1)}, bf16[5648,128]{1,0:T(8,128)(2,1)S(1)}, u32[]{:S(2)}, u32[]{:S(2)}) collective-permute-start(bf16[5648,128]{1,0:T(8,128)(2,1)S(1)} %pack_tiles.1.refs_3_), channel_id=1, source_target_pairs={{9,17},{11,19},{13,21},{15,23},{16,8},{18,10},{20,12},{22,14}} | collective-permute-start | bytes 4337672 | tf_op jit(solution)/shard_map/ppermute | solution.py:390
  19.0 3.4 %collective-permute-start.16 = (bf16[5648,128]{1,0:T(8,128)(2,1)S(1)}, bf16[5648,128]{1,0:T(8,128)(2,1)S(1)}, u32[]{:S(2)}, u32[]{:S(2)}) collective-permute-start(bf16[5648,128]{1,0:T(8,128)(2,1)S(1)} %pack_tiles.1.refs_3_), channel_id=1, source_target_pairs={{0,4},{2,6},{4,0},{6,2},{9,13},{11,15},{13,9},{15,11},{16,20},{18,... | collective-permute-start | bytes 4337672 | tf_op jit(solution)/shard_map/ppermute | solution.py:390
  22.5 11.6 %collective-permute-done.14.refs_4_ = bf16[5648,128]{1,0:T(8,128)(2,1)S(1)} collective-permute-done((bf16[5648,128]{1,0:T(8,128)(2,1)S(1)}, bf16[5648,128]{1,0:T(8,128)(2,1)S(1)}, u32[]{:S(2)}, u32[]{:S(2)}) %collective-permute-start.14) | collective-permute-done | bytes 1445920 | tf_op jit(solution)/shard_map/ppermute | solution.py:390
  34.1 1.4 %collective-permute-done.15.refs_6_ = bf16[5648,128]{1,0:T(8,128)(2,1)S(1)} collective-permute-done((bf16[5648,128]{1,0:T(8,128)(2,1)S(1)}, bf16[5648,128]{1,0:T(8,128)(2,1)S(1)}, u32[]{:S(2)}, u32[]{:S(2)}) %collective-permute-start.15) | collective-permute-done | bytes 1445920 | tf_op jit(solution)/shard_map/ppermute | solution.py:390
  35.5 4.5 %collective-permute-done.16.refs_3_ = bf16[5648,128]{1,0:T(8,128)(2,1)S(1)} collective-permute-done((bf16[5648,128]{1,0:T(8,128)(2,1)S(1)}, bf16[5648,128]{1,0:T(8,128)(2,1)S(1)}, u32[]{:S(2)}, u32[]{:S(2)}) %collective-permute-start.16) | collective-permute-done | bytes 1445920 | tf_op jit(solution)/shard_map/ppermute | solution.py:390
  40.0 0.7 collective-permute-start.17
  40.7 1.3 collective-permute-start.18
  42.0 0.8 collective-permute-start.19
  42.8 0.0 collective-permute-done.20.refs_2_.refs_3_
  42.8 5.0 %shard_product.5 = (f32[1024,256]{1,0:T(8,128)S(1)}, s16[1296,256]{1,0:T(8,128)(2,1)S(1)}, f32[8,128]{1,0:T(8,128)S(1)}) custom-call(s32[10]{0:T(128)S(1)} %stack.31.picks_ref, f32[8,128]{1,0:T(8,128)S(1)} %get-tuple-element.110.refs_0_, bf16[1024,2048]{1,0:T(8,128)(2,1)S(1)} %get-tuple-element.111.refs_1_.refs_2_, ...), custom_call_target="tpu_custom_call" | custom-call | flops 1 | bytes 1 | tf_op jit(solution)/shard_map/shard_product/pallas_call | solution.py:199
  47.8 0.0 collective-permute-done.17.refs_4_
  47.8 13.8 %collective-permute-done.18.refs_3_ = bf16[5648,128]{1,0:T(8,128)(2,1)S(1)} collective-permute-done((bf16[5648,128]{1,0:T(8,128)(2,1)S(1)}, bf16[5648,128]{1,0:T(8,128)(2,1)S(1)}, u32[]{:S(2)}, u32[]{:S(2)}) %collective-permute-start.18) | collective-permute-done | bytes 1445920 | tf_op jit(solution)/shard_map/ppermute | solution.py:390
  61.7 0.0 collective-permute-done.19.refs_4_
  61.7 1.4 %collective-permute-start.21 = (bf16[5648,128]{1,0:T(8,128)(2,1)S(1)}, bf16[5648,128]{1,0:T(8,128)(2,1)S(1)}, u32[]{:S(2)}, u32[]{:S(2)}) collective-permute-start(bf16[5648,128]{1,0:T(8,128)(2,1)S(1)} %collective-permute-done.18.refs_3_), channel_id=1, source_target_pairs={{9,1},{11,3},{13,5},{15,7},{16,24},{18,26},{20,28},{22,30}} | collective-permute-start | bytes 4337672 | tf_op jit(solution)/shard_map/ppermute | solution.py:390
  63.1 5.4 %collective-permute-start.22 = (bf16[5648,128]{1,0:T(8,128)(2,1)S(1)}, bf16[5648,128]{1,0:T(8,128)(2,1)S(1)}, u32[]{:S(2)}, u32[]{:S(2)}) collective-permute-start(bf16[5648,128]{1,0:T(8,128)(2,1)S(1)} %collective-permute-done.16.refs_3_), channel_id=1, source_target_pairs={{9,17},{11,19},{13,21},{15,23},{16,8},{18,10},{20,12},{22,14}} | collective-permute-start | bytes 4337672 | tf_op jit(solution)/shard_map/ppermute | solution.py:390
  68.5 0.8 collective-permute-start.23
  69.2 3.4 %collective-permute-start.24 = (bf16[5648,128]{1,0:T(8,128)(2,1)S(1)}, bf16[5648,128]{1,0:T(8,128)(2,1)S(1)}, u32[]{:S(2)}, u32[]{:S(2)}) collective-permute-start(bf16[5648,128]{1,0:T(8,128)(2,1)S(1)} %collective-permute-done.18.refs_3_), channel_id=1, source_target_pairs={{9,13},{11,15},{13,9},{15,11},{16,20},{18,22},{20,16},{22,18}} | collective-permute-start | bytes 4337672 | tf_op jit(solution)/shard_map/ppermute | solution.py:390
  72.7 2.4 %collective-permute-start.25 = (s16[1296,256]{1,0:T(8,128)(2,1)S(1)}, s16[1296,256]{1,0:T(8,128)(2,1)S(1)}, u32[]{:S(2)}, u32[]{:S(2)}) collective-permute-start(s16[1296,256]{1,0:T(8,128)(2,1)S(1)} %get-tuple-element.121), channel_id=1, source_target_pairs={{2,0},{3,1},{6,4},{7,5},{10,8},{11,9},{14,12},{15,13},{16,18},{17,... | collective-permute-start | bytes 1990664 | tf_op jit(solution)/shard_map/ppermute | solution.py:390
  75.1 4.5 %shard_product.6 = (f32[1024,256]{1,0:T(8,128)S(1)}, s16[1296,256]{1,0:T(8,128)(2,1)S(1)}, f32[8,128]{1,0:T(8,128)S(1)}) custom-call(s32[10]{0:T(128)S(1)} %stack.31.picks_ref, f32[8,128]{1,0:T(8,128)S(1)} %get-tuple-element.116.refs_0_, bf16[1024,2048]{1,0:T(8,128)(2,1)S(1)} %get-tuple-element.111.refs_1_.refs_2_, ...), custom_call_target="tpu_custom_call" | custom-call | flops 1 | bytes 1 | tf_op jit(solution)/shard_map/shard_product/pallas_call | solution.py:199
  79.6 5.2 %shard_product.7 = (f32[1024,256]{1,0:T(8,128)S(1)}, s16[1296,256]{1,0:T(8,128)(2,1)S(1)}, f32[8,128]{1,0:T(8,128)S(1)}) custom-call(s32[10]{0:T(128)S(1)} %stack.31.picks_ref, f32[8,128]{1,0:T(8,128)S(1)} %get-tuple-element.117.refs_0_, bf16[1024,2048]{1,0:T(8,128)(2,1)S(1)} %get-tuple-element.111.refs_1_.refs_2_, ...), custom_call_target="tpu_custom_call" | custom-call | flops 1 | bytes 1 | tf_op jit(solution)/shard_map/shard_product/pallas_call | solution.py:199
  84.8 0.0 collective-permute-done.25.coded_ref
  84.8 1.2 add_coded.5
  86.0 4.2 %collective-permute-done.24.two_ref.refs_4_ = bf16[5648,128]{1,0:T(8,128)(2,1)S(1)} collective-permute-done((bf16[5648,128]{1,0:T(8,128)(2,1)S(1)}, bf16[5648,128]{1,0:T(8,128)(2,1)S(1)}, u32[]{:S(2)}, u32[]{:S(2)}) %collective-permute-start.24) | collective-permute-done | bytes 1445920 | tf_op jit(solution)/shard_map/ppermute | solution.py:390
  90.2 0.6 top_and_rest.1
  90.8 1.3 %collective-permute-start.27 = (bf16[2832,128]{1,0:T(8,128)(2,1)S(1)}, bf16[2832,128]{1,0:T(8,128)(2,1)S(1)}, u32[]{:S(2)}, u32[]{:S(2)}) collective-permute-start(bf16[2832,128]{1,0:T(8,128)(2,1)S(1)} %get-tuple-element.126), channel_id=1, source_target_pairs={{9,1},{11,3},{13,5},{15,7},{16,24},{18,26},{20,28},{22,30}} | collective-permute-start | bytes 2174984 | tf_op jit(solution)/shard_map/ppermute | solution.py:390
  92.1 0.7 collective-permute-start.26
  92.8 1.3 collective-permute-start.28
  94.1 4.6 %collective-permute-start.32 = (s16[1296,256]{1,0:T(8,128)(2,1)S(1)}, s16[1296,256]{1,0:T(8,128)(2,1)S(1)}, u32[]{:S(2)}, u32[]{:S(2)}) collective-permute-start(s16[1296,256]{1,0:T(8,128)(2,1)S(1)} %get-tuple-element.149), channel_id=1, source_target_pairs={{2,0},{3,1},{6,4},{7,5},{10,8},{11,9},{14,12},{15,13},{16,18},{17,... | collective-permute-start | bytes 1990664 | tf_op jit(solution)/shard_map/ppermute | solution.py:390
  98.8 4.5 %shard_product.8 = (f32[1024,256]{1,0:T(8,128)S(1)}, s16[1296,256]{1,0:T(8,128)(2,1)S(1)}, f32[8,128]{1,0:T(8,128)S(1)}) custom-call(s32[10]{0:T(128)S(1)} %stack.31.picks_ref, f32[8,128]{1,0:T(8,128)S(1)} %get-tuple-element.127.refs_0_, f32[8,128]{1,0:T(8,128)S(1)} %get-tuple-element.128.refs_1_, bf16[1024,2048]{1,0:T(8,128)(2,1)S(1)} %get-tuple-element.111.refs_1_.refs_2_, ...), custom_call_target="tpu_custom_call" | custom-call | flops 1 | bytes 1 | tf_op jit(solution)/shard_map/shard_product/pallas_call | solution.py:199
  103.3 1.3 collective-permute-start.30
  104.6 7.9 %collective-permute-done.28.coded_ref = s16[1296,256]{1,0:T(8,128)(2,1)S(1)} collective-permute-done((s16[1296,256]{1,0:T(8,128)(2,1)S(1)}, s16[1296,256]{1,0:T(8,128)(2,1)S(1)}, u32[]{:S(2)}, u32[]{:S(2)}) %collective-permute-start.28) | collective-permute-done | bytes 663584 | tf_op jit(solution)/shard_map/ppermute | solution.py:390
  112.5 1.2 add_coded.6
  113.7 0.0 copy-start.15
  113.7 0.9 copy-done.16
  114.6 0.2 copy-done.15
  114.8 0.6 shard_product.9
  115.4 0.0 copy-start.6
  115.4 0.0 copy-start.17
  115.4 0.0 copy-start.18
  115.4 0.8 collective-permute-start.31
  116.2 0.1 collective-permute-start.29
  116.3 1.2 add_coded.9
  117.5 8.1 %collective-permute-done.30.coded_ref = s16[1296,256]{1,0:T(8,128)(2,1)S(1)} collective-permute-done((s16[1296,256]{1,0:T(8,128)(2,1)S(1)}, s16[1296,256]{1,0:T(8,128)(2,1)S(1)}, u32[]{:S(2)}, u32[]{:S(2)}) %collective-permute-start.30) | collective-permute-done | bytes 663584 | tf_op jit(solution)/shard_map/ppermute | solution.py:390
  125.7 1.2 add_coded.7
  126.8 0.6 add_reduce_fusion
  128.1 0.6 add_coded.8
  128.7 2.5 %conditional.1 = (bf16[1024,512]{1,0:T(8,128)(2,1)}) conditional(s32[]{:T(128)} %convert_element_type.32, (s32[]{:T(128)}, pred[]{:T(512)}, pred[]{:T(512)}, bf16[1024,256]{1,0:T(8,128)(2,1)}, bf16[1024,256]{1,0:T(8,128)(2,1)}, /*index=5*/bf16[1024,256]{1,0:T(8,128)(2,1)}, bf16[1024,256]{1,0:T(8,128)(2,1)S(1)}, ...), branch_computations={%region_1.2_spmd, %region_2.3_spmd} | conditional | flops 8594653184 | bytes 206655584 | solution.py:449
  128.7 1.4 %broadcast_select_fusion.1 = (bf16[1024,256]{1,0:T(8,128)(2,1)S(1)}, bf16[1024,256]{1,0:T(8,128)(2,1)S(1)}, bf16[1024,256]{1,0:T(8,128)(2,1)S(1)}) fusion(pred[]{:T(512)S(6)} %eq.26, bf16[1024,256]{1,0:T(8,128)(2,1)} %get-tuple-element.45, bf16[1024,256]{1,0:T(8,128)(2,1)} %get-tuple-element.47, bf16[1024,256]{1,0:T(8,128)(2,1)} %get-tuple-element.48, ...), kind=kLoop, calls=%fused_computation.4 | loop fusion | flops 1310720 | bytes 4194307 | tf_op jit(solution)/shard_map/cond/branch_0_fun/jit(_where)/select_n | solution.py:447
  130.1 0.1 broadcast_select_fusion
  130.2 1.1 pad_maximum_fusion
  (34 shorter events, 0.1 us)
Async XLA Ops:
  0.0 7.8 %collective-permute-start.13 = (bf16[2048,256]{1,0:T(8,128)(2,1)}, bf16[2048,256]{1,0:T(8,128)(2,1)S(1)}, u32[]{:S(2)}, u32[]{:S(2)}) collective-permute-start(bf16[2048,256]{1,0:T(8,128)(2,1)} %refs_4_.1), channel_id=1, source_target_pairs={{1,0},{3,2},{5,4},{7,6},{8,9},{10,11},{12,13},{14,15},{17,16},{19,... | collective-permute-start | bytes 3145736 | tf_op jit(solution)/shard_map/ppermute | solution.py:390
  2.0 2.8 %collective-permute-start.10 = (s32[16,2]{1,0:T(8,128)S(1)}, s32[16,2]{1,0:T(8,128)S(1)}, u32[]{:S(2)}, u32[]{:S(2)}) collective-permute-start(s32[16,2]{1,0:T(8,128)S(1)} %copy.11.refs_0_), channel_id=1, source_target_pairs={{0,1},{1,0},{2,3},{3,2},{4,5},{5,4},{6,7},{7,6},{8,9},{9,8},{10,11... | collective-permute-start | bytes 392 | tf_op jit(solution)/shard_map/ppermute | solution.py:405
  3.2 3.7 %collective-permute-start.11 = (s32[16,2]{1,0:T(8,128)S(1)}, s32[16,2]{1,0:T(8,128)S(1)}, u32[]{:S(2)}, u32[]{:S(2)}) collective-permute-start(s32[16,2]{1,0:T(8,128)S(1)} %copy.11.refs_0_), channel_id=1, source_target_pairs={{0,2},{2,0},{1,3},{3,1},{4,6},{6,4},{5,7},{7,5},{8,10},{10,8},{9,1... | collective-permute-start | bytes 392 | tf_op jit(solution)/shard_map/ppermute | solution.py:405
  4.8 3.1 %collective-permute-start.12 = (s32[16,2]{1,0:T(8,128)S(1)}, s32[16,2]{1,0:T(8,128)S(1)}, u32[]{:S(2)}, u32[]{:S(2)}) collective-permute-start(s32[16,2]{1,0:T(8,128)S(1)} %copy.11.refs_0_), channel_id=1, source_target_pairs={{0,3},{3,0},{1,2},{2,1},{4,7},{7,4},{5,6},{6,5},{8,11},{11,8},{9,1... | collective-permute-start | bytes 392 | tf_op jit(solution)/shard_map/ppermute | solution.py:405
  9.8 33.0 %copy-start.2 = (bf16[5648,128]{1,0:T(8,128)(2,1)}, bf16[5648,128]{1,0:T(8,128)(2,1)S(1)}, u32[]{:S(2)}) copy-start(bf16[5648,128]{1,0:T(8,128)(2,1)S(1)} %pack_tiles.1.refs_3_) | copy-start | bytes 4337668
  14.4 28.3 %collective-permute-start.20 = (bf16[1024,2048]{1,0:T(8,128)(2,1)S(1)}, bf16[1024,2048]{1,0:T(8,128)(2,1)S(1)}, u32[]{:S(2)}, u32[]{:S(2)}) collective-permute-start(bf16[1024,2048]{1,0:T(8,128)(2,1)S(1)} %get-tuple-element.111.refs_1_.refs_2_), channel_id=1, source_target_pairs={{0,1},{1,0},{2,3},{3,2},{4,5},{5,4},{6,7},{7,6},{8,9},{9,8},{10,11... | collective-permute-start | bytes 12582920 | tf_op jit(solution)/shard_map/ppermute | solution.py:410
  14.5 19.6 %collective-permute-start.14 = (bf16[5648,128]{1,0:T(8,128)(2,1)S(1)}, bf16[5648,128]{1,0:T(8,128)(2,1)S(1)}, u32[]{:S(2)}, u32[]{:S(2)}) collective-permute-start(bf16[5648,128]{1,0:T(8,128)(2,1)S(1)} %pack_tiles.1.refs_3_), channel_id=1, source_target_pairs={{0,8},{2,10},{4,12},{6,14},{9,1},{11,3},{13,5},{15,7},{16,24},{18,... | collective-permute-start | bytes 4337672 | tf_op jit(solution)/shard_map/ppermute | solution.py:390
  17.6 17.9 %collective-permute-start.15 = (bf16[5648,128]{1,0:T(8,128)(2,1)S(1)}, bf16[5648,128]{1,0:T(8,128)(2,1)S(1)}, u32[]{:S(2)}, u32[]{:S(2)}) collective-permute-start(bf16[5648,128]{1,0:T(8,128)(2,1)S(1)} %pack_tiles.1.refs_3_), channel_id=1, source_target_pairs={{9,17},{11,19},{13,21},{15,23},{16,8},{18,10},{20,12},{22,14}} | collective-permute-start | bytes 4337672 | tf_op jit(solution)/shard_map/ppermute | solution.py:390
  19.0 20.9 %collective-permute-start.16 = (bf16[5648,128]{1,0:T(8,128)(2,1)S(1)}, bf16[5648,128]{1,0:T(8,128)(2,1)S(1)}, u32[]{:S(2)}, u32[]{:S(2)}) collective-permute-start(bf16[5648,128]{1,0:T(8,128)(2,1)S(1)} %pack_tiles.1.refs_3_), channel_id=1, source_target_pairs={{0,4},{2,6},{4,0},{6,2},{9,13},{11,15},{13,9},{15,11},{16,20},{18,... | collective-permute-start | bytes 4337672 | tf_op jit(solution)/shard_map/ppermute | solution.py:390
  34.1 8.7 %copy-start.14 = (bf16[5648,128]{1,0:T(8,128)(2,1)}, bf16[5648,128]{1,0:T(8,128)(2,1)S(1)}, u32[]{:S(2)}) copy-start(bf16[5648,128]{1,0:T(8,128)(2,1)S(1)} %collective-permute-done.14.refs_4_) | copy-start | bytes 4337668
  35.5 12.3 %copy-start.7 = (bf16[5648,128]{1,0:T(8,128)(2,1)}, bf16[5648,128]{1,0:T(8,128)(2,1)S(1)}, u32[]{:S(2)}) copy-start(bf16[5648,128]{1,0:T(8,128)(2,1)S(1)} %collective-permute-done.15.refs_6_) | copy-start | bytes 4337668
  40.0 23.1 %copy-start.9 = (bf16[5648,128]{1,0:T(8,128)(2,1)}, bf16[5648,128]{1,0:T(8,128)(2,1)S(1)}, u32[]{:S(2)}) copy-start(bf16[5648,128]{1,0:T(8,128)(2,1)S(1)} %collective-permute-done.16.refs_3_) | copy-start | bytes 4337668
  40.0 7.8 %collective-permute-start.17 = (bf16[5648,128]{1,0:T(8,128)(2,1)S(1)}, bf16[5648,128]{1,0:T(8,128)(2,1)S(1)}, u32[]{:S(2)}, u32[]{:S(2)}) collective-permute-start(bf16[5648,128]{1,0:T(8,128)(2,1)S(1)} %collective-permute-done.15.refs_6_), channel_id=1, source_target_pairs={{8,0},{10,2},{12,4},{14,6},{17,25},{19,27},{21,29},{23,31}} | collective-permute-start | bytes 4337672 | tf_op jit(solution)/shard_map/ppermute | solution.py:390
  40.7 20.9 %collective-permute-start.18 = (bf16[5648,128]{1,0:T(8,128)(2,1)S(1)}, bf16[5648,128]{1,0:T(8,128)(2,1)S(1)}, u32[]{:S(2)}, u32[]{:S(2)}) collective-permute-start(bf16[5648,128]{1,0:T(8,128)(2,1)S(1)} %collective-permute-done.14.refs_4_), channel_id=1, source_target_pairs={{8,16},{10,18},{12,20},{14,22},{17,9},{19,11},{21,13},{23,15}} | collective-permute-start | bytes 4337672 | tf_op jit(solution)/shard_map/ppermute | solution.py:390
  42.0 19.7 %collective-permute-start.19 = (bf16[5648,128]{1,0:T(8,128)(2,1)S(1)}, bf16[5648,128]{1,0:T(8,128)(2,1)S(1)}, u32[]{:S(2)}, u32[]{:S(2)}) collective-permute-start(bf16[5648,128]{1,0:T(8,128)(2,1)S(1)} %collective-permute-done.14.refs_4_), channel_id=1, source_target_pairs={{1,5},{3,7},{5,1},{7,3},{8,12},{10,14},{12,8},{14,10},{17,21},{19,... | collective-permute-start | bytes 4337672 | tf_op jit(solution)/shard_map/ppermute | solution.py:390
  47.8 27.3 %copy-start.10 = (bf16[5648,128]{1,0:T(8,128)(2,1)}, bf16[5648,128]{1,0:T(8,128)(2,1)S(1)}, u32[]{:S(2)}) copy-start(bf16[5648,128]{1,0:T(8,128)(2,1)S(1)} %collective-permute-done.17.refs_4_) | copy-start | bytes 4337668
  61.7 13.4 %copy-start.11 = (bf16[5648,128]{1,0:T(8,128)(2,1)}, bf16[5648,128]{1,0:T(8,128)(2,1)S(1)}, u32[]{:S(2)}) copy-start(bf16[5648,128]{1,0:T(8,128)(2,1)S(1)} %collective-permute-done.18.refs_3_) | copy-start | bytes 4337668
  61.7 18.0 %copy-start.13 = (bf16[5648,128]{1,0:T(8,128)(2,1)}, bf16[5648,128]{1,0:T(8,128)(2,1)S(1)}, u32[]{:S(2)}) copy-start(bf16[5648,128]{1,0:T(8,128)(2,1)S(1)} %collective-permute-done.19.refs_4_) | copy-start | bytes 4337668
  61.7 24.3 %collective-permute-start.21 = (bf16[5648,128]{1,0:T(8,128)(2,1)S(1)}, bf16[5648,128]{1,0:T(8,128)(2,1)S(1)}, u32[]{:S(2)}, u32[]{:S(2)}) collective-permute-start(bf16[5648,128]{1,0:T(8,128)(2,1)S(1)} %collective-permute-done.18.refs_3_), channel_id=1, source_target_pairs={{9,1},{11,3},{13,5},{15,7},{16,24},{18,26},{20,28},{22,30}} | collective-permute-start | bytes 4337672 | tf_op jit(solution)/shard_map/ppermute | solution.py:390
  63.1 22.9 %collective-permute-start.22 = (bf16[5648,128]{1,0:T(8,128)(2,1)S(1)}, bf16[5648,128]{1,0:T(8,128)(2,1)S(1)}, u32[]{:S(2)}, u32[]{:S(2)}) collective-permute-start(bf16[5648,128]{1,0:T(8,128)(2,1)S(1)} %collective-permute-done.16.refs_3_), channel_id=1, source_target_pairs={{9,17},{11,19},{13,21},{15,23},{16,8},{18,10},{20,12},{22,14}} | collective-permute-start | bytes 4337672 | tf_op jit(solution)/shard_map/ppermute | solution.py:390
  68.5 17.5 %collective-permute-start.23 = (bf16[5648,128]{1,0:T(8,128)(2,1)S(1)}, bf16[5648,128]{1,0:T(8,128)(2,1)S(1)}, u32[]{:S(2)}, u32[]{:S(2)}) collective-permute-start(bf16[5648,128]{1,0:T(8,128)(2,1)S(1)} %collective-permute-done.17.refs_4_), channel_id=1, source_target_pairs={{0,4},{2,6},{4,0},{6,2},{25,29},{27,31},{29,25},{31,27}} | collective-permute-start | bytes 4337672 | tf_op jit(solution)/shard_map/ppermute | solution.py:390
  69.2 20.9 %collective-permute-start.24 = (bf16[5648,128]{1,0:T(8,128)(2,1)S(1)}, bf16[5648,128]{1,0:T(8,128)(2,1)S(1)}, u32[]{:S(2)}, u32[]{:S(2)}) collective-permute-start(bf16[5648,128]{1,0:T(8,128)(2,1)S(1)} %collective-permute-done.18.refs_3_), channel_id=1, source_target_pairs={{9,13},{11,15},{13,9},{15,11},{16,20},{18,22},{20,16},{22,18}} | collective-permute-start | bytes 4337672 | tf_op jit(solution)/shard_map/ppermute | solution.py:390
  72.7 12.1 %collective-permute-start.25 = (s16[1296,256]{1,0:T(8,128)(2,1)S(1)}, s16[1296,256]{1,0:T(8,128)(2,1)S(1)}, u32[]{:S(2)}, u32[]{:S(2)}) collective-permute-start(s16[1296,256]{1,0:T(8,128)(2,1)S(1)} %get-tuple-element.121), channel_id=1, source_target_pairs={{2,0},{3,1},{6,4},{7,5},{10,8},{11,9},{14,12},{15,13},{16,18},{17,... | collective-permute-start | bytes 1990664 | tf_op jit(solution)/shard_map/ppermute | solution.py:390
  86.0 12.8 %copy-start = (bf16[5648,128]{1,0:T(8,128)(2,1)}, bf16[5648,128]{1,0:T(8,128)(2,1)S(1)}, u32[]{:S(2)}) copy-start(bf16[5648,128]{1,0:T(8,128)(2,1)S(1)} %collective-permute-done.21.one_ref.refs_7_) | copy-start | bytes 4337668
  86.0 27.7 %copy-start.8 = (bf16[5648,128]{1,0:T(8,128)(2,1)}, bf16[5648,128]{1,0:T(8,128)(2,1)S(1)}, u32[]{:S(2)}) copy-start(bf16[5648,128]{1,0:T(8,128)(2,1)S(1)} %collective-permute-done.22.refs_4_) | copy-start | bytes 4337668
  86.0 12.8 %copy-start.12 = (bf16[5648,128]{1,0:T(8,128)(2,1)}, bf16[5648,128]{1,0:T(8,128)(2,1)S(1)}, u32[]{:S(2)}) copy-start(bf16[5648,128]{1,0:T(8,128)(2,1)S(1)} %collective-permute-done.23.refs_5_) | copy-start | bytes 4337668
  90.2 8.6 %copy-start.1 = (bf16[5648,128]{1,0:T(8,128)(2,1)}, bf16[5648,128]{1,0:T(8,128)(2,1)S(1)}, u32[]{:S(2)}) copy-start(bf16[5648,128]{1,0:T(8,128)(2,1)S(1)} %collective-permute-done.24.two_ref.refs_4_) | copy-start | bytes 4337668
  90.8 22.9 %collective-permute-start.27 = (bf16[2832,128]{1,0:T(8,128)(2,1)S(1)}, bf16[2832,128]{1,0:T(8,128)(2,1)S(1)}, u32[]{:S(2)}, u32[]{:S(2)}) collective-permute-start(bf16[2832,128]{1,0:T(8,128)(2,1)S(1)} %get-tuple-element.126), channel_id=1, source_target_pairs={{9,1},{11,3},{13,5},{15,7},{16,24},{18,26},{20,28},{22,30}} | collective-permute-start | bytes 2174984 | tf_op jit(solution)/shard_map/ppermute | solution.py:390
  92.1 21.6 %collective-permute-start.26 = (bf16[2816,128]{1,0:T(8,128)(2,1)S(1)}, bf16[2816,128]{1,0:T(8,128)(2,1)S(1)}, u32[]{:S(2)}, u32[]{:S(2)}) collective-permute-start(bf16[2816,128]{1,0:T(8,128)(2,1)S(1)} %get-tuple-element.125), channel_id=1, source_target_pairs={{1,5},{3,7},{5,1},{7,3},{24,28},{26,30},{28,24},{30,26}} | collective-permute-start | bytes 2162696 | tf_op jit(solution)/shard_map/ppermute | solution.py:390
  92.8 19.7 %collective-permute-start.28 = (s16[1296,256]{1,0:T(8,128)(2,1)S(1)}, s16[1296,256]{1,0:T(8,128)(2,1)S(1)}, u32[]{:S(2)}, u32[]{:S(2)}) collective-permute-start(s16[1296,256]{1,0:T(8,128)(2,1)S(1)} %get-tuple-element.132), channel_id=1, source_target_pairs={{0,2},{4,6},{9,11},{13,15},{18,16},{22,20},{27,25},{31,29}} | collective-permute-start | bytes 1990664 | tf_op jit(solution)/shard_map/ppermute | solution.py:390
  94.1 22.2 %collective-permute-start.32 = (s16[1296,256]{1,0:T(8,128)(2,1)S(1)}, s16[1296,256]{1,0:T(8,128)(2,1)S(1)}, u32[]{:S(2)}, u32[]{:S(2)}) collective-permute-start(s16[1296,256]{1,0:T(8,128)(2,1)S(1)} %get-tuple-element.149), channel_id=1, source_target_pairs={{2,0},{3,1},{6,4},{7,5},{10,8},{11,9},{14,12},{15,13},{16,18},{17,... | collective-permute-start | bytes 1990664 | tf_op jit(solution)/shard_map/ppermute | solution.py:390
  103.3 22.3 %collective-permute-start.30 = (s16[1296,256]{1,0:T(8,128)(2,1)S(1)}, s16[1296,256]{1,0:T(8,128)(2,1)S(1)}, u32[]{:S(2)}, u32[]{:S(2)}) collective-permute-start(s16[1296,256]{1,0:T(8,128)(2,1)S(1)} %get-tuple-element.142), channel_id=1, source_target_pairs={{0,2},{1,3},{4,6},{5,7},{8,10},{9,11},{12,14},{13,15},{18,16},{19,... | collective-permute-start | bytes 1990664 | tf_op jit(solution)/shard_map/ppermute | solution.py:390
  113.7 0.9 copy-start.16
  113.7 1.1 copy-start.15
  115.4 13.4 %copy-start.6 = (bf16[2048,256]{1,0:T(8,128)(2,1)S(1)}, bf16[2048,256]{1,0:T(8,128)(2,1)}, u32[]{:S(2)}) copy-start(bf16[2048,256]{1,0:T(8,128)(2,1)} %refs_4_.1) | copy-start | bytes 3145732
  115.4 13.3 %copy-start.17 = (s32[8,16]{1,0:T(8,128)S(1)}, s32[8,16]{1,0:T(8,128)}, u32[]{:S(2)}) copy-start(s32[8,16]{1,0:T(8,128)} %mask_ref.1) | copy-start | bytes 1540
  115.4 13.3 %copy-start.18 = (s32[16,2]{0,1:T(2,128)S(1)}, s32[16,2]{0,1:T(2,128)}, u32[]{:S(2)}) copy-start(s32[16,2]{0,1:T(2,128)} %param.9) | copy-start | bytes 388
  115.4 12.7 %collective-permute-start.31 = (s16[1296,256]{1,0:T(8,128)(2,1)S(1)}, s16[1296,256]{1,0:T(8,128)(2,1)S(1)}, u32[]{:S(2)}, u32[]{:S(2)}) collective-permute-start(s16[1296,256]{1,0:T(8,128)(2,1)S(1)} %get-tuple-element.146), channel_id=1, source_target_pairs={{1,3},{5,7},{8,10},{12,14},{19,17},{23,21},{26,24},{30,28}} | collective-permute-start | bytes 1990664 | tf_op jit(solution)/shard_map/ppermute | solution.py:390
  116.2 10.6 %collective-permute-start.29 = (f32[8,128]{1,0:T(8,128)S(1)}, f32[8,128]{1,0:T(8,128)S(1)}, u32[]{:S(2)}, u32[]{:S(2)}) collective-permute-start(f32[8,128]{1,0:T(8,128)S(1)} %get-tuple-element.139), channel_id=1, source_target_pairs={{0,1},{1,0},{2,3},{3,2},{4,5},{5,4},{6,7},{7,6},{8,9},{9,8},{10,11... | collective-permute-start | bytes 12296 | tf_op jit(solution)/shard_map/ppermute | solution.py:439

commit v4 on v3

--- a/solution.py
+++ b/solution.py
@@ -62,21 +62,21 @@
 ANY = pl.BlockSpec(memory_space=pl.ANY)
 
 
-def pack_tiles(shards, masks, across_masks, cap):
+def pack_tiles(shards, masks, cap):
     wide = shards[0].shape[1] // TILE
     tiles = masks[0].size
     count = len(shards)
 
     def kernel(*refs):
-        mask_refs, across_refs, b_refs, out_ref = refs[:count], refs[count:2 * count], refs[2 * count:-1], refs[-1]
-        place = across = jnp.int32(0)
+        mask_refs, b_refs, out_ref = refs[:count], refs[count:-1], refs[-1]
+        place = jnp.int32(0)
         lane = lax.broadcasted_iota(jnp.int32, (META, TILE), 1)
         sub = lax.broadcasted_iota(jnp.int32, (META, TILE), 0)
         meta = jnp.zeros((META, TILE), jnp.float32)
         for s in range(count):
             for t in range(tiles):
                 k, n = divmod(t, wide)
-                keep = mask_refs[s][k, n] != 0
+                keep = mask_refs[s][n, k] != 0
 
                 @pl.when(keep & (place < cap))
                 def _(s=s, k=k, n=n, place=place):
@@ -84,47 +84,41 @@
                     out_ref[pl.ds(at, TILE), :] = b_refs[s][k * TILE:(k + 1) * TILE, n * TILE:(n + 1) * TILE]
 
                 place = place + keep.astype(jnp.int32)
-                across = across + (across_refs[s][k, n] != 0).astype(jnp.int32)
                 meta = jnp.where((lane == s * tiles + t) & keep, 1.0, meta)
-        more = jnp.maximum(place, across) > cap
-        meta = jnp.where(sub == 0, meta, jnp.where((sub == 1) & more, 1.0, 0.0))
+        meta = jnp.where(sub == 0, meta, jnp.where((sub == 1) & (place > cap), 1.0, 0.0))
         out_ref[cap * TILE:, :] = meta.astype(out_ref.dtype)
 
     return call(
         kernel, "pack_tiles",
         out_shape=jax.ShapeDtypeStruct((cap * TILE + META, TILE), shards[0].dtype),
-        in_specs=[SMEM] * (2 * count) + [VMEM] * count,
+        in_specs=[SMEM] * count + [VMEM] * count,
         out_specs=VMEM,
-    )(*masks, *across_masks, *shards)
+    )(*masks, *shards)
 
 
 def mask_tiles(amplitudes, mask):
     rows, cols = amplitudes.shape
-    step = 2
-
-    def kernel(mask_ref, a_ref, out_ref, token_ref):
-        i = pl.program_id(0)
+
+    def kernel(mask_ref, a_any, out_ref, token_ref, sem):
         token_ref[...] = jnp.zeros_like(token_ref)
-        for r in range(step):
+        copies = [
+            pltpu.make_async_copy(a_any.at[pl.ds(at, TILE)], out_ref.at[pl.ds(at, TILE)], sem.at[at // TILE])
+            for at in range(0, rows, TILE)]
+        for copy in copies:
+            copy.start()
+        for r in range(rows // TILE):
+            copies[r].wait()
             for t in range(cols // TILE):
-                spot = (slice(r * TILE, (r + 1) * TILE), slice(t * TILE, (t + 1) * TILE))
-                keep = mask_ref[i * step + r, t] != 0
-
-                @pl.when(keep)
-                def _(spot=spot):
-                    out_ref[spot] = a_ref[spot]
-
-                @pl.when(jnp.logical_not(keep))
-                def _(spot=spot):
-                    out_ref[spot] = jnp.zeros((TILE, TILE), out_ref.dtype)
-
-    block = pl.BlockSpec((step * TILE, cols), lambda i: (i, 0))
-    return call(
-        kernel, "mask_tiles", pl.CostEstimate(flops=0, bytes_accessed=4 * amplitudes.size, transcendentals=0),
-        grid=(rows // TILE // step,),
+                @pl.when(mask_ref[r, t] == 0)
+                def _(r=r, t=t):
+                    out_ref[r * TILE:(r + 1) * TILE, t * TILE:(t + 1) * TILE] = jnp.zeros((TILE, TILE), out_ref.dtype)
+
+    return call(
+        kernel, "mask_tiles",
         out_shape=(jax.ShapeDtypeStruct(amplitudes.shape, amplitudes.dtype), TOKEN),
-        in_specs=[SMEM, block],
-        out_specs=(block, pl.BlockSpec(TOKEN.shape, lambda i: (0, 0))),
+        in_specs=[SMEM, ANY],
+        out_specs=(VMEM, VMEM),
+        scratch_shapes=[pltpu.SemaphoreType.DMA((rows // TILE,))],
     )(mask, amplitudes)
 
 
@@ -254,25 +248,30 @@
     coded_ref[rows + block:, :] = jnp.concatenate([exponent] * (META // groups)).astype(jnp.int16)
 
 
-def add_coded(sums, coded):
-    rows, cols = sums.shape
+def decode(coded_ref, rows, put):
     groups = rows // GROUP
     share = 16 // LOW
     block = rows // share
-
+    one, two = step_factors(coded_ref[rows + block:, :].astype(jnp.int32)[:groups])
+    one, two = 1.0 / one, 1.0 / two
+    for start in range(0, block, GROUP):
+        low = coded_ref[rows + start:rows + start + GROUP, :].astype(jnp.int32) + 32768
+        for part in range(share):
+            at = part * block + start
+            g = at // GROUP
+            high = coded_ref[at:at + GROUP, :].astype(jnp.int32)
+            value = (high << LOW) | ((low >> (LOW * part)) & ((1 << LOW) - 1))
+            put(at, value.astype(jnp.float32) * one[g:g + 1] * two[g:g + 1])
+
+
+def add_coded(sums, coded):
     def kernel(sums_ref, coded_ref, out_ref, token_ref):
         token_ref[...] = jnp.zeros_like(token_ref)
-        one, two = step_factors(coded_ref[rows + block:, :].astype(jnp.int32)[:groups])
-        one, two = 1.0 / one, 1.0 / two
-        for start in range(0, block, GROUP):
-            low = coded_ref[rows + start:rows + start + GROUP, :].astype(jnp.int32) + 32768
-            for part in range(share):
-                at = part * block + start
-                g = at // GROUP
-                high = coded_ref[at:at + GROUP, :].astype(jnp.int32)
-                value = (high << LOW) | ((low >> (LOW * part)) & ((1 << LOW) - 1))
-                far = value.astype(jnp.float32) * one[g:g + 1] * two[g:g + 1]
-                out_ref[at:at + GROUP, :] = (sums_ref[at:at + GROUP, :] + far).astype(out_ref.dtype)
+
+        def put(at, far):
+            out_ref[at:at + GROUP, :] = (sums_ref[at:at + GROUP, :] + far).astype(out_ref.dtype)
+
+        decode(coded_ref, sums.shape[0], put)
 
     return call(
         kernel, "add_coded",
@@ -280,6 +279,42 @@
         in_specs=[VMEM, VMEM],
         out_specs=(VMEM, VMEM),
     )(sums, coded)
+
+
+def lay_out(place, mine, rest):
+    rows, width = mine[0].shape
+    arrays = []
+    for choice in jax.tree.leaves((mine, rest)):
+        if not any(choice is array for array in arrays):
+            arrays.append(choice)
+
+    def index(array):
+        return [array is known for known in arrays].index(True)
+
+    def kernel(place_ref, *refs):
+        ins, out_ref = refs[:len(arrays)], refs[-1]
+        for x in range(2):
+            own, other = slice(x * width, (x + 1) * width), slice((1 - x) * width, (2 - x) * width)
+            for number in range(len(mine)):
+                @pl.when((place_ref[0] == number) & (place_ref[1] == x))
+                def _(own=own, other=other, number=number):
+                    out_ref[:, own] = ins[index(mine[number])][...]
+                    if isinstance(rest[number], tuple):
+                        sums_ref, coded_ref = [ins[index(array)] for array in rest[number]]
+
+                        def put(at, far):
+                            out_ref[at:at + GROUP, other] = (sums_ref[at:at + GROUP, :] + far).astype(out_ref.dtype)
+
+                        decode(coded_ref, rows, put)
+                    else:
+                        out_ref[:, other] = ins[index(rest[number])][...]
+
+    return call(
+        kernel, "lay_out",
+        out_shape=jax.ShapeDtypeStruct((rows, 2 * width), jnp.bfloat16),
+        in_specs=[SMEM] + [VMEM] * len(arrays),
+        out_specs=VMEM,
+    )(place, *arrays)
 
 
 def top_and_rest(one, two, at):
@@ -372,7 +407,6 @@
     (device(z, x, y, 1 - z % 2), device(z, x, y, z % 2)) for z in range(Z) for x in range(X) for y in range(Y)]
 CORES = [(0, 1), (1, 0), (2, 3), (3, 2)]
 CHIPS_Y = [(0, 2), (2, 0), (1, 3), (3, 1)]
-CROSSWISE = [(0, 3), (3, 0), (1, 2), (2, 1)]
 
 
 def sparse_ladder(amplitudes, integrals, amp_mask, int_mask):
@@ -402,8 +436,8 @@
     ] + [jnp.where(near, s, 1 - s) for s in (0, 1, 0, 1, 1)]).astype(jnp.int32)
 
     other = move(integrals, FROM_OTHER_CORE)
-    other_mask, across, other_across = [lax.ppermute(int_mask, "col", p) for p in (CORES, CHIPS_Y, CROSSWISE)]
-    own = pack_tiles((integrals, other), (int_mask, other_mask), (across, other_across), cap)
+    other_mask = lax.ppermute(int_mask.T, "col", CORES)
+    own = pack_tiles((integrals, other), (int_mask.T, other_mask), cap)
     own, picks, amplitudes_now = barrier((own, picks, amplitudes))
 
     masked, masked_token = mask_tiles(amplitudes_now, amp_mask)
@@ -420,7 +454,6 @@
     c_sum, c_coded, token = shard_product(amps, picks, 1, [[two_mid], [two_end]], tokens)
     c_far = move(c_coded, to_y(True, home_core))
     b_sum, b_coded, token = shard_product(amps, picks, 2, [[own_x], [one_x]], (token,))
-    b_far = move(b_coded, to_y(False, both))
     a_both, a_token = add_coded(a_sum, a_far)
     three_end, three_mid_x, two_x_end, two_x_mid, tokens = after(token, a_token)(
         move(two_mid, moves(outward)), move(own_x, moves(over_centre)),
@@ -428,6 +461,8 @@
 
     d_sum, d_coded, token = shard_product(
         amps, picks, 3, [[two_x_mid], [two_x_end], [centre], [three_end]], tokens)
+    b_coded, token = barrier((b_coded, token))
+    b_far = move(b_coded, to_y(False, both))
     top, rest = top_and_rest(three_end, two_x_mid, half)
     c_both, c_token = add_coded(c_sum, c_far)
     three_x, three_x_rest, tokens = after(token, c_token)(
@@ -436,15 +471,15 @@
     d_far = move(d_coded, to_y(True, both))
     e_sum, e_coded, token = shard_product(amps, picks, 4, [[three_mid_x], [three_x, three_x_rest]], tokens)
     e_far = move(e_coded, to_y(True, other_core))
-    excess = token + lax.ppermute(token, "col", CORES)
-    b_both, _ = add_coded(b_sum, b_far)
-    d_both, _ = add_coded(d_sum, d_far)
-    e_both, _ = add_coded(e_sum, e_far)
+    b_both, b_token = add_coded(b_sum, b_far)
+    d_both, d_token = add_coded(d_sum, d_far)
+    excess = token + lax.ppermute(token, "col", CHIPS_Y)
+    excess, b_both, d_both = barrier((excess, b_both, d_both))
+    excess = excess + lax.ppermute(excess, "col", CORES)
+    place = jnp.stack([jnp.where(near, 0, jnp.where(home, 1, 2)), x]).astype(jnp.int32)
 
     def finish():
-        mine = jnp.where(near, a_both, jnp.where(home, c_both, d_both))
-        rest = jnp.where(near, b_both, jnp.where(home, d_both, e_both))
-        return jnp.concatenate([jnp.where(x == 0, mine, rest), jnp.where(x == 0, rest, mine)], axis=1)
+        return lay_out(place, (a_both, c_both, d_both), (b_both, d_both, (e_sum, e_far)))
 
     return lax.cond(
         jnp.max(excess) > 0, lambda: dense_ladder(amplitudes, integrals, amp_mask, int_mask), finish)

time: 132 us -> 128 us (0.970)
  the two profiles are of different devices: /device:TPU:16 before, /device:TPU:17 now
where the time goes in v4:
time: 128 us
  waiting for transfers between devices  52.1 us (41%)
  starting transfers between devices  36.9 us (29%)
  Pallas kernels  34.8 us (27%)
  local copies, waits for them, and re-layouts  2.2 us (2%)
    ppermute x18, waiting for transfers between devices, move(): return lax.ppermute(value, AXES, pairs)  36 us
    ppermute x18, starting transfers between devices, move(): return lax.ppermute(value, AXES, pairs)  30.5 us
    pallas_call x5, Pallas kernels, shard_product(): call(kernel, 'shard_product', out_shape=(jax.ShapeDtypeStruct((rows, wide...  22.8 us
    ppermute x1, waiting for transfers between devices, sparse_ladder(): excess = token + lax.ppermute(token, 'col', CHIPS_Y)  13.2 us
    pallas_call x4, Pallas kernels, add_coded(): call(kernel, 'add_coded', out_shape=(jax.ShapeDtypeStruct(sums.shape, jnp...  4.12 us
    pallas_call x1, Pallas kernels, mask_tiles(): call(kernel, 'mask_tiles', out_shape=(jax.ShapeDtypeStruct(amplitudes.sha...  3.05 us
    ppermute x1, starting transfers between devices, sparse_ladder(): excess = token + lax.ppermute(token, 'col', CHIPS_Y)  2.92 us
    ppermute x1, starting transfers between devices, sparse_ladder(): excess = excess + lax.ppermute(excess, 'col', CORES)  2.9 us
  transfers between devices with their start and end apart: 22, of which 10 were waited for; matrix products, arithmetic and copies ran while one was open for 1% of the time, Pallas kernels for 21%

profile of v4, /device:TPU:17, one launch (start us, length us, event | category | flops | bytes accessed | tf_op | source)
XLA Modules:
  0.0 127.9 jit_solution(5486411200735813431)
XLA Ops:
  0.0 2.6 %collective-permute-start.11 = (bf16[2048,256]{1,0:T(8,128)(2,1)}, bf16[2048,256]{1,0:T(8,128)(2,1)S(1)}, u32[]{:S(2)}, u32[]{:S(2)}) collective-permute-start(bf16[2048,256]{1,0:T(8,128)(2,1)} %refs_2_.1), channel_id=1, source_target_pairs={{1,0},{3,2},{5,4},{7,6},{8,9},{10,11},{12,13},{14,15},{17,16},{19,... | collective-permute-start | bytes 3145736 | tf_op jit(solution)/shard_map/ppermute | solution.py:424
  2.6 0.1 collective-permute-start.10
  2.8 0.1 stack.40.picks_ref
  2.9 2.2 %collective-permute-done.10.refs_1_ = s32[2,16]{1,0:T(2,128)S(1)} collective-permute-done((s32[2,16]{1,0:T(2,128)}, s32[2,16]{1,0:T(2,128)S(1)}, u32[]{:S(2)}, u32[]{:S(2)}) %collective-permute-start.10) | collective-permute-done | bytes 160 | tf_op jit(solution)/shard_map/ppermute | solution.py:439
  5.1 0.0 collective-permute-done.11.refs_3_
  5.1 1.9 %pack_tiles.1.refs_3_ = bf16[5648,128]{1,0:T(8,128)(2,1)S(1)} custom-call(s32[2,16]{1,0:T(2,128)} %bitcast.38, s32[2,16]{1,0:T(2,128)S(1)} %collective-permute-done.10.refs_1_, bf16[2048,256]{1,0:T(8,128)(2,1)} %refs_2_.1, bf16[2048,256]{1,0:T(8,128)(2,1)S(1)} %collective-permute-done.11.refs_3_), custom_call_target="tpu_custom_call" | custom-call | flops 1 | bytes 1 | tf_op jit(solution)/shard_map/pack_tiles/pallas_call | solution.py:91
  7.0 3.0 %mask_tiles.1 = (bf16[1024,2048]{1,0:T(8,128)(2,1)S(1)}, f32[8,128]{1,0:T(8,128)S(1)}) custom-call(s32[8,16]{1,0:T(8,128)} %mask_ref.1, bf16[1024,2048]{1,0:T(8,128)(2,1)} %a_any), custom_call_target="tpu_custom_call" | custom-call | flops 1 | bytes 1 | tf_op jit(solution)/shard_map/mask_tiles/pallas_call | solution.py:116
  10.0 0.5 collective-permute-start.18
  10.5 1.3 %collective-permute-start.12 = (bf16[5648,128]{1,0:T(8,128)(2,1)S(1)}, bf16[5648,128]{1,0:T(8,128)(2,1)S(1)}, u32[]{:S(2)}, u32[]{:S(2)}) collective-permute-start(bf16[5648,128]{1,0:T(8,128)(2,1)S(1)} %pack_tiles.1.refs_3_), channel_id=1, source_target_pairs={{0,8},{2,10},{4,12},{6,14},{9,1},{11,3},{13,5},{15,7},{16,24},{18,... | collective-permute-start | bytes 4337672 | tf_op jit(solution)/shard_map/ppermute | solution.py:424
  11.8 1.3 %collective-permute-start.13 = (bf16[5648,128]{1,0:T(8,128)(2,1)S(1)}, bf16[5648,128]{1,0:T(8,128)(2,1)S(1)}, u32[]{:S(2)}, u32[]{:S(2)}) collective-permute-start(bf16[5648,128]{1,0:T(8,128)(2,1)S(1)} %pack_tiles.1.refs_3_), channel_id=1, source_target_pairs={{9,17},{11,19},{13,21},{15,23},{16,8},{18,10},{20,12},{22,14}} | collective-permute-start | bytes 4337672 | tf_op jit(solution)/shard_map/ppermute | solution.py:424
  13.1 0.8 collective-permute-start.14
  13.8 16.7 %collective-permute-done.12.refs_4_ = bf16[5648,128]{1,0:T(8,128)(2,1)S(1)} collective-permute-done((bf16[5648,128]{1,0:T(8,128)(2,1)S(1)}, bf16[5648,128]{1,0:T(8,128)(2,1)S(1)}, u32[]{:S(2)}, u32[]{:S(2)}) %collective-permute-start.12) | collective-permute-done | bytes 1445920 | tf_op jit(solution)/shard_map/ppermute | solution.py:424
  30.6 1.3 %collective-permute-done.13.refs_6_ = bf16[5648,128]{1,0:T(8,128)(2,1)S(1)} collective-permute-done((bf16[5648,128]{1,0:T(8,128)(2,1)S(1)}, bf16[5648,128]{1,0:T(8,128)(2,1)S(1)}, u32[]{:S(2)}, u32[]{:S(2)}) %collective-permute-start.13) | collective-permute-done | bytes 1445920 | tf_op jit(solution)/shard_map/ppermute | solution.py:424
  31.9 0.0 collective-permute-done.14.refs_3_
  31.9 4.6 %collective-permute-start.15 = (bf16[5648,128]{1,0:T(8,128)(2,1)S(1)}, bf16[5648,128]{1,0:T(8,128)(2,1)S(1)}, u32[]{:S(2)}, u32[]{:S(2)}) collective-permute-start(bf16[5648,128]{1,0:T(8,128)(2,1)S(1)} %collective-permute-done.13.refs_6_), channel_id=1, source_target_pairs={{8,0},{10,2},{12,4},{14,6},{17,25},{19,27},{21,29},{23,31}} | collective-permute-start | bytes 4337672 | tf_op jit(solution)/shard_map/ppermute | solution.py:424
  36.5 1.4 %collective-permute-start.16 = (bf16[5648,128]{1,0:T(8,128)(2,1)S(1)}, bf16[5648,128]{1,0:T(8,128)(2,1)S(1)}, u32[]{:S(2)}, u32[]{:S(2)}) collective-permute-start(bf16[5648,128]{1,0:T(8,128)(2,1)S(1)} %collective-permute-done.12.refs_4_), channel_id=1, source_target_pairs={{8,16},{10,18},{12,20},{14,22},{17,9},{19,11},{21,13},{23,15}} | collective-permute-start | bytes 4337672 | tf_op jit(solution)/shard_map/ppermute | solution.py:424
  37.9 3.1 %collective-permute-start.17 = (bf16[5648,128]{1,0:T(8,128)(2,1)S(1)}, bf16[5648,128]{1,0:T(8,128)(2,1)S(1)}, u32[]{:S(2)}, u32[]{:S(2)}) collective-permute-start(bf16[5648,128]{1,0:T(8,128)(2,1)S(1)} %collective-permute-done.12.refs_4_), channel_id=1, source_target_pairs={{1,5},{3,7},{5,1},{7,3},{8,12},{10,14},{12,8},{14,10},{17,21},{19,... | collective-permute-start | bytes 4337672 | tf_op jit(solution)/shard_map/ppermute | solution.py:424
  41.0 0.0 collective-permute-done.18.refs_2_.refs_3_
  41.0 5.0 %shard_product.5 = (f32[1024,256]{1,0:T(8,128)S(1)}, s16[1296,256]{1,0:T(8,128)(2,1)S(1)}, f32[8,128]{1,0:T(8,128)S(1)}) custom-call(s32[10]{0:T(128)S(1)} %stack.40.picks_ref, f32[8,128]{1,0:T(8,128)S(1)} %get-tuple-element.100.refs_0_, bf16[1024,2048]{1,0:T(8,128)(2,1)S(1)} %get-tuple-element.101.refs_1_.refs_2_, ...), custom_call_target="tpu_custom_call" | custom-call | flops 1 | bytes 1 | tf_op jit(solution)/shard_map/shard_product/pallas_call | solution.py:193
  46.0 6.4 %collective-permute-done.15.refs_4_ = bf16[5648,128]{1,0:T(8,128)(2,1)S(1)} collective-permute-done((bf16[5648,128]{1,0:T(8,128)(2,1)S(1)}, bf16[5648,128]{1,0:T(8,128)(2,1)S(1)}, u32[]{:S(2)}, u32[]{:S(2)}) %collective-permute-start.15) | collective-permute-done | bytes 1445920 | tf_op jit(solution)/shard_map/ppermute | solution.py:424
  52.4 1.4 %collective-permute-done.16.refs_3_ = bf16[5648,128]{1,0:T(8,128)(2,1)S(1)} collective-permute-done((bf16[5648,128]{1,0:T(8,128)(2,1)S(1)}, bf16[5648,128]{1,0:T(8,128)(2,1)S(1)}, u32[]{:S(2)}, u32[]{:S(2)}) %collective-permute-start.16) | collective-permute-done | bytes 1445920 | tf_op jit(solution)/shard_map/ppermute | solution.py:424
  53.8 3.9 %collective-permute-done.17.refs_4_ = bf16[5648,128]{1,0:T(8,128)(2,1)S(1)} collective-permute-done((bf16[5648,128]{1,0:T(8,128)(2,1)S(1)}, bf16[5648,128]{1,0:T(8,128)(2,1)S(1)}, u32[]{:S(2)}, u32[]{:S(2)}) %collective-permute-start.17) | collective-permute-done | bytes 1445920 | tf_op jit(solution)/shard_map/ppermute | solution.py:424
  57.7 0.7 collective-permute-start.19
  58.4 1.3 %collective-permute-start.20 = (bf16[5648,128]{1,0:T(8,128)(2,1)S(1)}, bf16[5648,128]{1,0:T(8,128)(2,1)S(1)}, u32[]{:S(2)}, u32[]{:S(2)}) collective-permute-start(bf16[5648,128]{1,0:T(8,128)(2,1)S(1)} %collective-permute-done.14.refs_3_), channel_id=1, source_target_pairs={{9,17},{11,19},{13,21},{15,23},{16,8},{18,10},{20,12},{22,14}} | collective-permute-start | bytes 4337672 | tf_op jit(solution)/shard_map/ppermute | solution.py:424
  59.7 0.8 collective-permute-start.21
  60.5 0.8 collective-permute-start.22
  61.3 3.2 %collective-permute-start.23 = (s16[1296,256]{1,0:T(8,128)(2,1)S(1)}, s16[1296,256]{1,0:T(8,128)(2,1)S(1)}, u32[]{:S(2)}, u32[]{:S(2)}) collective-permute-start(s16[1296,256]{1,0:T(8,128)(2,1)S(1)} %get-tuple-element.111), channel_id=1, source_target_pairs={{2,0},{3,1},{6,4},{7,5},{10,8},{11,9},{14,12},{15,13},{16,18},{17,... | collective-permute-start | bytes 1990664 | tf_op jit(solution)/shard_map/ppermute | solution.py:424
  64.5 0.6 shard_product.6
  65.1 6.1 %shard_product.7 = (f32[1024,256]{1,0:T(8,128)S(1)}, s16[1296,256]{1,0:T(8,128)(2,1)}, f32[8,128]{1,0:T(8,128)S(1)}) custom-call(s32[10]{0:T(128)S(1)} %stack.40.picks_ref, f32[8,128]{1,0:T(8,128)S(1)} %get-tuple-element.107.refs_0_, bf16[1024,2048]{1,0:T(8,128)(2,1)S(1)} %get-tuple-element.101.refs_1_.refs_2_, ...), custom_call_target="tpu_custom_call" | custom-call | flops 1 | bytes 1 | tf_op jit(solution)/shard_map/shard_product/pallas_call | solution.py:193
  71.1 0.9 collective-permute-done.23.coded_ref
  72.0 1.2 add_coded.4
  73.1 0.0 collective-permute-done.19.one_ref.refs_7_
  73.2 5.4 %collective-permute-done.20.refs_4_ = bf16[5648,128]{1,0:T(8,128)(2,1)S(1)} collective-permute-done((bf16[5648,128]{1,0:T(8,128)(2,1)S(1)}, bf16[5648,128]{1,0:T(8,128)(2,1)S(1)}, u32[]{:S(2)}, u32[]{:S(2)}) %collective-permute-start.20) | collective-permute-done | bytes 1445920 | tf_op jit(solution)/shard_map/ppermute | solution.py:424
  78.5 0.0 collective-permute-done.21.refs_5_
  78.5 0.0 collective-permute-done.22.two_ref.refs_4_
  78.6 0.6 top_and_rest.1
  79.2 0.7 collective-permute-start.25
  79.9 0.7 collective-permute-start.24
  80.6 0.7 collective-permute-start.26
  81.3 5.4 %shard_product.8 = (f32[1024,256]{1,0:T(8,128)S(1)}, s16[1296,256]{1,0:T(8,128)(2,1)}, f32[8,128]{1,0:T(8,128)S(1)}) custom-call(s32[10]{0:T(128)S(1)} %stack.40.picks_ref, f32[8,128]{1,0:T(8,128)S(1)} %get-tuple-element.118.refs_0_, f32[8,128]{1,0:T(8,128)S(1)} %get-tuple-element.119.refs_1_, bf16[1024,2048]{1,0:T(8,128)(2,1)S(1)} %get-tuple-element.101.refs_1_.refs_2_, ...), custom_call_target="tpu_custom_call" | custom-call | flops 1 | bytes 1 | tf_op jit(solution)/shard_map/shard_product/pallas_call | solution.py:193
  86.8 1.3 %collective-permute-start.29 = (s16[1296,256]{1,0:T(8,128)(2,1)}, s16[1296,256]{1,0:T(8,128)(2,1)S(1)}, u32[]{:S(2)}, u32[]{:S(2)}) collective-permute-start(s16[1296,256]{1,0:T(8,128)(2,1)} %get-tuple-element.136), channel_id=1, source_target_pairs={{0,2},{1,3},{4,6},{5,7},{8,10},{9,11},{12,14},{13,15},{18,16},{19,... | collective-permute-start | bytes 1990664 | tf_op jit(solution)/shard_map/ppermute | solution.py:424
  88.1 4.1 %collective-permute-start.28 = (s16[1296,256]{1,0:T(8,128)(2,1)}, s16[1296,256]{1,0:T(8,128)(2,1)S(1)}, u32[]{:S(2)}, u32[]{:S(2)}) collective-permute-start(s16[1296,256]{1,0:T(8,128)(2,1)} %get-tuple-element.133), channel_id=1, source_target_pairs={{2,0},{3,1},{6,4},{7,5},{10,8},{11,9},{14,12},{15,13},{16,18},{17,... | collective-permute-start | bytes 1990664 | tf_op jit(solution)/shard_map/ppermute | solution.py:424
  92.2 0.0 collective-permute-done.26.coded_ref
  92.2 1.2 add_coded.5
  93.4 0.0 collective-permute-done.25.refs_6_
  93.4 0.8 copy-done.16
  94.2 0.3 copy-done.15
  94.5 5.7 %shard_product.9 = (f32[1024,256]{1,0:T(8,128)}, s16[1296,256]{1,0:T(8,128)(2,1)}, f32[8,128]{1,0:T(8,128)S(1)}) custom-call(s32[10]{0:T(128)S(1)} %stack.40.picks_ref, f32[8,128]{1,0:T(8,128)S(1)} %get-tuple-element.126.refs_0_, f32[8,128]{1,0:T(8,128)S(1)} %get-tuple-element.127.refs_1_, bf16[1024,2048]{1,0:T(8,128)(2,1)S(1)} %get-tuple-element.101.refs_1_.refs_2_, ...), custom_call_target="tpu_custom_call" | custom-call | flops 1 | bytes 1 | tf_op jit(solution)/shard_map/shard_product/pallas_call | solution.py:193
  100.2 1.3 %collective-permute-start.31 = (s16[1296,256]{1,0:T(8,128)(2,1)}, s16[1296,256]{1,0:T(8,128)(2,1)}, u32[]{:S(2)}, u32[]{:S(2)}) collective-permute-start(s16[1296,256]{1,0:T(8,128)(2,1)} %get-tuple-element.144), channel_id=1, source_target_pairs={{1,3},{5,7},{8,10},{12,14},{19,17},{23,21},{26,24},{30,28}} | collective-permute-start | bytes 1990664 | tf_op jit(solution)/shard_map/ppermute | solution.py:424
  101.5 2.9 %collective-permute-start.27 = (f32[8,128]{1,0:T(8,128)S(1)}, f32[8,128]{1,0:T(8,128)S(1)}, u32[]{:S(2)}, u32[]{:S(2)}) collective-permute-start(f32[8,128]{1,0:T(8,128)S(1)} %get-tuple-element.131), channel_id=1, source_target_pairs={{0,2},{2,0},{1,3},{3,1},{4,6},{6,4},{5,7},{7,5},{8,10},{10,8},{9,1... | collective-permute-start | bytes 12296 | tf_op jit(solution)/shard_map/ppermute | solution.py:476
  104.4 0.0 collective-permute-done.29.coded_ref
  104.4 1.2 add_coded.7
  105.6 0.0 collective-permute-done.28.coded_ref
  105.6 0.6 add_coded.6
  106.2 13.2 %collective-permute-done.27 = f32[8,128]{1,0:T(8,128)S(1)} collective-permute-done((f32[8,128]{1,0:T(8,128)S(1)}, f32[8,128]{1,0:T(8,128)S(1)}, u32[]{:S(2)}, u32[]{:S(2)}) %collective-permute-start.27) | collective-permute-done | bytes 4128 | tf_op jit(solution)/shard_map/ppermute | solution.py:476
  119.4 2.9 %collective-permute-start.30 = (f32[8,128]{1,0:T(8,128)S(1)}, f32[8,128]{1,0:T(8,128)S(1)}, u32[]{:S(2)}, u32[]{:S(2)}) collective-permute-start(f32[8,128]{1,0:T(8,128)S(1)} %add.133), channel_id=1, source_target_pairs={{0,1},{1,0},{2,3},{3,2},{4,5},{5,4},{6,7},{7,6},{8,9},{9,8},{10,11... | collective-permute-start | bytes 12296 | tf_op jit(solution)/shard_map/ppermute | solution.py:478
  122.3 0.1 pad_add_fusion
  122.4 0.7 collective-permute-done.30
  123.1 0.7 add_reduce_fusion
  124.5 0.0 collective-permute-done.31
  124.5 2.4 %conditional.1 = (bf16[1024,512]{1,0:T(8,128)(2,1)S(1)}) conditional(s32[]{:T(128)} %convert_element_type.32, (s32[2]{0:T(128)S(1)}, bf16[1024,256]{1,0:T(8,128)(2,1)}, bf16[1024,256]{1,0:T(8,128)(2,1)}, bf16[1024,256]{1,0:T(8,128)(2,1)}, bf16[1024,256]{1,0:T(8,128)(2,1)S(1)}, /*index=5*/f32[1024,256]{1,0:T(8,128)}, ...), branch_computations={%region_1.2_spmd, %region_2.3_spmd} | conditional | flops 8594653184 | bytes 206655584 | solution.py:484
  124.5 2.3 %lay_out.1 = bf16[1024,512]{1,0:T(8,128)(2,1)S(1)} custom-call(s32[2]{0:T(128)S(1)} %get-tuple-element.30.place_ref, bf16[1024,256]{1,0:T(8,128)(2,1)} %get-tuple-element.31.refs_0_, bf16[1024,256]{1,0:T(8,128)(2,1)} %get-tuple-element.32.refs_1_, bf16[1024,256]{1,0:T(8,128)(2,1)} %get-tuple-element.33.refs_2_, ...), custom_call_target="tpu_custom_call" | custom-call | flops 1 | bytes 1 | tf_op jit(solution)/shard_map/cond/branch_0_fun/lay_out/pallas_call | solution.py:312
  126.9 0.0 copy-start.14
  126.9 1.0 copy-done.14
  (30 shorter events, 0.1 us)
Async XLA Ops:
  0.0 5.1 %collective-permute-start.11 = (bf16[2048,256]{1,0:T(8,128)(2,1)}, bf16[2048,256]{1,0:T(8,128)(2,1)S(1)}, u32[]{:S(2)}, u32[]{:S(2)}) collective-permute-start(bf16[2048,256]{1,0:T(8,128)(2,1)} %refs_2_.1), channel_id=1, source_target_pairs={{1,0},{3,2},{5,4},{7,6},{8,9},{10,11},{12,13},{14,15},{17,16},{19,... | collective-permute-start | bytes 3145736 | tf_op jit(solution)/shard_map/ppermute | solution.py:424
  2.6 2.4 %collective-permute-start.10 = (s32[2,16]{1,0:T(2,128)}, s32[2,16]{1,0:T(2,128)S(1)}, u32[]{:S(2)}, u32[]{:S(2)}) collective-permute-start(s32[2,16]{1,0:T(2,128)} %bitcast.37), channel_id=1, source_target_pairs={{0,1},{1,0},{2,3},{3,2},{4,5},{5,4},{6,7},{7,6},{8,9},{9,8},{10,11... | collective-permute-start | bytes 392 | tf_op jit(solution)/shard_map/ppermute | solution.py:439
  7.0 34.0 %copy-start.2 = (bf16[5648,128]{1,0:T(8,128)(2,1)}, bf16[5648,128]{1,0:T(8,128)(2,1)S(1)}, u32[]{:S(2)}) copy-start(bf16[5648,128]{1,0:T(8,128)(2,1)S(1)} %pack_tiles.1.refs_3_) | copy-start | bytes 4337668
  10.0 31.0 %collective-permute-start.18 = (bf16[1024,2048]{1,0:T(8,128)(2,1)S(1)}, bf16[1024,2048]{1,0:T(8,128)(2,1)S(1)}, u32[]{:S(2)}, u32[]{:S(2)}) collective-permute-start(bf16[1024,2048]{1,0:T(8,128)(2,1)S(1)} %get-tuple-element.101.refs_1_.refs_2_), channel_id=1, source_target_pairs={{0,1},{1,0},{2,3},{3,2},{4,5},{5,4},{6,7},{7,6},{8,9},{9,8},{10,11... | collective-permute-start | bytes 12582920 | tf_op jit(solution)/shard_map/ppermute | solution.py:444
  10.5 20.1 %collective-permute-start.12 = (bf16[5648,128]{1,0:T(8,128)(2,1)S(1)}, bf16[5648,128]{1,0:T(8,128)(2,1)S(1)}, u32[]{:S(2)}, u32[]{:S(2)}) collective-permute-start(bf16[5648,128]{1,0:T(8,128)(2,1)S(1)} %pack_tiles.1.refs_3_), channel_id=1, source_target_pairs={{0,8},{2,10},{4,12},{6,14},{9,1},{11,3},{13,5},{15,7},{16,24},{18,... | collective-permute-start | bytes 4337672 | tf_op jit(solution)/shard_map/ppermute | solution.py:424
  11.8 20.1 %collective-permute-start.13 = (bf16[5648,128]{1,0:T(8,128)(2,1)S(1)}, bf16[5648,128]{1,0:T(8,128)(2,1)S(1)}, u32[]{:S(2)}, u32[]{:S(2)}) collective-permute-start(bf16[5648,128]{1,0:T(8,128)(2,1)S(1)} %pack_tiles.1.refs_3_), channel_id=1, source_target_pairs={{9,17},{11,19},{13,21},{15,23},{16,8},{18,10},{20,12},{22,14}} | collective-permute-start | bytes 4337672 | tf_op jit(solution)/shard_map/ppermute | solution.py:424
  13.1 18.8 %collective-permute-start.14 = (bf16[5648,128]{1,0:T(8,128)(2,1)S(1)}, bf16[5648,128]{1,0:T(8,128)(2,1)S(1)}, u32[]{:S(2)}, u32[]{:S(2)}) collective-permute-start(bf16[5648,128]{1,0:T(8,128)(2,1)S(1)} %pack_tiles.1.refs_3_), channel_id=1, source_target_pairs={{0,4},{2,6},{4,0},{6,2},{9,13},{11,15},{13,9},{15,11},{16,20},{18,... | collective-permute-start | bytes 4337672 | tf_op jit(solution)/shard_map/ppermute | solution.py:424
  30.6 10.4 %copy-start.13 = (bf16[5648,128]{1,0:T(8,128)(2,1)}, bf16[5648,128]{1,0:T(8,128)(2,1)S(1)}, u32[]{:S(2)}) copy-start(bf16[5648,128]{1,0:T(8,128)(2,1)S(1)} %collective-permute-done.12.refs_4_) | copy-start | bytes 4337668
  31.9 14.1 %copy-start.6 = (bf16[5648,128]{1,0:T(8,128)(2,1)}, bf16[5648,128]{1,0:T(8,128)(2,1)S(1)}, u32[]{:S(2)}) copy-start(bf16[5648,128]{1,0:T(8,128)(2,1)S(1)} %collective-permute-done.13.refs_6_) | copy-start | bytes 4337668
  31.9 26.6 %copy-start.8 = (bf16[5648,128]{1,0:T(8,128)(2,1)}, bf16[5648,128]{1,0:T(8,128)(2,1)S(1)}, u32[]{:S(2)}) copy-start(bf16[5648,128]{1,0:T(8,128)(2,1)S(1)} %collective-permute-done.14.refs_3_) | copy-start | bytes 4337668
  31.9 20.5 %collective-permute-start.15 = (bf16[5648,128]{1,0:T(8,128)(2,1)S(1)}, bf16[5648,128]{1,0:T(8,128)(2,1)S(1)}, u32[]{:S(2)}, u32[]{:S(2)}) collective-permute-start(bf16[5648,128]{1,0:T(8,128)(2,1)S(1)} %collective-permute-done.13.refs_6_), channel_id=1, source_target_pairs={{8,0},{10,2},{12,4},{14,6},{17,25},{19,27},{21,29},{23,31}} | collective-permute-start | bytes 4337672 | tf_op jit(solution)/shard_map/ppermute | solution.py:424
  36.5 17.3 %collective-permute-start.16 = (bf16[5648,128]{1,0:T(8,128)(2,1)S(1)}, bf16[5648,128]{1,0:T(8,128)(2,1)S(1)}, u32[]{:S(2)}, u32[]{:S(2)}) collective-permute-start(bf16[5648,128]{1,0:T(8,128)(2,1)S(1)} %collective-permute-done.12.refs_4_), channel_id=1, source_target_pairs={{8,16},{10,18},{12,20},{14,22},{17,9},{19,11},{21,13},{23,15}} | collective-permute-start | bytes 4337672 | tf_op jit(solution)/shard_map/ppermute | solution.py:424
  37.9 19.8 %collective-permute-start.17 = (bf16[5648,128]{1,0:T(8,128)(2,1)S(1)}, bf16[5648,128]{1,0:T(8,128)(2,1)S(1)}, u32[]{:S(2)}, u32[]{:S(2)}) collective-permute-start(bf16[5648,128]{1,0:T(8,128)(2,1)S(1)} %collective-permute-done.12.refs_4_), channel_id=1, source_target_pairs={{1,5},{3,7},{5,1},{7,3},{8,12},{10,14},{12,8},{14,10},{17,21},{19,... | collective-permute-start | bytes 4337672 | tf_op jit(solution)/shard_map/ppermute | solution.py:424
  52.4 12.1 %copy-start.9 = (bf16[5648,128]{1,0:T(8,128)(2,1)}, bf16[5648,128]{1,0:T(8,128)(2,1)S(1)}, u32[]{:S(2)}) copy-start(bf16[5648,128]{1,0:T(8,128)(2,1)S(1)} %collective-permute-done.15.refs_4_) | copy-start | bytes 4337668
  53.8 10.7 %copy-start.10 = (bf16[5648,128]{1,0:T(8,128)(2,1)}, bf16[5648,128]{1,0:T(8,128)(2,1)S(1)}, u32[]{:S(2)}) copy-start(bf16[5648,128]{1,0:T(8,128)(2,1)S(1)} %collective-permute-done.16.refs_3_) | copy-start | bytes 4337668
  57.7 7.4 %copy-start.12 = (bf16[5648,128]{1,0:T(8,128)(2,1)}, bf16[5648,128]{1,0:T(8,128)(2,1)S(1)}, u32[]{:S(2)}) copy-start(bf16[5648,128]{1,0:T(8,128)(2,1)S(1)} %collective-permute-done.17.refs_4_) | copy-start | bytes 4337668
  57.7 15.5 %collective-permute-start.19 = (bf16[5648,128]{1,0:T(8,128)(2,1)S(1)}, bf16[5648,128]{1,0:T(8,128)(2,1)S(1)}, u32[]{:S(2)}, u32[]{:S(2)}) collective-permute-start(bf16[5648,128]{1,0:T(8,128)(2,1)S(1)} %collective-permute-done.16.refs_3_), channel_id=1, source_target_pairs={{9,1},{11,3},{13,5},{15,7},{16,24},{18,26},{20,28},{22,30}} | collective-permute-start | bytes 4337672 | tf_op jit(solution)/shard_map/ppermute | solution.py:424
  58.4 20.1 %collective-permute-start.20 = (bf16[5648,128]{1,0:T(8,128)(2,1)S(1)}, bf16[5648,128]{1,0:T(8,128)(2,1)S(1)}, u32[]{:S(2)}, u32[]{:S(2)}) collective-permute-start(bf16[5648,128]{1,0:T(8,128)(2,1)S(1)} %collective-permute-done.14.refs_3_), channel_id=1, source_target_pairs={{9,17},{11,19},{13,21},{15,23},{16,8},{18,10},{20,12},{22,14}} | collective-permute-start | bytes 4337672 | tf_op jit(solution)/shard_map/ppermute | solution.py:424
  59.7 18.8 %collective-permute-start.21 = (bf16[5648,128]{1,0:T(8,128)(2,1)S(1)}, bf16[5648,128]{1,0:T(8,128)(2,1)S(1)}, u32[]{:S(2)}, u32[]{:S(2)}) collective-permute-start(bf16[5648,128]{1,0:T(8,128)(2,1)S(1)} %collective-permute-done.15.refs_4_), channel_id=1, source_target_pairs={{0,4},{2,6},{4,0},{6,2},{25,29},{27,31},{29,25},{31,27}} | collective-permute-start | bytes 4337672 | tf_op jit(solution)/shard_map/ppermute | solution.py:424
  60.5 18.0 %collective-permute-start.22 = (bf16[5648,128]{1,0:T(8,128)(2,1)S(1)}, bf16[5648,128]{1,0:T(8,128)(2,1)S(1)}, u32[]{:S(2)}, u32[]{:S(2)}) collective-permute-start(bf16[5648,128]{1,0:T(8,128)(2,1)S(1)} %collective-permute-done.16.refs_3_), channel_id=1, source_target_pairs={{9,13},{11,15},{13,9},{15,11},{16,20},{18,22},{20,16},{22,18}} | collective-permute-start | bytes 4337672 | tf_op jit(solution)/shard_map/ppermute | solution.py:424
  61.3 10.7 %collective-permute-start.23 = (s16[1296,256]{1,0:T(8,128)(2,1)S(1)}, s16[1296,256]{1,0:T(8,128)(2,1)S(1)}, u32[]{:S(2)}, u32[]{:S(2)}) collective-permute-start(s16[1296,256]{1,0:T(8,128)(2,1)S(1)} %get-tuple-element.111), channel_id=1, source_target_pairs={{2,0},{3,1},{6,4},{7,5},{10,8},{11,9},{14,12},{15,13},{16,18},{17,... | collective-permute-start | bytes 1990664 | tf_op jit(solution)/shard_map/ppermute | solution.py:424
  73.2 8.2 %copy-start = (bf16[5648,128]{1,0:T(8,128)(2,1)}, bf16[5648,128]{1,0:T(8,128)(2,1)S(1)}, u32[]{:S(2)}) copy-start(bf16[5648,128]{1,0:T(8,128)(2,1)S(1)} %collective-permute-done.19.one_ref.refs_7_) | copy-start | bytes 4337668
  78.5 14.9 %copy-start.7 = (bf16[5648,128]{1,0:T(8,128)(2,1)}, bf16[5648,128]{1,0:T(8,128)(2,1)S(1)}, u32[]{:S(2)}) copy-start(bf16[5648,128]{1,0:T(8,128)(2,1)S(1)} %collective-permute-done.20.refs_4_) | copy-start | bytes 4337668
  78.5 2.8 %copy-start.11 = (bf16[5648,128]{1,0:T(8,128)(2,1)}, bf16[5648,128]{1,0:T(8,128)(2,1)S(1)}, u32[]{:S(2)}) copy-start(bf16[5648,128]{1,0:T(8,128)(2,1)S(1)} %collective-permute-done.21.refs_5_) | copy-start | bytes 4337668
  78.5 2.8 %copy-start.1 = (bf16[5648,128]{1,0:T(8,128)(2,1)}, bf16[5648,128]{1,0:T(8,128)(2,1)S(1)}, u32[]{:S(2)}) copy-start(bf16[5648,128]{1,0:T(8,128)(2,1)S(1)} %collective-permute-done.22.two_ref.refs_4_) | copy-start | bytes 4337668
  79.2 14.2 %collective-permute-start.25 = (bf16[2832,128]{1,0:T(8,128)(2,1)S(1)}, bf16[2832,128]{1,0:T(8,128)(2,1)S(1)}, u32[]{:S(2)}, u32[]{:S(2)}) collective-permute-start(bf16[2832,128]{1,0:T(8,128)(2,1)S(1)} %get-tuple-element.116), channel_id=1, source_target_pairs={{9,1},{11,3},{13,5},{15,7},{16,24},{18,26},{20,28},{22,30}} | collective-permute-start | bytes 2174984 | tf_op jit(solution)/shard_map/ppermute | solution.py:424
  79.9 13.5 %collective-permute-start.24 = (bf16[2816,128]{1,0:T(8,128)(2,1)S(1)}, bf16[2816,128]{1,0:T(8,128)(2,1)S(1)}, u32[]{:S(2)}, u32[]{:S(2)}) collective-permute-start(bf16[2816,128]{1,0:T(8,128)(2,1)S(1)} %get-tuple-element.115), channel_id=1, source_target_pairs={{1,5},{3,7},{5,1},{7,3},{24,28},{26,30},{28,24},{30,26}} | collective-permute-start | bytes 2162696 | tf_op jit(solution)/shard_map/ppermute | solution.py:424
  80.6 11.6 %collective-permute-start.26 = (s16[1296,256]{1,0:T(8,128)(2,1)S(1)}, s16[1296,256]{1,0:T(8,128)(2,1)S(1)}, u32[]{:S(2)}, u32[]{:S(2)}) collective-permute-start(s16[1296,256]{1,0:T(8,128)(2,1)S(1)} %get-tuple-element.124), channel_id=1, source_target_pairs={{0,2},{4,6},{9,11},{13,15},{18,16},{22,20},{27,25},{31,29}} | collective-permute-start | bytes 1990664 | tf_op jit(solution)/shard_map/ppermute | solution.py:424
  86.8 17.6 %collective-permute-start.29 = (s16[1296,256]{1,0:T(8,128)(2,1)}, s16[1296,256]{1,0:T(8,128)(2,1)S(1)}, u32[]{:S(2)}, u32[]{:S(2)}) collective-permute-start(s16[1296,256]{1,0:T(8,128)(2,1)} %get-tuple-element.136), channel_id=1, source_target_pairs={{0,2},{1,3},{4,6},{5,7},{8,10},{9,11},{12,14},{13,15},{18,16},{19,... | collective-permute-start | bytes 1990664 | tf_op jit(solution)/shard_map/ppermute | solution.py:424
  88.1 17.5 %collective-permute-start.28 = (s16[1296,256]{1,0:T(8,128)(2,1)}, s16[1296,256]{1,0:T(8,128)(2,1)S(1)}, u32[]{:S(2)}, u32[]{:S(2)}) collective-permute-start(s16[1296,256]{1,0:T(8,128)(2,1)} %get-tuple-element.133), channel_id=1, source_target_pairs={{2,0},{3,1},{6,4},{7,5},{10,8},{11,9},{14,12},{15,13},{16,18},{17,... | collective-permute-start | bytes 1990664 | tf_op jit(solution)/shard_map/ppermute | solution.py:424
  93.4 0.9 copy-start.16
  93.4 1.1 copy-start.15
  94.5 30.0 %copy-start.17 = (s32[8,16]{1,0:T(8,128)S(1)}, s32[8,16]{1,0:T(8,128)}, u32[]{:S(2)}) copy-start(s32[8,16]{1,0:T(8,128)} %mask_ref.1) | copy-start | bytes 1540
  94.5 30.0 %copy-start.18 = (s32[16,2]{0,1:T(2,128)S(1)}, s32[16,2]{0,1:T(2,128)}, u32[]{:S(2)}) copy-start(s32[16,2]{0,1:T(2,128)} %param.9) | copy-start | bytes 388
  100.2 24.3 %collective-permute-start.31 = (s16[1296,256]{1,0:T(8,128)(2,1)}, s16[1296,256]{1,0:T(8,128)(2,1)}, u32[]{:S(2)}, u32[]{:S(2)}) collective-permute-start(s16[1296,256]{1,0:T(8,128)(2,1)} %get-tuple-element.144), channel_id=1, source_target_pairs={{1,3},{5,7},{8,10},{12,14},{19,17},{23,21},{26,24},{30,28}} | collective-permute-start | bytes 1990664 | tf_op jit(solution)/shard_map/ppermute | solution.py:424
  101.5 17.9 %collective-permute-start.27 = (f32[8,128]{1,0:T(8,128)S(1)}, f32[8,128]{1,0:T(8,128)S(1)}, u32[]{:S(2)}, u32[]{:S(2)}) collective-permute-start(f32[8,128]{1,0:T(8,128)S(1)} %get-tuple-element.131), channel_id=1, source_target_pairs={{0,2},{2,0},{1,3},{3,1},{4,6},{6,4},{5,7},{7,5},{8,10},{10,8},{9,1... | collective-permute-start | bytes 12296 | tf_op jit(solution)/shard_map/ppermute | solution.py:476
  119.4 3.7 %collective-permute-start.30 = (f32[8,128]{1,0:T(8,128)S(1)}, f32[8,128]{1,0:T(8,128)S(1)}, u32[]{:S(2)}, u32[]{:S(2)}) collective-permute-start(f32[8,128]{1,0:T(8,128)S(1)} %add.133), channel_id=1, source_target_pairs={{0,1},{1,0},{2,3},{3,2},{4,5},{5,4},{6,7},{7,6},{8,9},{9,8},{10,11... | collective-permute-start | bytes 12296 | tf_op jit(solution)/shard_map/ppermute | solution.py:478
  126.9 1.0 copy-start.14

commit v5 on v4

--- a/solution.py
+++ b/solution.py
@@ -62,13 +62,23 @@
 ANY = pl.BlockSpec(memory_space=pl.ANY)
 
 
-def pack_tiles(shards, masks, cap):
+def pack_tiles(shards, masks, swap, cap):
     wide = shards[0].shape[1] // TILE
     tiles = masks[0].size
     count = len(shards)
 
-    def kernel(*refs):
+    def kernel(swap_ref, *refs):
         mask_refs, b_refs, out_ref = refs[:count], refs[count:-1], refs[-1]
+
+        @pl.when(swap_ref[0] == 0)
+        def _():
+            pack(mask_refs, b_refs, out_ref)
+
+        @pl.when(swap_ref[0] != 0)
+        def _():
+            pack(mask_refs[::-1], b_refs[::-1], out_ref)
+
+    def pack(mask_refs, b_refs, out_ref):
         place = jnp.int32(0)
         lane = lax.broadcasted_iota(jnp.int32, (META, TILE), 1)
         sub = lax.broadcasted_iota(jnp.int32, (META, TILE), 0)
@@ -91,9 +101,9 @@
     return call(
         kernel, "pack_tiles",
         out_shape=jax.ShapeDtypeStruct((cap * TILE + META, TILE), shards[0].dtype),
-        in_specs=[SMEM] * count + [VMEM] * count,
+        in_specs=[SMEM] * (1 + count) + [VMEM] * count,
         out_specs=VMEM,
-    )(*masks, *shards)
+    )(swap, *masks, *shards)
 
 
 def mask_tiles(amplitudes, mask):
@@ -122,7 +132,7 @@
     )(mask, amplitudes)
 
 
-def shard_product(amps, picks, step, choices, tokens):
+def shard_product(amps, picks, step, choices, tokens, before=None, held=in_hbm):
     rows, depth = amps[0].shape
     count = len(amps)
     height = sum(part.shape[0] for part in choices[0])
@@ -130,6 +140,7 @@
     wide = 2
     tiles = count * wide * depth // TILE
     word = 16
+    first_row = 0 if before is None else before.shape[0]
     parts = []
     for choice in choices:
         for part in choice:
@@ -137,6 +148,8 @@
                 parts.append(part)
 
     def kernel(picks_ref, *refs):
+        if first_row:
+            before_ref, refs = refs[0], refs[1:]
         token_refs, refs = refs[:len(tokens)], refs[len(tokens):]
         a_refs, refs = refs[:count], refs[count:]
         p_any, refs = refs[:len(parts)], refs[len(parts):]
@@ -188,22 +201,24 @@
 
         @pl.when((pick >= 0) & (picks_ref[STEPS + step] != 0))
         def _():
-            encode(out_ref, coded_ref)
+            if first_row:
+                coded_ref[:first_row, :] = before_ref[...]
+            encode(out_ref, coded_ref, first_row)
 
     return call(
         kernel, "shard_product",
         out_shape=(
             jax.ShapeDtypeStruct((rows, wide * TILE), jnp.float32),
-            jax.ShapeDtypeStruct((coded_rows(rows), wide * TILE), jnp.int16),
+            jax.ShapeDtypeStruct((first_row + coded_rows(rows), wide * TILE), jnp.int16),
             TOKEN),
-        in_specs=[SMEM] + [VMEM] * (len(tokens) + count) + [ANY] * len(parts),
+        in_specs=[SMEM] + [VMEM] * (bool(first_row) + len(tokens) + count) + [ANY] * len(parts),
         out_specs=(VMEM, VMEM, VMEM),
         scratch_shapes=[
             pltpu.VMEM((height, TILE), amps[0].dtype),
             pltpu.VMEM((count * depth, wide * TILE), amps[0].dtype),
             pltpu.SemaphoreType.DMA((2,)),
         ],
-    )(picks, *tokens, *amps, *map(in_hbm, parts))
+    )(picks, *([before] if first_row else []), *tokens, *amps, *map(held, parts))
 
 
 def coded_rows(rows):
@@ -221,7 +236,7 @@
     return factors
 
 
-def encode(sums_ref, coded_ref):
+def encode(sums_ref, coded_ref, first_row):
     rows, cols = sums_ref.shape
     groups = rows // GROUP
     largest = jnp.concatenate([
@@ -242,43 +257,51 @@
             g = at // GROUP
             value = sums_ref[at:at + GROUP, :] * one[g:g + 1] * two[g:g + 1]
             value = jnp.minimum(jnp.round(value).astype(jnp.int32), (1 << (BITS - 1)) - 1)
-            coded_ref[at:at + GROUP, :] = (value >> LOW).astype(jnp.int16)
+            coded_ref[first_row + at:first_row + at + GROUP, :] = (value >> LOW).astype(jnp.int16)
             low = low | ((value & ((1 << LOW) - 1)) << (LOW * part))
-        coded_ref[rows + start:rows + start + GROUP, :] = (low - 32768).astype(jnp.int16)
-    coded_ref[rows + block:, :] = jnp.concatenate([exponent] * (META // groups)).astype(jnp.int16)
-
-
-def decode(coded_ref, rows, put):
+        low_at = first_row + rows + start
+        coded_ref[low_at:low_at + GROUP, :] = (low - 32768).astype(jnp.int16)
+    coded_ref[first_row + rows + block:, :] = jnp.concatenate([exponent] * (META // groups)).astype(jnp.int16)
+
+
+def decode(coded_ref, rows, put, first_row=0):
     groups = rows // GROUP
     share = 16 // LOW
     block = rows // share
-    one, two = step_factors(coded_ref[rows + block:, :].astype(jnp.int32)[:groups])
+    exponent_at = first_row + rows + block
+    one, two = step_factors(coded_ref[exponent_at:exponent_at + META, :].astype(jnp.int32)[:groups])
     one, two = 1.0 / one, 1.0 / two
     for start in range(0, block, GROUP):
-        low = coded_ref[rows + start:rows + start + GROUP, :].astype(jnp.int32) + 32768
+        low_at = first_row + rows + start
+        low = coded_ref[low_at:low_at + GROUP, :].astype(jnp.int32) + 32768
         for part in range(share):
             at = part * block + start
             g = at // GROUP
-            high = coded_ref[at:at + GROUP, :].astype(jnp.int32)
+            high = coded_ref[first_row + at:first_row + at + GROUP, :].astype(jnp.int32)
             value = (high << LOW) | ((low >> (LOW * part)) & ((1 << LOW) - 1))
             put(at, value.astype(jnp.float32) * one[g:g + 1] * two[g:g + 1])
 
 
 def add_coded(sums, coded):
-    def kernel(sums_ref, coded_ref, out_ref, token_ref):
+    rows = sums[0].shape[0]
+    count = len(sums)
+
+    def kernel(*refs):
+        sums_refs, coded_ref, out_refs, token_ref = refs[:count], refs[count], refs[count + 1:-1], refs[-1]
         token_ref[...] = jnp.zeros_like(token_ref)
-
-        def put(at, far):
-            out_ref[at:at + GROUP, :] = (sums_ref[at:at + GROUP, :] + far).astype(out_ref.dtype)
-
-        decode(coded_ref, sums.shape[0], put)
+        for number in range(count):
+            def put(at, far, number=number):
+                out_refs[number][at:at + GROUP, :] = (
+                    sums_refs[number][at:at + GROUP, :] + far).astype(jnp.bfloat16)
+
+            decode(coded_ref, rows, put, number * coded_rows(rows))
 
     return call(
         kernel, "add_coded",
-        out_shape=(jax.ShapeDtypeStruct(sums.shape, jnp.bfloat16), TOKEN),
-        in_specs=[VMEM, VMEM],
-        out_specs=(VMEM, VMEM),
-    )(sums, coded)
+        out_shape=tuple(jax.ShapeDtypeStruct(part.shape, jnp.bfloat16) for part in sums) + (TOKEN,),
+        in_specs=[VMEM] * (count + 1),
+        out_specs=(VMEM,) * (count + 1),
+    )(*sums, coded)
 
 
 def lay_out(place, mine, rest):
@@ -292,7 +315,7 @@
         return [array is known for known in arrays].index(True)
 
     def kernel(place_ref, *refs):
-        ins, out_ref = refs[:len(arrays)], refs[-1]
+        ins, out_any, out_ref, sem = refs[:len(arrays)], *refs[len(arrays):]
         for x in range(2):
             own, other = slice(x * width, (x + 1) * width), slice((1 - x) * width, (2 - x) * width)
             for number in range(len(mine)):
@@ -308,12 +331,16 @@
                         decode(coded_ref, rows, put)
                     else:
                         out_ref[:, other] = ins[index(rest[number])][...]
+        copy = pltpu.make_async_copy(out_ref, out_any, sem)
+        copy.start()
+        copy.wait()
 
     return call(
         kernel, "lay_out",
-        out_shape=jax.ShapeDtypeStruct((rows, 2 * width), jnp.bfloat16),
+        out_shape=pltpu.HBM((rows, 2 * width), jnp.bfloat16),
         in_specs=[SMEM] + [VMEM] * len(arrays),
-        out_specs=VMEM,
+        out_specs=ANY,
+        scratch_shapes=[pltpu.VMEM((rows, 2 * width), jnp.bfloat16), pltpu.SemaphoreType.DMA],
     )(place, *arrays)
 
 
@@ -369,10 +396,6 @@
     return (z, 1 - x) if z in (1, 2) else None
 
 
-def to_pair(z, x):
-    return z ^ 1, x
-
-
 def over_centre(z, x):
     return (3 - z, x) if z in (1, 2) else None
 
@@ -403,10 +426,11 @@
     return (1 - z % 2,)
 
 
-FROM_OTHER_CORE = [
-    (device(z, x, y, 1 - z % 2), device(z, x, y, z % 2)) for z in range(Z) for x in range(X) for y in range(Y)]
+OWN_TO_PAIR = [
+    (device(z, x, y, 1 - z % 2), device(z ^ 1, x, y, z % 2)) for z in range(Z) for x in range(X) for y in range(Y)]
 CORES = [(0, 1), (1, 0), (2, 3), (3, 2)]
 CHIPS_Y = [(0, 2), (2, 0), (1, 3), (3, 1)]
+CROSSWISE = [(0, 3), (3, 0), (1, 2), (2, 1)]
 
 
 def sparse_ladder(amplitudes, integrals, amp_mask, int_mask):
@@ -435,54 +459,54 @@
         jnp.where(home, -1, is_end),
     ] + [jnp.where(near, s, 1 - s) for s in (0, 1, 0, 1, 1)]).astype(jnp.int32)
 
-    other = move(integrals, FROM_OTHER_CORE)
+    place = jnp.stack([jnp.where(near, 0, jnp.where(home, 1, 2)), x]).astype(jnp.int32)
+
+    other = lax.ppermute(integrals, "col", CORES)
     other_mask = lax.ppermute(int_mask.T, "col", CORES)
-    own = pack_tiles((integrals, other), (int_mask.T, other_mask), cap)
-    own, picks, amplitudes_now = barrier((own, picks, amplitudes))
+    swap = jnp.where(home, 0, 1).astype(jnp.int32).reshape(1)
+    own = pack_tiles((integrals, other), (int_mask.T, other_mask), swap, cap)
+    own, picks, place, amplitudes_now = barrier((own, picks, place, amplitudes))
 
     masked, masked_token = mask_tiles(amplitudes_now, amp_mask)
     amps = (masked, lax.ppermute(masked, "col", CORES))
     one, centre, own_x, tokens = after(masked_token)(
-        move(own, moves(to_pair)), move(own, moves(over_centre)), move(own, moves(across_x)))
+        move(own, OWN_TO_PAIR), move(own, moves(over_centre)), move(own, moves(across_x)))
 
     a_sum, a_coded, token = shard_product(amps, picks, 0, [[own], [one]], tokens)
-    a_far = move(a_coded, to_y(False, both))
     two_end, two_mid, one_x, own_x, tokens = after(token)(
         move(centre, moves(outward, False)), move(one, moves(over_centre, False)), move(one, moves(across_x, False)),
         own_x)
 
     c_sum, c_coded, token = shard_product(amps, picks, 1, [[two_mid], [two_end]], tokens)
     c_far = move(c_coded, to_y(True, home_core))
-    b_sum, b_coded, token = shard_product(amps, picks, 2, [[own_x], [one_x]], (token,))
-    a_both, a_token = add_coded(a_sum, a_far)
-    three_end, three_mid_x, two_x_end, two_x_mid, tokens = after(token, a_token)(
+    b_sum, ab_coded, token = shard_product(amps, picks, 2, [[own_x], [one_x]], (token,), a_coded)
+    c_both, c_token = add_coded((c_sum,), c_far)
+    three_end, three_mid_x, two_x_end, two_x_mid, tokens = after(token, c_token)(
         move(two_mid, moves(outward)), move(own_x, moves(over_centre)),
         move(two_end, moves(across_x_ends)), move(two_mid, moves(across_x_middle)))
 
     d_sum, d_coded, token = shard_product(
         amps, picks, 3, [[two_x_mid], [two_x_end], [centre], [three_end]], tokens)
-    b_coded, token = barrier((b_coded, token))
-    b_far = move(b_coded, to_y(False, both))
+    ab_far = move(ab_coded, to_y(False, both))
     top, rest = top_and_rest(three_end, two_x_mid, half)
-    c_both, c_token = add_coded(c_sum, c_far)
-    three_x, three_x_rest, tokens = after(token, c_token)(
+    three_x, three_x_rest, tokens = after(token)(
         move(top, moves(across_x_ends, False)), move(rest, moves(outward)))
 
     d_far = move(d_coded, to_y(True, both))
-    e_sum, e_coded, token = shard_product(amps, picks, 4, [[three_mid_x], [three_x, three_x_rest]], tokens)
+    e_sum, e_coded, token = shard_product(amps, picks, 4, [[three_mid_x], [three_x, three_x_rest]], tokens,
+        held=lambda part: in_hbm(part) if part is three_mid_x else part)
     e_far = move(e_coded, to_y(True, other_core))
-    b_both, b_token = add_coded(b_sum, b_far)
-    d_both, d_token = add_coded(d_sum, d_far)
-    excess = token + lax.ppermute(token, "col", CHIPS_Y)
-    excess, b_both, d_both = barrier((excess, b_both, d_both))
-    excess = excess + lax.ppermute(excess, "col", CORES)
-    place = jnp.stack([jnp.where(near, 0, jnp.where(home, 1, 2)), x]).astype(jnp.int32)
+    ab_far, token = barrier((ab_far, token))
+    a_both, b_both, _ = add_coded((a_sum, b_sum), ab_far)
+    d_both, _ = add_coded((d_sum,), d_far)
+    flags = [token] + [lax.ppermute(token, "col", pairs) for pairs in (CORES, CHIPS_Y, CROSSWISE)]
+    flags, a_both, b_both, d_both = barrier((flags, a_both, b_both, d_both))
 
     def finish():
         return lay_out(place, (a_both, c_both, d_both), (b_both, d_both, (e_sum, e_far)))
 
     return lax.cond(
-        jnp.max(excess) > 0, lambda: dense_ladder(amplitudes, integrals, amp_mask, int_mask), finish)
+        jnp.max(sum(flags)) > 0, lambda: dense_ladder(amplitudes, integrals, amp_mask, int_mask), finish)
 
 
 def solution(mesh):

time: 128 us -> 120 us (0.938)
  the two profiles are of different devices: /device:TPU:17 before, /device:TPU:24 now
where the time goes in v5:
time: 120 us; the launch traced here: 119 us
  waiting for transfers between devices  58.2 us (48%)
  Pallas kernels  31.3 us (26%)
  starting transfers between devices  27.4 us (23%)
  between operations  1.3 us (1%)
    ppermute x16, waiting for transfers between devices, move(): return lax.ppermute(value, AXES, pairs)  50.3 us
    ppermute x16, starting transfers between devices, move(): return lax.ppermute(value, AXES, pairs)  23.8 us
    pallas_call x5, Pallas kernels, shard_product(): call(kernel, 'shard_product', out_shape=(jax.ShapeDtypeStruct((rows, wide...  18.9 us
    ppermute x3, waiting for transfers between devices, sparse_ladder(): lax.ppermute(token, 'col', pairs)  5.73 us
    pallas_call x3, Pallas kernels, add_coded(): call(kernel, 'add_coded', out_shape=tuple((jax.ShapeDtypeStruct(part.shap...  3.9 us
    pallas_call x1, Pallas kernels, mask_tiles(): call(kernel, 'mask_tiles', out_shape=(jax.ShapeDtypeStruct(amplitudes.sha...  3.06 us
    pallas_call x1, Pallas kernels, lay_out(): call(kernel, 'lay_out', out_shape=pltpu.HBM((rows, 2 * width), jnp.bfloat...  2.95 us
    ppermute x3, starting transfers between devices, sparse_ladder(): lax.ppermute(token, 'col', pairs)  2.89 us
  transfers between devices with their start and end apart: 22, of which 7 were waited for; matrix products, arithmetic and copies ran while one was open for 1% of the time, Pallas kernels for 20%

profile of v5, /device:TPU:24, one launch (start us, length us, event | category | flops | bytes accessed | tf_op | source)
XLA Modules:
  0.0 119.3 jit_solution(10430296193392654122)
XLA Ops:
  0.0 0.0 collective-permute-start.11
  0.0 0.5 collective-permute-start.10
  0.5 0.1 pad_add_fusion
  0.6 0.1 stack.37.picks_ref
  0.7 2.2 %collective-permute-done.10.refs_1_ = s32[2,16]{1,0:T(2,128)S(1)} collective-permute-done((s32[2,16]{1,0:T(2,128)}, s32[2,16]{1,0:T(2,128)S(1)}, u32[]{:S(2)}, u32[]{:S(2)}) %collective-permute-start.10) | collective-permute-done | bytes 160 | tf_op jit(solution)/shard_map/ppermute | solution.py:465
  2.9 0.0 collective-permute-done.11.refs_3_
  2.9 1.9 %pack_tiles.1.refs_3_ = bf16[5648,128]{1,0:T(8,128)(2,1)S(1)} custom-call(s32[1]{0:T(128)} %bitcast.2.swap_ref, s32[2,16]{1,0:T(2,128)} %bitcast.38, s32[2,16]{1,0:T(2,128)S(1)} %collective-permute-done.10.refs_1_, bf16[2048,256]{1,0:T(8,128)(2,1)} %refs_2_.1, bf16[2048,256]{1,0:T(8,128)(2,1)S(1)} %collective-permute-done.11.refs_3_), custom_call_target="tpu_custom_call" | custom-call | flops 1 | bytes 1 | tf_op jit(solution)/shard_map/pack_tiles/pallas_call | solution.py:101
  4.8 3.1 %mask_tiles.1 = (bf16[1024,2048]{1,0:T(8,128)(2,1)S(1)}, f32[8,128]{1,0:T(8,128)S(1)}) custom-call(s32[8,16]{1,0:T(8,128)} %mask_ref.1, bf16[1024,2048]{1,0:T(8,128)(2,1)} %a_any), custom_call_target="tpu_custom_call" | custom-call | flops 1 | bytes 1 | tf_op jit(solution)/shard_map/mask_tiles/pallas_call | solution.py:126
  7.9 0.2 collective-permute-start.15
  8.1 2.3 %collective-permute-start.12 = (bf16[5648,128]{1,0:T(8,128)(2,1)S(1)}, bf16[5648,128]{1,0:T(8,128)(2,1)S(1)}, u32[]{:S(2)}, u32[]{:S(2)}) collective-permute-start(bf16[5648,128]{1,0:T(8,128)(2,1)S(1)} %pack_tiles.1.refs_3_), channel_id=1, source_target_pairs={{1,8},{3,10},{5,12},{7,14},{8,1},{10,3},{12,5},{14,7},{17,24},{19,... | collective-permute-start | bytes 4337672 | tf_op jit(solution)/shard_map/ppermute | solution.py:448
  10.4 0.8 collective-permute-start.13
  11.2 0.8 collective-permute-start.14
  11.9 16.5 %collective-permute-done.12.refs_4_ = bf16[5648,128]{1,0:T(8,128)(2,1)S(1)} collective-permute-done((bf16[5648,128]{1,0:T(8,128)(2,1)S(1)}, bf16[5648,128]{1,0:T(8,128)(2,1)S(1)}, u32[]{:S(2)}, u32[]{:S(2)}) %collective-permute-start.12) | collective-permute-done | bytes 1445920 | tf_op jit(solution)/shard_map/ppermute | solution.py:448
  28.4 0.0 collective-permute-done.13.refs_6_
  28.4 0.0 collective-permute-done.14.refs_4_
  28.4 0.0 copy-start.9
  28.4 0.8 collective-permute-start.16
  29.2 0.8 collective-permute-start.17
  30.0 3.4 %collective-permute-start.18 = (bf16[5648,128]{1,0:T(8,128)(2,1)S(1)}, bf16[5648,128]{1,0:T(8,128)(2,1)S(1)}, u32[]{:S(2)}, u32[]{:S(2)}) collective-permute-start(bf16[5648,128]{1,0:T(8,128)(2,1)S(1)} %collective-permute-done.12.refs_4_), channel_id=1, source_target_pairs={{1,5},{3,7},{5,1},{7,3},{8,12},{10,14},{12,8},{14,10},{17,21},{19,... | collective-permute-start | bytes 4337672 | tf_op jit(solution)/shard_map/ppermute | solution.py:448
  33.4 0.0 collective-permute-done.15.refs_2_.refs_3_
  33.4 5.0 %shard_product.5 = (f32[1024,256]{1,0:T(8,128)S(1)}, s16[1296,256]{1,0:T(8,128)(2,1)S(1)}, f32[8,128]{1,0:T(8,128)S(1)}) custom-call(s32[10]{0:T(128)S(1)} %stack.37.picks_ref, f32[8,128]{1,0:T(8,128)S(1)} %get-tuple-element.100.refs_0_, bf16[1024,2048]{1,0:T(8,128)(2,1)S(1)} %get-tuple-element.101.refs_1_.refs_2_, ...), custom_call_target="tpu_custom_call" | custom-call | flops 1 | bytes 1 | tf_op jit(solution)/shard_map/shard_product/pallas_call | solution.py:208
  38.4 0.0 collective-permute-done.16.refs_4_
  38.4 0.0 collective-permute-done.17.refs_3_
  38.4 12.5 %collective-permute-done.18.refs_5_ = bf16[5648,128]{1,0:T(8,128)(2,1)S(1)} collective-permute-done((bf16[5648,128]{1,0:T(8,128)(2,1)S(1)}, bf16[5648,128]{1,0:T(8,128)(2,1)S(1)}, u32[]{:S(2)}, u32[]{:S(2)}) %collective-permute-start.18) | collective-permute-done | bytes 1445920 | tf_op jit(solution)/shard_map/ppermute | solution.py:448
  50.9 1.3 %collective-permute-start.20 = (bf16[5648,128]{1,0:T(8,128)(2,1)S(1)}, bf16[5648,128]{1,0:T(8,128)(2,1)S(1)}, u32[]{:S(2)}, u32[]{:S(2)}) collective-permute-start(bf16[5648,128]{1,0:T(8,128)(2,1)S(1)} %collective-permute-done.17.refs_3_), channel_id=1, source_target_pairs={{9,1},{11,3},{13,5},{15,7},{16,24},{18,26},{20,28},{22,30}} | collective-permute-start | bytes 4337672 | tf_op jit(solution)/shard_map/ppermute | solution.py:448
  52.2 0.8 collective-permute-start.21
  53.0 0.8 collective-permute-start.22
  53.7 0.8 collective-permute-start.23
  54.5 0.6 shard_product.6
  55.1 0.7 collective-permute-start.24
  55.8 5.0 %shard_product.7 = (f32[1024,256]{1,0:T(8,128)S(1)}, s16[2592,256]{1,0:T(8,128)(2,1)S(1)}, f32[8,128]{1,0:T(8,128)S(1)}) custom-call(s32[10]{0:T(128)S(1)} %stack.37.picks_ref, s16[1296,256]{1,0:T(8,128)(2,1)S(1)} %get-tuple-element.103.refs_0_, f32[8,128]{1,0:T(8,128)S(1)} %get-tuple-element.110.refs_1_, ...), custom_call_target="tpu_custom_call" | custom-call | flops 1 | bytes 1 | tf_op jit(solution)/shard_map/shard_product/pallas_call | solution.py:208
  60.9 0.0 collective-permute-done.24.refs_1_
  60.9 3.1 %collective-permute-start.19 = (s16[2592,256]{1,0:T(8,128)(2,1)S(1)}, s16[2592,256]{1,0:T(8,128)(2,1)S(1)}, u32[]{:S(2)}, u32[]{:S(2)}) collective-permute-start(s16[2592,256]{1,0:T(8,128)(2,1)S(1)} %get-tuple-element.113), channel_id=1, source_target_pairs={{2,0},{3,1},{6,4},{7,5},{10,8},{11,9},{14,12},{15,13},{16,18},{17,... | collective-permute-start | bytes 3981320 | tf_op jit(solution)/shard_map/ppermute | solution.py:448
  63.9 1.2 add_coded.3
  65.1 8.7 %collective-permute-done.20.one_ref.refs_7_ = bf16[5648,128]{1,0:T(8,128)(2,1)S(1)} collective-permute-done((bf16[5648,128]{1,0:T(8,128)(2,1)S(1)}, bf16[5648,128]{1,0:T(8,128)(2,1)S(1)}, u32[]{:S(2)}, u32[]{:S(2)}) %collective-permute-start.20) | collective-permute-done | bytes 1445920 | tf_op jit(solution)/shard_map/ppermute | solution.py:448
  73.9 0.0 collective-permute-done.21.refs_3_
  73.9 0.0 collective-permute-done.22.refs_5_
  73.9 0.0 collective-permute-done.23.two_ref.refs_4_
  73.9 0.6 top_and_rest.1
  74.5 1.3 %collective-permute-start.26 = (bf16[2832,128]{1,0:T(8,128)(2,1)S(1)}, bf16[2832,128]{1,0:T(8,128)(2,1)S(1)}, u32[]{:S(2)}, u32[]{:S(2)}) collective-permute-start(bf16[2832,128]{1,0:T(8,128)(2,1)S(1)} %get-tuple-element.121), channel_id=1, source_target_pairs={{9,1},{11,3},{13,5},{15,7},{16,24},{18,26},{20,28},{22,30}} | collective-permute-start | bytes 2174984 | tf_op jit(solution)/shard_map/ppermute | solution.py:448
  75.8 3.8 %collective-permute-start.25 = (bf16[2816,128]{1,0:T(8,128)(2,1)S(1)}, bf16[2816,128]{1,0:T(8,128)(2,1)S(1)}, u32[]{:S(2)}, u32[]{:S(2)}) collective-permute-start(bf16[2816,128]{1,0:T(8,128)(2,1)S(1)} %get-tuple-element.120), channel_id=1, source_target_pairs={{1,5},{3,7},{5,1},{7,3},{24,28},{26,30},{28,24},{30,26}} | collective-permute-start | bytes 2162696 | tf_op jit(solution)/shard_map/ppermute | solution.py:448
  79.6 4.5 %shard_product.8 = (f32[1024,256]{1,0:T(8,128)S(1)}, s16[1296,256]{1,0:T(8,128)(2,1)S(1)}, f32[8,128]{1,0:T(8,128)S(1)}) custom-call(s32[10]{0:T(128)S(1)} %stack.37.picks_ref, f32[8,128]{1,0:T(8,128)S(1)} %get-tuple-element.122.refs_0_, f32[8,128]{1,0:T(8,128)S(1)} %get-tuple-element.123.refs_1_, bf16[1024,2048]{1,0:T(8,128)(2,1)S(1)} %get-tuple-element.101.refs_1_.refs_2_, ...), custom_call_target="tpu_custom_call" | custom-call | flops 1 | bytes 1 | tf_op jit(solution)/shard_map/shard_product/pallas_call | solution.py:208
  84.2 1.3 %collective-permute-start.30 = (s16[1296,256]{1,0:T(8,128)(2,1)S(1)}, s16[1296,256]{1,0:T(8,128)(2,1)S(1)}, u32[]{:S(2)}, u32[]{:S(2)}) collective-permute-start(s16[1296,256]{1,0:T(8,128)(2,1)S(1)} %get-tuple-element.138), channel_id=1, source_target_pairs={{0,2},{1,3},{4,6},{5,7},{8,10},{9,11},{12,14},{13,15},{18,16},{19,... | collective-permute-start | bytes 1990664 | tf_op jit(solution)/shard_map/ppermute | solution.py:448
  85.5 3.5 %collective-permute-done.25.refs_4_ = bf16[2816,128]{1,0:T(8,128)(2,1)S(1)} collective-permute-done((bf16[2816,128]{1,0:T(8,128)(2,1)S(1)}, bf16[2816,128]{1,0:T(8,128)(2,1)S(1)}, u32[]{:S(2)}, u32[]{:S(2)}) %collective-permute-start.25) | collective-permute-done | bytes 720928 | tf_op jit(solution)/shard_map/ppermute | solution.py:448
  89.0 9.0 %collective-permute-done.26.refs_5_ = bf16[2832,128]{1,0:T(8,128)(2,1)S(1)} collective-permute-done((bf16[2832,128]{1,0:T(8,128)(2,1)S(1)}, bf16[2832,128]{1,0:T(8,128)(2,1)S(1)}, u32[]{:S(2)}, u32[]{:S(2)}) %collective-permute-start.26) | collective-permute-done | bytes 725024 | tf_op jit(solution)/shard_map/ppermute | solution.py:448
  98.0 3.8 %shard_product.9 = (f32[1024,256]{1,0:T(8,128)S(1)}, s16[1296,256]{1,0:T(8,128)(2,1)S(1)}, f32[8,128]{1,0:T(8,128)S(1)}) custom-call(s32[10]{0:T(128)S(1)} %stack.37.picks_ref, f32[8,128]{1,0:T(8,128)S(1)} %get-tuple-element.126.refs_0_, bf16[1024,2048]{1,0:T(8,128)(2,1)S(1)} %get-tuple-element.101.refs_1_.refs_2_, ...), custom_call_target="tpu_custom_call" | custom-call | flops 1 | bytes 1 | tf_op jit(solution)/shard_map/shard_product/pallas_call | solution.py:208
  101.8 0.0 copy-start.6
  101.8 0.0 copy-start.15
  101.8 0.0 copy-start.16
  101.8 1.4 %collective-permute-start.31 = (s16[1296,256]{1,0:T(8,128)(2,1)S(1)}, s16[1296,256]{1,0:T(8,128)(2,1)S(1)}, u32[]{:S(2)}, u32[]{:S(2)}) collective-permute-start(s16[1296,256]{1,0:T(8,128)(2,1)S(1)} %get-tuple-element.150), channel_id=1, source_target_pairs={{1,3},{5,7},{8,10},{12,14},{19,17},{23,21},{26,24},{30,28}} | collective-permute-start | bytes 1990664 | tf_op jit(solution)/shard_map/ppermute | solution.py:448
  103.3 0.0 collective-permute-done.19.refs_2_
  103.3 0.1 collective-permute-start.27
  103.3 2.7 %collective-permute-start.28 = (f32[8,128]{1,0:T(8,128)S(1)}, f32[8,128]{1,0:T(8,128)S(1)}, u32[]{:S(2)}, u32[]{:S(2)}) collective-permute-start(f32[8,128]{1,0:T(8,128)S(1)} %get-tuple-element.140), channel_id=1, source_target_pairs={{0,2},{2,0},{1,3},{3,1},{4,6},{6,4},{5,7},{7,5},{8,10},{10,8},{9,1... | collective-permute-start | bytes 12296 | tf_op jit(solution)/shard_map/ppermute | solution.py:502
  106.1 0.1 collective-permute-start.29
  106.2 0.0 collective-permute-done.30.refs_1_
  106.2 1.2 add_coded.5
  107.3 1.5 %add_coded.4 = (bf16[1024,256]{1,0:T(8,128)(2,1)}, bf16[1024,256]{1,0:T(8,128)(2,1)}, f32[8,128]{1,0:T(8,128)}) custom-call(f32[1024,256]{1,0:T(8,128)S(1)} %get-tuple-element.132.refs_0_, f32[1024,256]{1,0:T(8,128)S(1)} %get-tuple-element.133.refs_1_, s16[2592,256]{1,0:T(8,128)(2,1)S(1)} %collective-permute-done.19.refs_2_), custom_call_target="tpu_custom_call" | custom-call | flops 1 | bytes 1 | tf_op jit(solution)/shard_map/add_coded/pallas_call | solution.py:299
  108.9 0.0 collective-permute-done.27
  108.9 5.7 %collective-permute-done.28 = f32[8,128]{1,0:T(8,128)S(1)} collective-permute-done((f32[8,128]{1,0:T(8,128)S(1)}, f32[8,128]{1,0:T(8,128)S(1)}, u32[]{:S(2)}, u32[]{:S(2)}) %collective-permute-start.28) | collective-permute-done | bytes 4128 | tf_op jit(solution)/shard_map/ppermute | solution.py:502
  114.6 0.0 collective-permute-done.29
  114.6 0.6 add_reduce_fusion
  115.9 0.0 collective-permute-done.31
  115.9 3.2 %conditional.1 = (bf16[1024,512]{1,0:T(8,128)(2,1)}) conditional(s32[]{:T(128)} %convert_element_type.32, (s32[2]{0:T(128)S(1)}, bf16[1024,256]{1,0:T(8,128)(2,1)}, bf16[1024,256]{1,0:T(8,128)(2,1)}, bf16[1024,256]{1,0:T(8,128)(2,1)}, bf16[1024,256]{1,0:T(8,128)(2,1)}, /*index=5*/f32[1024,256]{1,0:T(8,128)S(1)}, ...), branch_computations={%region_1.2_spmd, %region_2.3_spmd} | conditional | flops 8594653184 | bytes 206655584 | solution.py:508
  115.9 3.0 %lay_out.1 = bf16[1024,512]{1,0:T(8,128)(2,1)} custom-call(s32[2]{0:T(128)S(1)} %get-tuple-element.30.place_ref, bf16[1024,256]{1,0:T(8,128)(2,1)} %get-tuple-element.31.refs_0_, bf16[1024,256]{1,0:T(8,128)(2,1)} %get-tuple-element.32.refs_1_, bf16[1024,256]{1,0:T(8,128)(2,1)} %get-tuple-element.33.refs_2_, bf16[1024,256]{1,0:T(8,128)(2,1)} %get-tuple-element.34.refs_3_, ...), custom_call_target="tpu_custom_call" | custom-call | flops 1 | bytes 1 | tf_op jit(solution)/shard_map/cond/branch_0_fun/lay_out/pallas_call | solution.py:338
  (24 shorter events, 0.0 us)
Async XLA Ops:
  0.0 2.9 %collective-permute-start.11 = (bf16[2048,256]{1,0:T(8,128)(2,1)}, bf16[2048,256]{1,0:T(8,128)(2,1)S(1)}, u32[]{:S(2)}, u32[]{:S(2)}) collective-permute-start(bf16[2048,256]{1,0:T(8,128)(2,1)} %refs_2_.1), channel_id=1, source_target_pairs={{0,1},{1,0},{2,3},{3,2},{4,5},{5,4},{6,7},{7,6},{8,9},{9,8},{10,11... | collective-permute-start | bytes 3145736 | tf_op jit(solution)/shard_map/ppermute | solution.py:464
  0.0 2.9 %collective-permute-start.10 = (s32[2,16]{1,0:T(2,128)}, s32[2,16]{1,0:T(2,128)S(1)}, u32[]{:S(2)}, u32[]{:S(2)}) collective-permute-start(s32[2,16]{1,0:T(2,128)} %bitcast.37), channel_id=1, source_target_pairs={{0,1},{1,0},{2,3},{3,2},{4,5},{5,4},{6,7},{7,6},{8,9},{9,8},{10,11... | collective-permute-start | bytes 392 | tf_op jit(solution)/shard_map/ppermute | solution.py:465
  4.8 28.6 %copy-start.2 = (bf16[5648,128]{1,0:T(8,128)(2,1)}, bf16[5648,128]{1,0:T(8,128)(2,1)S(1)}, u32[]{:S(2)}) copy-start(bf16[5648,128]{1,0:T(8,128)(2,1)S(1)} %pack_tiles.1.refs_3_) | copy-start | bytes 4337668
  7.9 25.5 %collective-permute-start.15 = (bf16[1024,2048]{1,0:T(8,128)(2,1)S(1)}, bf16[1024,2048]{1,0:T(8,128)(2,1)S(1)}, u32[]{:S(2)}, u32[]{:S(2)}) collective-permute-start(bf16[1024,2048]{1,0:T(8,128)(2,1)S(1)} %get-tuple-element.101.refs_1_.refs_2_), channel_id=1, source_target_pairs={{0,1},{1,0},{2,3},{3,2},{4,5},{5,4},{6,7},{7,6},{8,9},{9,8},{10,11... | collective-permute-start | bytes 12582920 | tf_op jit(solution)/shard_map/ppermute | solution.py:471
  8.1 20.4 %collective-permute-start.12 = (bf16[5648,128]{1,0:T(8,128)(2,1)S(1)}, bf16[5648,128]{1,0:T(8,128)(2,1)S(1)}, u32[]{:S(2)}, u32[]{:S(2)}) collective-permute-start(bf16[5648,128]{1,0:T(8,128)(2,1)S(1)} %pack_tiles.1.refs_3_), channel_id=1, source_target_pairs={{1,8},{3,10},{5,12},{7,14},{8,1},{10,3},{12,5},{14,7},{17,24},{19,... | collective-permute-start | bytes 4337672 | tf_op jit(solution)/shard_map/ppermute | solution.py:448
  10.4 18.0 %collective-permute-start.13 = (bf16[5648,128]{1,0:T(8,128)(2,1)S(1)}, bf16[5648,128]{1,0:T(8,128)(2,1)S(1)}, u32[]{:S(2)}, u32[]{:S(2)}) collective-permute-start(bf16[5648,128]{1,0:T(8,128)(2,1)S(1)} %pack_tiles.1.refs_3_), channel_id=1, source_target_pairs={{9,17},{11,19},{13,21},{15,23},{16,8},{18,10},{20,12},{22,14}} | collective-permute-start | bytes 4337672 | tf_op jit(solution)/shard_map/ppermute | solution.py:448
  11.2 17.3 %collective-permute-start.14 = (bf16[5648,128]{1,0:T(8,128)(2,1)S(1)}, bf16[5648,128]{1,0:T(8,128)(2,1)S(1)}, u32[]{:S(2)}, u32[]{:S(2)}) collective-permute-start(bf16[5648,128]{1,0:T(8,128)(2,1)S(1)} %pack_tiles.1.refs_3_), channel_id=1, source_target_pairs={{0,4},{2,6},{4,0},{6,2},{9,13},{11,15},{13,9},{15,11},{16,20},{18,... | collective-permute-start | bytes 4337672 | tf_op jit(solution)/shard_map/ppermute | solution.py:448
  28.4 5.0 %copy-start.14 = (bf16[5648,128]{1,0:T(8,128)(2,1)}, bf16[5648,128]{1,0:T(8,128)(2,1)S(1)}, u32[]{:S(2)}) copy-start(bf16[5648,128]{1,0:T(8,128)(2,1)S(1)} %collective-permute-done.12.refs_4_) | copy-start | bytes 4337668
  28.4 10.0 %copy-start.7 = (bf16[5648,128]{1,0:T(8,128)(2,1)}, bf16[5648,128]{1,0:T(8,128)(2,1)S(1)}, u32[]{:S(2)}) copy-start(bf16[5648,128]{1,0:T(8,128)(2,1)S(1)} %collective-permute-done.13.refs_6_) | copy-start | bytes 4337668
  28.4 23.8 %copy-start.9 = (bf16[5648,128]{1,0:T(8,128)(2,1)}, bf16[5648,128]{1,0:T(8,128)(2,1)S(1)}, u32[]{:S(2)}) copy-start(bf16[5648,128]{1,0:T(8,128)(2,1)S(1)} %collective-permute-done.14.refs_4_) | copy-start | bytes 4337668
  28.4 10.0 %collective-permute-start.16 = (bf16[5648,128]{1,0:T(8,128)(2,1)S(1)}, bf16[5648,128]{1,0:T(8,128)(2,1)S(1)}, u32[]{:S(2)}, u32[]{:S(2)}) collective-permute-start(bf16[5648,128]{1,0:T(8,128)(2,1)S(1)} %collective-permute-done.13.refs_6_), channel_id=1, source_target_pairs={{8,0},{10,2},{12,4},{14,6},{17,25},{19,27},{21,29},{23,31}} | collective-permute-start | bytes 4337672 | tf_op jit(solution)/shard_map/ppermute | solution.py:448
  29.2 9.2 %collective-permute-start.17 = (bf16[5648,128]{1,0:T(8,128)(2,1)S(1)}, bf16[5648,128]{1,0:T(8,128)(2,1)S(1)}, u32[]{:S(2)}, u32[]{:S(2)}) collective-permute-start(bf16[5648,128]{1,0:T(8,128)(2,1)S(1)} %collective-permute-done.12.refs_4_), channel_id=1, source_target_pairs={{8,16},{10,18},{12,20},{14,22},{17,9},{19,11},{21,13},{23,15}} | collective-permute-start | bytes 4337672 | tf_op jit(solution)/shard_map/ppermute | solution.py:448
  30.0 20.9 %collective-permute-start.18 = (bf16[5648,128]{1,0:T(8,128)(2,1)S(1)}, bf16[5648,128]{1,0:T(8,128)(2,1)S(1)}, u32[]{:S(2)}, u32[]{:S(2)}) collective-permute-start(bf16[5648,128]{1,0:T(8,128)(2,1)S(1)} %collective-permute-done.12.refs_4_), channel_id=1, source_target_pairs={{1,5},{3,7},{5,1},{7,3},{8,12},{10,14},{12,8},{14,10},{17,21},{19,... | collective-permute-start | bytes 4337672 | tf_op jit(solution)/shard_map/ppermute | solution.py:448
  38.4 16.1 %copy-start.10 = (bf16[5648,128]{1,0:T(8,128)(2,1)}, bf16[5648,128]{1,0:T(8,128)(2,1)S(1)}, u32[]{:S(2)}) copy-start(bf16[5648,128]{1,0:T(8,128)(2,1)S(1)} %collective-permute-done.16.refs_4_) | copy-start | bytes 4337668
  38.4 16.1 %copy-start.11 = (bf16[5648,128]{1,0:T(8,128)(2,1)}, bf16[5648,128]{1,0:T(8,128)(2,1)S(1)}, u32[]{:S(2)}) copy-start(bf16[5648,128]{1,0:T(8,128)(2,1)S(1)} %collective-permute-done.17.refs_3_) | copy-start | bytes 4337668
  50.9 4.2 %copy-start.13 = (bf16[5648,128]{1,0:T(8,128)(2,1)}, bf16[5648,128]{1,0:T(8,128)(2,1)S(1)}, u32[]{:S(2)}) copy-start(bf16[5648,128]{1,0:T(8,128)(2,1)S(1)} %collective-permute-done.18.refs_5_) | copy-start | bytes 4337668
  50.9 22.9 %collective-permute-start.20 = (bf16[5648,128]{1,0:T(8,128)(2,1)S(1)}, bf16[5648,128]{1,0:T(8,128)(2,1)S(1)}, u32[]{:S(2)}, u32[]{:S(2)}) collective-permute-start(bf16[5648,128]{1,0:T(8,128)(2,1)S(1)} %collective-permute-done.17.refs_3_), channel_id=1, source_target_pairs={{9,1},{11,3},{13,5},{15,7},{16,24},{18,26},{20,28},{22,30}} | collective-permute-start | bytes 4337672 | tf_op jit(solution)/shard_map/ppermute | solution.py:448
  52.2 21.6 %collective-permute-start.21 = (bf16[5648,128]{1,0:T(8,128)(2,1)S(1)}, bf16[5648,128]{1,0:T(8,128)(2,1)S(1)}, u32[]{:S(2)}, u32[]{:S(2)}) collective-permute-start(bf16[5648,128]{1,0:T(8,128)(2,1)S(1)} %collective-permute-done.14.refs_4_), channel_id=1, source_target_pairs={{9,17},{11,19},{13,21},{15,23},{16,8},{18,10},{20,12},{22,14}} | collective-permute-start | bytes 4337672 | tf_op jit(solution)/shard_map/ppermute | solution.py:448
  53.0 20.9 %collective-permute-start.22 = (bf16[5648,128]{1,0:T(8,128)(2,1)S(1)}, bf16[5648,128]{1,0:T(8,128)(2,1)S(1)}, u32[]{:S(2)}, u32[]{:S(2)}) collective-permute-start(bf16[5648,128]{1,0:T(8,128)(2,1)S(1)} %collective-permute-done.16.refs_4_), channel_id=1, source_target_pairs={{0,4},{2,6},{4,0},{6,2},{25,29},{27,31},{29,25},{31,27}} | collective-permute-start | bytes 4337672 | tf_op jit(solution)/shard_map/ppermute | solution.py:448
  53.7 20.1 %collective-permute-start.23 = (bf16[5648,128]{1,0:T(8,128)(2,1)S(1)}, bf16[5648,128]{1,0:T(8,128)(2,1)S(1)}, u32[]{:S(2)}, u32[]{:S(2)}) collective-permute-start(bf16[5648,128]{1,0:T(8,128)(2,1)S(1)} %collective-permute-done.17.refs_3_), channel_id=1, source_target_pairs={{9,13},{11,15},{13,9},{15,11},{16,20},{18,22},{20,16},{22,18}} | collective-permute-start | bytes 4337672 | tf_op jit(solution)/shard_map/ppermute | solution.py:448
  55.1 5.7 %collective-permute-start.24 = (s16[1296,256]{1,0:T(8,128)(2,1)S(1)}, s16[1296,256]{1,0:T(8,128)(2,1)S(1)}, u32[]{:S(2)}, u32[]{:S(2)}) collective-permute-start(s16[1296,256]{1,0:T(8,128)(2,1)S(1)} %get-tuple-element.116), channel_id=1, source_target_pairs={{0,2},{4,6},{9,11},{13,15},{18,16},{22,20},{27,25},{31,29}} | collective-permute-start | bytes 1990664 | tf_op jit(solution)/shard_map/ppermute | solution.py:448
  60.9 42.4 %collective-permute-start.19 = (s16[2592,256]{1,0:T(8,128)(2,1)S(1)}, s16[2592,256]{1,0:T(8,128)(2,1)S(1)}, u32[]{:S(2)}, u32[]{:S(2)}) collective-permute-start(s16[2592,256]{1,0:T(8,128)(2,1)S(1)} %get-tuple-element.113), channel_id=1, source_target_pairs={{2,0},{3,1},{6,4},{7,5},{10,8},{11,9},{14,12},{15,13},{16,18},{17,... | collective-permute-start | bytes 3981320 | tf_op jit(solution)/shard_map/ppermute | solution.py:448
  73.9 5.8 %copy-start = (bf16[5648,128]{1,0:T(8,128)(2,1)}, bf16[5648,128]{1,0:T(8,128)(2,1)S(1)}, u32[]{:S(2)}) copy-start(bf16[5648,128]{1,0:T(8,128)(2,1)S(1)} %collective-permute-done.20.one_ref.refs_7_) | copy-start | bytes 4337668
  73.9 24.2 %copy-start.8 = (bf16[5648,128]{1,0:T(8,128)(2,1)}, bf16[5648,128]{1,0:T(8,128)(2,1)S(1)}, u32[]{:S(2)}) copy-start(bf16[5648,128]{1,0:T(8,128)(2,1)S(1)} %collective-permute-done.21.refs_3_) | copy-start | bytes 4337668
  73.9 5.8 %copy-start.12 = (bf16[5648,128]{1,0:T(8,128)(2,1)}, bf16[5648,128]{1,0:T(8,128)(2,1)S(1)}, u32[]{:S(2)}) copy-start(bf16[5648,128]{1,0:T(8,128)(2,1)S(1)} %collective-permute-done.22.refs_5_) | copy-start | bytes 4337668
  73.9 5.7 %copy-start.1 = (bf16[5648,128]{1,0:T(8,128)(2,1)}, bf16[5648,128]{1,0:T(8,128)(2,1)S(1)}, u32[]{:S(2)}) copy-start(bf16[5648,128]{1,0:T(8,128)(2,1)S(1)} %collective-permute-done.23.two_ref.refs_4_) | copy-start | bytes 4337668
  74.5 23.5 %collective-permute-start.26 = (bf16[2832,128]{1,0:T(8,128)(2,1)S(1)}, bf16[2832,128]{1,0:T(8,128)(2,1)S(1)}, u32[]{:S(2)}, u32[]{:S(2)}) collective-permute-start(bf16[2832,128]{1,0:T(8,128)(2,1)S(1)} %get-tuple-element.121), channel_id=1, source_target_pairs={{9,1},{11,3},{13,5},{15,7},{16,24},{18,26},{20,28},{22,30}} | collective-permute-start | bytes 2174984 | tf_op jit(solution)/shard_map/ppermute | solution.py:448
  75.8 13.2 %collective-permute-start.25 = (bf16[2816,128]{1,0:T(8,128)(2,1)S(1)}, bf16[2816,128]{1,0:T(8,128)(2,1)S(1)}, u32[]{:S(2)}, u32[]{:S(2)}) collective-permute-start(bf16[2816,128]{1,0:T(8,128)(2,1)S(1)} %get-tuple-element.120), channel_id=1, source_target_pairs={{1,5},{3,7},{5,1},{7,3},{24,28},{26,30},{28,24},{30,26}} | collective-permute-start | bytes 2162696 | tf_op jit(solution)/shard_map/ppermute | solution.py:448
  84.2 22.0 %collective-permute-start.30 = (s16[1296,256]{1,0:T(8,128)(2,1)S(1)}, s16[1296,256]{1,0:T(8,128)(2,1)S(1)}, u32[]{:S(2)}, u32[]{:S(2)}) collective-permute-start(s16[1296,256]{1,0:T(8,128)(2,1)S(1)} %get-tuple-element.138), channel_id=1, source_target_pairs={{0,2},{1,3},{4,6},{5,7},{8,10},{9,11},{12,14},{13,15},{18,16},{19,... | collective-permute-start | bytes 1990664 | tf_op jit(solution)/shard_map/ppermute | solution.py:448
  101.8 14.1 %copy-start.6 = (bf16[2048,256]{1,0:T(8,128)(2,1)S(1)}, bf16[2048,256]{1,0:T(8,128)(2,1)}, u32[]{:S(2)}) copy-start(bf16[2048,256]{1,0:T(8,128)(2,1)} %refs_2_.1) | copy-start | bytes 3145732
  101.8 14.1 %copy-start.15 = (s32[8,16]{1,0:T(8,128)S(1)}, s32[8,16]{1,0:T(8,128)}, u32[]{:S(2)}) copy-start(s32[8,16]{1,0:T(8,128)} %mask_ref.1) | copy-start | bytes 1540
  101.8 14.1 %copy-start.16 = (s32[16,2]{0,1:T(2,128)S(1)}, s32[16,2]{0,1:T(2,128)}, u32[]{:S(2)}) copy-start(s32[16,2]{0,1:T(2,128)} %param.9) | copy-start | bytes 388
  101.8 14.1 %collective-permute-start.31 = (s16[1296,256]{1,0:T(8,128)(2,1)S(1)}, s16[1296,256]{1,0:T(8,128)(2,1)S(1)}, u32[]{:S(2)}, u32[]{:S(2)}) collective-permute-start(s16[1296,256]{1,0:T(8,128)(2,1)S(1)} %get-tuple-element.150), channel_id=1, source_target_pairs={{1,3},{5,7},{8,10},{12,14},{19,17},{23,21},{26,24},{30,28}} | collective-permute-start | bytes 1990664 | tf_op jit(solution)/shard_map/ppermute | solution.py:448
  103.3 5.6 %collective-permute-start.27 = (f32[8,128]{1,0:T(8,128)S(1)}, f32[8,128]{1,0:T(8,128)S(1)}, u32[]{:S(2)}, u32[]{:S(2)}) collective-permute-start(f32[8,128]{1,0:T(8,128)S(1)} %get-tuple-element.140), channel_id=1, source_target_pairs={{0,1},{1,0},{2,3},{3,2},{4,5},{5,4},{6,7},{7,6},{8,9},{9,8},{10,11... | collective-permute-start | bytes 12296 | tf_op jit(solution)/shard_map/ppermute | solution.py:502
  103.3 11.3 %collective-permute-start.28 = (f32[8,128]{1,0:T(8,128)S(1)}, f32[8,128]{1,0:T(8,128)S(1)}, u32[]{:S(2)}, u32[]{:S(2)}) collective-permute-start(f32[8,128]{1,0:T(8,128)S(1)} %get-tuple-element.140), channel_id=1, source_target_pairs={{0,2},{2,0},{1,3},{3,1},{4,6},{6,4},{5,7},{7,5},{8,10},{10,8},{9,1... | collective-permute-start | bytes 12296 | tf_op jit(solution)/shard_map/ppermute | solution.py:502
  106.1 8.5 %collective-permute-start.29 = (f32[8,128]{1,0:T(8,128)S(1)}, f32[8,128]{1,0:T(8,128)S(1)}, u32[]{:S(2)}, u32[]{:S(2)}) collective-permute-start(f32[8,128]{1,0:T(8,128)S(1)} %get-tuple-element.140), channel_id=1, source_target_pairs={{0,3},{3,0},{1,2},{2,1},{4,7},{7,4},{5,6},{6,5},{8,11},{11,8},{9,1... | collective-permute-start | bytes 12296 | tf_op jit(solution)/shard_map/ppermute | solution.py:502

commit v6 on v5

--- a/solution.py
+++ b/solution.py
@@ -106,33 +106,38 @@
     )(swap, *masks, *shards)
 
 
-def mask_tiles(amplitudes, mask):
-    rows, cols = amplitudes.shape
-
-    def kernel(mask_ref, a_any, out_ref, token_ref, sem):
+def mask_tiles(amplitudes, masks):
+    rows, cols = amplitudes[0].shape
+    count = len(amplitudes)
+
+    def kernel(*refs):
+        mask_refs, a_refs, out_refs, token_ref, sem = (
+            refs[:count], refs[count:2 * count], refs[2 * count:3 * count], *refs[3 * count:])
         token_ref[...] = jnp.zeros_like(token_ref)
         copies = [
-            pltpu.make_async_copy(a_any.at[pl.ds(at, TILE)], out_ref.at[pl.ds(at, TILE)], sem.at[at // TILE])
-            for at in range(0, rows, TILE)]
-        for copy in copies:
+            [pltpu.make_async_copy(a_refs[s].at[pl.ds(at, TILE)], out_refs[s].at[pl.ds(at, TILE)], sem.at[s, at // TILE])
+             for at in range(0, rows, TILE)] for s in range(count)]
+        for copy in sum(copies, []):
             copy.start()
-        for r in range(rows // TILE):
-            copies[r].wait()
-            for t in range(cols // TILE):
-                @pl.when(mask_ref[r, t] == 0)
-                def _(r=r, t=t):
-                    out_ref[r * TILE:(r + 1) * TILE, t * TILE:(t + 1) * TILE] = jnp.zeros((TILE, TILE), out_ref.dtype)
+        for s in range(count):
+            for r in range(rows // TILE):
+                copies[s][r].wait()
+                for t in range(cols // TILE):
+                    @pl.when(mask_refs[s][r, t] == 0)
+                    def _(s=s, r=r, t=t):
+                        out_refs[s][r * TILE:(r + 1) * TILE, t * TILE:(t + 1) * TILE] = jnp.zeros(
+                            (TILE, TILE), out_refs[s].dtype)
 
     return call(
         kernel, "mask_tiles",
-        out_shape=(jax.ShapeDtypeStruct(amplitudes.shape, amplitudes.dtype), TOKEN),
-        in_specs=[SMEM, ANY],
-        out_specs=(VMEM, VMEM),
-        scratch_shapes=[pltpu.SemaphoreType.DMA((rows // TILE,))],
-    )(mask, amplitudes)
-
-
-def shard_product(amps, picks, step, choices, tokens, before=None, held=in_hbm):
+        out_shape=tuple(jax.ShapeDtypeStruct(part.shape, part.dtype) for part in amplitudes) + (TOKEN,),
+        in_specs=[SMEM] * count + [ANY] * count,
+        out_specs=(VMEM,) * (count + 1),
+        scratch_shapes=[pltpu.SemaphoreType.DMA((count, rows // TILE))],
+    )(*masks, *amplitudes)
+
+
+def shard_product(amps, picks, step, choices, tokens, before=None, split=False, held=in_hbm):
     rows, depth = amps[0].shape
     count = len(amps)
     height = sum(part.shape[0] for part in choices[0])
@@ -141,6 +146,7 @@
     tiles = count * wide * depth // TILE
     word = 16
     first_row = 0 if before is None else before.shape[0]
+    half_rows = coded_rows(rows // 2)
     parts = []
     for choice in choices:
         for part in choice:
@@ -153,7 +159,7 @@
         token_refs, refs = refs[:len(tokens)], refs[len(tokens):]
         a_refs, refs = refs[:count], refs[count:]
         p_any, refs = refs[:len(parts)], refs[len(parts):]
-        out_ref, coded_ref, token_ref, packed, wide_ref, sem = refs
+        out_ref, *coded_refs, token_ref, packed, wide_ref, sem = refs
         pick = picks_ref[step]
         token_ref[...] = sum(ref[...] for ref in token_refs)
         for number, choice in enumerate(choices):
@@ -202,17 +208,20 @@
         @pl.when((pick >= 0) & (picks_ref[STEPS + step] != 0))
         def _():
             if first_row:
-                coded_ref[:first_row, :] = before_ref[...]
-            encode(out_ref, coded_ref, first_row)
+                coded_refs[0][:first_row, :] = before_ref[...]
+            for h, (first, length, at) in enumerate(halves(rows, first_row)):
+                spot = coded_refs[h] if split else coded_refs[0].at[pl.ds(at, coded_rows(length))]
+                encode(out_ref.at[pl.ds(first, length)], spot)
 
     return call(
         kernel, "shard_product",
         out_shape=(
             jax.ShapeDtypeStruct((rows, wide * TILE), jnp.float32),
-            jax.ShapeDtypeStruct((first_row + coded_rows(rows), wide * TILE), jnp.int16),
+            *([jax.ShapeDtypeStruct((half_rows, wide * TILE), jnp.int16)] * 2 if split else
+              [jax.ShapeDtypeStruct((first_row + 2 * half_rows, wide * TILE), jnp.int16)]),
             TOKEN),
         in_specs=[SMEM] + [VMEM] * (bool(first_row) + len(tokens) + count) + [ANY] * len(parts),
-        out_specs=(VMEM, VMEM, VMEM),
+        out_specs=(VMEM,) * (4 if split else 3),
         scratch_shapes=[
             pltpu.VMEM((height, TILE), amps[0].dtype),
             pltpu.VMEM((count * depth, wide * TILE), amps[0].dtype),
@@ -223,6 +232,11 @@
 
 def coded_rows(rows):
     return rows + rows // (16 // LOW) + META
+
+
+def halves(rows, first_row=0):
+    half = rows // 2
+    return [(h * half, half, first_row + h * coded_rows(half)) for h in range(2)]
 
 
 def step_factors(exponent):
@@ -236,7 +250,7 @@
     return factors
 
 
-def encode(sums_ref, coded_ref, first_row):
+def encode(sums_ref, coded_ref):
     rows, cols = sums_ref.shape
     groups = rows // GROUP
     largest = jnp.concatenate([
@@ -257,112 +271,125 @@
             g = at // GROUP
             value = sums_ref[at:at + GROUP, :] * one[g:g + 1] * two[g:g + 1]
             value = jnp.minimum(jnp.round(value).astype(jnp.int32), (1 << (BITS - 1)) - 1)
-            coded_ref[first_row + at:first_row + at + GROUP, :] = (value >> LOW).astype(jnp.int16)
+            coded_ref[at:at + GROUP, :] = (value >> LOW).astype(jnp.int16)
             low = low | ((value & ((1 << LOW) - 1)) << (LOW * part))
-        low_at = first_row + rows + start
-        coded_ref[low_at:low_at + GROUP, :] = (low - 32768).astype(jnp.int16)
-    coded_ref[first_row + rows + block:, :] = jnp.concatenate([exponent] * (META // groups)).astype(jnp.int16)
-
-
-def decode(coded_ref, rows, put, first_row=0):
+        coded_ref[rows + start:rows + start + GROUP, :] = (low - 32768).astype(jnp.int16)
+    coded_ref[rows + block:, :] = jnp.concatenate([exponent] * (META // groups)).astype(jnp.int16)
+
+
+def decode(coded_ref, rows, put):
     groups = rows // GROUP
     share = 16 // LOW
     block = rows // share
-    exponent_at = first_row + rows + block
-    one, two = step_factors(coded_ref[exponent_at:exponent_at + META, :].astype(jnp.int32)[:groups])
+    one, two = step_factors(coded_ref[rows + block:, :].astype(jnp.int32)[:groups])
     one, two = 1.0 / one, 1.0 / two
     for start in range(0, block, GROUP):
-        low_at = first_row + rows + start
-        low = coded_ref[low_at:low_at + GROUP, :].astype(jnp.int32) + 32768
+        low = coded_ref[rows + start:rows + start + GROUP, :].astype(jnp.int32) + 32768
         for part in range(share):
             at = part * block + start
             g = at // GROUP
-            high = coded_ref[first_row + at:first_row + at + GROUP, :].astype(jnp.int32)
+            high = coded_ref[at:at + GROUP, :].astype(jnp.int32)
             value = (high << LOW) | ((low >> (LOW * part)) & ((1 << LOW) - 1))
             put(at, value.astype(jnp.float32) * one[g:g + 1] * two[g:g + 1])
 
 
-def add_coded(sums, coded):
-    rows = sums[0].shape[0]
+def add_coded(sums, coded, tokens=()):
     count = len(sums)
+    arrays = []
+    for array, _ in [pair for one in coded for pair in one]:
+        if not any(array is known for known in arrays):
+            arrays.append(array)
 
     def kernel(*refs):
-        sums_refs, coded_ref, out_refs, token_ref = refs[:count], refs[count], refs[count + 1:-1], refs[-1]
-        token_ref[...] = jnp.zeros_like(token_ref)
+        token_refs, refs = refs[:len(tokens)], refs[len(tokens):]
+        sums_refs, coded_refs, out_refs, token_ref = refs[:count], refs[count:-count - 1], refs[-count - 1:-1], refs[-1]
+        token_ref[...] = sum((ref[...] for ref in token_refs), jnp.zeros(token_ref.shape, token_ref.dtype))
         for number in range(count):
-            def put(at, far, number=number):
-                out_refs[number][at:at + GROUP, :] = (
-                    sums_refs[number][at:at + GROUP, :] + far).astype(jnp.bfloat16)
-
-            decode(coded_ref, rows, put, number * coded_rows(rows))
+            for (first, length, _), (array, at) in zip(halves(sums[number].shape[0]), coded[number]):
+                ref = coded_refs[[array is known for known in arrays].index(True)]
+                add_half(sums_refs[number], ref.at[pl.ds(at, coded_rows(length))], out_refs[number], first, length)
 
     return call(
         kernel, "add_coded",
         out_shape=tuple(jax.ShapeDtypeStruct(part.shape, jnp.bfloat16) for part in sums) + (TOKEN,),
-        in_specs=[VMEM] * (count + 1),
+        in_specs=[VMEM] * (len(tokens) + count + len(arrays)),
         out_specs=(VMEM,) * (count + 1),
-    )(*sums, coded)
+    )(*tokens, *sums, *arrays)
+
+
+def add_half(sums_ref, coded_ref, out_ref, first, length):
+    def put(at, far):
+        spot = pl.ds(first + at, GROUP)
+        out_ref[spot, :] = (sums_ref[spot, :] + far).astype(out_ref.dtype)
+
+    decode(coded_ref, length, put)
+
+
+def both_halves(sums, coded, first_row=0):
+    return [(coded, at) for _, _, at in halves(sums.shape[0], first_row)]
 
 
 def lay_out(place, mine, rest):
-    rows, width = mine[0].shape
+    choices = [(one if isinstance(one, tuple) else (one,), two if isinstance(two, tuple) else (two,))
+               for one, two in zip(mine, rest)]
     arrays = []
-    for choice in jax.tree.leaves((mine, rest)):
-        if not any(choice is array for array in arrays):
-            arrays.append(choice)
-
-    def index(array):
-        return [array is known for known in arrays].index(True)
+    for array in jax.tree.leaves(choices):
+        if not any(array is known for known in arrays):
+            arrays.append(array)
+    rows, width = arrays[0].shape
 
     def kernel(place_ref, *refs):
-        ins, out_any, out_ref, sem = refs[:len(arrays)], *refs[len(arrays):]
-        for x in range(2):
-            own, other = slice(x * width, (x + 1) * width), slice((1 - x) * width, (2 - x) * width)
-            for number in range(len(mine)):
-                @pl.when((place_ref[0] == number) & (place_ref[1] == x))
-                def _(own=own, other=other, number=number):
-                    out_ref[:, own] = ins[index(mine[number])][...]
-                    if isinstance(rest[number], tuple):
-                        sums_ref, coded_ref = [ins[index(array)] for array in rest[number]]
-
-                        def put(at, far):
-                            out_ref[at:at + GROUP, other] = (sums_ref[at:at + GROUP, :] + far).astype(out_ref.dtype)
-
-                        decode(coded_ref, rows, put)
-                    else:
-                        out_ref[:, other] = ins[index(rest[number])][...]
-        copy = pltpu.make_async_copy(out_ref, out_any, sem)
-        copy.start()
-        copy.wait()
+        ins = refs[:len(arrays)]
+        out_any, round_ref, sums_ref, coded_ref, sems = refs[len(arrays):]
+        parts_of = halves(rows)
+
+        def store(side, first, length):
+            at = pl.multiple_of((place_ref[1] ^ side) * width, width)
+            return pltpu.make_async_copy(
+                round_ref.at[side, pl.ds(first, length)], out_any.at[pl.ds(first, length), pl.ds(at, width)],
+                sems.at[2, 2 * side + first // length])
+
+        for number, choice in enumerate(choices):
+            @pl.when(place_ref[0] == number)
+            def _(choice=choice):
+                fetch = {}
+                for side, parts in enumerate(choice):
+                    refs_in = [ins[[part is array for array in arrays].index(True)] for part in parts]
+                    for h, (first, length, at) in enumerate(parts_of):
+                        wanted = [(refs_in[0], first, length, (round_ref if len(parts) == 1 else sums_ref).at[side])]
+                        if len(parts) == 2:
+                            wanted.append((refs_in[1], at, coded_rows(length), coded_ref.at[side]))
+                        fetch[side, h] = [
+                            pltpu.make_async_copy(
+                                source.at[pl.ds(start, size)], target.at[pl.ds(start, size)], sems.at[n, 2 * side + h])
+                            for n, (source, start, size, target) in enumerate(wanted)]
+                for copy in sum(fetch.values(), []):
+                    copy.start()
+                for side, parts in enumerate(choice):
+                    for h, (first, length, at) in enumerate(parts_of):
+                        for copy in fetch[side, h]:
+                            copy.wait()
+                        if len(parts) == 2:
+                            add_half(
+                                sums_ref.at[side], coded_ref.at[side, pl.ds(at, coded_rows(length))],
+                                round_ref.at[side], first, length)
+                        store(side, first, length).start()
+
+        for side in range(2):
+            for first, length, _ in parts_of:
+                store(side, first, length).wait()
 
     return call(
         kernel, "lay_out",
         out_shape=pltpu.HBM((rows, 2 * width), jnp.bfloat16),
-        in_specs=[SMEM] + [VMEM] * len(arrays),
+        in_specs=[SMEM] + [ANY] * len(arrays),
         out_specs=ANY,
-        scratch_shapes=[pltpu.VMEM((rows, 2 * width), jnp.bfloat16), pltpu.SemaphoreType.DMA],
+        scratch_shapes=[
+            pltpu.VMEM((2, rows, width), jnp.bfloat16),
+            pltpu.VMEM((2, rows, width), jnp.float32),
+            pltpu.VMEM((2, 2 * coded_rows(rows // 2), width), jnp.int16),
+            pltpu.SemaphoreType.DMA((3, 4))],
     )(place, *arrays)
-
-
-def top_and_rest(one, two, at):
-    def kernel(one_ref, two_ref, top_ref, rest_ref, sem):
-        copies = [
-            pltpu.make_async_copy(one_ref.at[pl.ds(0, at)], top_ref, sem.at[0]),
-            pltpu.make_async_copy(two_ref.at[pl.ds(at, two.shape[0] - at)], rest_ref, sem.at[1])]
-        for copy in copies:
-            copy.start()
-        for copy in copies:
-            copy.wait()
-
-    return call(
-        kernel, "top_and_rest",
-        out_shape=(
-            jax.ShapeDtypeStruct((at, one.shape[1]), one.dtype),
-            jax.ShapeDtypeStruct((two.shape[0] - at, two.shape[1]), two.dtype)),
-        in_specs=[ANY, ANY],
-        out_specs=(VMEM, VMEM),
-        scratch_shapes=[pltpu.SemaphoreType.DMA((2,))],
-    )(one, two)
 
 
 Z, X, Y = 4, 2, 2
@@ -418,26 +445,24 @@
     return 0, 1
 
 
-def home_core(z):
-    return (z % 2,)
-
-
-def other_core(z):
-    return (1 - z % 2,)
+def early_cores(z):
+    return (0, 1) if z in (1, 2) else (z % 2,)
+
+
+def late_cores(z):
+    return () if z in (1, 2) else (1 - z % 2,)
 
 
 OWN_TO_PAIR = [
     (device(z, x, y, 1 - z % 2), device(z ^ 1, x, y, z % 2)) for z in range(Z) for x in range(X) for y in range(Y)]
 CORES = [(0, 1), (1, 0), (2, 3), (3, 2)]
 CHIPS_Y = [(0, 2), (2, 0), (1, 3), (3, 1)]
-CROSSWISE = [(0, 3), (3, 0), (1, 2), (2, 1)]
 
 
 def sparse_ladder(amplitudes, integrals, amp_mask, int_mask):
     barrier = lax.optimization_barrier
     tiles = int_mask.size
     cap = 2 * tiles * 11 // 16
-    half = cap * TILE // 2
     row, col = lax.axis_index("row"), lax.axis_index("col")
     z, x = row // X, row % X
     y, c = col // 2, col % 2
@@ -453,57 +478,57 @@
     near = z // 2 == y
     picks = jnp.stack([
         jnp.where(home, 0, 1),
-        jnp.where(home, is_end, -1),
+        jnp.where(home, is_end, jnp.where(is_end, -1, 2)),
         jnp.where(home, 0, 1),
         jnp.where(home, is_end, 2 + is_end),
-        jnp.where(home, -1, is_end),
+        jnp.where(home, -1, is_end - 1),
     ] + [jnp.where(near, s, 1 - s) for s in (0, 1, 0, 1, 1)]).astype(jnp.int32)
 
-    place = jnp.stack([jnp.where(near, 0, jnp.where(home, 1, 2)), x]).astype(jnp.int32)
+    place = jnp.stack([jnp.where(near, 0, jnp.where(home | (is_end == 0), 1, 2)), x]).astype(jnp.int32)
 
     other = lax.ppermute(integrals, "col", CORES)
     other_mask = lax.ppermute(int_mask.T, "col", CORES)
+    other_amp_mask = lax.ppermute(amp_mask, "col", CORES)
     swap = jnp.where(home, 0, 1).astype(jnp.int32).reshape(1)
     own = pack_tiles((integrals, other), (int_mask.T, other_mask), swap, cap)
-    own, picks, place, amplitudes_now = barrier((own, picks, place, amplitudes))
-
-    masked, masked_token = mask_tiles(amplitudes_now, amp_mask)
-    amps = (masked, lax.ppermute(masked, "col", CORES))
+    own, picks, place, other_amp_mask, amplitudes_now = barrier((own, picks, place, other_amp_mask, amplitudes))
+    other_amps = lax.ppermute(amplitudes_now, "col", CORES)
+
+    *amps, masked_token = mask_tiles((amplitudes, other_amps), (amp_mask, other_amp_mask))
     one, centre, own_x, tokens = after(masked_token)(
         move(own, OWN_TO_PAIR), move(own, moves(over_centre)), move(own, moves(across_x)))
 
-    a_sum, a_coded, token = shard_product(amps, picks, 0, [[own], [one]], tokens)
-    two_end, two_mid, one_x, own_x, tokens = after(token)(
+    a_sum, a_coded, a_rest, token = shard_product(amps, picks, 0, [[own], [one]], tokens, split=True)
+    a_far = move(a_coded, to_y(False, both))
+    two_end, two_mid, one_x, own_x, a_far, tokens = after(token)(
         move(centre, moves(outward, False)), move(one, moves(over_centre, False)), move(one, moves(across_x, False)),
-        own_x)
-
-    c_sum, c_coded, token = shard_product(amps, picks, 1, [[two_mid], [two_end]], tokens)
-    c_far = move(c_coded, to_y(True, home_core))
-    b_sum, ab_coded, token = shard_product(amps, picks, 2, [[own_x], [one_x]], (token,), a_coded)
-    c_both, c_token = add_coded((c_sum,), c_far)
-    three_end, three_mid_x, two_x_end, two_x_mid, tokens = after(token, c_token)(
+        own_x, a_far)
+
+    c_sum, c_coded, token = shard_product(amps, picks, 1, [[two_mid], [two_end], [centre]], tokens)
+    c_far = move(c_coded, to_y(True, early_cores))
+    b_sum, ab_coded, token = shard_product(amps, picks, 2, [[own_x], [one_x]], (token,), a_rest)
+    three_end, three_mid_x, two_x_end, two_x_mid, c_far, tokens = after(token)(
         move(two_mid, moves(outward)), move(own_x, moves(over_centre)),
-        move(two_end, moves(across_x_ends)), move(two_mid, moves(across_x_middle)))
+        move(two_end, moves(across_x_ends)), move(two_mid, moves(across_x_middle)), c_far)
 
     d_sum, d_coded, token = shard_product(
-        amps, picks, 3, [[two_x_mid], [two_x_end], [centre], [three_end]], tokens)
+        amps, picks, 3, [[two_x_mid], [two_x_end], [three_mid_x], [three_end]], tokens)
     ab_far = move(ab_coded, to_y(False, both))
-    top, rest = top_and_rest(three_end, two_x_mid, half)
-    three_x, three_x_rest, tokens = after(token)(
-        move(top, moves(across_x_ends, False)), move(rest, moves(outward)))
+    three_x, tokens = after(token)(move(three_end, moves(across_x_ends, False)))
 
     d_far = move(d_coded, to_y(True, both))
-    e_sum, e_coded, token = shard_product(amps, picks, 4, [[three_mid_x], [three_x, three_x_rest]], tokens,
-        held=lambda part: in_hbm(part) if part is three_mid_x else part)
-    e_far = move(e_coded, to_y(True, other_core))
-    ab_far, token = barrier((ab_far, token))
-    a_both, b_both, _ = add_coded((a_sum, b_sum), ab_far)
-    d_both, _ = add_coded((d_sum,), d_far)
-    flags = [token] + [lax.ppermute(token, "col", pairs) for pairs in (CORES, CHIPS_Y, CROSSWISE)]
-    flags, a_both, b_both, d_both = barrier((flags, a_both, b_both, d_both))
+    e_sum, e_coded, token = shard_product(amps, picks, 4, [[three_x]], tokens, held=lambda part: part)
+    e_far = move(e_coded, to_y(True, late_cores))
+    c_far, _ = barrier((c_far, token))
+    ab_far, a_far, _ = barrier((ab_far, a_far, token))
+    c_both, token = add_coded((c_sum,), [both_halves(c_sum, c_far)], (token, lax.ppermute(token, "col", CORES)))
+    a_both, b_both, _ = add_coded(
+        (a_sum, b_sum), ([(a_far, 0), (ab_far, 0)], both_halves(b_sum, ab_far, a_rest.shape[0])))
+    flags = [token, lax.ppermute(token, "col", CHIPS_Y)]
+    flags, a_both, b_both, c_both, d_far = barrier((flags, a_both, b_both, c_both, d_far))
 
     def finish():
-        return lay_out(place, (a_both, c_both, d_both), (b_both, d_both, (e_sum, e_far)))
+        return lay_out(place, (a_both, c_both, (d_sum, d_far)), (b_both, (d_sum, d_far), (e_sum, e_far)))
 
     return lax.cond(
         jnp.max(sum(flags)) > 0, lambda: dense_ladder(amplitudes, integrals, amp_mask, int_mask), finish)

time: 120 us -> 117 us (0.975)
  the two profiles are of different devices: /device:TPU:24 before, /device:TPU:11 now
where the time goes in v6:
time: 117 us; the launch traced here: 116 us
  waiting for transfers between devices  48.2 us (41%)
  starting transfers between devices  33.1 us (28%)
  Pallas kernels  32.4 us (28%)
  between operations  1.26 us (1%)
    ppermute x16, waiting for transfers between devices, move(): return lax.ppermute(value, AXES, pairs)  45.3 us
    ppermute x16, starting transfers between devices, move(): return lax.ppermute(value, AXES, pairs)  31.4 us
    pallas_call x5, Pallas kernels, shard_product(): call(kernel, 'shard_product', out_shape=(jax.ShapeDtypeStruct((rows, wide...  21 us
    pallas_call x1, Pallas kernels, mask_tiles(): call(kernel, 'mask_tiles', out_shape=tuple((jax.ShapeDtypeStruct(part.sha...  4.16 us
    pallas_call x2, Pallas kernels, add_coded(): call(kernel, 'add_coded', out_shape=tuple((jax.ShapeDtypeStruct(part.shap...  2.8 us
    pallas_call x1, Pallas kernels, lay_out(): call(kernel, 'lay_out', out_shape=pltpu.HBM((rows, 2 * width), jnp.bfloat...  2.56 us
  transfers between devices with their start and end apart: 22, of which 8 were waited for; matrix products, arithmetic and copies ran while one was open for 1% of the time, Pallas kernels for 26%

profile of v6, /device:TPU:11, one launch (start us, length us, event | category | flops | bytes accessed | tf_op | source)
XLA Modules:
  0.0 116.4 jit_solution(11569474110829162720)
XLA Ops:
  0.0 0.7 collective-permute-start.11
  0.7 0.0 collective-permute-start.10
  0.7 0.5 collective-permute-start.12
  1.2 0.1 pad_add_fusion
  1.3 0.1 stack.37.picks_ref
  1.3 1.8 %collective-permute-done.10.refs_1_ = s32[2,16]{1,0:T(2,128)S(1)} collective-permute-done((s32[2,16]{1,0:T(2,128)}, s32[2,16]{1,0:T(2,128)S(1)}, u32[]{:S(2)}, u32[]{:S(2)}) %collective-permute-start.10) | collective-permute-done | bytes 160 | tf_op jit(solution)/shard_map/ppermute | solution.py:490
  3.2 0.0 collective-permute-done.11.refs_3_
  3.2 1.9 %pack_tiles.1.refs_3_ = bf16[5648,128]{1,0:T(8,128)(2,1)S(1)} custom-call(s32[1]{0:T(128)} %bitcast.2.swap_ref, s32[2,16]{1,0:T(2,128)} %bitcast.38, s32[2,16]{1,0:T(2,128)S(1)} %collective-permute-done.10.refs_1_, bf16[2048,256]{1,0:T(8,128)(2,1)} %refs_2_.2, bf16[2048,256]{1,0:T(8,128)(2,1)S(1)} %collective-permute-done.11.refs_3_), custom_call_target="tpu_custom_call" | custom-call | flops 1 | bytes 1 | tf_op jit(solution)/shard_map/pack_tiles/pallas_call | solution.py:101
  5.1 0.0 copy-start
  5.1 0.0 collective-permute-done.12.refs_1_
  5.1 0.4 collective-permute-start.16
  5.6 0.7 collective-permute-start.13
  6.3 5.8 %collective-permute-start.14 = (bf16[5648,128]{1,0:T(8,128)(2,1)S(1)}, bf16[5648,128]{1,0:T(8,128)(2,1)S(1)}, u32[]{:S(2)}, u32[]{:S(2)}) collective-permute-start(bf16[5648,128]{1,0:T(8,128)(2,1)S(1)} %pack_tiles.1.refs_3_), channel_id=1, source_target_pairs={{9,17},{11,19},{13,21},{15,23},{16,8},{18,10},{20,12},{22,14}} | collective-permute-start | bytes 4337672 | tf_op jit(solution)/shard_map/ppermute | solution.py:473
  12.1 2.2 %collective-permute-start.15 = (bf16[5648,128]{1,0:T(8,128)(2,1)S(1)}, bf16[5648,128]{1,0:T(8,128)(2,1)S(1)}, u32[]{:S(2)}, u32[]{:S(2)}) collective-permute-start(bf16[5648,128]{1,0:T(8,128)(2,1)S(1)} %pack_tiles.1.refs_3_), channel_id=1, source_target_pairs={{0,4},{2,6},{4,0},{6,2},{9,13},{11,15},{13,9},{15,11},{16,20},{18,... | collective-permute-start | bytes 4337672 | tf_op jit(solution)/shard_map/ppermute | solution.py:473
  14.2 0.0 collective-permute-done.16.refs_3_
  14.3 4.2 %mask_tiles.1 = (bf16[1024,2048]{1,0:T(8,128)(2,1)S(1)}, bf16[1024,2048]{1,0:T(8,128)(2,1)S(1)}, f32[8,128]{1,0:T(8,128)S(1)}) custom-call(s32[8,16]{1,0:T(8,128)} %refs_0_.1, s32[8,16]{1,0:T(8,128)S(1)} %collective-permute-done.12.refs_1_, bf16[1024,2048]{1,0:T(8,128)(2,1)} %refs_2_.3, bf16[1024,2048]{1,0:T(8,128)(2,1)S(1)} %collective-permute-done.16.refs_3_), custom_call_target="tpu_custom_call" | custom-call | flops 1 | bytes 1 | tf_op jit(solution)/shard_map/mask_tiles/pallas_call | solution.py:131
  18.4 0.0 copy-done
  18.4 0.0 collective-permute-done.13.refs_4_
  18.5 9.5 %collective-permute-done.14.refs_5_ = bf16[5648,128]{1,0:T(8,128)(2,1)S(1)} collective-permute-done((bf16[5648,128]{1,0:T(8,128)(2,1)S(1)}, bf16[5648,128]{1,0:T(8,128)(2,1)S(1)}, u32[]{:S(2)}, u32[]{:S(2)}) %collective-permute-start.14) | collective-permute-done | bytes 1445920 | tf_op jit(solution)/shard_map/ppermute | solution.py:473
  28.0 3.9 %collective-permute-done.15.refs_4_ = bf16[5648,128]{1,0:T(8,128)(2,1)S(1)} collective-permute-done((bf16[5648,128]{1,0:T(8,128)(2,1)S(1)}, bf16[5648,128]{1,0:T(8,128)(2,1)S(1)}, u32[]{:S(2)}, u32[]{:S(2)}) %collective-permute-start.15) | collective-permute-done | bytes 1445920 | tf_op jit(solution)/shard_map/ppermute | solution.py:473
  31.9 0.7 collective-permute-start.17
  32.6 1.3 %collective-permute-start.18 = (bf16[5648,128]{1,0:T(8,128)(2,1)S(1)}, bf16[5648,128]{1,0:T(8,128)(2,1)S(1)}, u32[]{:S(2)}, u32[]{:S(2)}) collective-permute-start(bf16[5648,128]{1,0:T(8,128)(2,1)S(1)} %collective-permute-done.13.refs_4_), channel_id=1, source_target_pairs={{8,16},{10,18},{12,20},{14,22},{17,9},{19,11},{21,13},{23,15}} | collective-permute-start | bytes 4337672 | tf_op jit(solution)/shard_map/ppermute | solution.py:473
  33.9 0.8 collective-permute-start.19
  34.7 4.6 %shard_product.5 = (f32[1024,256]{1,0:T(8,128)S(1)}, s16[656,256]{1,0:T(8,128)(2,1)S(1)}, s16[656,256]{1,0:T(8,128)(2,1)S(1)}, f32[8,128]{1,0:T(8,128)S(1)}) custom-call(s32[10]{0:T(128)S(1)} %stack.37.picks_ref, f32[8,128]{1,0:T(8,128)S(1)} %get-tuple-element.107.refs_0_, bf16[1024,2048]{1,0:T(8,128)(2,1)S(1)} %get-tuple-element.108.refs_1_.refs_2_, ...), custom_call_target="tpu_custom_call" | custom-call | flops 1 | bytes 1 | tf_op jit(solution)/shard_map/shard_product/pallas_call | solution.py:216
  39.3 1.3 %collective-permute-start.20 = (s16[656,256]{1,0:T(8,128)(2,1)S(1)}, s16[656,256]{1,0:T(8,128)(2,1)S(1)}, u32[]{:S(2)}, u32[]{:S(2)}) collective-permute-start(s16[656,256]{1,0:T(8,128)(2,1)S(1)} %get-tuple-element.110), channel_id=1, source_target_pairs={{2,0},{3,1},{6,4},{7,5},{10,8},{11,9},{14,12},{15,13},{16,18},{17,... | collective-permute-start | bytes 1007624 | tf_op jit(solution)/shard_map/ppermute | solution.py:473
  40.6 6.9 %collective-permute-done.20.refs_2_ = s16[656,256]{1,0:T(8,128)(2,1)S(1)} collective-permute-done((s16[656,256]{1,0:T(8,128)(2,1)S(1)}, s16[656,256]{1,0:T(8,128)(2,1)S(1)}, u32[]{:S(2)}, u32[]{:S(2)}) %collective-permute-start.20) | collective-permute-done | bytes 335904 | tf_op jit(solution)/shard_map/ppermute | solution.py:473
  47.5 0.0 collective-permute-done.17.refs_4_
  47.6 5.2 %collective-permute-done.18.refs_3_ = bf16[5648,128]{1,0:T(8,128)(2,1)S(1)} collective-permute-done((bf16[5648,128]{1,0:T(8,128)(2,1)S(1)}, bf16[5648,128]{1,0:T(8,128)(2,1)S(1)}, u32[]{:S(2)}, u32[]{:S(2)}) %collective-permute-start.18) | collective-permute-done | bytes 1445920 | tf_op jit(solution)/shard_map/ppermute | solution.py:473
  52.7 0.0 collective-permute-done.19.refs_5_
  52.7 1.4 %collective-permute-start.21 = (bf16[5648,128]{1,0:T(8,128)(2,1)S(1)}, bf16[5648,128]{1,0:T(8,128)(2,1)S(1)}, u32[]{:S(2)}, u32[]{:S(2)}) collective-permute-start(bf16[5648,128]{1,0:T(8,128)(2,1)S(1)} %collective-permute-done.18.refs_3_), channel_id=1, source_target_pairs={{9,1},{11,3},{13,5},{15,7},{16,24},{18,26},{20,28},{22,30}} | collective-permute-start | bytes 4337672 | tf_op jit(solution)/shard_map/ppermute | solution.py:473
  54.1 4.5 %collective-permute-start.22 = (bf16[5648,128]{1,0:T(8,128)(2,1)S(1)}, bf16[5648,128]{1,0:T(8,128)(2,1)S(1)}, u32[]{:S(2)}, u32[]{:S(2)}) collective-permute-start(bf16[5648,128]{1,0:T(8,128)(2,1)S(1)} %collective-permute-done.15.refs_4_), channel_id=1, source_target_pairs={{9,17},{11,19},{13,21},{15,23},{16,8},{18,10},{20,12},{22,14}} | collective-permute-start | bytes 4337672 | tf_op jit(solution)/shard_map/ppermute | solution.py:473
  58.7 0.8 collective-permute-start.23
  59.4 2.2 %collective-permute-start.24 = (bf16[5648,128]{1,0:T(8,128)(2,1)S(1)}, bf16[5648,128]{1,0:T(8,128)(2,1)S(1)}, u32[]{:S(2)}, u32[]{:S(2)}) collective-permute-start(bf16[5648,128]{1,0:T(8,128)(2,1)S(1)} %collective-permute-done.18.refs_3_), channel_id=1, source_target_pairs={{9,13},{11,15},{13,9},{15,11},{16,20},{18,22},{20,16},{22,18}} | collective-permute-start | bytes 4337672 | tf_op jit(solution)/shard_map/ppermute | solution.py:473
  61.6 5.1 %shard_product.6 = (f32[1024,256]{1,0:T(8,128)S(1)}, s16[1312,256]{1,0:T(8,128)(2,1)S(1)}, f32[8,128]{1,0:T(8,128)S(1)}) custom-call(s32[10]{0:T(128)S(1)} %stack.37.picks_ref, f32[8,128]{1,0:T(8,128)S(1)} %get-tuple-element.115.refs_0_, bf16[1024,2048]{1,0:T(8,128)(2,1)S(1)} %get-tuple-element.108.refs_1_.refs_2_, ...), custom_call_target="tpu_custom_call" | custom-call | flops 1 | bytes 1 | tf_op jit(solution)/shard_map/shard_product/pallas_call | solution.py:216
  66.7 2.7 %collective-permute-start.25 = (s16[1312,256]{1,0:T(8,128)(2,1)S(1)}, s16[1312,256]{1,0:T(8,128)(2,1)S(1)}, u32[]{:S(2)}, u32[]{:S(2)}) collective-permute-start(s16[1312,256]{1,0:T(8,128)(2,1)S(1)} %get-tuple-element.116), channel_id=1, source_target_pairs={{0,2},{4,6},{8,10},{9,11},{12,14},{13,15},{18,16},{19,17},{22,20},... | collective-permute-start | bytes 2015240 | tf_op jit(solution)/shard_map/ppermute | solution.py:473
  69.5 4.6 %shard_product.7 = (f32[1024,256]{1,0:T(8,128)S(1)}, s16[1968,256]{1,0:T(8,128)(2,1)S(1)}, f32[8,128]{1,0:T(8,128)S(1)}) custom-call(s32[10]{0:T(128)S(1)} %stack.37.picks_ref, s16[656,256]{1,0:T(8,128)(2,1)S(1)} %get-tuple-element.117.refs_0_, f32[8,128]{1,0:T(8,128)S(1)} %get-tuple-element.118.refs_1_, ...), custom_call_target="tpu_custom_call" | custom-call | flops 1 | bytes 1 | tf_op jit(solution)/shard_map/shard_product/pallas_call | solution.py:216
  74.1 9.4 %collective-permute-done.25.refs_3_ = s16[1312,256]{1,0:T(8,128)(2,1)S(1)} collective-permute-done((s16[1312,256]{1,0:T(8,128)(2,1)S(1)}, s16[1312,256]{1,0:T(8,128)(2,1)S(1)}, u32[]{:S(2)}, u32[]{:S(2)}) %collective-permute-start.25) | collective-permute-done | bytes 671776 | tf_op jit(solution)/shard_map/ppermute | solution.py:473
  83.4 0.0 collective-permute-done.21.refs_6_
  83.5 0.0 collective-permute-done.22.refs_5_
  83.5 0.0 collective-permute-done.23.refs_4_
  83.5 0.0 collective-permute-done.24.refs_3_
  83.5 0.8 collective-permute-start.26
  84.3 1.3 %collective-permute-start.29 = (s16[1968,256]{1,0:T(8,128)(2,1)S(1)}, s16[1968,256]{1,0:T(8,128)(2,1)S(1)}, u32[]{:S(2)}, u32[]{:S(2)}) collective-permute-start(s16[1968,256]{1,0:T(8,128)(2,1)S(1)} %get-tuple-element.136), channel_id=1, source_target_pairs={{2,0},{3,1},{6,4},{7,5},{10,8},{11,9},{14,12},{15,13},{16,18},{17,... | collective-permute-start | bytes 3022856 | tf_op jit(solution)/shard_map/ppermute | solution.py:473
  85.6 0.3 copy-done.14
  85.9 5.1 %shard_product.8 = (f32[1024,256]{1,0:T(8,128)S(1)}, s16[1312,256]{1,0:T(8,128)(2,1)S(1)}, f32[8,128]{1,0:T(8,128)S(1)}) custom-call(s32[10]{0:T(128)S(1)} %stack.37.picks_ref, f32[8,128]{1,0:T(8,128)S(1)} %get-tuple-element.122.refs_0_, bf16[1024,2048]{1,0:T(8,128)(2,1)S(1)} %get-tuple-element.108.refs_1_.refs_2_, ...), custom_call_target="tpu_custom_call" | custom-call | flops 1 | bytes 1 | tf_op jit(solution)/shard_map/shard_product/pallas_call | solution.py:216
  91.0 3.4 %collective-permute-start.30 = (s16[1312,256]{1,0:T(8,128)(2,1)S(1)}, s16[1312,256]{1,0:T(8,128)(2,1)S(1)}, u32[]{:S(2)}, u32[]{:S(2)}) collective-permute-start(s16[1312,256]{1,0:T(8,128)(2,1)S(1)} %get-tuple-element.143), channel_id=1, source_target_pairs={{0,2},{1,3},{4,6},{5,7},{8,10},{9,11},{12,14},{13,15},{18,16},{19,... | collective-permute-start | bytes 2015240 | tf_op jit(solution)/shard_map/ppermute | solution.py:473
  94.4 0.0 collective-permute-done.26.refs_3_
  94.4 1.6 %shard_product.9 = (f32[1024,256]{1,0:T(8,128)}, s16[1312,256]{1,0:T(8,128)(2,1)S(1)}, f32[8,128]{1,0:T(8,128)S(1)}) custom-call(s32[10]{0:T(128)S(1)} %stack.37.picks_ref, f32[8,128]{1,0:T(8,128)S(1)} %get-tuple-element.127.refs_0_, bf16[1024,2048]{1,0:T(8,128)(2,1)S(1)} %get-tuple-element.108.refs_1_.refs_2_, ...), custom_call_target="tpu_custom_call" | custom-call | flops 1 | bytes 1 | tf_op jit(solution)/shard_map/shard_product/pallas_call | solution.py:216
  96.0 0.0 copy-start.4
  96.0 0.0 copy-start.15
  96.0 0.0 copy-start.16
  96.0 1.6 %collective-permute-start.31 = (s16[1312,256]{1,0:T(8,128)(2,1)S(1)}, s16[1312,256]{1,0:T(8,128)(2,1)}, u32[]{:S(2)}, u32[]{:S(2)}) collective-permute-start(s16[1312,256]{1,0:T(8,128)(2,1)S(1)} %get-tuple-element.153), channel_id=1, source_target_pairs={{1,3},{5,7},{26,24},{30,28}} | collective-permute-start | bytes 2015240 | tf_op jit(solution)/shard_map/ppermute | solution.py:473
  97.7 0.1 collective-permute-start.27
  97.8 1.0 collective-permute-done.27.refs_1_
  98.8 1.2 %add_coded.2 = (bf16[1024,256]{1,0:T(8,128)(2,1)}, f32[8,128]{1,0:T(8,128)S(1)}) custom-call(f32[8,128]{1,0:T(8,128)S(1)} %get-tuple-element.129.refs_0_, f32[8,128]{1,0:T(8,128)S(1)} %collective-permute-done.27.refs_1_, f32[1024,256]{1,0:T(8,128)S(1)} %get-tuple-element.130.refs_2_, s16[1312,256]{1,0:T(8,128)(2,1)S(1)} %collective-permute-done.25.refs_3_), custom_call_target="tpu_custom_call" | custom-call | flops 1 | bytes 1 | tf_op jit(solution)/shard_map/add_coded/pallas_call | solution.py:312
  100.0 0.0 collective-permute-start.28
  100.0 10.4 %collective-permute-done.29.refs_3_ = s16[1968,256]{1,0:T(8,128)(2,1)S(1)} collective-permute-done((s16[1968,256]{1,0:T(8,128)(2,1)S(1)}, s16[1968,256]{1,0:T(8,128)(2,1)S(1)}, u32[]{:S(2)}, u32[]{:S(2)}) %collective-permute-start.29) | collective-permute-done | bytes 1007648 | tf_op jit(solution)/shard_map/ppermute | solution.py:473
  110.4 1.6 %add_coded.3 = (bf16[1024,256]{1,0:T(8,128)(2,1)}, bf16[1024,256]{1,0:T(8,128)(2,1)}, f32[8,128]{1,0:T(8,128)}) custom-call(f32[1024,256]{1,0:T(8,128)S(1)} %get-tuple-element.134.refs_0_, f32[1024,256]{1,0:T(8,128)S(1)} %get-tuple-element.135.refs_1_, s16[656,256]{1,0:T(8,128)(2,1)S(1)} %collective-permute-done.20.refs_2_, ...), custom_call_target="tpu_custom_call" | custom-call | flops 1 | bytes 1 | tf_op jit(solution)/shard_map/add_coded/pallas_call | solution.py:312
  112.0 0.0 collective-permute-done.30
  112.0 0.0 collective-permute-done.28
  112.0 0.6 add_reduce_fusion
  113.3 0.0 collective-permute-done.31
  113.3 2.8 %conditional.1 = (bf16[1024,512]{1,0:T(8,128)(2,1)}) conditional(s32[]{:T(128)} %convert_element_type.32, (s32[2]{0:T(128)S(1)}, bf16[1024,256]{1,0:T(8,128)(2,1)}, bf16[1024,256]{1,0:T(8,128)(2,1)}, bf16[1024,256]{1,0:T(8,128)(2,1)}, f32[1024,256]{1,0:T(8,128)S(1)}, /*index=5*/s16[1312,256]{1,0:T(8,128)(2,1)S(1)}, f32[1024,256]{1,0:T(8,128)}, ...), branch_computations={%region_1.2_spmd, %region_2.3_spmd} | conditional | flops 8594653184 | bytes 206655584 | solution.py:533
  113.3 2.6 %lay_out.1 = bf16[1024,512]{1,0:T(8,128)(2,1)} custom-call(s32[2]{0:T(128)S(1)} %get-tuple-element.32.place_ref, bf16[1024,256]{1,0:T(8,128)(2,1)} %get-tuple-element.33.refs_0_, bf16[1024,256]{1,0:T(8,128)(2,1)} %get-tuple-element.34.refs_1_, bf16[1024,256]{1,0:T(8,128)(2,1)} %get-tuple-element.35.refs_2_, f32[1024,256]{1,0:T(8,128)S(1)} %get-tuple-element.36.refs_3_, ...), custom_call_target="tpu_custom_call" | custom-call | flops 1 | bytes 1 | tf_op jit(solution)/shard_map/cond/branch_0_fun/lay_out/pallas_call | solution.py:382
  (22 shorter events, 0.0 us)
Async XLA Ops:
  0.0 3.2 %collective-permute-start.11 = (bf16[2048,256]{1,0:T(8,128)(2,1)}, bf16[2048,256]{1,0:T(8,128)(2,1)S(1)}, u32[]{:S(2)}, u32[]{:S(2)}) collective-permute-start(bf16[2048,256]{1,0:T(8,128)(2,1)} %refs_2_.2), channel_id=1, source_target_pairs={{0,1},{1,0},{2,3},{3,2},{4,5},{5,4},{6,7},{7,6},{8,9},{9,8},{10,11... | collective-permute-start | bytes 3145736 | tf_op jit(solution)/shard_map/ppermute | solution.py:489
  0.7 2.5 %collective-permute-start.10 = (s32[2,16]{1,0:T(2,128)}, s32[2,16]{1,0:T(2,128)S(1)}, u32[]{:S(2)}, u32[]{:S(2)}) collective-permute-start(s32[2,16]{1,0:T(2,128)} %bitcast.37), channel_id=1, source_target_pairs={{0,1},{1,0},{2,3},{3,2},{4,5},{5,4},{6,7},{7,6},{8,9},{9,8},{10,11... | collective-permute-start | bytes 392 | tf_op jit(solution)/shard_map/ppermute | solution.py:490
  0.7 4.4 %collective-permute-start.12 = (s32[8,16]{1,0:T(8,128)}, s32[8,16]{1,0:T(8,128)S(1)}, u32[]{:S(2)}, u32[]{:S(2)}) collective-permute-start(s32[8,16]{1,0:T(8,128)} %refs_0_.1), channel_id=1, source_target_pairs={{0,1},{1,0},{2,3},{3,2},{4,5},{5,4},{6,7},{7,6},{8,9},{9,8},{10,11... | collective-permute-start | bytes 1544 | tf_op jit(solution)/shard_map/ppermute | solution.py:491
  5.1 13.3 %copy-start = (bf16[5648,128]{1,0:T(8,128)(2,1)}, bf16[5648,128]{1,0:T(8,128)(2,1)S(1)}, u32[]{:S(2)}) copy-start(bf16[5648,128]{1,0:T(8,128)(2,1)S(1)} %pack_tiles.1.refs_3_) | copy-start | bytes 4337668
  5.1 9.1 %collective-permute-start.16 = (bf16[1024,2048]{1,0:T(8,128)(2,1)}, bf16[1024,2048]{1,0:T(8,128)(2,1)S(1)}, u32[]{:S(2)}, u32[]{:S(2)}) collective-permute-start(bf16[1024,2048]{1,0:T(8,128)(2,1)} %refs_2_.3), channel_id=1, source_target_pairs={{0,1},{1,0},{2,3},{3,2},{4,5},{5,4},{6,7},{7,6},{8,9},{9,8},{10,11... | collective-permute-start | bytes 12582920 | tf_op jit(solution)/shard_map/ppermute | solution.py:495
  5.6 12.9 %collective-permute-start.13 = (bf16[5648,128]{1,0:T(8,128)(2,1)S(1)}, bf16[5648,128]{1,0:T(8,128)(2,1)S(1)}, u32[]{:S(2)}, u32[]{:S(2)}) collective-permute-start(bf16[5648,128]{1,0:T(8,128)(2,1)S(1)} %pack_tiles.1.refs_3_), channel_id=1, source_target_pairs={{1,8},{3,10},{5,12},{7,14},{8,1},{10,3},{12,5},{14,7},{17,24},{19,... | collective-permute-start | bytes 4337672 | tf_op jit(solution)/shard_map/ppermute | solution.py:473
  6.3 21.7 %collective-permute-start.14 = (bf16[5648,128]{1,0:T(8,128)(2,1)S(1)}, bf16[5648,128]{1,0:T(8,128)(2,1)S(1)}, u32[]{:S(2)}, u32[]{:S(2)}) collective-permute-start(bf16[5648,128]{1,0:T(8,128)(2,1)S(1)} %pack_tiles.1.refs_3_), channel_id=1, source_target_pairs={{9,17},{11,19},{13,21},{15,23},{16,8},{18,10},{20,12},{22,14}} | collective-permute-start | bytes 4337672 | tf_op jit(solution)/shard_map/ppermute | solution.py:473
  12.1 19.8 %collective-permute-start.15 = (bf16[5648,128]{1,0:T(8,128)(2,1)S(1)}, bf16[5648,128]{1,0:T(8,128)(2,1)S(1)}, u32[]{:S(2)}, u32[]{:S(2)}) collective-permute-start(bf16[5648,128]{1,0:T(8,128)(2,1)S(1)} %pack_tiles.1.refs_3_), channel_id=1, source_target_pairs={{0,4},{2,6},{4,0},{6,2},{9,13},{11,15},{13,9},{15,11},{16,20},{18,... | collective-permute-start | bytes 4337672 | tf_op jit(solution)/shard_map/ppermute | solution.py:473
  18.4 16.3 %copy-start.8 = (bf16[5648,128]{1,0:T(8,128)(2,1)}, bf16[5648,128]{1,0:T(8,128)(2,1)S(1)}, u32[]{:S(2)}) copy-start(bf16[5648,128]{1,0:T(8,128)(2,1)S(1)} %collective-permute-done.13.refs_4_) | copy-start | bytes 4337668
  28.0 11.4 %copy-start.5 = (bf16[5648,128]{1,0:T(8,128)(2,1)}, bf16[5648,128]{1,0:T(8,128)(2,1)S(1)}, u32[]{:S(2)}) copy-start(bf16[5648,128]{1,0:T(8,128)(2,1)S(1)} %collective-permute-done.14.refs_5_) | copy-start | bytes 4337668
  31.9 22.2 %copy-start.9 = (bf16[5648,128]{1,0:T(8,128)(2,1)}, bf16[5648,128]{1,0:T(8,128)(2,1)S(1)}, u32[]{:S(2)}) copy-start(bf16[5648,128]{1,0:T(8,128)(2,1)S(1)} %collective-permute-done.15.refs_4_) | copy-start | bytes 4337668
  31.9 15.7 %collective-permute-start.17 = (bf16[5648,128]{1,0:T(8,128)(2,1)S(1)}, bf16[5648,128]{1,0:T(8,128)(2,1)S(1)}, u32[]{:S(2)}, u32[]{:S(2)}) collective-permute-start(bf16[5648,128]{1,0:T(8,128)(2,1)S(1)} %collective-permute-done.14.refs_5_), channel_id=1, source_target_pairs={{8,0},{10,2},{12,4},{14,6},{17,25},{19,27},{21,29},{23,31}} | collective-permute-start | bytes 4337672 | tf_op jit(solution)/shard_map/ppermute | solution.py:473
  32.6 20.1 %collective-permute-start.18 = (bf16[5648,128]{1,0:T(8,128)(2,1)S(1)}, bf16[5648,128]{1,0:T(8,128)(2,1)S(1)}, u32[]{:S(2)}, u32[]{:S(2)}) collective-permute-start(bf16[5648,128]{1,0:T(8,128)(2,1)S(1)} %collective-permute-done.13.refs_4_), channel_id=1, source_target_pairs={{8,16},{10,18},{12,20},{14,22},{17,9},{19,11},{21,13},{23,15}} | collective-permute-start | bytes 4337672 | tf_op jit(solution)/shard_map/ppermute | solution.py:473
  33.9 18.8 %collective-permute-start.19 = (bf16[5648,128]{1,0:T(8,128)(2,1)S(1)}, bf16[5648,128]{1,0:T(8,128)(2,1)S(1)}, u32[]{:S(2)}, u32[]{:S(2)}) collective-permute-start(bf16[5648,128]{1,0:T(8,128)(2,1)S(1)} %collective-permute-done.13.refs_4_), channel_id=1, source_target_pairs={{1,5},{3,7},{5,1},{7,3},{8,12},{10,14},{12,8},{14,10},{17,21},{19,... | collective-permute-start | bytes 4337672 | tf_op jit(solution)/shard_map/ppermute | solution.py:473
  39.3 8.2 %collective-permute-start.20 = (s16[656,256]{1,0:T(8,128)(2,1)S(1)}, s16[656,256]{1,0:T(8,128)(2,1)S(1)}, u32[]{:S(2)}, u32[]{:S(2)}) collective-permute-start(s16[656,256]{1,0:T(8,128)(2,1)S(1)} %get-tuple-element.110), channel_id=1, source_target_pairs={{2,0},{3,1},{6,4},{7,5},{10,8},{11,9},{14,12},{15,13},{16,18},{17,... | collective-permute-start | bytes 1007624 | tf_op jit(solution)/shard_map/ppermute | solution.py:473
  47.5 14.0 %copy-start.6 = (bf16[5648,128]{1,0:T(8,128)(2,1)}, bf16[5648,128]{1,0:T(8,128)(2,1)S(1)}, u32[]{:S(2)}) copy-start(bf16[5648,128]{1,0:T(8,128)(2,1)S(1)} %collective-permute-done.17.refs_4_) | copy-start | bytes 4337668
  52.7 8.9 %copy-start.7 = (bf16[5648,128]{1,0:T(8,128)(2,1)}, bf16[5648,128]{1,0:T(8,128)(2,1)S(1)}, u32[]{:S(2)}) copy-start(bf16[5648,128]{1,0:T(8,128)(2,1)S(1)} %collective-permute-done.18.refs_3_) | copy-start | bytes 4337668
  52.7 14.0 %copy-start.11 = (bf16[5648,128]{1,0:T(8,128)(2,1)}, bf16[5648,128]{1,0:T(8,128)(2,1)S(1)}, u32[]{:S(2)}) copy-start(bf16[5648,128]{1,0:T(8,128)(2,1)S(1)} %collective-permute-done.19.refs_5_) | copy-start | bytes 4337668
  52.7 30.7 %collective-permute-start.21 = (bf16[5648,128]{1,0:T(8,128)(2,1)S(1)}, bf16[5648,128]{1,0:T(8,128)(2,1)S(1)}, u32[]{:S(2)}, u32[]{:S(2)}) collective-permute-start(bf16[5648,128]{1,0:T(8,128)(2,1)S(1)} %collective-permute-done.18.refs_3_), channel_id=1, source_target_pairs={{9,1},{11,3},{13,5},{15,7},{16,24},{18,26},{20,28},{22,30}} | collective-permute-start | bytes 4337672 | tf_op jit(solution)/shard_map/ppermute | solution.py:473
  54.1 29.3 %collective-permute-start.22 = (bf16[5648,128]{1,0:T(8,128)(2,1)S(1)}, bf16[5648,128]{1,0:T(8,128)(2,1)S(1)}, u32[]{:S(2)}, u32[]{:S(2)}) collective-permute-start(bf16[5648,128]{1,0:T(8,128)(2,1)S(1)} %collective-permute-done.15.refs_4_), channel_id=1, source_target_pairs={{9,17},{11,19},{13,21},{15,23},{16,8},{18,10},{20,12},{22,14}} | collective-permute-start | bytes 4337672 | tf_op jit(solution)/shard_map/ppermute | solution.py:473
  58.7 24.8 %collective-permute-start.23 = (bf16[5648,128]{1,0:T(8,128)(2,1)S(1)}, bf16[5648,128]{1,0:T(8,128)(2,1)S(1)}, u32[]{:S(2)}, u32[]{:S(2)}) collective-permute-start(bf16[5648,128]{1,0:T(8,128)(2,1)S(1)} %collective-permute-done.17.refs_4_), channel_id=1, source_target_pairs={{0,4},{2,6},{4,0},{6,2},{25,29},{27,31},{29,25},{31,27}} | collective-permute-start | bytes 4337672 | tf_op jit(solution)/shard_map/ppermute | solution.py:473
  59.4 24.0 %collective-permute-start.24 = (bf16[5648,128]{1,0:T(8,128)(2,1)S(1)}, bf16[5648,128]{1,0:T(8,128)(2,1)S(1)}, u32[]{:S(2)}, u32[]{:S(2)}) collective-permute-start(bf16[5648,128]{1,0:T(8,128)(2,1)S(1)} %collective-permute-done.18.refs_3_), channel_id=1, source_target_pairs={{9,13},{11,15},{13,9},{15,11},{16,20},{18,22},{20,16},{22,18}} | collective-permute-start | bytes 4337672 | tf_op jit(solution)/shard_map/ppermute | solution.py:473
  66.7 16.7 %collective-permute-start.25 = (s16[1312,256]{1,0:T(8,128)(2,1)S(1)}, s16[1312,256]{1,0:T(8,128)(2,1)S(1)}, u32[]{:S(2)}, u32[]{:S(2)}) collective-permute-start(s16[1312,256]{1,0:T(8,128)(2,1)S(1)} %get-tuple-element.116), channel_id=1, source_target_pairs={{0,2},{4,6},{8,10},{9,11},{12,14},{13,15},{18,16},{19,17},{22,20},... | collective-permute-start | bytes 2015240 | tf_op jit(solution)/shard_map/ppermute | solution.py:473
  83.4 2.1 %copy-start.10 = (bf16[5648,128]{1,0:T(8,128)(2,1)}, bf16[5648,128]{1,0:T(8,128)(2,1)S(1)}, u32[]{:S(2)}) copy-start(bf16[5648,128]{1,0:T(8,128)(2,1)S(1)} %collective-permute-done.21.refs_6_) | copy-start | bytes 4337668
  83.5 2.1 %copy-start.12 = (bf16[5648,128]{1,0:T(8,128)(2,1)}, bf16[5648,128]{1,0:T(8,128)(2,1)S(1)}, u32[]{:S(2)}) copy-start(bf16[5648,128]{1,0:T(8,128)(2,1)S(1)} %collective-permute-done.22.refs_5_) | copy-start | bytes 4337668
  83.5 2.1 %copy-start.13 = (bf16[5648,128]{1,0:T(8,128)(2,1)}, bf16[5648,128]{1,0:T(8,128)(2,1)S(1)}, u32[]{:S(2)}) copy-start(bf16[5648,128]{1,0:T(8,128)(2,1)S(1)} %collective-permute-done.23.refs_4_) | copy-start | bytes 4337668
  83.5 2.4 %copy-start.14 = (bf16[5648,128]{1,0:T(8,128)(2,1)}, bf16[5648,128]{1,0:T(8,128)(2,1)S(1)}, u32[]{:S(2)}) copy-start(bf16[5648,128]{1,0:T(8,128)(2,1)S(1)} %collective-permute-done.24.refs_3_) | copy-start | bytes 4337668
  83.5 10.9 %collective-permute-start.26 = (bf16[5648,128]{1,0:T(8,128)(2,1)S(1)}, bf16[5648,128]{1,0:T(8,128)(2,1)S(1)}, u32[]{:S(2)}, u32[]{:S(2)}) collective-permute-start(bf16[5648,128]{1,0:T(8,128)(2,1)S(1)} %collective-permute-done.21.refs_6_), channel_id=1, source_target_pairs={{1,5},{3,7},{5,1},{7,3},{24,28},{26,30},{28,24},{30,26}} | collective-permute-start | bytes 4337672 | tf_op jit(solution)/shard_map/ppermute | solution.py:473
  84.3 26.2 %collective-permute-start.29 = (s16[1968,256]{1,0:T(8,128)(2,1)S(1)}, s16[1968,256]{1,0:T(8,128)(2,1)S(1)}, u32[]{:S(2)}, u32[]{:S(2)}) collective-permute-start(s16[1968,256]{1,0:T(8,128)(2,1)S(1)} %get-tuple-element.136), channel_id=1, source_target_pairs={{2,0},{3,1},{6,4},{7,5},{10,8},{11,9},{14,12},{15,13},{16,18},{17,... | collective-permute-start | bytes 3022856 | tf_op jit(solution)/shard_map/ppermute | solution.py:473
  91.0 21.0 %collective-permute-start.30 = (s16[1312,256]{1,0:T(8,128)(2,1)S(1)}, s16[1312,256]{1,0:T(8,128)(2,1)S(1)}, u32[]{:S(2)}, u32[]{:S(2)}) collective-permute-start(s16[1312,256]{1,0:T(8,128)(2,1)S(1)} %get-tuple-element.143), channel_id=1, source_target_pairs={{0,2},{1,3},{4,6},{5,7},{8,10},{9,11},{12,14},{13,15},{18,16},{19,... | collective-permute-start | bytes 2015240 | tf_op jit(solution)/shard_map/ppermute | solution.py:473
  96.0 17.3 %copy-start.4 = (bf16[2048,256]{1,0:T(8,128)(2,1)S(1)}, bf16[2048,256]{1,0:T(8,128)(2,1)}, u32[]{:S(2)}) copy-start(bf16[2048,256]{1,0:T(8,128)(2,1)} %refs_2_.2) | copy-start | bytes 3145732
  96.0 17.3 %copy-start.15 = (s32[8,16]{1,0:T(8,128)S(1)}, s32[8,16]{1,0:T(8,128)}, u32[]{:S(2)}) copy-start(s32[8,16]{1,0:T(8,128)} %refs_0_.1) | copy-start | bytes 1540
  96.0 17.3 %copy-start.16 = (s32[16,2]{0,1:T(2,128)S(1)}, s32[16,2]{0,1:T(2,128)}, u32[]{:S(2)}) copy-start(s32[16,2]{0,1:T(2,128)} %param.9) | copy-start | bytes 388
  96.0 17.3 %collective-permute-start.31 = (s16[1312,256]{1,0:T(8,128)(2,1)S(1)}, s16[1312,256]{1,0:T(8,128)(2,1)}, u32[]{:S(2)}, u32[]{:S(2)}) collective-permute-start(s16[1312,256]{1,0:T(8,128)(2,1)S(1)} %get-tuple-element.153), channel_id=1, source_target_pairs={{1,3},{5,7},{26,24},{30,28}} | collective-permute-start | bytes 2015240 | tf_op jit(solution)/shard_map/ppermute | solution.py:473
  97.7 1.2 %collective-permute-start.27 = (f32[8,128]{1,0:T(8,128)S(1)}, f32[8,128]{1,0:T(8,128)S(1)}, u32[]{:S(2)}, u32[]{:S(2)}) collective-permute-start(f32[8,128]{1,0:T(8,128)S(1)} %get-tuple-element.129.refs_0_), channel_id=1, source_target_pairs={{0,1},{1,0},{2,3},{3,2},{4,5},{5,4},{6,7},{7,6},{8,9},{9,8},{10,11... | collective-permute-start | bytes 12296 | tf_op jit(solution)/shard_map/ppermute | solution.py:524
  100.0 12.0 %collective-permute-start.28 = (f32[8,128]{1,0:T(8,128)S(1)}, f32[8,128]{1,0:T(8,128)S(1)}, u32[]{:S(2)}, u32[]{:S(2)}) collective-permute-start(f32[8,128]{1,0:T(8,128)S(1)} %get-tuple-element.144), channel_id=1, source_target_pairs={{0,2},{2,0},{1,3},{3,1},{4,6},{6,4},{5,7},{7,5},{8,10},{10,8},{9,1... | collective-permute-start | bytes 12296 | tf_op jit(solution)/shard_map/ppermute | solution.py:527

commit v7 on v6

--- a/solution.py
+++ b/solution.py
@@ -330,18 +330,22 @@
 
 
 def lay_out(place, mine, rest):
-    choices = [(one if isinstance(one, tuple) else (one,), two if isinstance(two, tuple) else (two,))
-               for one, two in zip(mine, rest)]
+    choices = list(zip(mine, rest))
     arrays = []
-    for array in jax.tree.leaves(choices):
-        if not any(array is known for known in arrays):
-            arrays.append(array)
+    for choice in choices:
+        for sums, *coded in choice:
+            for array in (sums, *[array for array, _ in coded]):
+                if not any(array is known for known in arrays):
+                    arrays.append(array)
     rows, width = arrays[0].shape
+    parts = halves(rows)
 
     def kernel(place_ref, *refs):
         ins = refs[:len(arrays)]
         out_any, round_ref, sums_ref, coded_ref, sems = refs[len(arrays):]
-        parts_of = halves(rows)
+
+        def place_of(array):
+            return ins[[array is known for known in arrays].index(True)]
 
         def store(side, first, length):
             at = pl.multiple_of((place_ref[1] ^ side) * width, width)
@@ -353,30 +357,28 @@
             @pl.when(place_ref[0] == number)
             def _(choice=choice):
                 fetch = {}
-                for side, parts in enumerate(choice):
-                    refs_in = [ins[[part is array for array in arrays].index(True)] for part in parts]
-                    for h, (first, length, at) in enumerate(parts_of):
-                        wanted = [(refs_in[0], first, length, (round_ref if len(parts) == 1 else sums_ref).at[side])]
-                        if len(parts) == 2:
-                            wanted.append((refs_in[1], at, coded_rows(length), coded_ref.at[side]))
-                        fetch[side, h] = [
-                            pltpu.make_async_copy(
-                                source.at[pl.ds(start, size)], target.at[pl.ds(start, size)], sems.at[n, 2 * side + h])
-                            for n, (source, start, size, target) in enumerate(wanted)]
+                for side, (sums, *coded) in enumerate(choice):
+                    for h, (first, length, _) in enumerate(parts):
+                        fetch[side, h] = [pltpu.make_async_copy(
+                            place_of(sums).at[pl.ds(first, length)],
+                            (sums_ref if coded else round_ref).at[side, pl.ds(first, length)], sems.at[0, 2 * side + h])]
+                        if coded:
+                            array, at = coded[h]
+                            fetch[side, h].append(pltpu.make_async_copy(
+                                place_of(array).at[pl.ds(at, coded_rows(length))], coded_ref.at[side, h],
+                                sems.at[1, 2 * side + h]))
                 for copy in sum(fetch.values(), []):
                     copy.start()
-                for side, parts in enumerate(choice):
-                    for h, (first, length, at) in enumerate(parts_of):
+                for side, (sums, *coded) in enumerate(choice):
+                    for h, (first, length, _) in enumerate(parts):
                         for copy in fetch[side, h]:
                             copy.wait()
-                        if len(parts) == 2:
-                            add_half(
-                                sums_ref.at[side], coded_ref.at[side, pl.ds(at, coded_rows(length))],
-                                round_ref.at[side], first, length)
+                        if coded:
+                            add_half(sums_ref.at[side], coded_ref.at[side, h], round_ref.at[side], first, length)
                         store(side, first, length).start()
 
         for side in range(2):
-            for first, length, _ in parts_of:
+            for first, length, _ in parts:
                 store(side, first, length).wait()
 
     return call(
@@ -387,7 +389,7 @@
         scratch_shapes=[
             pltpu.VMEM((2, rows, width), jnp.bfloat16),
             pltpu.VMEM((2, rows, width), jnp.float32),
-            pltpu.VMEM((2, 2 * coded_rows(rows // 2), width), jnp.int16),
+            pltpu.VMEM((2, 2, coded_rows(rows // 2), width), jnp.int16),
             pltpu.SemaphoreType.DMA((3, 4))],
     )(place, *arrays)
 
@@ -495,13 +497,13 @@
     other_amps = lax.ppermute(amplitudes_now, "col", CORES)
 
     *amps, masked_token = mask_tiles((amplitudes, other_amps), (amp_mask, other_amp_mask))
-    one, centre, own_x, tokens = after(masked_token)(
-        move(own, OWN_TO_PAIR), move(own, moves(over_centre)), move(own, moves(across_x)))
+    own_x, one, centre, tokens = after(masked_token)(
+        move(own, moves(across_x)), move(own, OWN_TO_PAIR), move(own, moves(over_centre)))
 
     a_sum, a_coded, a_rest, token = shard_product(amps, picks, 0, [[own], [one]], tokens, split=True)
     a_far = move(a_coded, to_y(False, both))
-    two_end, two_mid, one_x, own_x, a_far, tokens = after(token)(
-        move(centre, moves(outward, False)), move(one, moves(over_centre, False)), move(one, moves(across_x, False)),
+    one_x, two_mid, two_end, own_x, a_far, tokens = after(token)(
+        move(one, moves(across_x, False)), move(one, moves(over_centre, False)), move(centre, moves(outward, False)),
         own_x, a_far)
 
     c_sum, c_coded, token = shard_product(amps, picks, 1, [[two_mid], [two_end], [centre]], tokens)
@@ -520,15 +522,15 @@
     e_sum, e_coded, token = shard_product(amps, picks, 4, [[three_x]], tokens, held=lambda part: part)
     e_far = move(e_coded, to_y(True, late_cores))
     c_far, _ = barrier((c_far, token))
-    ab_far, a_far, _ = barrier((ab_far, a_far, token))
     c_both, token = add_coded((c_sum,), [both_halves(c_sum, c_far)], (token, lax.ppermute(token, "col", CORES)))
-    a_both, b_both, _ = add_coded(
-        (a_sum, b_sum), ([(a_far, 0), (ab_far, 0)], both_halves(b_sum, ab_far, a_rest.shape[0])))
     flags = [token, lax.ppermute(token, "col", CHIPS_Y)]
-    flags, a_both, b_both, c_both, d_far = barrier((flags, a_both, b_both, c_both, d_far))
+    a = [a_sum, (a_far, 0), (ab_far, 0)]
+    b = [b_sum, *both_halves(b_sum, ab_far, a_rest.shape[0])]
+    d = [d_sum, *both_halves(d_sum, d_far)]
+    e = [e_sum, *both_halves(e_sum, e_far)]
 
     def finish():
-        return lay_out(place, (a_both, c_both, (d_sum, d_far)), (b_both, (d_sum, d_far), (e_sum, e_far)))
+        return lay_out(place, (a, [c_both], d), (b, d, e))
 
     return lax.cond(
         jnp.max(sum(flags)) > 0, lambda: dense_ladder(amplitudes, integrals, amp_mask, int_mask), finish)

time: 117 us -> 115 us (0.983)
  the two profiles are of different devices: /device:TPU:11 before, /device:TPU:24 now
where the time goes in v7:
time: 115 us
  waiting for transfers between devices  49.5 us (43%)
  Pallas kernels  33.3 us (29%)
  starting transfers between devices  29.7 us (26%)
  between operations  1.25 us (1%)
    ppermute x16, waiting for transfers between devices, move(): return lax.ppermute(value, AXES, pairs)  35.9 us
    ppermute x16, starting transfers between devices, move(): return lax.ppermute(value, AXES, pairs)  25.4 us
    pallas_call x5, Pallas kernels, shard_product(): call(kernel, 'shard_product', out_shape=(jax.ShapeDtypeStruct((rows, wide...  22.5 us
    ppermute x1, waiting for transfers between devices, sparse_ladder(): flags = [token, lax.ppermute(token, 'col', CHIPS_Y)]  6.89 us
    pallas_call x1, Pallas kernels, mask_tiles(): call(kernel, 'mask_tiles', out_shape=tuple((jax.ShapeDtypeStruct(part.sha...  4.17 us
    ppermute x1, starting transfers between devices, sparse_ladder(): flags = [token, lax.ppermute(token, 'col', CHIPS_Y)]  3.5 us
    pallas_call x1, Pallas kernels, lay_out(): call(kernel, 'lay_out', out_shape=pltpu.HBM((rows, 2 * width), jnp.bfloat...  3.49 us
    ppermute x1, waiting for transfers between devices, sparse_ladder(): other_amps = lax.ppermute(amplitudes_now, 'col', CORES)  3.38 us
  transfers between devices with their start and end apart: 22, of which 9 were waited for; matrix products, arithmetic and copies ran while one was open for 1% of the time, Pallas kernels for 26%

profile of v7, /device:TPU:24, one launch (start us, length us, event | category | flops | bytes accessed | tf_op | source)
XLA Modules:
  0.0 114.8 jit_solution(7462577196966258185)
XLA Ops:
  0.0 0.0 collective-permute-start.11
  0.0 0.5 collective-permute-start.10
  0.5 0.0 collective-permute-start.12
  0.5 0.1 pad_add_fusion
  0.6 0.1 stack.37.picks_ref
  0.7 2.2 %collective-permute-done.10.refs_1_ = s32[2,16]{1,0:T(2,128)S(1)} collective-permute-done((s32[2,16]{1,0:T(2,128)}, s32[2,16]{1,0:T(2,128)S(1)}, u32[]{:S(2)}, u32[]{:S(2)}) %collective-permute-start.10) | collective-permute-done | bytes 160 | tf_op jit(solution)/shard_map/ppermute | solution.py:492
  2.9 0.0 collective-permute-done.11.refs_3_
  2.9 1.9 %pack_tiles.1.refs_3_ = bf16[5648,128]{1,0:T(8,128)(2,1)S(1)} custom-call(s32[1]{0:T(128)} %bitcast.2.swap_ref, s32[2,16]{1,0:T(2,128)} %bitcast.38, s32[2,16]{1,0:T(2,128)S(1)} %collective-permute-done.10.refs_1_, bf16[2048,256]{1,0:T(8,128)(2,1)} %refs_2_.2, bf16[2048,256]{1,0:T(8,128)(2,1)S(1)} %collective-permute-done.11.refs_3_), custom_call_target="tpu_custom_call" | custom-call | flops 1 | bytes 1 | tf_op jit(solution)/shard_map/pack_tiles/pallas_call | solution.py:101
  4.8 0.0 copy-start
  4.8 0.0 collective-permute-done.12.refs_1_
  4.8 0.2 collective-permute-start.16
  5.0 0.7 collective-permute-start.13
  5.8 2.3 %collective-permute-start.14 = (bf16[5648,128]{1,0:T(8,128)(2,1)S(1)}, bf16[5648,128]{1,0:T(8,128)(2,1)S(1)}, u32[]{:S(2)}, u32[]{:S(2)}) collective-permute-start(bf16[5648,128]{1,0:T(8,128)(2,1)S(1)} %pack_tiles.1.refs_3_), channel_id=1, source_target_pairs={{1,8},{3,10},{5,12},{7,14},{8,1},{10,3},{12,5},{14,7},{17,24},{19,... | collective-permute-start | bytes 4337672 | tf_op jit(solution)/shard_map/ppermute | solution.py:475
  8.1 0.8 collective-permute-start.15
  8.9 3.4 %collective-permute-done.16.refs_3_ = bf16[1024,2048]{1,0:T(8,128)(2,1)S(1)} collective-permute-done((bf16[1024,2048]{1,0:T(8,128)(2,1)}, bf16[1024,2048]{1,0:T(8,128)(2,1)S(1)}, u32[]{:S(2)}, u32[]{:S(2)}) %collective-permute-start.16) | collective-permute-done | bytes 4194336 | tf_op jit(solution)/shard_map/ppermute | solution.py:497
  12.2 4.2 %mask_tiles.1 = (bf16[1024,2048]{1,0:T(8,128)(2,1)S(1)}, bf16[1024,2048]{1,0:T(8,128)(2,1)S(1)}, f32[8,128]{1,0:T(8,128)S(1)}) custom-call(s32[8,16]{1,0:T(8,128)} %refs_0_.1, s32[8,16]{1,0:T(8,128)S(1)} %collective-permute-done.12.refs_1_, bf16[1024,2048]{1,0:T(8,128)(2,1)} %refs_2_.3, bf16[1024,2048]{1,0:T(8,128)(2,1)S(1)} %collective-permute-done.16.refs_3_), custom_call_target="tpu_custom_call" | custom-call | flops 1 | bytes 1 | tf_op jit(solution)/shard_map/mask_tiles/pallas_call | solution.py:131
  16.4 0.0 copy-done
  16.4 0.0 collective-permute-done.13.refs_4_
  16.4 0.0 copy-start.9
  16.4 9.7 %collective-permute-done.14.refs_4_ = bf16[5648,128]{1,0:T(8,128)(2,1)S(1)} collective-permute-done((bf16[5648,128]{1,0:T(8,128)(2,1)S(1)}, bf16[5648,128]{1,0:T(8,128)(2,1)S(1)}, u32[]{:S(2)}, u32[]{:S(2)}) %collective-permute-start.14) | collective-permute-done | bytes 1445920 | tf_op jit(solution)/shard_map/ppermute | solution.py:475
  26.1 0.0 collective-permute-done.15.refs_5_
  26.1 3.4 %collective-permute-start.17 = (bf16[5648,128]{1,0:T(8,128)(2,1)S(1)}, bf16[5648,128]{1,0:T(8,128)(2,1)S(1)}, u32[]{:S(2)}, u32[]{:S(2)}) collective-permute-start(bf16[5648,128]{1,0:T(8,128)(2,1)S(1)} %collective-permute-done.14.refs_4_), channel_id=1, source_target_pairs={{1,5},{3,7},{5,1},{7,3},{8,12},{10,14},{12,8},{14,10},{17,21},{19,... | collective-permute-start | bytes 4337672 | tf_op jit(solution)/shard_map/ppermute | solution.py:475
  29.5 0.8 collective-permute-start.18
  30.3 0.8 collective-permute-start.19
  31.1 0.0 copy-done.8
  31.1 6.0 %shard_product.5 = (f32[1024,256]{1,0:T(8,128)}, s16[656,256]{1,0:T(8,128)(2,1)S(1)}, s16[656,256]{1,0:T(8,128)(2,1)S(1)}, f32[8,128]{1,0:T(8,128)S(1)}) custom-call(s32[10]{0:T(128)S(1)} %stack.37.picks_ref, f32[8,128]{1,0:T(8,128)S(1)} %get-tuple-element.103.refs_0_, bf16[1024,2048]{1,0:T(8,128)(2,1)S(1)} %get-tuple-element.104.refs_1_.refs_2_, ...), custom_call_target="tpu_custom_call" | custom-call | flops 1 | bytes 1 | tf_op jit(solution)/shard_map/shard_product/pallas_call | solution.py:216
  37.1 0.0 copy-done.6
  37.1 3.0 %collective-permute-start.20 = (s16[656,256]{1,0:T(8,128)(2,1)S(1)}, s16[656,256]{1,0:T(8,128)(2,1)S(1)}, u32[]{:S(2)}, u32[]{:S(2)}) collective-permute-start(s16[656,256]{1,0:T(8,128)(2,1)S(1)} %get-tuple-element.106), channel_id=1, source_target_pairs={{2,0},{3,1},{6,4},{7,5},{10,8},{11,9},{14,12},{15,13},{16,18},{17,... | collective-permute-start | bytes 1007624 | tf_op jit(solution)/shard_map/ppermute | solution.py:475
  40.1 4.6 %collective-permute-done.20 = s16[656,256]{1,0:T(8,128)(2,1)S(1)} collective-permute-done((s16[656,256]{1,0:T(8,128)(2,1)S(1)}, s16[656,256]{1,0:T(8,128)(2,1)S(1)}, u32[]{:S(2)}, u32[]{:S(2)}) %collective-permute-start.20) | collective-permute-done | bytes 335904 | tf_op jit(solution)/shard_map/ppermute | solution.py:475
  44.7 2.4 %collective-permute-done.17.refs_5_ = bf16[5648,128]{1,0:T(8,128)(2,1)S(1)} collective-permute-done((bf16[5648,128]{1,0:T(8,128)(2,1)S(1)}, bf16[5648,128]{1,0:T(8,128)(2,1)S(1)}, u32[]{:S(2)}, u32[]{:S(2)}) %collective-permute-start.17) | collective-permute-done | bytes 1445920 | tf_op jit(solution)/shard_map/ppermute | solution.py:475
  47.1 0.0 collective-permute-done.18.refs_3_
  47.1 0.0 collective-permute-done.19.refs_4_
  47.1 1.3 %collective-permute-start.21 = (bf16[5648,128]{1,0:T(8,128)(2,1)S(1)}, bf16[5648,128]{1,0:T(8,128)(2,1)S(1)}, u32[]{:S(2)}, u32[]{:S(2)}) collective-permute-start(bf16[5648,128]{1,0:T(8,128)(2,1)S(1)} %collective-permute-done.18.refs_3_), channel_id=1, source_target_pairs={{9,1},{11,3},{13,5},{15,7},{16,24},{18,26},{20,28},{22,30}} | collective-permute-start | bytes 4337672 | tf_op jit(solution)/shard_map/ppermute | solution.py:475
  48.4 0.8 collective-permute-start.22
  49.2 0.8 collective-permute-start.23
  49.9 0.8 collective-permute-start.24
  50.7 0.6 shard_product.6
  51.3 0.7 collective-permute-start.25
  52.0 6.0 %shard_product.7 = (f32[1024,256]{1,0:T(8,128)}, s16[1968,256]{1,0:T(8,128)(2,1)S(1)}, f32[8,128]{1,0:T(8,128)S(1)}) custom-call(s32[10]{0:T(128)S(1)} %stack.37.picks_ref, s16[656,256]{1,0:T(8,128)(2,1)S(1)} %get-tuple-element.113.refs_0_, f32[8,128]{1,0:T(8,128)S(1)} %get-tuple-element.114.refs_1_, ...), custom_call_target="tpu_custom_call" | custom-call | flops 1 | bytes 1 | tf_op jit(solution)/shard_map/shard_product/pallas_call | solution.py:216
  58.1 0.0 collective-permute-done.25.refs_3_
  58.1 11.9 %collective-permute-done.21.refs_6_ = bf16[5648,128]{1,0:T(8,128)(2,1)S(1)} collective-permute-done((bf16[5648,128]{1,0:T(8,128)(2,1)S(1)}, bf16[5648,128]{1,0:T(8,128)(2,1)S(1)}, u32[]{:S(2)}, u32[]{:S(2)}) %collective-permute-start.21) | collective-permute-done | bytes 1445920 | tf_op jit(solution)/shard_map/ppermute | solution.py:475
  70.0 0.0 collective-permute-done.22.refs_5_
  70.0 0.0 collective-permute-done.23.refs_4_
  70.0 0.0 copy-start.13
  70.0 0.0 collective-permute-done.24.refs_3_
  70.0 2.4 %collective-permute-start.26 = (bf16[5648,128]{1,0:T(8,128)(2,1)S(1)}, bf16[5648,128]{1,0:T(8,128)(2,1)S(1)}, u32[]{:S(2)}, u32[]{:S(2)}) collective-permute-start(bf16[5648,128]{1,0:T(8,128)(2,1)S(1)} %collective-permute-done.21.refs_6_), channel_id=1, source_target_pairs={{1,5},{3,7},{5,1},{7,3},{24,28},{26,30},{28,24},{30,26}} | collective-permute-start | bytes 4337672 | tf_op jit(solution)/shard_map/ppermute | solution.py:475
  72.5 4.4 %collective-permute-start.29 = (s16[1968,256]{1,0:T(8,128)(2,1)S(1)}, s16[1968,256]{1,0:T(8,128)(2,1)}, u32[]{:S(2)}, u32[]{:S(2)}) collective-permute-start(s16[1968,256]{1,0:T(8,128)(2,1)S(1)} %get-tuple-element.133), channel_id=1, source_target_pairs={{2,0},{3,1},{6,4},{7,5},{10,8},{11,9},{14,12},{15,13},{16,18},{17,... | collective-permute-start | bytes 3022856 | tf_op jit(solution)/shard_map/ppermute | solution.py:475
  76.9 0.0 copy-done.13
  76.9 5.5 %shard_product.8 = (f32[1024,256]{1,0:T(8,128)}, s16[1312,256]{1,0:T(8,128)(2,1)S(1)}, f32[8,128]{1,0:T(8,128)S(1)}) custom-call(s32[10]{0:T(128)S(1)} %stack.37.picks_ref, f32[8,128]{1,0:T(8,128)S(1)} %get-tuple-element.118.refs_0_, bf16[1024,2048]{1,0:T(8,128)(2,1)S(1)} %get-tuple-element.104.refs_1_.refs_2_, ...), custom_call_target="tpu_custom_call" | custom-call | flops 1 | bytes 1 | tf_op jit(solution)/shard_map/shard_product/pallas_call | solution.py:216
  82.4 1.3 %collective-permute-start.30 = (s16[1312,256]{1,0:T(8,128)(2,1)S(1)}, s16[1312,256]{1,0:T(8,128)(2,1)}, u32[]{:S(2)}, u32[]{:S(2)}) collective-permute-start(s16[1312,256]{1,0:T(8,128)(2,1)S(1)} %get-tuple-element.137), channel_id=1, source_target_pairs={{0,2},{1,3},{4,6},{5,7},{8,10},{9,11},{12,14},{13,15},{18,16},{19,... | collective-permute-start | bytes 2015240 | tf_op jit(solution)/shard_map/ppermute | solution.py:475
  83.7 7.3 %collective-permute-done.26.refs_3_ = bf16[5648,128]{1,0:T(8,128)(2,1)S(1)} collective-permute-done((bf16[5648,128]{1,0:T(8,128)(2,1)S(1)}, bf16[5648,128]{1,0:T(8,128)(2,1)S(1)}, u32[]{:S(2)}, u32[]{:S(2)}) %collective-permute-start.26) | collective-permute-done | bytes 1445920 | tf_op jit(solution)/shard_map/ppermute | solution.py:475
  91.0 4.4 %shard_product.9 = (f32[1024,256]{1,0:T(8,128)}, s16[1312,256]{1,0:T(8,128)(2,1)S(1)}, f32[8,128]{1,0:T(8,128)S(1)}) custom-call(s32[10]{0:T(128)S(1)} %stack.37.picks_ref, f32[8,128]{1,0:T(8,128)S(1)} %get-tuple-element.123.refs_0_, bf16[1024,2048]{1,0:T(8,128)(2,1)S(1)} %get-tuple-element.104.refs_1_.refs_2_, ...), custom_call_target="tpu_custom_call" | custom-call | flops 1 | bytes 1 | tf_op jit(solution)/shard_map/shard_product/pallas_call | solution.py:216
  95.4 1.3 %collective-permute-start.31 = (s16[1312,256]{1,0:T(8,128)(2,1)S(1)}, s16[1312,256]{1,0:T(8,128)(2,1)}, u32[]{:S(2)}, u32[]{:S(2)}) collective-permute-start(s16[1312,256]{1,0:T(8,128)(2,1)S(1)} %get-tuple-element.139), channel_id=1, source_target_pairs={{1,3},{5,7},{26,24},{30,28}} | collective-permute-start | bytes 2015240 | tf_op jit(solution)/shard_map/ppermute | solution.py:475
  96.7 0.1 collective-permute-start.27
  96.8 1.2 %collective-permute-done.27.refs_1_ = f32[8,128]{1,0:T(8,128)S(1)} collective-permute-done((f32[8,128]{1,0:T(8,128)S(1)}, f32[8,128]{1,0:T(8,128)S(1)}, u32[]{:S(2)}, u32[]{:S(2)}) %collective-permute-start.27) | collective-permute-done | bytes 4128 | tf_op jit(solution)/shard_map/ppermute | solution.py:525
  97.9 1.2 %add_coded.1 = (bf16[1024,256]{1,0:T(8,128)(2,1)}, f32[8,128]{1,0:T(8,128)S(1)}) custom-call(f32[8,128]{1,0:T(8,128)S(1)} %get-tuple-element.125.refs_0_, f32[8,128]{1,0:T(8,128)S(1)} %collective-permute-done.27.refs_1_, f32[1024,256]{1,0:T(8,128)S(1)} %get-tuple-element.126.refs_2_, s16[1312,256]{1,0:T(8,128)(2,1)S(1)} %collective-permute-done.25.refs_3_), custom_call_target="tpu_custom_call" | custom-call | flops 1 | bytes 1 | tf_op jit(solution)/shard_map/add_coded/pallas_call | solution.py:312
  99.1 3.5 %collective-permute-start.28 = (f32[8,128]{1,0:T(8,128)S(1)}, f32[8,128]{1,0:T(8,128)S(1)}, u32[]{:S(2)}, u32[]{:S(2)}) collective-permute-start(f32[8,128]{1,0:T(8,128)S(1)} %get-tuple-element.129), channel_id=1, source_target_pairs={{0,2},{2,0},{1,3},{3,1},{4,6},{6,4},{5,7},{7,5},{8,10},{10,8},{9,1... | collective-permute-start | bytes 12296 | tf_op jit(solution)/shard_map/ppermute | solution.py:526
  102.6 6.9 %collective-permute-done.28 = f32[8,128]{1,0:T(8,128)S(1)} collective-permute-done((f32[8,128]{1,0:T(8,128)S(1)}, f32[8,128]{1,0:T(8,128)S(1)}, u32[]{:S(2)}, u32[]{:S(2)}) %collective-permute-start.28) | collective-permute-done | bytes 4128 | tf_op jit(solution)/shard_map/ppermute | solution.py:526
  109.5 0.6 add_reduce_fusion
  110.8 0.0 collective-permute-done.29
  110.8 0.0 collective-permute-done.30
  110.8 0.0 collective-permute-done.31
  110.9 3.8 %conditional.1 = (bf16[1024,512]{1,0:T(8,128)(2,1)}) conditional(s32[]{:T(128)} %convert_element_type.32, (s32[2]{0:T(128)S(1)}, f32[1024,256]{1,0:T(8,128)}, s16[656,256]{1,0:T(8,128)(2,1)}, s16[1968,256]{1,0:T(8,128)(2,1)}, f32[1024,256]{1,0:T(8,128)}, /*index=5*/bf16[1024,256]{1,0:T(8,128)(2,1)}, f32[1024,256]{1,0:T(8,128)}, ...), branch_computations={%region_1.2_spmd, %region_2.3_spmd} | conditional | flops 8594653184 | bytes 206655584 | solution.py:535
  110.9 3.5 %lay_out.1 = bf16[1024,512]{1,0:T(8,128)(2,1)} custom-call(s32[2]{0:T(128)S(1)} %get-tuple-element.36.place_ref, f32[1024,256]{1,0:T(8,128)} %get-tuple-element.37.refs_0_, s16[656,256]{1,0:T(8,128)(2,1)} %get-tuple-element.38.refs_1_, s16[1968,256]{1,0:T(8,128)(2,1)} %get-tuple-element.39.refs_2_, f32[1024,256]{1,0:T(8,128)} %get-tuple-element.40.refs_3_, ...), custom_call_target="tpu_custom_call" | custom-call | flops 1 | bytes 1 | tf_op jit(solution)/shard_map/cond/branch_0_fun/lay_out/pallas_call | solution.py:384
  (23 shorter events, 0.0 us)
Async XLA Ops:
  0.0 2.9 %collective-permute-start.11 = (bf16[2048,256]{1,0:T(8,128)(2,1)}, bf16[2048,256]{1,0:T(8,128)(2,1)S(1)}, u32[]{:S(2)}, u32[]{:S(2)}) collective-permute-start(bf16[2048,256]{1,0:T(8,128)(2,1)} %refs_2_.2), channel_id=1, source_target_pairs={{0,1},{1,0},{2,3},{3,2},{4,5},{5,4},{6,7},{7,6},{8,9},{9,8},{10,11... | collective-permute-start | bytes 3145736 | tf_op jit(solution)/shard_map/ppermute | solution.py:491
  0.0 2.9 %collective-permute-start.10 = (s32[2,16]{1,0:T(2,128)}, s32[2,16]{1,0:T(2,128)S(1)}, u32[]{:S(2)}, u32[]{:S(2)}) collective-permute-start(s32[2,16]{1,0:T(2,128)} %bitcast.37), channel_id=1, source_target_pairs={{0,1},{1,0},{2,3},{3,2},{4,5},{5,4},{6,7},{7,6},{8,9},{9,8},{10,11... | collective-permute-start | bytes 392 | tf_op jit(solution)/shard_map/ppermute | solution.py:492
  0.5 4.3 %collective-permute-start.12 = (s32[8,16]{1,0:T(8,128)}, s32[8,16]{1,0:T(8,128)S(1)}, u32[]{:S(2)}, u32[]{:S(2)}) collective-permute-start(s32[8,16]{1,0:T(8,128)} %refs_0_.1), channel_id=1, source_target_pairs={{0,1},{1,0},{2,3},{3,2},{4,5},{5,4},{6,7},{7,6},{8,9},{9,8},{10,11... | collective-permute-start | bytes 1544 | tf_op jit(solution)/shard_map/ppermute | solution.py:493
  4.8 11.6 %copy-start = (bf16[5648,128]{1,0:T(8,128)(2,1)}, bf16[5648,128]{1,0:T(8,128)(2,1)S(1)}, u32[]{:S(2)}) copy-start(bf16[5648,128]{1,0:T(8,128)(2,1)S(1)} %pack_tiles.1.refs_3_) | copy-start | bytes 4337668
  4.8 7.4 %collective-permute-start.16 = (bf16[1024,2048]{1,0:T(8,128)(2,1)}, bf16[1024,2048]{1,0:T(8,128)(2,1)S(1)}, u32[]{:S(2)}, u32[]{:S(2)}) collective-permute-start(bf16[1024,2048]{1,0:T(8,128)(2,1)} %refs_2_.3), channel_id=1, source_target_pairs={{0,1},{1,0},{2,3},{3,2},{4,5},{5,4},{6,7},{7,6},{8,9},{9,8},{10,11... | collective-permute-start | bytes 12582920 | tf_op jit(solution)/shard_map/ppermute | solution.py:497
  5.0 11.4 %collective-permute-start.13 = (bf16[5648,128]{1,0:T(8,128)(2,1)S(1)}, bf16[5648,128]{1,0:T(8,128)(2,1)S(1)}, u32[]{:S(2)}, u32[]{:S(2)}) collective-permute-start(bf16[5648,128]{1,0:T(8,128)(2,1)S(1)} %pack_tiles.1.refs_3_), channel_id=1, source_target_pairs={{0,4},{2,6},{4,0},{6,2},{9,13},{11,15},{13,9},{15,11},{16,20},{18,... | collective-permute-start | bytes 4337672 | tf_op jit(solution)/shard_map/ppermute | solution.py:475
  5.8 20.4 %collective-permute-start.14 = (bf16[5648,128]{1,0:T(8,128)(2,1)S(1)}, bf16[5648,128]{1,0:T(8,128)(2,1)S(1)}, u32[]{:S(2)}, u32[]{:S(2)}) collective-permute-start(bf16[5648,128]{1,0:T(8,128)(2,1)S(1)} %pack_tiles.1.refs_3_), channel_id=1, source_target_pairs={{1,8},{3,10},{5,12},{7,14},{8,1},{10,3},{12,5},{14,7},{17,24},{19,... | collective-permute-start | bytes 4337672 | tf_op jit(solution)/shard_map/ppermute | solution.py:475
  8.1 18.0 %collective-permute-start.15 = (bf16[5648,128]{1,0:T(8,128)(2,1)S(1)}, bf16[5648,128]{1,0:T(8,128)(2,1)S(1)}, u32[]{:S(2)}, u32[]{:S(2)}) collective-permute-start(bf16[5648,128]{1,0:T(8,128)(2,1)S(1)} %pack_tiles.1.refs_3_), channel_id=1, source_target_pairs={{9,17},{11,19},{13,21},{15,23},{16,8},{18,10},{20,12},{22,14}} | collective-permute-start | bytes 4337672 | tf_op jit(solution)/shard_map/ppermute | solution.py:475
  16.4 35.6 %copy-start.9 = (bf16[5648,128]{1,0:T(8,128)(2,1)}, bf16[5648,128]{1,0:T(8,128)(2,1)S(1)}, u32[]{:S(2)}) copy-start(bf16[5648,128]{1,0:T(8,128)(2,1)S(1)} %collective-permute-done.13.refs_4_) | copy-start | bytes 4337668
  26.1 4.9 %copy-start.8 = (bf16[5648,128]{1,0:T(8,128)(2,1)}, bf16[5648,128]{1,0:T(8,128)(2,1)S(1)}, u32[]{:S(2)}) copy-start(bf16[5648,128]{1,0:T(8,128)(2,1)S(1)} %collective-permute-done.14.refs_4_) | copy-start | bytes 4337668
  26.1 10.9 %copy-start.6 = (bf16[5648,128]{1,0:T(8,128)(2,1)}, bf16[5648,128]{1,0:T(8,128)(2,1)S(1)}, u32[]{:S(2)}) copy-start(bf16[5648,128]{1,0:T(8,128)(2,1)S(1)} %collective-permute-done.15.refs_5_) | copy-start | bytes 4337668
  26.1 20.9 %collective-permute-start.17 = (bf16[5648,128]{1,0:T(8,128)(2,1)S(1)}, bf16[5648,128]{1,0:T(8,128)(2,1)S(1)}, u32[]{:S(2)}, u32[]{:S(2)}) collective-permute-start(bf16[5648,128]{1,0:T(8,128)(2,1)S(1)} %collective-permute-done.14.refs_4_), channel_id=1, source_target_pairs={{1,5},{3,7},{5,1},{7,3},{8,12},{10,14},{12,8},{14,10},{17,21},{19,... | collective-permute-start | bytes 4337672 | tf_op jit(solution)/shard_map/ppermute | solution.py:475
  29.5 17.5 %collective-permute-start.18 = (bf16[5648,128]{1,0:T(8,128)(2,1)S(1)}, bf16[5648,128]{1,0:T(8,128)(2,1)S(1)}, u32[]{:S(2)}, u32[]{:S(2)}) collective-permute-start(bf16[5648,128]{1,0:T(8,128)(2,1)S(1)} %collective-permute-done.14.refs_4_), channel_id=1, source_target_pairs={{8,16},{10,18},{12,20},{14,22},{17,9},{19,11},{21,13},{23,15}} | collective-permute-start | bytes 4337672 | tf_op jit(solution)/shard_map/ppermute | solution.py:475
  30.3 16.8 %collective-permute-start.19 = (bf16[5648,128]{1,0:T(8,128)(2,1)S(1)}, bf16[5648,128]{1,0:T(8,128)(2,1)S(1)}, u32[]{:S(2)}, u32[]{:S(2)}) collective-permute-start(bf16[5648,128]{1,0:T(8,128)(2,1)S(1)} %collective-permute-done.15.refs_5_), channel_id=1, source_target_pairs={{8,0},{10,2},{12,4},{14,6},{17,25},{19,27},{21,29},{23,31}} | collective-permute-start | bytes 4337672 | tf_op jit(solution)/shard_map/ppermute | solution.py:475
  37.1 7.6 %collective-permute-start.20 = (s16[656,256]{1,0:T(8,128)(2,1)S(1)}, s16[656,256]{1,0:T(8,128)(2,1)S(1)}, u32[]{:S(2)}, u32[]{:S(2)}) collective-permute-start(s16[656,256]{1,0:T(8,128)(2,1)S(1)} %get-tuple-element.106), channel_id=1, source_target_pairs={{2,0},{3,1},{6,4},{7,5},{10,8},{11,9},{14,12},{15,13},{16,18},{17,... | collective-permute-start | bytes 1007624 | tf_op jit(solution)/shard_map/ppermute | solution.py:475
  44.7 5.2 %copy-start.15 = (s16[656,256]{1,0:T(8,128)(2,1)}, s16[656,256]{1,0:T(8,128)(2,1)S(1)}, u32[]{:S(2)}) copy-start(s16[656,256]{1,0:T(8,128)(2,1)S(1)} %collective-permute-done.20) | copy-start | bytes 1007620
  47.1 5.0 %copy-start.11 = (bf16[5648,128]{1,0:T(8,128)(2,1)}, bf16[5648,128]{1,0:T(8,128)(2,1)S(1)}, u32[]{:S(2)}) copy-start(bf16[5648,128]{1,0:T(8,128)(2,1)S(1)} %collective-permute-done.17.refs_5_) | copy-start | bytes 4337668
  47.1 3.6 %copy-start.5 = (bf16[5648,128]{1,0:T(8,128)(2,1)}, bf16[5648,128]{1,0:T(8,128)(2,1)S(1)}, u32[]{:S(2)}) copy-start(bf16[5648,128]{1,0:T(8,128)(2,1)S(1)} %collective-permute-done.18.refs_3_) | copy-start | bytes 4337668
  47.1 3.6 %copy-start.7 = (bf16[5648,128]{1,0:T(8,128)(2,1)}, bf16[5648,128]{1,0:T(8,128)(2,1)S(1)}, u32[]{:S(2)}) copy-start(bf16[5648,128]{1,0:T(8,128)(2,1)S(1)} %collective-permute-done.19.refs_4_) | copy-start | bytes 4337668
  47.1 22.9 %collective-permute-start.21 = (bf16[5648,128]{1,0:T(8,128)(2,1)S(1)}, bf16[5648,128]{1,0:T(8,128)(2,1)S(1)}, u32[]{:S(2)}, u32[]{:S(2)}) collective-permute-start(bf16[5648,128]{1,0:T(8,128)(2,1)S(1)} %collective-permute-done.18.refs_3_), channel_id=1, source_target_pairs={{9,1},{11,3},{13,5},{15,7},{16,24},{18,26},{20,28},{22,30}} | collective-permute-start | bytes 4337672 | tf_op jit(solution)/shard_map/ppermute | solution.py:475
  48.4 21.6 %collective-permute-start.22 = (bf16[5648,128]{1,0:T(8,128)(2,1)S(1)}, bf16[5648,128]{1,0:T(8,128)(2,1)S(1)}, u32[]{:S(2)}, u32[]{:S(2)}) collective-permute-start(bf16[5648,128]{1,0:T(8,128)(2,1)S(1)} %collective-permute-done.13.refs_4_), channel_id=1, source_target_pairs={{9,17},{11,19},{13,21},{15,23},{16,8},{18,10},{20,12},{22,14}} | collective-permute-start | bytes 4337672 | tf_op jit(solution)/shard_map/ppermute | solution.py:475
  49.2 20.8 %collective-permute-start.23 = (bf16[5648,128]{1,0:T(8,128)(2,1)S(1)}, bf16[5648,128]{1,0:T(8,128)(2,1)S(1)}, u32[]{:S(2)}, u32[]{:S(2)}) collective-permute-start(bf16[5648,128]{1,0:T(8,128)(2,1)S(1)} %collective-permute-done.19.refs_4_), channel_id=1, source_target_pairs={{0,4},{2,6},{4,0},{6,2},{25,29},{27,31},{29,25},{31,27}} | collective-permute-start | bytes 4337672 | tf_op jit(solution)/shard_map/ppermute | solution.py:475
  49.9 20.1 %collective-permute-start.24 = (bf16[5648,128]{1,0:T(8,128)(2,1)S(1)}, bf16[5648,128]{1,0:T(8,128)(2,1)S(1)}, u32[]{:S(2)}, u32[]{:S(2)}) collective-permute-start(bf16[5648,128]{1,0:T(8,128)(2,1)S(1)} %collective-permute-done.18.refs_3_), channel_id=1, source_target_pairs={{9,13},{11,15},{13,9},{15,11},{16,20},{18,22},{20,16},{22,18}} | collective-permute-start | bytes 4337672 | tf_op jit(solution)/shard_map/ppermute | solution.py:475
  51.3 6.8 %collective-permute-start.25 = (s16[1312,256]{1,0:T(8,128)(2,1)S(1)}, s16[1312,256]{1,0:T(8,128)(2,1)S(1)}, u32[]{:S(2)}, u32[]{:S(2)}) collective-permute-start(s16[1312,256]{1,0:T(8,128)(2,1)S(1)} %get-tuple-element.112), channel_id=1, source_target_pairs={{0,2},{4,6},{8,10},{9,11},{12,14},{13,15},{18,16},{19,17},{22,20},... | collective-permute-start | bytes 2015240 | tf_op jit(solution)/shard_map/ppermute | solution.py:475
  70.0 6.9 %copy-start.10 = (bf16[5648,128]{1,0:T(8,128)(2,1)}, bf16[5648,128]{1,0:T(8,128)(2,1)S(1)}, u32[]{:S(2)}) copy-start(bf16[5648,128]{1,0:T(8,128)(2,1)S(1)} %collective-permute-done.21.refs_6_) | copy-start | bytes 4337668
  70.0 6.9 %copy-start.12 = (bf16[5648,128]{1,0:T(8,128)(2,1)}, bf16[5648,128]{1,0:T(8,128)(2,1)S(1)}, u32[]{:S(2)}) copy-start(bf16[5648,128]{1,0:T(8,128)(2,1)S(1)} %collective-permute-done.22.refs_5_) | copy-start | bytes 4337668
  70.0 6.9 %copy-start.13 = (bf16[5648,128]{1,0:T(8,128)(2,1)}, bf16[5648,128]{1,0:T(8,128)(2,1)S(1)}, u32[]{:S(2)}) copy-start(bf16[5648,128]{1,0:T(8,128)(2,1)S(1)} %collective-permute-done.23.refs_4_) | copy-start | bytes 4337668
  70.0 6.9 %copy-start.14 = (bf16[5648,128]{1,0:T(8,128)(2,1)}, bf16[5648,128]{1,0:T(8,128)(2,1)S(1)}, u32[]{:S(2)}) copy-start(bf16[5648,128]{1,0:T(8,128)(2,1)S(1)} %collective-permute-done.24.refs_3_) | copy-start | bytes 4337668
  70.0 20.9 %collective-permute-start.26 = (bf16[5648,128]{1,0:T(8,128)(2,1)S(1)}, bf16[5648,128]{1,0:T(8,128)(2,1)S(1)}, u32[]{:S(2)}, u32[]{:S(2)}) collective-permute-start(bf16[5648,128]{1,0:T(8,128)(2,1)S(1)} %collective-permute-done.21.refs_6_), channel_id=1, source_target_pairs={{1,5},{3,7},{5,1},{7,3},{24,28},{26,30},{28,24},{30,26}} | collective-permute-start | bytes 4337672 | tf_op jit(solution)/shard_map/ppermute | solution.py:475
  72.5 38.3 %collective-permute-start.29 = (s16[1968,256]{1,0:T(8,128)(2,1)S(1)}, s16[1968,256]{1,0:T(8,128)(2,1)}, u32[]{:S(2)}, u32[]{:S(2)}) collective-permute-start(s16[1968,256]{1,0:T(8,128)(2,1)S(1)} %get-tuple-element.133), channel_id=1, source_target_pairs={{2,0},{3,1},{6,4},{7,5},{10,8},{11,9},{14,12},{15,13},{16,18},{17,... | collective-permute-start | bytes 3022856 | tf_op jit(solution)/shard_map/ppermute | solution.py:475
  82.4 28.4 %collective-permute-start.30 = (s16[1312,256]{1,0:T(8,128)(2,1)S(1)}, s16[1312,256]{1,0:T(8,128)(2,1)}, u32[]{:S(2)}, u32[]{:S(2)}) collective-permute-start(s16[1312,256]{1,0:T(8,128)(2,1)S(1)} %get-tuple-element.137), channel_id=1, source_target_pairs={{0,2},{1,3},{4,6},{5,7},{8,10},{9,11},{12,14},{13,15},{18,16},{19,... | collective-permute-start | bytes 2015240 | tf_op jit(solution)/shard_map/ppermute | solution.py:475
  91.0 19.9 %copy-start.4 = (bf16[2048,256]{1,0:T(8,128)(2,1)S(1)}, bf16[2048,256]{1,0:T(8,128)(2,1)}, u32[]{:S(2)}) copy-start(bf16[2048,256]{1,0:T(8,128)(2,1)} %refs_2_.2) | copy-start | bytes 3145732
  91.0 19.9 %copy-start.16 = (s32[8,16]{1,0:T(8,128)S(1)}, s32[8,16]{1,0:T(8,128)}, u32[]{:S(2)}) copy-start(s32[8,16]{1,0:T(8,128)} %refs_0_.1) | copy-start | bytes 1540
  91.0 19.9 %copy-start.17 = (s32[16,2]{0,1:T(2,128)S(1)}, s32[16,2]{0,1:T(2,128)}, u32[]{:S(2)}) copy-start(s32[16,2]{0,1:T(2,128)} %param.9) | copy-start | bytes 388
  95.4 15.4 %collective-permute-start.31 = (s16[1312,256]{1,0:T(8,128)(2,1)S(1)}, s16[1312,256]{1,0:T(8,128)(2,1)}, u32[]{:S(2)}, u32[]{:S(2)}) collective-permute-start(s16[1312,256]{1,0:T(8,128)(2,1)S(1)} %get-tuple-element.139), channel_id=1, source_target_pairs={{1,3},{5,7},{26,24},{30,28}} | collective-permute-start | bytes 2015240 | tf_op jit(solution)/shard_map/ppermute | solution.py:475
  96.7 1.2 %collective-permute-start.27 = (f32[8,128]{1,0:T(8,128)S(1)}, f32[8,128]{1,0:T(8,128)S(1)}, u32[]{:S(2)}, u32[]{:S(2)}) collective-permute-start(f32[8,128]{1,0:T(8,128)S(1)} %get-tuple-element.125.refs_0_), channel_id=1, source_target_pairs={{0,1},{1,0},{2,3},{3,2},{4,5},{5,4},{6,7},{7,6},{8,9},{9,8},{10,11... | collective-permute-start | bytes 12296 | tf_op jit(solution)/shard_map/ppermute | solution.py:525
  99.1 10.4 %collective-permute-start.28 = (f32[8,128]{1,0:T(8,128)S(1)}, f32[8,128]{1,0:T(8,128)S(1)}, u32[]{:S(2)}, u32[]{:S(2)}) collective-permute-start(f32[8,128]{1,0:T(8,128)S(1)} %get-tuple-element.129), channel_id=1, source_target_pairs={{0,2},{2,0},{1,3},{3,1},{4,6},{6,4},{5,7},{7,5},{8,10},{10,8},{9,1... | collective-permute-start | bytes 12296 | tf_op jit(solution)/shard_map/ppermute | solution.py:526

commit v8 on v7

--- a/solution.py
+++ b/solution.py
@@ -509,9 +509,9 @@
     c_sum, c_coded, token = shard_product(amps, picks, 1, [[two_mid], [two_end], [centre]], tokens)
     c_far = move(c_coded, to_y(True, early_cores))
     b_sum, ab_coded, token = shard_product(amps, picks, 2, [[own_x], [one_x]], (token,), a_rest)
-    three_end, three_mid_x, two_x_end, two_x_mid, c_far, tokens = after(token)(
-        move(two_mid, moves(outward)), move(own_x, moves(over_centre)),
-        move(two_end, moves(across_x_ends)), move(two_mid, moves(across_x_middle)), c_far)
+    two_x_end, three_end, two_x_mid, three_mid_x, c_far, tokens = after(token)(
+        move(two_end, moves(across_x_ends)), move(two_mid, moves(outward)),
+        move(two_mid, moves(across_x_middle)), move(own_x, moves(over_centre)), c_far)
 
     d_sum, d_coded, token = shard_product(
         amps, picks, 3, [[two_x_mid], [two_x_end], [three_mid_x], [three_end]], tokens)

time: 115 us -> 115 us (level)
    ppermute x1, waiting for transfers between devices: 6.89 us -> 5.57 us  [sparse_ladder(): flags = [token, lax.ppermute(token, 'col', CHIPS_Y)]]
where the time goes in v8:
time: 115 us; the launch traced here: 114 us
  waiting for transfers between devices  48.9 us (43%)
  Pallas kernels  33.3 us (29%)
  starting transfers between devices  29.7 us (26%)
  between operations  1.25 us (1%)
    ppermute x16, waiting for transfers between devices, move(): return lax.ppermute(value, AXES, pairs)  36.6 us
    ppermute x16, starting transfers between devices, move(): return lax.ppermute(value, AXES, pairs)  25.4 us
    pallas_call x5, Pallas kernels, shard_product(): call(kernel, 'shard_product', out_shape=(jax.ShapeDtypeStruct((rows, wide...  22.5 us
    ppermute x1, waiting for transfers between devices, sparse_ladder(): flags = [token, lax.ppermute(token, 'col', CHIPS_Y)]  5.57 us
    pallas_call x1, Pallas kernels, mask_tiles(): call(kernel, 'mask_tiles', out_shape=tuple((jax.ShapeDtypeStruct(part.sha...  4.17 us
    ppermute x1, starting transfers between devices, sparse_ladder(): flags = [token, lax.ppermute(token, 'col', CHIPS_Y)]  3.5 us
    pallas_call x1, Pallas kernels, lay_out(): call(kernel, 'lay_out', out_shape=pltpu.HBM((rows, 2 * width), jnp.bfloat...  3.49 us
    ppermute x1, waiting for transfers between devices, sparse_ladder(): other_amps = lax.ppermute(amplitudes_now, 'col', CORES)  3.4 us
  transfers between devices with their start and end apart: 22, of which 9 were waited for; matrix products, arithmetic and copies ran while one was open for 1% of the time, Pallas kernels for 26%

profile of v8, /device:TPU:24, one launch (start us, length us, event | category | flops | bytes accessed | tf_op | source)
XLA Modules:
  0.0 114.2 jit_solution(13259681865402332042)
XLA Ops:
  0.0 0.0 collective-permute-start.11
  0.0 0.5 collective-permute-start.10
  0.5 0.0 collective-permute-start.12
  0.5 0.1 pad_add_fusion
  0.6 0.1 stack.37.picks_ref
  0.7 2.2 %collective-permute-done.10.refs_1_ = s32[2,16]{1,0:T(2,128)S(1)} collective-permute-done((s32[2,16]{1,0:T(2,128)}, s32[2,16]{1,0:T(2,128)S(1)}, u32[]{:S(2)}, u32[]{:S(2)}) %collective-permute-start.10) | collective-permute-done | bytes 160 | tf_op jit(solution)/shard_map/ppermute | solution.py:492
  2.9 0.0 collective-permute-done.11.refs_3_
  2.9 1.9 %pack_tiles.1.refs_3_ = bf16[5648,128]{1,0:T(8,128)(2,1)S(1)} custom-call(s32[1]{0:T(128)} %bitcast.2.swap_ref, s32[2,16]{1,0:T(2,128)} %bitcast.38, s32[2,16]{1,0:T(2,128)S(1)} %collective-permute-done.10.refs_1_, bf16[2048,256]{1,0:T(8,128)(2,1)} %refs_2_.2, bf16[2048,256]{1,0:T(8,128)(2,1)S(1)} %collective-permute-done.11.refs_3_), custom_call_target="tpu_custom_call" | custom-call | flops 1 | bytes 1 | tf_op jit(solution)/shard_map/pack_tiles/pallas_call | solution.py:101
  4.8 0.0 copy-start
  4.8 0.0 collective-permute-done.12.refs_1_
  4.8 0.2 collective-permute-start.16
  5.0 0.7 collective-permute-start.13
  5.8 2.3 %collective-permute-start.14 = (bf16[5648,128]{1,0:T(8,128)(2,1)S(1)}, bf16[5648,128]{1,0:T(8,128)(2,1)S(1)}, u32[]{:S(2)}, u32[]{:S(2)}) collective-permute-start(bf16[5648,128]{1,0:T(8,128)(2,1)S(1)} %pack_tiles.1.refs_3_), channel_id=1, source_target_pairs={{1,8},{3,10},{5,12},{7,14},{8,1},{10,3},{12,5},{14,7},{17,24},{19,... | collective-permute-start | bytes 4337672 | tf_op jit(solution)/shard_map/ppermute | solution.py:475
  8.1 0.8 collective-permute-start.15
  8.9 3.4 %collective-permute-done.16.refs_3_ = bf16[1024,2048]{1,0:T(8,128)(2,1)S(1)} collective-permute-done((bf16[1024,2048]{1,0:T(8,128)(2,1)}, bf16[1024,2048]{1,0:T(8,128)(2,1)S(1)}, u32[]{:S(2)}, u32[]{:S(2)}) %collective-permute-start.16) | collective-permute-done | bytes 4194336 | tf_op jit(solution)/shard_map/ppermute | solution.py:497
  12.3 4.2 %mask_tiles.1 = (bf16[1024,2048]{1,0:T(8,128)(2,1)S(1)}, bf16[1024,2048]{1,0:T(8,128)(2,1)S(1)}, f32[8,128]{1,0:T(8,128)S(1)}) custom-call(s32[8,16]{1,0:T(8,128)} %refs_0_.1, s32[8,16]{1,0:T(8,128)S(1)} %collective-permute-done.12.refs_1_, bf16[1024,2048]{1,0:T(8,128)(2,1)} %refs_2_.3, bf16[1024,2048]{1,0:T(8,128)(2,1)S(1)} %collective-permute-done.16.refs_3_), custom_call_target="tpu_custom_call" | custom-call | flops 1 | bytes 1 | tf_op jit(solution)/shard_map/mask_tiles/pallas_call | solution.py:131
  16.4 0.0 copy-done
  16.4 0.0 collective-permute-done.13.refs_4_
  16.5 0.0 copy-start.9
  16.5 9.7 %collective-permute-done.14.refs_4_ = bf16[5648,128]{1,0:T(8,128)(2,1)S(1)} collective-permute-done((bf16[5648,128]{1,0:T(8,128)(2,1)S(1)}, bf16[5648,128]{1,0:T(8,128)(2,1)S(1)}, u32[]{:S(2)}, u32[]{:S(2)}) %collective-permute-start.14) | collective-permute-done | bytes 1445920 | tf_op jit(solution)/shard_map/ppermute | solution.py:475
  26.1 0.0 collective-permute-done.15.refs_5_
  26.2 3.4 %collective-permute-start.17 = (bf16[5648,128]{1,0:T(8,128)(2,1)S(1)}, bf16[5648,128]{1,0:T(8,128)(2,1)S(1)}, u32[]{:S(2)}, u32[]{:S(2)}) collective-permute-start(bf16[5648,128]{1,0:T(8,128)(2,1)S(1)} %collective-permute-done.14.refs_4_), channel_id=1, source_target_pairs={{1,5},{3,7},{5,1},{7,3},{8,12},{10,14},{12,8},{14,10},{17,21},{19,... | collective-permute-start | bytes 4337672 | tf_op jit(solution)/shard_map/ppermute | solution.py:475
  29.6 0.8 collective-permute-start.18
  30.3 0.8 collective-permute-start.19
  31.1 6.0 %shard_product.5 = (f32[1024,256]{1,0:T(8,128)}, s16[656,256]{1,0:T(8,128)(2,1)S(1)}, s16[656,256]{1,0:T(8,128)(2,1)S(1)}, f32[8,128]{1,0:T(8,128)S(1)}) custom-call(s32[10]{0:T(128)S(1)} %stack.37.picks_ref, f32[8,128]{1,0:T(8,128)S(1)} %get-tuple-element.103.refs_0_, bf16[1024,2048]{1,0:T(8,128)(2,1)S(1)} %get-tuple-element.104.refs_1_.refs_2_, ...), custom_call_target="tpu_custom_call" | custom-call | flops 1 | bytes 1 | tf_op jit(solution)/shard_map/shard_product/pallas_call | solution.py:216
  37.1 3.0 %collective-permute-start.20 = (s16[656,256]{1,0:T(8,128)(2,1)S(1)}, s16[656,256]{1,0:T(8,128)(2,1)S(1)}, u32[]{:S(2)}, u32[]{:S(2)}) collective-permute-start(s16[656,256]{1,0:T(8,128)(2,1)S(1)} %get-tuple-element.106), channel_id=1, source_target_pairs={{2,0},{3,1},{6,4},{7,5},{10,8},{11,9},{14,12},{15,13},{16,18},{17,... | collective-permute-start | bytes 1007624 | tf_op jit(solution)/shard_map/ppermute | solution.py:475
  40.1 4.6 %collective-permute-done.20 = s16[656,256]{1,0:T(8,128)(2,1)S(1)} collective-permute-done((s16[656,256]{1,0:T(8,128)(2,1)S(1)}, s16[656,256]{1,0:T(8,128)(2,1)S(1)}, u32[]{:S(2)}, u32[]{:S(2)}) %collective-permute-start.20) | collective-permute-done | bytes 335904 | tf_op jit(solution)/shard_map/ppermute | solution.py:475
  44.7 2.4 %collective-permute-done.17.refs_5_ = bf16[5648,128]{1,0:T(8,128)(2,1)S(1)} collective-permute-done((bf16[5648,128]{1,0:T(8,128)(2,1)S(1)}, bf16[5648,128]{1,0:T(8,128)(2,1)S(1)}, u32[]{:S(2)}, u32[]{:S(2)}) %collective-permute-start.17) | collective-permute-done | bytes 1445920 | tf_op jit(solution)/shard_map/ppermute | solution.py:475
  47.1 0.0 collective-permute-done.18.refs_3_
  47.1 0.0 collective-permute-done.19.refs_4_
  47.1 0.8 collective-permute-start.21
  47.9 1.3 %collective-permute-start.22 = (bf16[5648,128]{1,0:T(8,128)(2,1)S(1)}, bf16[5648,128]{1,0:T(8,128)(2,1)S(1)}, u32[]{:S(2)}, u32[]{:S(2)}) collective-permute-start(bf16[5648,128]{1,0:T(8,128)(2,1)S(1)} %collective-permute-done.18.refs_3_), channel_id=1, source_target_pairs={{9,1},{11,3},{13,5},{15,7},{16,24},{18,26},{20,28},{22,30}} | collective-permute-start | bytes 4337672 | tf_op jit(solution)/shard_map/ppermute | solution.py:475
  49.2 0.8 collective-permute-start.23
  50.0 0.8 collective-permute-start.24
  50.7 0.6 shard_product.6
  51.3 0.7 collective-permute-start.25
  52.0 0.0 copy-done.9
  52.1 0.0 copy-done.10
  52.1 6.0 %shard_product.7 = (f32[1024,256]{1,0:T(8,128)}, s16[1968,256]{1,0:T(8,128)(2,1)S(1)}, f32[8,128]{1,0:T(8,128)S(1)}) custom-call(s32[10]{0:T(128)S(1)} %stack.37.picks_ref, s16[656,256]{1,0:T(8,128)(2,1)S(1)} %get-tuple-element.113.refs_0_, f32[8,128]{1,0:T(8,128)S(1)} %get-tuple-element.114.refs_1_, ...), custom_call_target="tpu_custom_call" | custom-call | flops 1 | bytes 1 | tf_op jit(solution)/shard_map/shard_product/pallas_call | solution.py:216
  58.1 0.0 collective-permute-done.25.refs_3_
  58.1 0.0 collective-permute-done.21.refs_4_
  58.1 0.0 copy-start.12
  58.1 12.6 %collective-permute-done.22.refs_6_ = bf16[5648,128]{1,0:T(8,128)(2,1)S(1)} collective-permute-done((bf16[5648,128]{1,0:T(8,128)(2,1)S(1)}, bf16[5648,128]{1,0:T(8,128)(2,1)S(1)}, u32[]{:S(2)}, u32[]{:S(2)}) %collective-permute-start.22) | collective-permute-done | bytes 1445920 | tf_op jit(solution)/shard_map/ppermute | solution.py:475
  70.7 0.0 collective-permute-done.23.refs_3_
  70.8 0.0 collective-permute-done.24.refs_5_
  70.8 2.4 %collective-permute-start.26 = (bf16[5648,128]{1,0:T(8,128)(2,1)S(1)}, bf16[5648,128]{1,0:T(8,128)(2,1)S(1)}, u32[]{:S(2)}, u32[]{:S(2)}) collective-permute-start(bf16[5648,128]{1,0:T(8,128)(2,1)S(1)} %collective-permute-done.22.refs_6_), channel_id=1, source_target_pairs={{1,5},{3,7},{5,1},{7,3},{24,28},{26,30},{28,24},{30,26}} | collective-permute-start | bytes 4337672 | tf_op jit(solution)/shard_map/ppermute | solution.py:475
  73.2 4.4 %collective-permute-start.29 = (s16[1968,256]{1,0:T(8,128)(2,1)S(1)}, s16[1968,256]{1,0:T(8,128)(2,1)}, u32[]{:S(2)}, u32[]{:S(2)}) collective-permute-start(s16[1968,256]{1,0:T(8,128)(2,1)S(1)} %get-tuple-element.133), channel_id=1, source_target_pairs={{2,0},{3,1},{6,4},{7,5},{10,8},{11,9},{14,12},{15,13},{16,18},{17,... | collective-permute-start | bytes 3022856 | tf_op jit(solution)/shard_map/ppermute | solution.py:475
  77.6 0.0 copy-done.12
  77.6 5.5 %shard_product.8 = (f32[1024,256]{1,0:T(8,128)}, s16[1312,256]{1,0:T(8,128)(2,1)S(1)}, f32[8,128]{1,0:T(8,128)S(1)}) custom-call(s32[10]{0:T(128)S(1)} %stack.37.picks_ref, f32[8,128]{1,0:T(8,128)S(1)} %get-tuple-element.118.refs_0_, bf16[1024,2048]{1,0:T(8,128)(2,1)S(1)} %get-tuple-element.104.refs_1_.refs_2_, ...), custom_call_target="tpu_custom_call" | custom-call | flops 1 | bytes 1 | tf_op jit(solution)/shard_map/shard_product/pallas_call | solution.py:216
  83.2 1.3 %collective-permute-start.30 = (s16[1312,256]{1,0:T(8,128)(2,1)S(1)}, s16[1312,256]{1,0:T(8,128)(2,1)}, u32[]{:S(2)}, u32[]{:S(2)}) collective-permute-start(s16[1312,256]{1,0:T(8,128)(2,1)S(1)} %get-tuple-element.137), channel_id=1, source_target_pairs={{0,2},{1,3},{4,6},{5,7},{8,10},{9,11},{12,14},{13,15},{18,16},{19,... | collective-permute-start | bytes 2015240 | tf_op jit(solution)/shard_map/ppermute | solution.py:475
  84.5 7.3 %collective-permute-done.26.refs_3_ = bf16[5648,128]{1,0:T(8,128)(2,1)S(1)} collective-permute-done((bf16[5648,128]{1,0:T(8,128)(2,1)S(1)}, bf16[5648,128]{1,0:T(8,128)(2,1)S(1)}, u32[]{:S(2)}, u32[]{:S(2)}) %collective-permute-start.26) | collective-permute-done | bytes 1445920 | tf_op jit(solution)/shard_map/ppermute | solution.py:475
  91.7 4.4 %shard_product.9 = (f32[1024,256]{1,0:T(8,128)}, s16[1312,256]{1,0:T(8,128)(2,1)S(1)}, f32[8,128]{1,0:T(8,128)S(1)}) custom-call(s32[10]{0:T(128)S(1)} %stack.37.picks_ref, f32[8,128]{1,0:T(8,128)S(1)} %get-tuple-element.123.refs_0_, bf16[1024,2048]{1,0:T(8,128)(2,1)S(1)} %get-tuple-element.104.refs_1_.refs_2_, ...), custom_call_target="tpu_custom_call" | custom-call | flops 1 | bytes 1 | tf_op jit(solution)/shard_map/shard_product/pallas_call | solution.py:216
  96.2 1.3 %collective-permute-start.31 = (s16[1312,256]{1,0:T(8,128)(2,1)S(1)}, s16[1312,256]{1,0:T(8,128)(2,1)}, u32[]{:S(2)}, u32[]{:S(2)}) collective-permute-start(s16[1312,256]{1,0:T(8,128)(2,1)S(1)} %get-tuple-element.139), channel_id=1, source_target_pairs={{1,3},{5,7},{26,24},{30,28}} | collective-permute-start | bytes 2015240 | tf_op jit(solution)/shard_map/ppermute | solution.py:475
  97.5 0.1 collective-permute-start.27
  97.5 1.2 %collective-permute-done.27.refs_1_ = f32[8,128]{1,0:T(8,128)S(1)} collective-permute-done((f32[8,128]{1,0:T(8,128)S(1)}, f32[8,128]{1,0:T(8,128)S(1)}, u32[]{:S(2)}, u32[]{:S(2)}) %collective-permute-start.27) | collective-permute-done | bytes 4128 | tf_op jit(solution)/shard_map/ppermute | solution.py:525
  98.7 1.2 %add_coded.1 = (bf16[1024,256]{1,0:T(8,128)(2,1)}, f32[8,128]{1,0:T(8,128)S(1)}) custom-call(f32[8,128]{1,0:T(8,128)S(1)} %get-tuple-element.125.refs_0_, f32[8,128]{1,0:T(8,128)S(1)} %collective-permute-done.27.refs_1_, f32[1024,256]{1,0:T(8,128)S(1)} %get-tuple-element.126.refs_2_, s16[1312,256]{1,0:T(8,128)(2,1)S(1)} %collective-permute-done.25.refs_3_), custom_call_target="tpu_custom_call" | custom-call | flops 1 | bytes 1 | tf_op jit(solution)/shard_map/add_coded/pallas_call | solution.py:312
  99.9 3.5 %collective-permute-start.28 = (f32[8,128]{1,0:T(8,128)S(1)}, f32[8,128]{1,0:T(8,128)S(1)}, u32[]{:S(2)}, u32[]{:S(2)}) collective-permute-start(f32[8,128]{1,0:T(8,128)S(1)} %get-tuple-element.129), channel_id=1, source_target_pairs={{0,2},{2,0},{1,3},{3,1},{4,6},{6,4},{5,7},{7,5},{8,10},{10,8},{9,1... | collective-permute-start | bytes 12296 | tf_op jit(solution)/shard_map/ppermute | solution.py:526
  103.4 5.6 %collective-permute-done.28 = f32[8,128]{1,0:T(8,128)S(1)} collective-permute-done((f32[8,128]{1,0:T(8,128)S(1)}, f32[8,128]{1,0:T(8,128)S(1)}, u32[]{:S(2)}, u32[]{:S(2)}) %collective-permute-start.28) | collective-permute-done | bytes 4128 | tf_op jit(solution)/shard_map/ppermute | solution.py:526
  109.0 0.6 add_reduce_fusion
  110.2 0.0 collective-permute-done.29
  110.2 0.0 collective-permute-done.30
  110.2 0.0 collective-permute-done.31
  110.3 3.8 %conditional.1 = (bf16[1024,512]{1,0:T(8,128)(2,1)}) conditional(s32[]{:T(128)} %convert_element_type.32, (s32[2]{0:T(128)S(1)}, f32[1024,256]{1,0:T(8,128)}, s16[656,256]{1,0:T(8,128)(2,1)}, s16[1968,256]{1,0:T(8,128)(2,1)}, f32[1024,256]{1,0:T(8,128)}, /*index=5*/bf16[1024,256]{1,0:T(8,128)(2,1)}, f32[1024,256]{1,0:T(8,128)}, ...), branch_computations={%region_1.2_spmd, %region_2.3_spmd} | conditional | flops 8594653184 | bytes 206655584 | solution.py:535
  110.3 3.5 %lay_out.1 = bf16[1024,512]{1,0:T(8,128)(2,1)} custom-call(s32[2]{0:T(128)S(1)} %get-tuple-element.36.place_ref, f32[1024,256]{1,0:T(8,128)} %get-tuple-element.37.refs_0_, s16[656,256]{1,0:T(8,128)(2,1)} %get-tuple-element.38.refs_1_, s16[1968,256]{1,0:T(8,128)(2,1)} %get-tuple-element.39.refs_2_, f32[1024,256]{1,0:T(8,128)} %get-tuple-element.40.refs_3_, ...), custom_call_target="tpu_custom_call" | custom-call | flops 1 | bytes 1 | tf_op jit(solution)/shard_map/cond/branch_0_fun/lay_out/pallas_call | solution.py:384
  (23 shorter events, 0.0 us)
Async XLA Ops:
  0.0 2.9 %collective-permute-start.11 = (bf16[2048,256]{1,0:T(8,128)(2,1)}, bf16[2048,256]{1,0:T(8,128)(2,1)S(1)}, u32[]{:S(2)}, u32[]{:S(2)}) collective-permute-start(bf16[2048,256]{1,0:T(8,128)(2,1)} %refs_2_.2), channel_id=1, source_target_pairs={{0,1},{1,0},{2,3},{3,2},{4,5},{5,4},{6,7},{7,6},{8,9},{9,8},{10,11... | collective-permute-start | bytes 3145736 | tf_op jit(solution)/shard_map/ppermute | solution.py:491
  0.0 2.9 %collective-permute-start.10 = (s32[2,16]{1,0:T(2,128)}, s32[2,16]{1,0:T(2,128)S(1)}, u32[]{:S(2)}, u32[]{:S(2)}) collective-permute-start(s32[2,16]{1,0:T(2,128)} %bitcast.37), channel_id=1, source_target_pairs={{0,1},{1,0},{2,3},{3,2},{4,5},{5,4},{6,7},{7,6},{8,9},{9,8},{10,11... | collective-permute-start | bytes 392 | tf_op jit(solution)/shard_map/ppermute | solution.py:492
  0.5 4.3 %collective-permute-start.12 = (s32[8,16]{1,0:T(8,128)}, s32[8,16]{1,0:T(8,128)S(1)}, u32[]{:S(2)}, u32[]{:S(2)}) collective-permute-start(s32[8,16]{1,0:T(8,128)} %refs_0_.1), channel_id=1, source_target_pairs={{0,1},{1,0},{2,3},{3,2},{4,5},{5,4},{6,7},{7,6},{8,9},{9,8},{10,11... | collective-permute-start | bytes 1544 | tf_op jit(solution)/shard_map/ppermute | solution.py:493
  4.8 11.6 %copy-start = (bf16[5648,128]{1,0:T(8,128)(2,1)}, bf16[5648,128]{1,0:T(8,128)(2,1)S(1)}, u32[]{:S(2)}) copy-start(bf16[5648,128]{1,0:T(8,128)(2,1)S(1)} %pack_tiles.1.refs_3_) | copy-start | bytes 4337668
  4.8 7.4 %collective-permute-start.16 = (bf16[1024,2048]{1,0:T(8,128)(2,1)}, bf16[1024,2048]{1,0:T(8,128)(2,1)S(1)}, u32[]{:S(2)}, u32[]{:S(2)}) collective-permute-start(bf16[1024,2048]{1,0:T(8,128)(2,1)} %refs_2_.3), channel_id=1, source_target_pairs={{0,1},{1,0},{2,3},{3,2},{4,5},{5,4},{6,7},{7,6},{8,9},{9,8},{10,11... | collective-permute-start | bytes 12582920 | tf_op jit(solution)/shard_map/ppermute | solution.py:497
  5.0 11.4 %collective-permute-start.13 = (bf16[5648,128]{1,0:T(8,128)(2,1)S(1)}, bf16[5648,128]{1,0:T(8,128)(2,1)S(1)}, u32[]{:S(2)}, u32[]{:S(2)}) collective-permute-start(bf16[5648,128]{1,0:T(8,128)(2,1)S(1)} %pack_tiles.1.refs_3_), channel_id=1, source_target_pairs={{0,4},{2,6},{4,0},{6,2},{9,13},{11,15},{13,9},{15,11},{16,20},{18,... | collective-permute-start | bytes 4337672 | tf_op jit(solution)/shard_map/ppermute | solution.py:475
  5.8 20.4 %collective-permute-start.14 = (bf16[5648,128]{1,0:T(8,128)(2,1)S(1)}, bf16[5648,128]{1,0:T(8,128)(2,1)S(1)}, u32[]{:S(2)}, u32[]{:S(2)}) collective-permute-start(bf16[5648,128]{1,0:T(8,128)(2,1)S(1)} %pack_tiles.1.refs_3_), channel_id=1, source_target_pairs={{1,8},{3,10},{5,12},{7,14},{8,1},{10,3},{12,5},{14,7},{17,24},{19,... | collective-permute-start | bytes 4337672 | tf_op jit(solution)/shard_map/ppermute | solution.py:475
  8.1 18.1 %collective-permute-start.15 = (bf16[5648,128]{1,0:T(8,128)(2,1)S(1)}, bf16[5648,128]{1,0:T(8,128)(2,1)S(1)}, u32[]{:S(2)}, u32[]{:S(2)}) collective-permute-start(bf16[5648,128]{1,0:T(8,128)(2,1)S(1)} %pack_tiles.1.refs_3_), channel_id=1, source_target_pairs={{9,17},{11,19},{13,21},{15,23},{16,8},{18,10},{20,12},{22,14}} | collective-permute-start | bytes 4337672 | tf_op jit(solution)/shard_map/ppermute | solution.py:475
  16.5 35.6 %copy-start.9 = (bf16[5648,128]{1,0:T(8,128)(2,1)}, bf16[5648,128]{1,0:T(8,128)(2,1)S(1)}, u32[]{:S(2)}) copy-start(bf16[5648,128]{1,0:T(8,128)(2,1)S(1)} %collective-permute-done.13.refs_4_) | copy-start | bytes 4337668
  26.1 4.9 %copy-start.8 = (bf16[5648,128]{1,0:T(8,128)(2,1)}, bf16[5648,128]{1,0:T(8,128)(2,1)S(1)}, u32[]{:S(2)}) copy-start(bf16[5648,128]{1,0:T(8,128)(2,1)S(1)} %collective-permute-done.14.refs_4_) | copy-start | bytes 4337668
  26.2 10.9 %copy-start.5 = (bf16[5648,128]{1,0:T(8,128)(2,1)}, bf16[5648,128]{1,0:T(8,128)(2,1)S(1)}, u32[]{:S(2)}) copy-start(bf16[5648,128]{1,0:T(8,128)(2,1)S(1)} %collective-permute-done.15.refs_5_) | copy-start | bytes 4337668
  26.2 20.9 %collective-permute-start.17 = (bf16[5648,128]{1,0:T(8,128)(2,1)S(1)}, bf16[5648,128]{1,0:T(8,128)(2,1)S(1)}, u32[]{:S(2)}, u32[]{:S(2)}) collective-permute-start(bf16[5648,128]{1,0:T(8,128)(2,1)S(1)} %collective-permute-done.14.refs_4_), channel_id=1, source_target_pairs={{1,5},{3,7},{5,1},{7,3},{8,12},{10,14},{12,8},{14,10},{17,21},{19,... | collective-permute-start | bytes 4337672 | tf_op jit(solution)/shard_map/ppermute | solution.py:475
  29.6 17.5 %collective-permute-start.18 = (bf16[5648,128]{1,0:T(8,128)(2,1)S(1)}, bf16[5648,128]{1,0:T(8,128)(2,1)S(1)}, u32[]{:S(2)}, u32[]{:S(2)}) collective-permute-start(bf16[5648,128]{1,0:T(8,128)(2,1)S(1)} %collective-permute-done.14.refs_4_), channel_id=1, source_target_pairs={{8,16},{10,18},{12,20},{14,22},{17,9},{19,11},{21,13},{23,15}} | collective-permute-start | bytes 4337672 | tf_op jit(solution)/shard_map/ppermute | solution.py:475
  30.3 16.8 %collective-permute-start.19 = (bf16[5648,128]{1,0:T(8,128)(2,1)S(1)}, bf16[5648,128]{1,0:T(8,128)(2,1)S(1)}, u32[]{:S(2)}, u32[]{:S(2)}) collective-permute-start(bf16[5648,128]{1,0:T(8,128)(2,1)S(1)} %collective-permute-done.15.refs_5_), channel_id=1, source_target_pairs={{8,0},{10,2},{12,4},{14,6},{17,25},{19,27},{21,29},{23,31}} | collective-permute-start | bytes 4337672 | tf_op jit(solution)/shard_map/ppermute | solution.py:475
  37.1 7.6 %collective-permute-start.20 = (s16[656,256]{1,0:T(8,128)(2,1)S(1)}, s16[656,256]{1,0:T(8,128)(2,1)S(1)}, u32[]{:S(2)}, u32[]{:S(2)}) collective-permute-start(s16[656,256]{1,0:T(8,128)(2,1)S(1)} %get-tuple-element.106), channel_id=1, source_target_pairs={{2,0},{3,1},{6,4},{7,5},{10,8},{11,9},{14,12},{15,13},{16,18},{17,... | collective-permute-start | bytes 1007624 | tf_op jit(solution)/shard_map/ppermute | solution.py:475
  44.7 5.2 %copy-start.15 = (s16[656,256]{1,0:T(8,128)(2,1)}, s16[656,256]{1,0:T(8,128)(2,1)S(1)}, u32[]{:S(2)}) copy-start(s16[656,256]{1,0:T(8,128)(2,1)S(1)} %collective-permute-done.20) | copy-start | bytes 1007620
  47.1 5.0 %copy-start.10 = (bf16[5648,128]{1,0:T(8,128)(2,1)}, bf16[5648,128]{1,0:T(8,128)(2,1)S(1)}, u32[]{:S(2)}) copy-start(bf16[5648,128]{1,0:T(8,128)(2,1)S(1)} %collective-permute-done.17.refs_5_) | copy-start | bytes 4337668
  47.1 3.6 %copy-start.6 = (bf16[5648,128]{1,0:T(8,128)(2,1)}, bf16[5648,128]{1,0:T(8,128)(2,1)S(1)}, u32[]{:S(2)}) copy-start(bf16[5648,128]{1,0:T(8,128)(2,1)S(1)} %collective-permute-done.18.refs_3_) | copy-start | bytes 4337668
  47.1 3.6 %copy-start.7 = (bf16[5648,128]{1,0:T(8,128)(2,1)}, bf16[5648,128]{1,0:T(8,128)(2,1)S(1)}, u32[]{:S(2)}) copy-start(bf16[5648,128]{1,0:T(8,128)(2,1)S(1)} %collective-permute-done.19.refs_4_) | copy-start | bytes 4337668
  47.1 11.0 %collective-permute-start.21 = (bf16[5648,128]{1,0:T(8,128)(2,1)S(1)}, bf16[5648,128]{1,0:T(8,128)(2,1)S(1)}, u32[]{:S(2)}, u32[]{:S(2)}) collective-permute-start(bf16[5648,128]{1,0:T(8,128)(2,1)S(1)} %collective-permute-done.19.refs_4_), channel_id=1, source_target_pairs={{0,4},{2,6},{4,0},{6,2},{25,29},{27,31},{29,25},{31,27}} | collective-permute-start | bytes 4337672 | tf_op jit(solution)/shard_map/ppermute | solution.py:475
  47.9 22.9 %collective-permute-start.22 = (bf16[5648,128]{1,0:T(8,128)(2,1)S(1)}, bf16[5648,128]{1,0:T(8,128)(2,1)S(1)}, u32[]{:S(2)}, u32[]{:S(2)}) collective-permute-start(bf16[5648,128]{1,0:T(8,128)(2,1)S(1)} %collective-permute-done.18.refs_3_), channel_id=1, source_target_pairs={{9,1},{11,3},{13,5},{15,7},{16,24},{18,26},{20,28},{22,30}} | collective-permute-start | bytes 4337672 | tf_op jit(solution)/shard_map/ppermute | solution.py:475
  49.2 21.6 %collective-permute-start.23 = (bf16[5648,128]{1,0:T(8,128)(2,1)S(1)}, bf16[5648,128]{1,0:T(8,128)(2,1)S(1)}, u32[]{:S(2)}, u32[]{:S(2)}) collective-permute-start(bf16[5648,128]{1,0:T(8,128)(2,1)S(1)} %collective-permute-done.18.refs_3_), channel_id=1, source_target_pairs={{9,13},{11,15},{13,9},{15,11},{16,20},{18,22},{20,16},{22,18}} | collective-permute-start | bytes 4337672 | tf_op jit(solution)/shard_map/ppermute | solution.py:475
  50.0 20.8 %collective-permute-start.24 = (bf16[5648,128]{1,0:T(8,128)(2,1)S(1)}, bf16[5648,128]{1,0:T(8,128)(2,1)S(1)}, u32[]{:S(2)}, u32[]{:S(2)}) collective-permute-start(bf16[5648,128]{1,0:T(8,128)(2,1)S(1)} %collective-permute-done.13.refs_4_), channel_id=1, source_target_pairs={{9,17},{11,19},{13,21},{15,23},{16,8},{18,10},{20,12},{22,14}} | collective-permute-start | bytes 4337672 | tf_op jit(solution)/shard_map/ppermute | solution.py:475
  51.3 6.8 %collective-permute-start.25 = (s16[1312,256]{1,0:T(8,128)(2,1)S(1)}, s16[1312,256]{1,0:T(8,128)(2,1)S(1)}, u32[]{:S(2)}, u32[]{:S(2)}) collective-permute-start(s16[1312,256]{1,0:T(8,128)(2,1)S(1)} %get-tuple-element.112), channel_id=1, source_target_pairs={{0,2},{4,6},{8,10},{9,11},{12,14},{13,15},{18,16},{19,17},{22,20},... | collective-permute-start | bytes 2015240 | tf_op jit(solution)/shard_map/ppermute | solution.py:475
  58.1 19.5 %copy-start.12 = (bf16[5648,128]{1,0:T(8,128)(2,1)}, bf16[5648,128]{1,0:T(8,128)(2,1)S(1)}, u32[]{:S(2)}) copy-start(bf16[5648,128]{1,0:T(8,128)(2,1)S(1)} %collective-permute-done.21.refs_4_) | copy-start | bytes 4337668
  70.7 6.9 %copy-start.11 = (bf16[5648,128]{1,0:T(8,128)(2,1)}, bf16[5648,128]{1,0:T(8,128)(2,1)S(1)}, u32[]{:S(2)}) copy-start(bf16[5648,128]{1,0:T(8,128)(2,1)S(1)} %collective-permute-done.22.refs_6_) | copy-start | bytes 4337668
  70.8 6.9 %copy-start.13 = (bf16[5648,128]{1,0:T(8,128)(2,1)}, bf16[5648,128]{1,0:T(8,128)(2,1)S(1)}, u32[]{:S(2)}) copy-start(bf16[5648,128]{1,0:T(8,128)(2,1)S(1)} %collective-permute-done.23.refs_3_) | copy-start | bytes 4337668
  70.8 6.9 %copy-start.14 = (bf16[5648,128]{1,0:T(8,128)(2,1)}, bf16[5648,128]{1,0:T(8,128)(2,1)S(1)}, u32[]{:S(2)}) copy-start(bf16[5648,128]{1,0:T(8,128)(2,1)S(1)} %collective-permute-done.24.refs_5_) | copy-start | bytes 4337668
  70.8 20.9 %collective-permute-start.26 = (bf16[5648,128]{1,0:T(8,128)(2,1)S(1)}, bf16[5648,128]{1,0:T(8,128)(2,1)S(1)}, u32[]{:S(2)}, u32[]{:S(2)}) collective-permute-start(bf16[5648,128]{1,0:T(8,128)(2,1)S(1)} %collective-permute-done.22.refs_6_), channel_id=1, source_target_pairs={{1,5},{3,7},{5,1},{7,3},{24,28},{26,30},{28,24},{30,26}} | collective-permute-start | bytes 4337672 | tf_op jit(solution)/shard_map/ppermute | solution.py:475
  73.2 37.0 %collective-permute-start.29 = (s16[1968,256]{1,0:T(8,128)(2,1)S(1)}, s16[1968,256]{1,0:T(8,128)(2,1)}, u32[]{:S(2)}, u32[]{:S(2)}) collective-permute-start(s16[1968,256]{1,0:T(8,128)(2,1)S(1)} %get-tuple-element.133), channel_id=1, source_target_pairs={{2,0},{3,1},{6,4},{7,5},{10,8},{11,9},{14,12},{15,13},{16,18},{17,... | collective-permute-start | bytes 3022856 | tf_op jit(solution)/shard_map/ppermute | solution.py:475
  83.2 27.1 %collective-permute-start.30 = (s16[1312,256]{1,0:T(8,128)(2,1)S(1)}, s16[1312,256]{1,0:T(8,128)(2,1)}, u32[]{:S(2)}, u32[]{:S(2)}) collective-permute-start(s16[1312,256]{1,0:T(8,128)(2,1)S(1)} %get-tuple-element.137), channel_id=1, source_target_pairs={{0,2},{1,3},{4,6},{5,7},{8,10},{9,11},{12,14},{13,15},{18,16},{19,... | collective-permute-start | bytes 2015240 | tf_op jit(solution)/shard_map/ppermute | solution.py:475
  91.7 18.5 %copy-start.4 = (bf16[2048,256]{1,0:T(8,128)(2,1)S(1)}, bf16[2048,256]{1,0:T(8,128)(2,1)}, u32[]{:S(2)}) copy-start(bf16[2048,256]{1,0:T(8,128)(2,1)} %refs_2_.2) | copy-start | bytes 3145732
  91.7 18.5 %copy-start.16 = (s32[8,16]{1,0:T(8,128)S(1)}, s32[8,16]{1,0:T(8,128)}, u32[]{:S(2)}) copy-start(s32[8,16]{1,0:T(8,128)} %refs_0_.1) | copy-start | bytes 1540
  91.7 18.5 %copy-start.17 = (s32[16,2]{0,1:T(2,128)S(1)}, s32[16,2]{0,1:T(2,128)}, u32[]{:S(2)}) copy-start(s32[16,2]{0,1:T(2,128)} %param.9) | copy-start | bytes 388
  96.2 14.1 %collective-permute-start.31 = (s16[1312,256]{1,0:T(8,128)(2,1)S(1)}, s16[1312,256]{1,0:T(8,128)(2,1)}, u32[]{:S(2)}, u32[]{:S(2)}) collective-permute-start(s16[1312,256]{1,0:T(8,128)(2,1)S(1)} %get-tuple-element.139), channel_id=1, source_target_pairs={{1,3},{5,7},{26,24},{30,28}} | collective-permute-start | bytes 2015240 | tf_op jit(solution)/shard_map/ppermute | solution.py:475
  97.5 1.2 %collective-permute-start.27 = (f32[8,128]{1,0:T(8,128)S(1)}, f32[8,128]{1,0:T(8,128)S(1)}, u32[]{:S(2)}, u32[]{:S(2)}) collective-permute-start(f32[8,128]{1,0:T(8,128)S(1)} %get-tuple-element.125.refs_0_), channel_id=1, source_target_pairs={{0,1},{1,0},{2,3},{3,2},{4,5},{5,4},{6,7},{7,6},{8,9},{9,8},{10,11... | collective-permute-start | bytes 12296 | tf_op jit(solution)/shard_map/ppermute | solution.py:525
  99.9 9.1 %collective-permute-start.28 = (f32[8,128]{1,0:T(8,128)S(1)}, f32[8,128]{1,0:T(8,128)S(1)}, u32[]{:S(2)}, u32[]{:S(2)}) collective-permute-start(f32[8,128]{1,0:T(8,128)S(1)} %get-tuple-element.129), channel_id=1, source_target_pairs={{0,2},{2,0},{1,3},{3,1},{4,6},{6,4},{5,7},{7,5},{8,10},{10,8},{9,1... | collective-permute-start | bytes 12296 | tf_op jit(solution)/shard_map/ppermute | solution.py:526

commit v9 on v8

--- a/solution.py
+++ b/solution.py
@@ -526,7 +526,8 @@
     flags = [token, lax.ppermute(token, "col", CHIPS_Y)]
     a = [a_sum, (a_far, 0), (ab_far, 0)]
     b = [b_sum, *both_halves(b_sum, ab_far, a_rest.shape[0])]
-    d = [d_sum, *both_halves(d_sum, d_far)]
+    d_both, _ = add_coded((d_sum,), [both_halves(d_sum, d_far)])
+    d = [d_both]
     e = [e_sum, *both_halves(e_sum, e_far)]
 
     def finish():

time: 115 us -> 114 us (level)
    pallas_call x1 -> x2, Pallas kernels: 1.2 us -> 2.38 us  [add_coded(): call(kernel, 'add_coded', out_shape=tuple((jax.ShapeDtypeStruct(part.shap...]
where the time goes in v9:
time: 114 us
  waiting for transfers between devices  49.5 us (43%)
  Pallas kernels  33 us (29%)
  starting transfers between devices  28.9 us (25%)
  between operations  1.24 us (1%)
    ppermute x16, waiting for transfers between devices, move(): return lax.ppermute(value, AXES, pairs)  37.6 us
    ppermute x16, starting transfers between devices, move(): return lax.ppermute(value, AXES, pairs)  25.4 us
    pallas_call x5, Pallas kernels, shard_product(): call(kernel, 'shard_product', out_shape=(jax.ShapeDtypeStruct((rows, wide...  21.5 us
    ppermute x1, waiting for transfers between devices, sparse_ladder(): flags = [token, lax.ppermute(token, 'col', CHIPS_Y)]  5.14 us
    pallas_call x1, Pallas kernels, mask_tiles(): call(kernel, 'mask_tiles', out_shape=tuple((jax.ShapeDtypeStruct(part.sha...  4.17 us
    ppermute x1, waiting for transfers between devices, sparse_ladder(): other_amps = lax.ppermute(amplitudes_now, 'col', CORES)  3.37 us
    pallas_call x1, Pallas kernels, lay_out(): call(kernel, 'lay_out', out_shape=pltpu.HBM((rows, 2 * width), jnp.bfloat...  3.02 us
    ppermute x1, starting transfers between devices, sparse_ladder(): flags = [token, lax.ppermute(token, 'col', CHIPS_Y)]  2.68 us
  transfers between devices with their start and end apart: 22, of which 9 were waited for; matrix products, arithmetic and copies ran while one was open for 1% of the time, Pallas kernels for 26%

profile of v9, /device:TPU:24, one launch (start us, length us, event | category | flops | bytes accessed | tf_op | source)
XLA Modules:
  0.0 113.7 jit_solution(3630927506263542372)
XLA Ops:
  0.0 0.0 collective-permute-start.11
  0.0 0.5 collective-permute-start.10
  0.5 0.0 collective-permute-start.12
  0.5 0.1 pad_add_fusion
  0.6 0.1 stack.37.picks_ref
  0.7 2.2 %collective-permute-done.10.refs_1_ = s32[2,16]{1,0:T(2,128)S(1)} collective-permute-done((s32[2,16]{1,0:T(2,128)}, s32[2,16]{1,0:T(2,128)S(1)}, u32[]{:S(2)}, u32[]{:S(2)}) %collective-permute-start.10) | collective-permute-done | bytes 160 | tf_op jit(solution)/shard_map/ppermute | solution.py:492
  2.9 0.0 collective-permute-done.11.refs_3_
  2.9 1.9 %pack_tiles.1.refs_3_ = bf16[5648,128]{1,0:T(8,128)(2,1)S(1)} custom-call(s32[1]{0:T(128)} %bitcast.2.swap_ref, s32[2,16]{1,0:T(2,128)} %bitcast.38, s32[2,16]{1,0:T(2,128)S(1)} %collective-permute-done.10.refs_1_, bf16[2048,256]{1,0:T(8,128)(2,1)} %refs_2_.2, bf16[2048,256]{1,0:T(8,128)(2,1)S(1)} %collective-permute-done.11.refs_3_), custom_call_target="tpu_custom_call" | custom-call | flops 1 | bytes 1 | tf_op jit(solution)/shard_map/pack_tiles/pallas_call | solution.py:101
  4.8 0.0 copy-start
  4.8 0.0 collective-permute-done.12.refs_1_
  4.8 0.2 collective-permute-start.16
  5.0 0.7 collective-permute-start.13
  5.8 2.3 %collective-permute-start.14 = (bf16[5648,128]{1,0:T(8,128)(2,1)S(1)}, bf16[5648,128]{1,0:T(8,128)(2,1)S(1)}, u32[]{:S(2)}, u32[]{:S(2)}) collective-permute-start(bf16[5648,128]{1,0:T(8,128)(2,1)S(1)} %pack_tiles.1.refs_3_), channel_id=1, source_target_pairs={{1,8},{3,10},{5,12},{7,14},{8,1},{10,3},{12,5},{14,7},{17,24},{19,... | collective-permute-start | bytes 4337672 | tf_op jit(solution)/shard_map/ppermute | solution.py:475
  8.1 0.8 collective-permute-start.15
  8.9 3.4 %collective-permute-done.16.refs_3_ = bf16[1024,2048]{1,0:T(8,128)(2,1)S(1)} collective-permute-done((bf16[1024,2048]{1,0:T(8,128)(2,1)}, bf16[1024,2048]{1,0:T(8,128)(2,1)S(1)}, u32[]{:S(2)}, u32[]{:S(2)}) %collective-permute-start.16) | collective-permute-done | bytes 4194336 | tf_op jit(solution)/shard_map/ppermute | solution.py:497
  12.2 4.2 %mask_tiles.1 = (bf16[1024,2048]{1,0:T(8,128)(2,1)S(1)}, bf16[1024,2048]{1,0:T(8,128)(2,1)S(1)}, f32[8,128]{1,0:T(8,128)S(1)}) custom-call(s32[8,16]{1,0:T(8,128)} %refs_0_.1, s32[8,16]{1,0:T(8,128)S(1)} %collective-permute-done.12.refs_1_, bf16[1024,2048]{1,0:T(8,128)(2,1)} %refs_2_.3, bf16[1024,2048]{1,0:T(8,128)(2,1)S(1)} %collective-permute-done.16.refs_3_), custom_call_target="tpu_custom_call" | custom-call | flops 1 | bytes 1 | tf_op jit(solution)/shard_map/mask_tiles/pallas_call | solution.py:131
  16.4 0.0 collective-permute-done.13.refs_4_
  16.4 9.7 %collective-permute-done.14.refs_4_ = bf16[5648,128]{1,0:T(8,128)(2,1)S(1)} collective-permute-done((bf16[5648,128]{1,0:T(8,128)(2,1)S(1)}, bf16[5648,128]{1,0:T(8,128)(2,1)S(1)}, u32[]{:S(2)}, u32[]{:S(2)}) %collective-permute-start.14) | collective-permute-done | bytes 1445920 | tf_op jit(solution)/shard_map/ppermute | solution.py:475
  26.1 0.0 collective-permute-done.15.refs_5_
  26.1 3.4 %collective-permute-start.17 = (bf16[5648,128]{1,0:T(8,128)(2,1)S(1)}, bf16[5648,128]{1,0:T(8,128)(2,1)S(1)}, u32[]{:S(2)}, u32[]{:S(2)}) collective-permute-start(bf16[5648,128]{1,0:T(8,128)(2,1)S(1)} %collective-permute-done.14.refs_4_), channel_id=1, source_target_pairs={{1,5},{3,7},{5,1},{7,3},{8,12},{10,14},{12,8},{14,10},{17,21},{19,... | collective-permute-start | bytes 4337672 | tf_op jit(solution)/shard_map/ppermute | solution.py:475
  29.5 0.8 collective-permute-start.18
  30.3 0.8 collective-permute-start.19
  31.1 6.0 %shard_product.5 = (f32[1024,256]{1,0:T(8,128)}, s16[656,256]{1,0:T(8,128)(2,1)S(1)}, s16[656,256]{1,0:T(8,128)(2,1)S(1)}, f32[8,128]{1,0:T(8,128)S(1)}) custom-call(s32[10]{0:T(128)S(1)} %stack.37.picks_ref, f32[8,128]{1,0:T(8,128)S(1)} %get-tuple-element.101.refs_0_, bf16[1024,2048]{1,0:T(8,128)(2,1)S(1)} %get-tuple-element.102.refs_1_.refs_2_, ...), custom_call_target="tpu_custom_call" | custom-call | flops 1 | bytes 1 | tf_op jit(solution)/shard_map/shard_product/pallas_call | solution.py:216
  37.1 3.0 %collective-permute-start.20 = (s16[656,256]{1,0:T(8,128)(2,1)S(1)}, s16[656,256]{1,0:T(8,128)(2,1)S(1)}, u32[]{:S(2)}, u32[]{:S(2)}) collective-permute-start(s16[656,256]{1,0:T(8,128)(2,1)S(1)} %get-tuple-element.104), channel_id=1, source_target_pairs={{2,0},{3,1},{6,4},{7,5},{10,8},{11,9},{14,12},{15,13},{16,18},{17,... | collective-permute-start | bytes 1007624 | tf_op jit(solution)/shard_map/ppermute | solution.py:475
  40.1 4.6 %collective-permute-done.20 = s16[656,256]{1,0:T(8,128)(2,1)S(1)} collective-permute-done((s16[656,256]{1,0:T(8,128)(2,1)S(1)}, s16[656,256]{1,0:T(8,128)(2,1)S(1)}, u32[]{:S(2)}, u32[]{:S(2)}) %collective-permute-start.20) | collective-permute-done | bytes 335904 | tf_op jit(solution)/shard_map/ppermute | solution.py:475
  44.7 2.4 %collective-permute-done.17.refs_5_ = bf16[5648,128]{1,0:T(8,128)(2,1)S(1)} collective-permute-done((bf16[5648,128]{1,0:T(8,128)(2,1)S(1)}, bf16[5648,128]{1,0:T(8,128)(2,1)S(1)}, u32[]{:S(2)}, u32[]{:S(2)}) %collective-permute-start.17) | collective-permute-done | bytes 1445920 | tf_op jit(solution)/shard_map/ppermute | solution.py:475
  47.1 0.0 collective-permute-done.18.refs_3_
  47.1 0.0 collective-permute-done.19.refs_4_
  47.1 0.0 copy-start.7
  47.1 0.8 collective-permute-start.21
  47.9 1.3 %collective-permute-start.22 = (bf16[5648,128]{1,0:T(8,128)(2,1)S(1)}, bf16[5648,128]{1,0:T(8,128)(2,1)S(1)}, u32[]{:S(2)}, u32[]{:S(2)}) collective-permute-start(bf16[5648,128]{1,0:T(8,128)(2,1)S(1)} %collective-permute-done.18.refs_3_), channel_id=1, source_target_pairs={{9,1},{11,3},{13,5},{15,7},{16,24},{18,26},{20,28},{22,30}} | collective-permute-start | bytes 4337672 | tf_op jit(solution)/shard_map/ppermute | solution.py:475
  49.2 0.8 collective-permute-start.23
  49.9 0.0 copy-done.15
  49.9 0.8 collective-permute-start.24
  50.7 0.0 copy-done.6
  50.7 0.0 copy-done.7
  50.7 0.6 shard_product.6
  51.3 0.7 collective-permute-start.25
  52.1 6.0 %shard_product.7 = (f32[1024,256]{1,0:T(8,128)}, s16[1968,256]{1,0:T(8,128)(2,1)S(1)}, f32[8,128]{1,0:T(8,128)S(1)}) custom-call(s32[10]{0:T(128)S(1)} %stack.37.picks_ref, s16[656,256]{1,0:T(8,128)(2,1)S(1)} %get-tuple-element.111.refs_0_, f32[8,128]{1,0:T(8,128)S(1)} %get-tuple-element.112.refs_1_, ...), custom_call_target="tpu_custom_call" | custom-call | flops 1 | bytes 1 | tf_op jit(solution)/shard_map/shard_product/pallas_call | solution.py:216
  58.0 0.0 collective-permute-done.25.refs_3_
  58.1 0.0 collective-permute-done.21.refs_4_
  58.1 12.7 %collective-permute-done.22.refs_6_ = bf16[5648,128]{1,0:T(8,128)(2,1)S(1)} collective-permute-done((bf16[5648,128]{1,0:T(8,128)(2,1)S(1)}, bf16[5648,128]{1,0:T(8,128)(2,1)S(1)}, u32[]{:S(2)}, u32[]{:S(2)}) %collective-permute-start.22) | collective-permute-done | bytes 1445920 | tf_op jit(solution)/shard_map/ppermute | solution.py:475
  70.7 0.0 collective-permute-done.23.refs_3_
  70.7 0.0 collective-permute-done.24.refs_5_
  70.7 0.0 copy-start.14
  70.8 2.5 %collective-permute-start.26 = (bf16[5648,128]{1,0:T(8,128)(2,1)S(1)}, bf16[5648,128]{1,0:T(8,128)(2,1)S(1)}, u32[]{:S(2)}, u32[]{:S(2)}) collective-permute-start(bf16[5648,128]{1,0:T(8,128)(2,1)S(1)} %collective-permute-done.22.refs_6_), channel_id=1, source_target_pairs={{1,5},{3,7},{5,1},{7,3},{24,28},{26,30},{28,24},{30,26}} | collective-permute-start | bytes 4337672 | tf_op jit(solution)/shard_map/ppermute | solution.py:475
  73.2 4.4 %collective-permute-start.29 = (s16[1968,256]{1,0:T(8,128)(2,1)S(1)}, s16[1968,256]{1,0:T(8,128)(2,1)}, u32[]{:S(2)}, u32[]{:S(2)}) collective-permute-start(s16[1968,256]{1,0:T(8,128)(2,1)S(1)} %get-tuple-element.131), channel_id=1, source_target_pairs={{2,0},{3,1},{6,4},{7,5},{10,8},{11,9},{14,12},{15,13},{16,18},{17,... | collective-permute-start | bytes 3022856 | tf_op jit(solution)/shard_map/ppermute | solution.py:475
  77.6 4.5 %shard_product.8 = (f32[1024,256]{1,0:T(8,128)S(1)}, s16[1312,256]{1,0:T(8,128)(2,1)S(1)}, f32[8,128]{1,0:T(8,128)S(1)}) custom-call(s32[10]{0:T(128)S(1)} %stack.37.picks_ref, f32[8,128]{1,0:T(8,128)S(1)} %get-tuple-element.116.refs_0_, bf16[1024,2048]{1,0:T(8,128)(2,1)S(1)} %get-tuple-element.102.refs_1_.refs_2_, ...), custom_call_target="tpu_custom_call" | custom-call | flops 1 | bytes 1 | tf_op jit(solution)/shard_map/shard_product/pallas_call | solution.py:216
  82.2 1.3 %collective-permute-start.30 = (s16[1312,256]{1,0:T(8,128)(2,1)S(1)}, s16[1312,256]{1,0:T(8,128)(2,1)S(1)}, u32[]{:S(2)}, u32[]{:S(2)}) collective-permute-start(s16[1312,256]{1,0:T(8,128)(2,1)S(1)} %get-tuple-element.135), channel_id=1, source_target_pairs={{0,2},{1,3},{4,6},{5,7},{8,10},{9,11},{12,14},{13,15},{18,16},{19,... | collective-permute-start | bytes 2015240 | tf_op jit(solution)/shard_map/ppermute | solution.py:475
  83.5 8.2 %collective-permute-done.26.refs_3_ = bf16[5648,128]{1,0:T(8,128)(2,1)S(1)} collective-permute-done((bf16[5648,128]{1,0:T(8,128)(2,1)S(1)}, bf16[5648,128]{1,0:T(8,128)(2,1)S(1)}, u32[]{:S(2)}, u32[]{:S(2)}) %collective-permute-start.26) | collective-permute-done | bytes 1445920 | tf_op jit(solution)/shard_map/ppermute | solution.py:475
  91.7 4.4 %shard_product.9 = (f32[1024,256]{1,0:T(8,128)}, s16[1312,256]{1,0:T(8,128)(2,1)S(1)}, f32[8,128]{1,0:T(8,128)S(1)}) custom-call(s32[10]{0:T(128)S(1)} %stack.37.picks_ref, f32[8,128]{1,0:T(8,128)S(1)} %get-tuple-element.121.refs_0_, bf16[1024,2048]{1,0:T(8,128)(2,1)S(1)} %get-tuple-element.102.refs_1_.refs_2_, ...), custom_call_target="tpu_custom_call" | custom-call | flops 1 | bytes 1 | tf_op jit(solution)/shard_map/shard_product/pallas_call | solution.py:216
  96.2 1.3 %collective-permute-start.31 = (s16[1312,256]{1,0:T(8,128)(2,1)S(1)}, s16[1312,256]{1,0:T(8,128)(2,1)S(1)}, u32[]{:S(2)}, u32[]{:S(2)}) collective-permute-start(s16[1312,256]{1,0:T(8,128)(2,1)S(1)} %get-tuple-element.138), channel_id=1, source_target_pairs={{1,3},{5,7},{26,24},{30,28}} | collective-permute-start | bytes 2015240 | tf_op jit(solution)/shard_map/ppermute | solution.py:475
  97.5 0.1 collective-permute-start.27
  97.5 1.2 %collective-permute-done.27.refs_1_ = f32[8,128]{1,0:T(8,128)S(1)} collective-permute-done((f32[8,128]{1,0:T(8,128)S(1)}, f32[8,128]{1,0:T(8,128)S(1)}, u32[]{:S(2)}, u32[]{:S(2)}) %collective-permute-start.27) | collective-permute-done | bytes 4128 | tf_op jit(solution)/shard_map/ppermute | solution.py:525
  98.7 1.2 %add_coded.2 = (bf16[1024,256]{1,0:T(8,128)(2,1)}, f32[8,128]{1,0:T(8,128)S(1)}) custom-call(f32[8,128]{1,0:T(8,128)S(1)} %get-tuple-element.123.refs_0_, f32[8,128]{1,0:T(8,128)S(1)} %collective-permute-done.27.refs_1_, f32[1024,256]{1,0:T(8,128)S(1)} %get-tuple-element.124.refs_2_, s16[1312,256]{1,0:T(8,128)(2,1)S(1)} %collective-permute-done.25.refs_3_), custom_call_target="tpu_custom_call" | custom-call | flops 1 | bytes 1 | tf_op jit(solution)/shard_map/add_coded/pallas_call | solution.py:312
  99.9 2.7 %collective-permute-start.28 = (f32[8,128]{1,0:T(8,128)S(1)}, f32[8,128]{1,0:T(8,128)S(1)}, u32[]{:S(2)}, u32[]{:S(2)}) collective-permute-start(f32[8,128]{1,0:T(8,128)S(1)} %get-tuple-element.127), channel_id=1, source_target_pairs={{0,2},{2,0},{1,3},{3,1},{4,6},{6,4},{5,7},{7,5},{8,10},{10,8},{9,1... | collective-permute-start | bytes 12296 | tf_op jit(solution)/shard_map/ppermute | solution.py:526
  102.6 0.0 collective-permute-done.30.refs_1_
  102.6 1.2 %add_coded.3 = (bf16[1024,256]{1,0:T(8,128)(2,1)}, f32[8,128]{1,0:T(8,128)}) custom-call(f32[1024,256]{1,0:T(8,128)S(1)} %get-tuple-element.134.refs_0_, s16[1312,256]{1,0:T(8,128)(2,1)S(1)} %collective-permute-done.30.refs_1_), custom_call_target="tpu_custom_call" | custom-call | flops 1 | bytes 1 | tf_op jit(solution)/shard_map/add_coded/pallas_call | solution.py:312
  103.8 5.1 %collective-permute-done.28 = f32[8,128]{1,0:T(8,128)S(1)} collective-permute-done((f32[8,128]{1,0:T(8,128)S(1)}, f32[8,128]{1,0:T(8,128)S(1)}, u32[]{:S(2)}, u32[]{:S(2)}) %collective-permute-start.28) | collective-permute-done | bytes 4128 | tf_op jit(solution)/shard_map/ppermute | solution.py:526
  108.9 0.6 add_reduce_fusion
  110.2 0.0 collective-permute-done.29
  110.2 0.0 collective-permute-done.31
  110.2 3.3 %conditional.1 = (bf16[1024,512]{1,0:T(8,128)(2,1)}) conditional(s32[]{:T(128)} %convert_element_type.32, (s32[2]{0:T(128)S(1)}, f32[1024,256]{1,0:T(8,128)}, s16[656,256]{1,0:T(8,128)(2,1)}, s16[1968,256]{1,0:T(8,128)(2,1)}, f32[1024,256]{1,0:T(8,128)}, /*index=5*/bf16[1024,256]{1,0:T(8,128)(2,1)}, bf16[1024,256]{1,0:T(8,128)(2,1)}, ...), branch_computations={%region_1.2_spmd, %region_2.3_spmd} | conditional | flops 8594653184 | bytes 206655584 | solution.py:536
  110.2 3.0 %lay_out.1 = bf16[1024,512]{1,0:T(8,128)(2,1)} custom-call(s32[2]{0:T(128)S(1)} %get-tuple-element.34.place_ref, f32[1024,256]{1,0:T(8,128)} %get-tuple-element.35.refs_0_, s16[656,256]{1,0:T(8,128)(2,1)} %get-tuple-element.36.refs_1_, s16[1968,256]{1,0:T(8,128)(2,1)} %get-tuple-element.37.refs_2_, f32[1024,256]{1,0:T(8,128)} %get-tuple-element.38.refs_3_, ...), custom_call_target="tpu_custom_call" | custom-call | flops 1 | bytes 1 | tf_op jit(solution)/shard_map/cond/branch_0_fun/lay_out/pallas_call | solution.py:384
  (24 shorter events, 0.0 us)
Async XLA Ops:
  0.0 2.9 %collective-permute-start.11 = (bf16[2048,256]{1,0:T(8,128)(2,1)}, bf16[2048,256]{1,0:T(8,128)(2,1)S(1)}, u32[]{:S(2)}, u32[]{:S(2)}) collective-permute-start(bf16[2048,256]{1,0:T(8,128)(2,1)} %refs_2_.2), channel_id=1, source_target_pairs={{0,1},{1,0},{2,3},{3,2},{4,5},{5,4},{6,7},{7,6},{8,9},{9,8},{10,11... | collective-permute-start | bytes 3145736 | tf_op jit(solution)/shard_map/ppermute | solution.py:491
  0.0 2.9 %collective-permute-start.10 = (s32[2,16]{1,0:T(2,128)}, s32[2,16]{1,0:T(2,128)S(1)}, u32[]{:S(2)}, u32[]{:S(2)}) collective-permute-start(s32[2,16]{1,0:T(2,128)} %bitcast.37), channel_id=1, source_target_pairs={{0,1},{1,0},{2,3},{3,2},{4,5},{5,4},{6,7},{7,6},{8,9},{9,8},{10,11... | collective-permute-start | bytes 392 | tf_op jit(solution)/shard_map/ppermute | solution.py:492
  0.5 4.3 %collective-permute-start.12 = (s32[8,16]{1,0:T(8,128)}, s32[8,16]{1,0:T(8,128)S(1)}, u32[]{:S(2)}, u32[]{:S(2)}) collective-permute-start(s32[8,16]{1,0:T(8,128)} %refs_0_.1), channel_id=1, source_target_pairs={{0,1},{1,0},{2,3},{3,2},{4,5},{5,4},{6,7},{7,6},{8,9},{9,8},{10,11... | collective-permute-start | bytes 1544 | tf_op jit(solution)/shard_map/ppermute | solution.py:493
  4.8 11.6 %copy-start = (bf16[5648,128]{1,0:T(8,128)(2,1)}, bf16[5648,128]{1,0:T(8,128)(2,1)S(1)}, u32[]{:S(2)}) copy-start(bf16[5648,128]{1,0:T(8,128)(2,1)S(1)} %pack_tiles.1.refs_3_) | copy-start | bytes 4337668
  4.8 7.4 %collective-permute-start.16 = (bf16[1024,2048]{1,0:T(8,128)(2,1)}, bf16[1024,2048]{1,0:T(8,128)(2,1)S(1)}, u32[]{:S(2)}, u32[]{:S(2)}) collective-permute-start(bf16[1024,2048]{1,0:T(8,128)(2,1)} %refs_2_.3), channel_id=1, source_target_pairs={{0,1},{1,0},{2,3},{3,2},{4,5},{5,4},{6,7},{7,6},{8,9},{9,8},{10,11... | collective-permute-start | bytes 12582920 | tf_op jit(solution)/shard_map/ppermute | solution.py:497
  5.0 11.4 %collective-permute-start.13 = (bf16[5648,128]{1,0:T(8,128)(2,1)S(1)}, bf16[5648,128]{1,0:T(8,128)(2,1)S(1)}, u32[]{:S(2)}, u32[]{:S(2)}) collective-permute-start(bf16[5648,128]{1,0:T(8,128)(2,1)S(1)} %pack_tiles.1.refs_3_), channel_id=1, source_target_pairs={{0,4},{2,6},{4,0},{6,2},{9,13},{11,15},{13,9},{15,11},{16,20},{18,... | collective-permute-start | bytes 4337672 | tf_op jit(solution)/shard_map/ppermute | solution.py:475
  5.8 20.4 %collective-permute-start.14 = (bf16[5648,128]{1,0:T(8,128)(2,1)S(1)}, bf16[5648,128]{1,0:T(8,128)(2,1)S(1)}, u32[]{:S(2)}, u32[]{:S(2)}) collective-permute-start(bf16[5648,128]{1,0:T(8,128)(2,1)S(1)} %pack_tiles.1.refs_3_), channel_id=1, source_target_pairs={{1,8},{3,10},{5,12},{7,14},{8,1},{10,3},{12,5},{14,7},{17,24},{19,... | collective-permute-start | bytes 4337672 | tf_op jit(solution)/shard_map/ppermute | solution.py:475
  8.1 18.0 %collective-permute-start.15 = (bf16[5648,128]{1,0:T(8,128)(2,1)S(1)}, bf16[5648,128]{1,0:T(8,128)(2,1)S(1)}, u32[]{:S(2)}, u32[]{:S(2)}) collective-permute-start(bf16[5648,128]{1,0:T(8,128)(2,1)S(1)} %pack_tiles.1.refs_3_), channel_id=1, source_target_pairs={{9,17},{11,19},{13,21},{15,23},{16,8},{18,10},{20,12},{22,14}} | collective-permute-start | bytes 4337672 | tf_op jit(solution)/shard_map/ppermute | solution.py:475
  16.4 35.6 %copy-start.9 = (bf16[5648,128]{1,0:T(8,128)(2,1)}, bf16[5648,128]{1,0:T(8,128)(2,1)S(1)}, u32[]{:S(2)}) copy-start(bf16[5648,128]{1,0:T(8,128)(2,1)S(1)} %collective-permute-done.13.refs_4_) | copy-start | bytes 4337668
  26.1 4.9 %copy-start.8 = (bf16[5648,128]{1,0:T(8,128)(2,1)}, bf16[5648,128]{1,0:T(8,128)(2,1)S(1)}, u32[]{:S(2)}) copy-start(bf16[5648,128]{1,0:T(8,128)(2,1)S(1)} %collective-permute-done.14.refs_4_) | copy-start | bytes 4337668
  26.1 10.9 %copy-start.5 = (bf16[5648,128]{1,0:T(8,128)(2,1)}, bf16[5648,128]{1,0:T(8,128)(2,1)S(1)}, u32[]{:S(2)}) copy-start(bf16[5648,128]{1,0:T(8,128)(2,1)S(1)} %collective-permute-done.15.refs_5_) | copy-start | bytes 4337668
  26.1 20.9 %collective-permute-start.17 = (bf16[5648,128]{1,0:T(8,128)(2,1)S(1)}, bf16[5648,128]{1,0:T(8,128)(2,1)S(1)}, u32[]{:S(2)}, u32[]{:S(2)}) collective-permute-start(bf16[5648,128]{1,0:T(8,128)(2,1)S(1)} %collective-permute-done.14.refs_4_), channel_id=1, source_target_pairs={{1,5},{3,7},{5,1},{7,3},{8,12},{10,14},{12,8},{14,10},{17,21},{19,... | collective-permute-start | bytes 4337672 | tf_op jit(solution)/shard_map/ppermute | solution.py:475
  29.5 17.5 %collective-permute-start.18 = (bf16[5648,128]{1,0:T(8,128)(2,1)S(1)}, bf16[5648,128]{1,0:T(8,128)(2,1)S(1)}, u32[]{:S(2)}, u32[]{:S(2)}) collective-permute-start(bf16[5648,128]{1,0:T(8,128)(2,1)S(1)} %collective-permute-done.14.refs_4_), channel_id=1, source_target_pairs={{8,16},{10,18},{12,20},{14,22},{17,9},{19,11},{21,13},{23,15}} | collective-permute-start | bytes 4337672 | tf_op jit(solution)/shard_map/ppermute | solution.py:475
  30.3 16.8 %collective-permute-start.19 = (bf16[5648,128]{1,0:T(8,128)(2,1)S(1)}, bf16[5648,128]{1,0:T(8,128)(2,1)S(1)}, u32[]{:S(2)}, u32[]{:S(2)}) collective-permute-start(bf16[5648,128]{1,0:T(8,128)(2,1)S(1)} %collective-permute-done.15.refs_5_), channel_id=1, source_target_pairs={{8,0},{10,2},{12,4},{14,6},{17,25},{19,27},{21,29},{23,31}} | collective-permute-start | bytes 4337672 | tf_op jit(solution)/shard_map/ppermute | solution.py:475
  37.1 7.7 %collective-permute-start.20 = (s16[656,256]{1,0:T(8,128)(2,1)S(1)}, s16[656,256]{1,0:T(8,128)(2,1)S(1)}, u32[]{:S(2)}, u32[]{:S(2)}) collective-permute-start(s16[656,256]{1,0:T(8,128)(2,1)S(1)} %get-tuple-element.104), channel_id=1, source_target_pairs={{2,0},{3,1},{6,4},{7,5},{10,8},{11,9},{14,12},{15,13},{16,18},{17,... | collective-permute-start | bytes 1007624 | tf_op jit(solution)/shard_map/ppermute | solution.py:475
  44.7 5.2 %copy-start.15 = (s16[656,256]{1,0:T(8,128)(2,1)}, s16[656,256]{1,0:T(8,128)(2,1)S(1)}, u32[]{:S(2)}) copy-start(s16[656,256]{1,0:T(8,128)(2,1)S(1)} %collective-permute-done.20) | copy-start | bytes 1007620
  47.1 5.0 %copy-start.10 = (bf16[5648,128]{1,0:T(8,128)(2,1)}, bf16[5648,128]{1,0:T(8,128)(2,1)S(1)}, u32[]{:S(2)}) copy-start(bf16[5648,128]{1,0:T(8,128)(2,1)S(1)} %collective-permute-done.17.refs_5_) | copy-start | bytes 4337668
  47.1 3.6 %copy-start.6 = (bf16[5648,128]{1,0:T(8,128)(2,1)}, bf16[5648,128]{1,0:T(8,128)(2,1)S(1)}, u32[]{:S(2)}) copy-start(bf16[5648,128]{1,0:T(8,128)(2,1)S(1)} %collective-permute-done.18.refs_3_) | copy-start | bytes 4337668
  47.1 3.6 %copy-start.7 = (bf16[5648,128]{1,0:T(8,128)(2,1)}, bf16[5648,128]{1,0:T(8,128)(2,1)S(1)}, u32[]{:S(2)}) copy-start(bf16[5648,128]{1,0:T(8,128)(2,1)S(1)} %collective-permute-done.19.refs_4_) | copy-start | bytes 4337668
  47.1 10.9 %collective-permute-start.21 = (bf16[5648,128]{1,0:T(8,128)(2,1)S(1)}, bf16[5648,128]{1,0:T(8,128)(2,1)S(1)}, u32[]{:S(2)}, u32[]{:S(2)}) collective-permute-start(bf16[5648,128]{1,0:T(8,128)(2,1)S(1)} %collective-permute-done.19.refs_4_), channel_id=1, source_target_pairs={{0,4},{2,6},{4,0},{6,2},{25,29},{27,31},{29,25},{31,27}} | collective-permute-start | bytes 4337672 | tf_op jit(solution)/shard_map/ppermute | solution.py:475
  47.9 22.9 %collective-permute-start.22 = (bf16[5648,128]{1,0:T(8,128)(2,1)S(1)}, bf16[5648,128]{1,0:T(8,128)(2,1)S(1)}, u32[]{:S(2)}, u32[]{:S(2)}) collective-permute-start(bf16[5648,128]{1,0:T(8,128)(2,1)S(1)} %collective-permute-done.18.refs_3_), channel_id=1, source_target_pairs={{9,1},{11,3},{13,5},{15,7},{16,24},{18,26},{20,28},{22,30}} | collective-permute-start | bytes 4337672 | tf_op jit(solution)/shard_map/ppermute | solution.py:475
  49.2 21.6 %collective-permute-start.23 = (bf16[5648,128]{1,0:T(8,128)(2,1)S(1)}, bf16[5648,128]{1,0:T(8,128)(2,1)S(1)}, u32[]{:S(2)}, u32[]{:S(2)}) collective-permute-start(bf16[5648,128]{1,0:T(8,128)(2,1)S(1)} %collective-permute-done.18.refs_3_), channel_id=1, source_target_pairs={{9,13},{11,15},{13,9},{15,11},{16,20},{18,22},{20,16},{22,18}} | collective-permute-start | bytes 4337672 | tf_op jit(solution)/shard_map/ppermute | solution.py:475
  49.9 20.8 %collective-permute-start.24 = (bf16[5648,128]{1,0:T(8,128)(2,1)S(1)}, bf16[5648,128]{1,0:T(8,128)(2,1)S(1)}, u32[]{:S(2)}, u32[]{:S(2)}) collective-permute-start(bf16[5648,128]{1,0:T(8,128)(2,1)S(1)} %collective-permute-done.13.refs_4_), channel_id=1, source_target_pairs={{9,17},{11,19},{13,21},{15,23},{16,8},{18,10},{20,12},{22,14}} | collective-permute-start | bytes 4337672 | tf_op jit(solution)/shard_map/ppermute | solution.py:475
  51.3 6.7 %collective-permute-start.25 = (s16[1312,256]{1,0:T(8,128)(2,1)S(1)}, s16[1312,256]{1,0:T(8,128)(2,1)S(1)}, u32[]{:S(2)}, u32[]{:S(2)}) collective-permute-start(s16[1312,256]{1,0:T(8,128)(2,1)S(1)} %get-tuple-element.110), channel_id=1, source_target_pairs={{0,2},{4,6},{8,10},{9,11},{12,14},{13,15},{18,16},{19,17},{22,20},... | collective-permute-start | bytes 2015240 | tf_op jit(solution)/shard_map/ppermute | solution.py:475
  58.1 19.6 %copy-start.12 = (bf16[5648,128]{1,0:T(8,128)(2,1)}, bf16[5648,128]{1,0:T(8,128)(2,1)S(1)}, u32[]{:S(2)}) copy-start(bf16[5648,128]{1,0:T(8,128)(2,1)S(1)} %collective-permute-done.21.refs_4_) | copy-start | bytes 4337668
  70.7 6.9 %copy-start.11 = (bf16[5648,128]{1,0:T(8,128)(2,1)}, bf16[5648,128]{1,0:T(8,128)(2,1)S(1)}, u32[]{:S(2)}) copy-start(bf16[5648,128]{1,0:T(8,128)(2,1)S(1)} %collective-permute-done.22.refs_6_) | copy-start | bytes 4337668
  70.7 6.9 %copy-start.13 = (bf16[5648,128]{1,0:T(8,128)(2,1)}, bf16[5648,128]{1,0:T(8,128)(2,1)S(1)}, u32[]{:S(2)}) copy-start(bf16[5648,128]{1,0:T(8,128)(2,1)S(1)} %collective-permute-done.23.refs_3_) | copy-start | bytes 4337668
  70.7 6.9 %copy-start.14 = (bf16[5648,128]{1,0:T(8,128)(2,1)}, bf16[5648,128]{1,0:T(8,128)(2,1)S(1)}, u32[]{:S(2)}) copy-start(bf16[5648,128]{1,0:T(8,128)(2,1)S(1)} %collective-permute-done.24.refs_5_) | copy-start | bytes 4337668
  70.8 20.9 %collective-permute-start.26 = (bf16[5648,128]{1,0:T(8,128)(2,1)S(1)}, bf16[5648,128]{1,0:T(8,128)(2,1)S(1)}, u32[]{:S(2)}, u32[]{:S(2)}) collective-permute-start(bf16[5648,128]{1,0:T(8,128)(2,1)S(1)} %collective-permute-done.22.refs_6_), channel_id=1, source_target_pairs={{1,5},{3,7},{5,1},{7,3},{24,28},{26,30},{28,24},{30,26}} | collective-permute-start | bytes 4337672 | tf_op jit(solution)/shard_map/ppermute | solution.py:475
  73.2 36.9 %collective-permute-start.29 = (s16[1968,256]{1,0:T(8,128)(2,1)S(1)}, s16[1968,256]{1,0:T(8,128)(2,1)}, u32[]{:S(2)}, u32[]{:S(2)}) collective-permute-start(s16[1968,256]{1,0:T(8,128)(2,1)S(1)} %get-tuple-element.131), channel_id=1, source_target_pairs={{2,0},{3,1},{6,4},{7,5},{10,8},{11,9},{14,12},{15,13},{16,18},{17,... | collective-permute-start | bytes 3022856 | tf_op jit(solution)/shard_map/ppermute | solution.py:475
  82.2 20.4 %collective-permute-start.30 = (s16[1312,256]{1,0:T(8,128)(2,1)S(1)}, s16[1312,256]{1,0:T(8,128)(2,1)S(1)}, u32[]{:S(2)}, u32[]{:S(2)}) collective-permute-start(s16[1312,256]{1,0:T(8,128)(2,1)S(1)} %get-tuple-element.135), channel_id=1, source_target_pairs={{0,2},{1,3},{4,6},{5,7},{8,10},{9,11},{12,14},{13,15},{18,16},{19,... | collective-permute-start | bytes 2015240 | tf_op jit(solution)/shard_map/ppermute | solution.py:475
  91.7 18.5 %copy-start.4 = (bf16[2048,256]{1,0:T(8,128)(2,1)S(1)}, bf16[2048,256]{1,0:T(8,128)(2,1)}, u32[]{:S(2)}) copy-start(bf16[2048,256]{1,0:T(8,128)(2,1)} %refs_2_.2) | copy-start | bytes 3145732
  91.7 18.5 %copy-start.16 = (s32[8,16]{1,0:T(8,128)S(1)}, s32[8,16]{1,0:T(8,128)}, u32[]{:S(2)}) copy-start(s32[8,16]{1,0:T(8,128)} %refs_0_.1) | copy-start | bytes 1540
  91.7 18.5 %copy-start.17 = (s32[16,2]{0,1:T(2,128)S(1)}, s32[16,2]{0,1:T(2,128)}, u32[]{:S(2)}) copy-start(s32[16,2]{0,1:T(2,128)} %param.9) | copy-start | bytes 388
  96.2 14.0 %collective-permute-start.31 = (s16[1312,256]{1,0:T(8,128)(2,1)S(1)}, s16[1312,256]{1,0:T(8,128)(2,1)S(1)}, u32[]{:S(2)}, u32[]{:S(2)}) collective-permute-start(s16[1312,256]{1,0:T(8,128)(2,1)S(1)} %get-tuple-element.138), channel_id=1, source_target_pairs={{1,3},{5,7},{26,24},{30,28}} | collective-permute-start | bytes 2015240 | tf_op jit(solution)/shard_map/ppermute | solution.py:475
  97.5 1.2 %collective-permute-start.27 = (f32[8,128]{1,0:T(8,128)S(1)}, f32[8,128]{1,0:T(8,128)S(1)}, u32[]{:S(2)}, u32[]{:S(2)}) collective-permute-start(f32[8,128]{1,0:T(8,128)S(1)} %get-tuple-element.123.refs_0_), channel_id=1, source_target_pairs={{0,1},{1,0},{2,3},{3,2},{4,5},{5,4},{6,7},{7,6},{8,9},{9,8},{10,11... | collective-permute-start | bytes 12296 | tf_op jit(solution)/shard_map/ppermute | solution.py:525
  99.9 9.0 %collective-permute-start.28 = (f32[8,128]{1,0:T(8,128)S(1)}, f32[8,128]{1,0:T(8,128)S(1)}, u32[]{:S(2)}, u32[]{:S(2)}) collective-permute-start(f32[8,128]{1,0:T(8,128)S(1)} %get-tuple-element.127), channel_id=1, source_target_pairs={{0,2},{2,0},{1,3},{3,1},{4,6},{6,4},{5,7},{7,5},{8,10},{10,8},{9,1... | collective-permute-start | bytes 12296 | tf_op jit(solution)/shard_map/ppermute | solution.py:526

commit v10 on v9

--- a/solution.py
+++ b/solution.py
@@ -6,7 +6,7 @@
 from jax.sharding import PartitionSpec as P
 
 TILE = 128
-VMEM_LIMIT = 12 * 1024 * 1024
+VMEM_LIMIT = 7 * 1024 * 1024
 
 
 def expand(mask):

time: 114 us -> 114 us (level)
  no operation moved by 1% of the time
where the time goes in v10:
time: 114 us
  waiting for transfers between devices  49.5 us (43%)
  Pallas kernels  33 us (29%)
  starting transfers between devices  28.9 us (25%)
  between operations  1.24 us (1%)
    ppermute x16, waiting for transfers between devices, move(): return lax.ppermute(value, AXES, pairs)  37.6 us
    ppermute x16, starting transfers between devices, move(): return lax.ppermute(value, AXES, pairs)  25.4 us
    pallas_call x5, Pallas kernels, shard_product(): call(kernel, 'shard_product', out_shape=(jax.ShapeDtypeStruct((rows, wide...  21.5 us
    ppermute x1, waiting for transfers between devices, sparse_ladder(): flags = [token, lax.ppermute(token, 'col', CHIPS_Y)]  5.14 us
    pallas_call x1, Pallas kernels, mask_tiles(): call(kernel, 'mask_tiles', out_shape=tuple((jax.ShapeDtypeStruct(part.sha...  4.15 us
    ppermute x1, waiting for transfers between devices, sparse_ladder(): other_amps = lax.ppermute(amplitudes_now, 'col', CORES)  3.38 us
    pallas_call x1, Pallas kernels, lay_out(): call(kernel, 'lay_out', out_shape=pltpu.HBM((rows, 2 * width), jnp.bfloat...  3.02 us
    ppermute x1, starting transfers between devices, sparse_ladder(): flags = [token, lax.ppermute(token, 'col', CHIPS_Y)]  2.68 us
  transfers between devices with their start and end apart: 22, of which 9 were waited for; matrix products, arithmetic and copies ran while one was open for 1% of the time, Pallas kernels for 26%

profile of v10, /device:TPU:24, one launch (start us, length us, event | category | flops | bytes accessed | tf_op | source)
XLA Modules:
  0.0 113.7 jit_solution(3682066243558306068)
XLA Ops:
  0.0 0.0 collective-permute-start.11
  0.0 0.5 collective-permute-start.10
  0.5 0.0 collective-permute-start.12
  0.5 0.1 pad_add_fusion
  0.6 0.1 stack.37.picks_ref
  0.7 2.2 %collective-permute-done.10.refs_1_ = s32[2,16]{1,0:T(2,128)S(1)} collective-permute-done((s32[2,16]{1,0:T(2,128)}, s32[2,16]{1,0:T(2,128)S(1)}, u32[]{:S(2)}, u32[]{:S(2)}) %collective-permute-start.10) | collective-permute-done | bytes 160 | tf_op jit(solution)/shard_map/ppermute | solution.py:492
  2.9 0.0 collective-permute-done.11.refs_3_
  2.9 1.9 %pack_tiles.1.refs_3_ = bf16[5648,128]{1,0:T(8,128)(2,1)S(1)} custom-call(s32[1]{0:T(128)} %bitcast.2.swap_ref, s32[2,16]{1,0:T(2,128)} %bitcast.38, s32[2,16]{1,0:T(2,128)S(1)} %collective-permute-done.10.refs_1_, bf16[2048,256]{1,0:T(8,128)(2,1)} %refs_2_.2, bf16[2048,256]{1,0:T(8,128)(2,1)S(1)} %collective-permute-done.11.refs_3_), custom_call_target="tpu_custom_call" | custom-call | flops 1 | bytes 1 | tf_op jit(solution)/shard_map/pack_tiles/pallas_call | solution.py:101
  4.8 0.0 copy-start
  4.8 0.0 collective-permute-done.12.refs_1_
  4.8 0.2 collective-permute-start.16
  5.0 0.7 collective-permute-start.13
  5.8 2.3 %collective-permute-start.14 = (bf16[5648,128]{1,0:T(8,128)(2,1)S(1)}, bf16[5648,128]{1,0:T(8,128)(2,1)S(1)}, u32[]{:S(2)}, u32[]{:S(2)}) collective-permute-start(bf16[5648,128]{1,0:T(8,128)(2,1)S(1)} %pack_tiles.1.refs_3_), channel_id=1, source_target_pairs={{1,8},{3,10},{5,12},{7,14},{8,1},{10,3},{12,5},{14,7},{17,24},{19,... | collective-permute-start | bytes 4337672 | tf_op jit(solution)/shard_map/ppermute | solution.py:475
  8.1 0.8 collective-permute-start.15
  8.9 3.4 %collective-permute-done.16.refs_3_ = bf16[1024,2048]{1,0:T(8,128)(2,1)S(1)} collective-permute-done((bf16[1024,2048]{1,0:T(8,128)(2,1)}, bf16[1024,2048]{1,0:T(8,128)(2,1)S(1)}, u32[]{:S(2)}, u32[]{:S(2)}) %collective-permute-start.16) | collective-permute-done | bytes 4194336 | tf_op jit(solution)/shard_map/ppermute | solution.py:497
  12.2 4.1 %mask_tiles.1 = (bf16[1024,2048]{1,0:T(8,128)(2,1)S(1)}, bf16[1024,2048]{1,0:T(8,128)(2,1)S(1)}, f32[8,128]{1,0:T(8,128)S(1)}) custom-call(s32[8,16]{1,0:T(8,128)} %refs_0_.1, s32[8,16]{1,0:T(8,128)S(1)} %collective-permute-done.12.refs_1_, bf16[1024,2048]{1,0:T(8,128)(2,1)} %refs_2_.3, bf16[1024,2048]{1,0:T(8,128)(2,1)S(1)} %collective-permute-done.16.refs_3_), custom_call_target="tpu_custom_call" | custom-call | flops 1 | bytes 1 | tf_op jit(solution)/shard_map/mask_tiles/pallas_call | solution.py:131
  16.4 0.0 collective-permute-done.13.refs_4_
  16.4 0.0 copy-start.9
  16.4 9.7 %collective-permute-done.14.refs_4_ = bf16[5648,128]{1,0:T(8,128)(2,1)S(1)} collective-permute-done((bf16[5648,128]{1,0:T(8,128)(2,1)S(1)}, bf16[5648,128]{1,0:T(8,128)(2,1)S(1)}, u32[]{:S(2)}, u32[]{:S(2)}) %collective-permute-start.14) | collective-permute-done | bytes 1445920 | tf_op jit(solution)/shard_map/ppermute | solution.py:475
  26.1 0.0 collective-permute-done.15.refs_5_
  26.1 3.4 %collective-permute-start.17 = (bf16[5648,128]{1,0:T(8,128)(2,1)S(1)}, bf16[5648,128]{1,0:T(8,128)(2,1)S(1)}, u32[]{:S(2)}, u32[]{:S(2)}) collective-permute-start(bf16[5648,128]{1,0:T(8,128)(2,1)S(1)} %collective-permute-done.14.refs_4_), channel_id=1, source_target_pairs={{1,5},{3,7},{5,1},{7,3},{8,12},{10,14},{12,8},{14,10},{17,21},{19,... | collective-permute-start | bytes 4337672 | tf_op jit(solution)/shard_map/ppermute | solution.py:475
  29.5 0.8 collective-permute-start.18
  30.3 0.8 collective-permute-start.19
  31.1 0.0 copy-done.8
  31.1 6.0 %shard_product.5 = (f32[1024,256]{1,0:T(8,128)}, s16[656,256]{1,0:T(8,128)(2,1)S(1)}, s16[656,256]{1,0:T(8,128)(2,1)S(1)}, f32[8,128]{1,0:T(8,128)S(1)}) custom-call(s32[10]{0:T(128)S(1)} %stack.37.picks_ref, f32[8,128]{1,0:T(8,128)S(1)} %get-tuple-element.101.refs_0_, bf16[1024,2048]{1,0:T(8,128)(2,1)S(1)} %get-tuple-element.102.refs_1_.refs_2_, ...), custom_call_target="tpu_custom_call" | custom-call | flops 1 | bytes 1 | tf_op jit(solution)/shard_map/shard_product/pallas_call | solution.py:216
  37.1 3.0 %collective-permute-start.20 = (s16[656,256]{1,0:T(8,128)(2,1)S(1)}, s16[656,256]{1,0:T(8,128)(2,1)S(1)}, u32[]{:S(2)}, u32[]{:S(2)}) collective-permute-start(s16[656,256]{1,0:T(8,128)(2,1)S(1)} %get-tuple-element.104), channel_id=1, source_target_pairs={{2,0},{3,1},{6,4},{7,5},{10,8},{11,9},{14,12},{15,13},{16,18},{17,... | collective-permute-start | bytes 1007624 | tf_op jit(solution)/shard_map/ppermute | solution.py:475
  40.1 4.6 %collective-permute-done.20 = s16[656,256]{1,0:T(8,128)(2,1)S(1)} collective-permute-done((s16[656,256]{1,0:T(8,128)(2,1)S(1)}, s16[656,256]{1,0:T(8,128)(2,1)S(1)}, u32[]{:S(2)}, u32[]{:S(2)}) %collective-permute-start.20) | collective-permute-done | bytes 335904 | tf_op jit(solution)/shard_map/ppermute | solution.py:475
  44.7 2.4 %collective-permute-done.17.refs_5_ = bf16[5648,128]{1,0:T(8,128)(2,1)S(1)} collective-permute-done((bf16[5648,128]{1,0:T(8,128)(2,1)S(1)}, bf16[5648,128]{1,0:T(8,128)(2,1)S(1)}, u32[]{:S(2)}, u32[]{:S(2)}) %collective-permute-start.17) | collective-permute-done | bytes 1445920 | tf_op jit(solution)/shard_map/ppermute | solution.py:475
  47.1 0.0 collective-permute-done.18.refs_3_
  47.1 0.0 collective-permute-done.19.refs_4_
  47.1 0.8 collective-permute-start.21
  47.9 1.3 %collective-permute-start.22 = (bf16[5648,128]{1,0:T(8,128)(2,1)S(1)}, bf16[5648,128]{1,0:T(8,128)(2,1)S(1)}, u32[]{:S(2)}, u32[]{:S(2)}) collective-permute-start(bf16[5648,128]{1,0:T(8,128)(2,1)S(1)} %collective-permute-done.18.refs_3_), channel_id=1, source_target_pairs={{9,1},{11,3},{13,5},{15,7},{16,24},{18,26},{20,28},{22,30}} | collective-permute-start | bytes 4337672 | tf_op jit(solution)/shard_map/ppermute | solution.py:475
  49.2 0.8 collective-permute-start.23
  49.9 0.8 collective-permute-start.24
  50.7 0.6 shard_product.6
  51.3 0.7 collective-permute-start.25
  52.0 0.0 copy-done.9
  52.0 0.0 copy-done.10
  52.0 6.0 %shard_product.7 = (f32[1024,256]{1,0:T(8,128)}, s16[1968,256]{1,0:T(8,128)(2,1)S(1)}, f32[8,128]{1,0:T(8,128)S(1)}) custom-call(s32[10]{0:T(128)S(1)} %stack.37.picks_ref, s16[656,256]{1,0:T(8,128)(2,1)S(1)} %get-tuple-element.111.refs_0_, f32[8,128]{1,0:T(8,128)S(1)} %get-tuple-element.112.refs_1_, ...), custom_call_target="tpu_custom_call" | custom-call | flops 1 | bytes 1 | tf_op jit(solution)/shard_map/shard_product/pallas_call | solution.py:216
  58.0 0.0 collective-permute-done.25.refs_3_
  58.0 0.0 collective-permute-done.21.refs_4_
  58.1 12.7 %collective-permute-done.22.refs_6_ = bf16[5648,128]{1,0:T(8,128)(2,1)S(1)} collective-permute-done((bf16[5648,128]{1,0:T(8,128)(2,1)S(1)}, bf16[5648,128]{1,0:T(8,128)(2,1)S(1)}, u32[]{:S(2)}, u32[]{:S(2)}) %collective-permute-start.22) | collective-permute-done | bytes 1445920 | tf_op jit(solution)/shard_map/ppermute | solution.py:475
  70.7 0.0 collective-permute-done.23.refs_3_
  70.7 0.0 collective-permute-done.24.refs_5_
  70.7 2.5 %collective-permute-start.26 = (bf16[5648,128]{1,0:T(8,128)(2,1)S(1)}, bf16[5648,128]{1,0:T(8,128)(2,1)S(1)}, u32[]{:S(2)}, u32[]{:S(2)}) collective-permute-start(bf16[5648,128]{1,0:T(8,128)(2,1)S(1)} %collective-permute-done.22.refs_6_), channel_id=1, source_target_pairs={{1,5},{3,7},{5,1},{7,3},{24,28},{26,30},{28,24},{30,26}} | collective-permute-start | bytes 4337672 | tf_op jit(solution)/shard_map/ppermute | solution.py:475
  73.2 4.4 %collective-permute-start.29 = (s16[1968,256]{1,0:T(8,128)(2,1)S(1)}, s16[1968,256]{1,0:T(8,128)(2,1)}, u32[]{:S(2)}, u32[]{:S(2)}) collective-permute-start(s16[1968,256]{1,0:T(8,128)(2,1)S(1)} %get-tuple-element.131), channel_id=1, source_target_pairs={{2,0},{3,1},{6,4},{7,5},{10,8},{11,9},{14,12},{15,13},{16,18},{17,... | collective-permute-start | bytes 3022856 | tf_op jit(solution)/shard_map/ppermute | solution.py:475
  77.6 0.0 copy-done.12
  77.6 4.5 %shard_product.8 = (f32[1024,256]{1,0:T(8,128)S(1)}, s16[1312,256]{1,0:T(8,128)(2,1)S(1)}, f32[8,128]{1,0:T(8,128)S(1)}) custom-call(s32[10]{0:T(128)S(1)} %stack.37.picks_ref, f32[8,128]{1,0:T(8,128)S(1)} %get-tuple-element.116.refs_0_, bf16[1024,2048]{1,0:T(8,128)(2,1)S(1)} %get-tuple-element.102.refs_1_.refs_2_, ...), custom_call_target="tpu_custom_call" | custom-call | flops 1 | bytes 1 | tf_op jit(solution)/shard_map/shard_product/pallas_call | solution.py:216
  82.2 1.3 %collective-permute-start.30 = (s16[1312,256]{1,0:T(8,128)(2,1)S(1)}, s16[1312,256]{1,0:T(8,128)(2,1)S(1)}, u32[]{:S(2)}, u32[]{:S(2)}) collective-permute-start(s16[1312,256]{1,0:T(8,128)(2,1)S(1)} %get-tuple-element.135), channel_id=1, source_target_pairs={{0,2},{1,3},{4,6},{5,7},{8,10},{9,11},{12,14},{13,15},{18,16},{19,... | collective-permute-start | bytes 2015240 | tf_op jit(solution)/shard_map/ppermute | solution.py:475
  83.5 8.2 %collective-permute-done.26.refs_3_ = bf16[5648,128]{1,0:T(8,128)(2,1)S(1)} collective-permute-done((bf16[5648,128]{1,0:T(8,128)(2,1)S(1)}, bf16[5648,128]{1,0:T(8,128)(2,1)S(1)}, u32[]{:S(2)}, u32[]{:S(2)}) %collective-permute-start.26) | collective-permute-done | bytes 1445920 | tf_op jit(solution)/shard_map/ppermute | solution.py:475
  91.7 4.4 %shard_product.9 = (f32[1024,256]{1,0:T(8,128)}, s16[1312,256]{1,0:T(8,128)(2,1)S(1)}, f32[8,128]{1,0:T(8,128)S(1)}) custom-call(s32[10]{0:T(128)S(1)} %stack.37.picks_ref, f32[8,128]{1,0:T(8,128)S(1)} %get-tuple-element.121.refs_0_, bf16[1024,2048]{1,0:T(8,128)(2,1)S(1)} %get-tuple-element.102.refs_1_.refs_2_, ...), custom_call_target="tpu_custom_call" | custom-call | flops 1 | bytes 1 | tf_op jit(solution)/shard_map/shard_product/pallas_call | solution.py:216
  96.2 1.3 %collective-permute-start.31 = (s16[1312,256]{1,0:T(8,128)(2,1)S(1)}, s16[1312,256]{1,0:T(8,128)(2,1)S(1)}, u32[]{:S(2)}, u32[]{:S(2)}) collective-permute-start(s16[1312,256]{1,0:T(8,128)(2,1)S(1)} %get-tuple-element.138), channel_id=1, source_target_pairs={{1,3},{5,7},{26,24},{30,28}} | collective-permute-start | bytes 2015240 | tf_op jit(solution)/shard_map/ppermute | solution.py:475
  97.5 0.1 collective-permute-start.27
  97.5 1.2 %collective-permute-done.27.refs_1_ = f32[8,128]{1,0:T(8,128)S(1)} collective-permute-done((f32[8,128]{1,0:T(8,128)S(1)}, f32[8,128]{1,0:T(8,128)S(1)}, u32[]{:S(2)}, u32[]{:S(2)}) %collective-permute-start.27) | collective-permute-done | bytes 4128 | tf_op jit(solution)/shard_map/ppermute | solution.py:525
  98.7 1.2 %add_coded.2 = (bf16[1024,256]{1,0:T(8,128)(2,1)}, f32[8,128]{1,0:T(8,128)S(1)}) custom-call(f32[8,128]{1,0:T(8,128)S(1)} %get-tuple-element.123.refs_0_, f32[8,128]{1,0:T(8,128)S(1)} %collective-permute-done.27.refs_1_, f32[1024,256]{1,0:T(8,128)S(1)} %get-tuple-element.124.refs_2_, s16[1312,256]{1,0:T(8,128)(2,1)S(1)} %collective-permute-done.25.refs_3_), custom_call_target="tpu_custom_call" | custom-call | flops 1 | bytes 1 | tf_op jit(solution)/shard_map/add_coded/pallas_call | solution.py:312
  99.9 2.7 %collective-permute-start.28 = (f32[8,128]{1,0:T(8,128)S(1)}, f32[8,128]{1,0:T(8,128)S(1)}, u32[]{:S(2)}, u32[]{:S(2)}) collective-permute-start(f32[8,128]{1,0:T(8,128)S(1)} %get-tuple-element.127), channel_id=1, source_target_pairs={{0,2},{2,0},{1,3},{3,1},{4,6},{6,4},{5,7},{7,5},{8,10},{10,8},{9,1... | collective-permute-start | bytes 12296 | tf_op jit(solution)/shard_map/ppermute | solution.py:526
  102.6 0.0 collective-permute-done.30.refs_1_
  102.6 1.2 %add_coded.3 = (bf16[1024,256]{1,0:T(8,128)(2,1)}, f32[8,128]{1,0:T(8,128)}) custom-call(f32[1024,256]{1,0:T(8,128)S(1)} %get-tuple-element.134.refs_0_, s16[1312,256]{1,0:T(8,128)(2,1)S(1)} %collective-permute-done.30.refs_1_), custom_call_target="tpu_custom_call" | custom-call | flops 1 | bytes 1 | tf_op jit(solution)/shard_map/add_coded/pallas_call | solution.py:312
  103.8 5.1 %collective-permute-done.28 = f32[8,128]{1,0:T(8,128)S(1)} collective-permute-done((f32[8,128]{1,0:T(8,128)S(1)}, f32[8,128]{1,0:T(8,128)S(1)}, u32[]{:S(2)}, u32[]{:S(2)}) %collective-permute-start.28) | collective-permute-done | bytes 4128 | tf_op jit(solution)/shard_map/ppermute | solution.py:526
  108.9 0.6 add_reduce_fusion
  110.1 0.0 collective-permute-done.29
  110.2 0.0 collective-permute-done.31
  110.2 3.3 %conditional.1 = (bf16[1024,512]{1,0:T(8,128)(2,1)}) conditional(s32[]{:T(128)} %convert_element_type.32, (s32[2]{0:T(128)S(1)}, f32[1024,256]{1,0:T(8,128)}, s16[656,256]{1,0:T(8,128)(2,1)}, s16[1968,256]{1,0:T(8,128)(2,1)}, f32[1024,256]{1,0:T(8,128)}, /*index=5*/bf16[1024,256]{1,0:T(8,128)(2,1)}, bf16[1024,256]{1,0:T(8,128)(2,1)}, ...), branch_computations={%region_1.2_spmd, %region_2.3_spmd} | conditional | flops 8594653184 | bytes 206655584 | solution.py:536
  110.2 3.0 %lay_out.1 = bf16[1024,512]{1,0:T(8,128)(2,1)} custom-call(s32[2]{0:T(128)S(1)} %get-tuple-element.34.place_ref, f32[1024,256]{1,0:T(8,128)} %get-tuple-element.35.refs_0_, s16[656,256]{1,0:T(8,128)(2,1)} %get-tuple-element.36.refs_1_, s16[1968,256]{1,0:T(8,128)(2,1)} %get-tuple-element.37.refs_2_, f32[1024,256]{1,0:T(8,128)} %get-tuple-element.38.refs_3_, ...), custom_call_target="tpu_custom_call" | custom-call | flops 1 | bytes 1 | tf_op jit(solution)/shard_map/cond/branch_0_fun/lay_out/pallas_call | solution.py:384
  (24 shorter events, 0.0 us)
Async XLA Ops:
  0.0 2.9 %collective-permute-start.11 = (bf16[2048,256]{1,0:T(8,128)(2,1)}, bf16[2048,256]{1,0:T(8,128)(2,1)S(1)}, u32[]{:S(2)}, u32[]{:S(2)}) collective-permute-start(bf16[2048,256]{1,0:T(8,128)(2,1)} %refs_2_.2), channel_id=1, source_target_pairs={{0,1},{1,0},{2,3},{3,2},{4,5},{5,4},{6,7},{7,6},{8,9},{9,8},{10,11... | collective-permute-start | bytes 3145736 | tf_op jit(solution)/shard_map/ppermute | solution.py:491
  0.0 2.9 %collective-permute-start.10 = (s32[2,16]{1,0:T(2,128)}, s32[2,16]{1,0:T(2,128)S(1)}, u32[]{:S(2)}, u32[]{:S(2)}) collective-permute-start(s32[2,16]{1,0:T(2,128)} %bitcast.37), channel_id=1, source_target_pairs={{0,1},{1,0},{2,3},{3,2},{4,5},{5,4},{6,7},{7,6},{8,9},{9,8},{10,11... | collective-permute-start | bytes 392 | tf_op jit(solution)/shard_map/ppermute | solution.py:492
  0.5 4.3 %collective-permute-start.12 = (s32[8,16]{1,0:T(8,128)}, s32[8,16]{1,0:T(8,128)S(1)}, u32[]{:S(2)}, u32[]{:S(2)}) collective-permute-start(s32[8,16]{1,0:T(8,128)} %refs_0_.1), channel_id=1, source_target_pairs={{0,1},{1,0},{2,3},{3,2},{4,5},{5,4},{6,7},{7,6},{8,9},{9,8},{10,11... | collective-permute-start | bytes 1544 | tf_op jit(solution)/shard_map/ppermute | solution.py:493
  4.8 11.6 %copy-start = (bf16[5648,128]{1,0:T(8,128)(2,1)}, bf16[5648,128]{1,0:T(8,128)(2,1)S(1)}, u32[]{:S(2)}) copy-start(bf16[5648,128]{1,0:T(8,128)(2,1)S(1)} %pack_tiles.1.refs_3_) | copy-start | bytes 4337668
  4.8 7.4 %collective-permute-start.16 = (bf16[1024,2048]{1,0:T(8,128)(2,1)}, bf16[1024,2048]{1,0:T(8,128)(2,1)S(1)}, u32[]{:S(2)}, u32[]{:S(2)}) collective-permute-start(bf16[1024,2048]{1,0:T(8,128)(2,1)} %refs_2_.3), channel_id=1, source_target_pairs={{0,1},{1,0},{2,3},{3,2},{4,5},{5,4},{6,7},{7,6},{8,9},{9,8},{10,11... | collective-permute-start | bytes 12582920 | tf_op jit(solution)/shard_map/ppermute | solution.py:497
  5.0 11.4 %collective-permute-start.13 = (bf16[5648,128]{1,0:T(8,128)(2,1)S(1)}, bf16[5648,128]{1,0:T(8,128)(2,1)S(1)}, u32[]{:S(2)}, u32[]{:S(2)}) collective-permute-start(bf16[5648,128]{1,0:T(8,128)(2,1)S(1)} %pack_tiles.1.refs_3_), channel_id=1, source_target_pairs={{0,4},{2,6},{4,0},{6,2},{9,13},{11,15},{13,9},{15,11},{16,20},{18,... | collective-permute-start | bytes 4337672 | tf_op jit(solution)/shard_map/ppermute | solution.py:475
  5.8 20.4 %collective-permute-start.14 = (bf16[5648,128]{1,0:T(8,128)(2,1)S(1)}, bf16[5648,128]{1,0:T(8,128)(2,1)S(1)}, u32[]{:S(2)}, u32[]{:S(2)}) collective-permute-start(bf16[5648,128]{1,0:T(8,128)(2,1)S(1)} %pack_tiles.1.refs_3_), channel_id=1, source_target_pairs={{1,8},{3,10},{5,12},{7,14},{8,1},{10,3},{12,5},{14,7},{17,24},{19,... | collective-permute-start | bytes 4337672 | tf_op jit(solution)/shard_map/ppermute | solution.py:475
  8.1 18.0 %collective-permute-start.15 = (bf16[5648,128]{1,0:T(8,128)(2,1)S(1)}, bf16[5648,128]{1,0:T(8,128)(2,1)S(1)}, u32[]{:S(2)}, u32[]{:S(2)}) collective-permute-start(bf16[5648,128]{1,0:T(8,128)(2,1)S(1)} %pack_tiles.1.refs_3_), channel_id=1, source_target_pairs={{9,17},{11,19},{13,21},{15,23},{16,8},{18,10},{20,12},{22,14}} | collective-permute-start | bytes 4337672 | tf_op jit(solution)/shard_map/ppermute | solution.py:475
  16.4 35.6 %copy-start.9 = (bf16[5648,128]{1,0:T(8,128)(2,1)}, bf16[5648,128]{1,0:T(8,128)(2,1)S(1)}, u32[]{:S(2)}) copy-start(bf16[5648,128]{1,0:T(8,128)(2,1)S(1)} %collective-permute-done.13.refs_4_) | copy-start | bytes 4337668
  26.1 4.9 %copy-start.8 = (bf16[5648,128]{1,0:T(8,128)(2,1)}, bf16[5648,128]{1,0:T(8,128)(2,1)S(1)}, u32[]{:S(2)}) copy-start(bf16[5648,128]{1,0:T(8,128)(2,1)S(1)} %collective-permute-done.14.refs_4_) | copy-start | bytes 4337668
  26.1 10.9 %copy-start.5 = (bf16[5648,128]{1,0:T(8,128)(2,1)}, bf16[5648,128]{1,0:T(8,128)(2,1)S(1)}, u32[]{:S(2)}) copy-start(bf16[5648,128]{1,0:T(8,128)(2,1)S(1)} %collective-permute-done.15.refs_5_) | copy-start | bytes 4337668
  26.1 20.9 %collective-permute-start.17 = (bf16[5648,128]{1,0:T(8,128)(2,1)S(1)}, bf16[5648,128]{1,0:T(8,128)(2,1)S(1)}, u32[]{:S(2)}, u32[]{:S(2)}) collective-permute-start(bf16[5648,128]{1,0:T(8,128)(2,1)S(1)} %collective-permute-done.14.refs_4_), channel_id=1, source_target_pairs={{1,5},{3,7},{5,1},{7,3},{8,12},{10,14},{12,8},{14,10},{17,21},{19,... | collective-permute-start | bytes 4337672 | tf_op jit(solution)/shard_map/ppermute | solution.py:475
  29.5 17.5 %collective-permute-start.18 = (bf16[5648,128]{1,0:T(8,128)(2,1)S(1)}, bf16[5648,128]{1,0:T(8,128)(2,1)S(1)}, u32[]{:S(2)}, u32[]{:S(2)}) collective-permute-start(bf16[5648,128]{1,0:T(8,128)(2,1)S(1)} %collective-permute-done.14.refs_4_), channel_id=1, source_target_pairs={{8,16},{10,18},{12,20},{14,22},{17,9},{19,11},{21,13},{23,15}} | collective-permute-start | bytes 4337672 | tf_op jit(solution)/shard_map/ppermute | solution.py:475
  30.3 16.8 %collective-permute-start.19 = (bf16[5648,128]{1,0:T(8,128)(2,1)S(1)}, bf16[5648,128]{1,0:T(8,128)(2,1)S(1)}, u32[]{:S(2)}, u32[]{:S(2)}) collective-permute-start(bf16[5648,128]{1,0:T(8,128)(2,1)S(1)} %collective-permute-done.15.refs_5_), channel_id=1, source_target_pairs={{8,0},{10,2},{12,4},{14,6},{17,25},{19,27},{21,29},{23,31}} | collective-permute-start | bytes 4337672 | tf_op jit(solution)/shard_map/ppermute | solution.py:475
  37.1 7.7 %collective-permute-start.20 = (s16[656,256]{1,0:T(8,128)(2,1)S(1)}, s16[656,256]{1,0:T(8,128)(2,1)S(1)}, u32[]{:S(2)}, u32[]{:S(2)}) collective-permute-start(s16[656,256]{1,0:T(8,128)(2,1)S(1)} %get-tuple-element.104), channel_id=1, source_target_pairs={{2,0},{3,1},{6,4},{7,5},{10,8},{11,9},{14,12},{15,13},{16,18},{17,... | collective-permute-start | bytes 1007624 | tf_op jit(solution)/shard_map/ppermute | solution.py:475
  44.7 5.2 %copy-start.15 = (s16[656,256]{1,0:T(8,128)(2,1)}, s16[656,256]{1,0:T(8,128)(2,1)S(1)}, u32[]{:S(2)}) copy-start(s16[656,256]{1,0:T(8,128)(2,1)S(1)} %collective-permute-done.20) | copy-start | bytes 1007620
  47.1 5.0 %copy-start.10 = (bf16[5648,128]{1,0:T(8,128)(2,1)}, bf16[5648,128]{1,0:T(8,128)(2,1)S(1)}, u32[]{:S(2)}) copy-start(bf16[5648,128]{1,0:T(8,128)(2,1)S(1)} %collective-permute-done.17.refs_5_) | copy-start | bytes 4337668
  47.1 3.6 %copy-start.6 = (bf16[5648,128]{1,0:T(8,128)(2,1)}, bf16[5648,128]{1,0:T(8,128)(2,1)S(1)}, u32[]{:S(2)}) copy-start(bf16[5648,128]{1,0:T(8,128)(2,1)S(1)} %collective-permute-done.18.refs_3_) | copy-start | bytes 4337668
  47.1 3.6 %copy-start.7 = (bf16[5648,128]{1,0:T(8,128)(2,1)}, bf16[5648,128]{1,0:T(8,128)(2,1)S(1)}, u32[]{:S(2)}) copy-start(bf16[5648,128]{1,0:T(8,128)(2,1)S(1)} %collective-permute-done.19.refs_4_) | copy-start | bytes 4337668
  47.1 10.9 %collective-permute-start.21 = (bf16[5648,128]{1,0:T(8,128)(2,1)S(1)}, bf16[5648,128]{1,0:T(8,128)(2,1)S(1)}, u32[]{:S(2)}, u32[]{:S(2)}) collective-permute-start(bf16[5648,128]{1,0:T(8,128)(2,1)S(1)} %collective-permute-done.19.refs_4_), channel_id=1, source_target_pairs={{0,4},{2,6},{4,0},{6,2},{25,29},{27,31},{29,25},{31,27}} | collective-permute-start | bytes 4337672 | tf_op jit(solution)/shard_map/ppermute | solution.py:475
  47.9 22.9 %collective-permute-start.22 = (bf16[5648,128]{1,0:T(8,128)(2,1)S(1)}, bf16[5648,128]{1,0:T(8,128)(2,1)S(1)}, u32[]{:S(2)}, u32[]{:S(2)}) collective-permute-start(bf16[5648,128]{1,0:T(8,128)(2,1)S(1)} %collective-permute-done.18.refs_3_), channel_id=1, source_target_pairs={{9,1},{11,3},{13,5},{15,7},{16,24},{18,26},{20,28},{22,30}} | collective-permute-start | bytes 4337672 | tf_op jit(solution)/shard_map/ppermute | solution.py:475
  49.2 21.6 %collective-permute-start.23 = (bf16[5648,128]{1,0:T(8,128)(2,1)S(1)}, bf16[5648,128]{1,0:T(8,128)(2,1)S(1)}, u32[]{:S(2)}, u32[]{:S(2)}) collective-permute-start(bf16[5648,128]{1,0:T(8,128)(2,1)S(1)} %collective-permute-done.18.refs_3_), channel_id=1, source_target_pairs={{9,13},{11,15},{13,9},{15,11},{16,20},{18,22},{20,16},{22,18}} | collective-permute-start | bytes 4337672 | tf_op jit(solution)/shard_map/ppermute | solution.py:475
  49.9 20.8 %collective-permute-start.24 = (bf16[5648,128]{1,0:T(8,128)(2,1)S(1)}, bf16[5648,128]{1,0:T(8,128)(2,1)S(1)}, u32[]{:S(2)}, u32[]{:S(2)}) collective-permute-start(bf16[5648,128]{1,0:T(8,128)(2,1)S(1)} %collective-permute-done.13.refs_4_), channel_id=1, source_target_pairs={{9,17},{11,19},{13,21},{15,23},{16,8},{18,10},{20,12},{22,14}} | collective-permute-start | bytes 4337672 | tf_op jit(solution)/shard_map/ppermute | solution.py:475
  51.3 6.7 %collective-permute-start.25 = (s16[1312,256]{1,0:T(8,128)(2,1)S(1)}, s16[1312,256]{1,0:T(8,128)(2,1)S(1)}, u32[]{:S(2)}, u32[]{:S(2)}) collective-permute-start(s16[1312,256]{1,0:T(8,128)(2,1)S(1)} %get-tuple-element.110), channel_id=1, source_target_pairs={{0,2},{4,6},{8,10},{9,11},{12,14},{13,15},{18,16},{19,17},{22,20},... | collective-permute-start | bytes 2015240 | tf_op jit(solution)/shard_map/ppermute | solution.py:475
  58.1 19.5 %copy-start.12 = (bf16[5648,128]{1,0:T(8,128)(2,1)}, bf16[5648,128]{1,0:T(8,128)(2,1)S(1)}, u32[]{:S(2)}) copy-start(bf16[5648,128]{1,0:T(8,128)(2,1)S(1)} %collective-permute-done.21.refs_4_) | copy-start | bytes 4337668
  70.7 6.9 %copy-start.11 = (bf16[5648,128]{1,0:T(8,128)(2,1)}, bf16[5648,128]{1,0:T(8,128)(2,1)S(1)}, u32[]{:S(2)}) copy-start(bf16[5648,128]{1,0:T(8,128)(2,1)S(1)} %collective-permute-done.22.refs_6_) | copy-start | bytes 4337668
  70.7 6.9 %copy-start.13 = (bf16[5648,128]{1,0:T(8,128)(2,1)}, bf16[5648,128]{1,0:T(8,128)(2,1)S(1)}, u32[]{:S(2)}) copy-start(bf16[5648,128]{1,0:T(8,128)(2,1)S(1)} %collective-permute-done.23.refs_3_) | copy-start | bytes 4337668
  70.7 6.9 %copy-start.14 = (bf16[5648,128]{1,0:T(8,128)(2,1)}, bf16[5648,128]{1,0:T(8,128)(2,1)S(1)}, u32[]{:S(2)}) copy-start(bf16[5648,128]{1,0:T(8,128)(2,1)S(1)} %collective-permute-done.24.refs_5_) | copy-start | bytes 4337668
  70.7 20.9 %collective-permute-start.26 = (bf16[5648,128]{1,0:T(8,128)(2,1)S(1)}, bf16[5648,128]{1,0:T(8,128)(2,1)S(1)}, u32[]{:S(2)}, u32[]{:S(2)}) collective-permute-start(bf16[5648,128]{1,0:T(8,128)(2,1)S(1)} %collective-permute-done.22.refs_6_), channel_id=1, source_target_pairs={{1,5},{3,7},{5,1},{7,3},{24,28},{26,30},{28,24},{30,26}} | collective-permute-start | bytes 4337672 | tf_op jit(solution)/shard_map/ppermute | solution.py:475
  73.2 36.9 %collective-permute-start.29 = (s16[1968,256]{1,0:T(8,128)(2,1)S(1)}, s16[1968,256]{1,0:T(8,128)(2,1)}, u32[]{:S(2)}, u32[]{:S(2)}) collective-permute-start(s16[1968,256]{1,0:T(8,128)(2,1)S(1)} %get-tuple-element.131), channel_id=1, source_target_pairs={{2,0},{3,1},{6,4},{7,5},{10,8},{11,9},{14,12},{15,13},{16,18},{17,... | collective-permute-start | bytes 3022856 | tf_op jit(solution)/shard_map/ppermute | solution.py:475
  82.2 20.4 %collective-permute-start.30 = (s16[1312,256]{1,0:T(8,128)(2,1)S(1)}, s16[1312,256]{1,0:T(8,128)(2,1)S(1)}, u32[]{:S(2)}, u32[]{:S(2)}) collective-permute-start(s16[1312,256]{1,0:T(8,128)(2,1)S(1)} %get-tuple-element.135), channel_id=1, source_target_pairs={{0,2},{1,3},{4,6},{5,7},{8,10},{9,11},{12,14},{13,15},{18,16},{19,... | collective-permute-start | bytes 2015240 | tf_op jit(solution)/shard_map/ppermute | solution.py:475
  91.7 18.5 %copy-start.4 = (bf16[2048,256]{1,0:T(8,128)(2,1)S(1)}, bf16[2048,256]{1,0:T(8,128)(2,1)}, u32[]{:S(2)}) copy-start(bf16[2048,256]{1,0:T(8,128)(2,1)} %refs_2_.2) | copy-start | bytes 3145732
  91.7 18.5 %copy-start.16 = (s32[8,16]{1,0:T(8,128)S(1)}, s32[8,16]{1,0:T(8,128)}, u32[]{:S(2)}) copy-start(s32[8,16]{1,0:T(8,128)} %refs_0_.1) | copy-start | bytes 1540
  91.7 18.5 %copy-start.17 = (s32[16,2]{0,1:T(2,128)S(1)}, s32[16,2]{0,1:T(2,128)}, u32[]{:S(2)}) copy-start(s32[16,2]{0,1:T(2,128)} %param.9) | copy-start | bytes 388
  96.2 14.0 %collective-permute-start.31 = (s16[1312,256]{1,0:T(8,128)(2,1)S(1)}, s16[1312,256]{1,0:T(8,128)(2,1)S(1)}, u32[]{:S(2)}, u32[]{:S(2)}) collective-permute-start(s16[1312,256]{1,0:T(8,128)(2,1)S(1)} %get-tuple-element.138), channel_id=1, source_target_pairs={{1,3},{5,7},{26,24},{30,28}} | collective-permute-start | bytes 2015240 | tf_op jit(solution)/shard_map/ppermute | solution.py:475
  97.5 1.2 %collective-permute-start.27 = (f32[8,128]{1,0:T(8,128)S(1)}, f32[8,128]{1,0:T(8,128)S(1)}, u32[]{:S(2)}, u32[]{:S(2)}) collective-permute-start(f32[8,128]{1,0:T(8,128)S(1)} %get-tuple-element.123.refs_0_), channel_id=1, source_target_pairs={{0,1},{1,0},{2,3},{3,2},{4,5},{5,4},{6,7},{7,6},{8,9},{9,8},{10,11... | collective-permute-start | bytes 12296 | tf_op jit(solution)/shard_map/ppermute | solution.py:525
  99.9 9.0 %collective-permute-start.28 = (f32[8,128]{1,0:T(8,128)S(1)}, f32[8,128]{1,0:T(8,128)S(1)}, u32[]{:S(2)}, u32[]{:S(2)}) collective-permute-start(f32[8,128]{1,0:T(8,128)S(1)} %get-tuple-element.127), channel_id=1, source_target_pairs={{0,2},{2,0},{1,3},{3,1},{4,6},{6,4},{5,7},{7,5},{8,10},{10,8},{9,1... | collective-permute-start | bytes 12296 | tf_op jit(solution)/shard_map/ppermute | solution.py:526

commit v11 on v10

--- a/solution.py
+++ b/solution.py
@@ -147,6 +147,7 @@
     word = 16
     first_row = 0 if before is None else before.shape[0]
     half_rows = coded_rows(rows // 2)
+    direct = len(choices) == 1
     parts = []
     for choice in choices:
         for part in choice:
@@ -160,9 +161,11 @@
         a_refs, refs = refs[:count], refs[count:]
         p_any, refs = refs[:len(parts)], refs[len(parts):]
         out_ref, *coded_refs, token_ref, packed, wide_ref, sem = refs
+        if direct:
+            packed = p_any[0]
         pick = picks_ref[step]
         token_ref[...] = sum(ref[...] for ref in token_refs)
-        for number, choice in enumerate(choices):
+        for number, choice in enumerate([] if direct else choices):
             @pl.when(pick == number)
             def _(choice=choice):
                 at = 0
@@ -220,10 +223,10 @@
             *([jax.ShapeDtypeStruct((half_rows, wide * TILE), jnp.int16)] * 2 if split else
               [jax.ShapeDtypeStruct((first_row + 2 * half_rows, wide * TILE), jnp.int16)]),
             TOKEN),
-        in_specs=[SMEM] + [VMEM] * (bool(first_row) + len(tokens) + count) + [ANY] * len(parts),
+        in_specs=[SMEM] + [VMEM] * (bool(first_row) + len(tokens) + count) + [VMEM if direct else ANY] * len(parts),
         out_specs=(VMEM,) * (4 if split else 3),
         scratch_shapes=[
-            pltpu.VMEM((height, TILE), amps[0].dtype),
+            pltpu.VMEM((META if direct else height, TILE), amps[0].dtype),
             pltpu.VMEM((count * depth, wide * TILE), amps[0].dtype),
             pltpu.SemaphoreType.DMA((2,)),
         ],

time: 114 us -> 114 us (level)
  no operation moved by 1% of the time
where the time goes in v11:
time: 114 us; the launch traced here: 113 us
  waiting for transfers between devices  49.5 us (43%)
  Pallas kernels  32.8 us (29%)
  starting transfers between devices  28.9 us (25%)
  between operations  1.24 us (1%)
    ppermute x16, waiting for transfers between devices, move(): return lax.ppermute(value, AXES, pairs)  37.6 us
    ppermute x16, starting transfers between devices, move(): return lax.ppermute(value, AXES, pairs)  25.4 us
    pallas_call x5, Pallas kernels, shard_product(): call(kernel, 'shard_product', out_shape=(jax.ShapeDtypeStruct((rows, wide...  21.3 us
    ppermute x1, waiting for transfers between devices, sparse_ladder(): flags = [token, lax.ppermute(token, 'col', CHIPS_Y)]  5.14 us
    pallas_call x1, Pallas kernels, mask_tiles(): call(kernel, 'mask_tiles', out_shape=tuple((jax.ShapeDtypeStruct(part.sha...  4.17 us
    ppermute x1, waiting for transfers between devices, sparse_ladder(): other_amps = lax.ppermute(amplitudes_now, 'col', CORES)  3.38 us
    pallas_call x1, Pallas kernels, lay_out(): call(kernel, 'lay_out', out_shape=pltpu.HBM((rows, 2 * width), jnp.bfloat...  3.02 us
    ppermute x1, starting transfers between devices, sparse_ladder(): flags = [token, lax.ppermute(token, 'col', CHIPS_Y)]  2.68 us
  transfers between devices with their start and end apart: 22, of which 9 were waited for; matrix products, arithmetic and copies ran while one was open for 1% of the time, Pallas kernels for 26%

profile of v11, /device:TPU:24, one launch (start us, length us, event | category | flops | bytes accessed | tf_op | source)
XLA Modules:
  0.0 113.5 jit_solution(12541264092312669969)
XLA Ops:
  0.0 0.0 collective-permute-start.11
  0.0 0.5 collective-permute-start.10
  0.5 0.0 collective-permute-start.12
  0.5 0.1 pad_add_fusion
  0.6 0.1 stack.37.picks_ref
  0.7 2.2 %collective-permute-done.10.refs_1_ = s32[2,16]{1,0:T(2,128)S(1)} collective-permute-done((s32[2,16]{1,0:T(2,128)}, s32[2,16]{1,0:T(2,128)S(1)}, u32[]{:S(2)}, u32[]{:S(2)}) %collective-permute-start.10) | collective-permute-done | bytes 160 | tf_op jit(solution)/shard_map/ppermute | solution.py:495
  2.9 0.0 collective-permute-done.11.refs_3_
  2.9 1.9 %pack_tiles.1.refs_3_ = bf16[5648,128]{1,0:T(8,128)(2,1)S(1)} custom-call(s32[1]{0:T(128)} %bitcast.2.swap_ref, s32[2,16]{1,0:T(2,128)} %bitcast.38, s32[2,16]{1,0:T(2,128)S(1)} %collective-permute-done.10.refs_1_, bf16[2048,256]{1,0:T(8,128)(2,1)} %refs_2_.2, bf16[2048,256]{1,0:T(8,128)(2,1)S(1)} %collective-permute-done.11.refs_3_), custom_call_target="tpu_custom_call" | custom-call | flops 1 | bytes 1 | tf_op jit(solution)/shard_map/pack_tiles/pallas_call | solution.py:101
  4.8 0.0 copy-start
  4.8 0.0 collective-permute-done.12.refs_1_
  4.8 0.2 collective-permute-start.16
  5.0 0.7 collective-permute-start.13
  5.8 2.3 %collective-permute-start.14 = (bf16[5648,128]{1,0:T(8,128)(2,1)S(1)}, bf16[5648,128]{1,0:T(8,128)(2,1)S(1)}, u32[]{:S(2)}, u32[]{:S(2)}) collective-permute-start(bf16[5648,128]{1,0:T(8,128)(2,1)S(1)} %pack_tiles.1.refs_3_), channel_id=1, source_target_pairs={{1,8},{3,10},{5,12},{7,14},{8,1},{10,3},{12,5},{14,7},{17,24},{19,... | collective-permute-start | bytes 4337672 | tf_op jit(solution)/shard_map/ppermute | solution.py:478
  8.1 0.8 collective-permute-start.15
  8.9 3.4 %collective-permute-done.16.refs_3_ = bf16[1024,2048]{1,0:T(8,128)(2,1)S(1)} collective-permute-done((bf16[1024,2048]{1,0:T(8,128)(2,1)}, bf16[1024,2048]{1,0:T(8,128)(2,1)S(1)}, u32[]{:S(2)}, u32[]{:S(2)}) %collective-permute-start.16) | collective-permute-done | bytes 4194336 | tf_op jit(solution)/shard_map/ppermute | solution.py:500
  12.2 4.2 %mask_tiles.1 = (bf16[1024,2048]{1,0:T(8,128)(2,1)S(1)}, bf16[1024,2048]{1,0:T(8,128)(2,1)S(1)}, f32[8,128]{1,0:T(8,128)S(1)}) custom-call(s32[8,16]{1,0:T(8,128)} %refs_0_.1, s32[8,16]{1,0:T(8,128)S(1)} %collective-permute-done.12.refs_1_, bf16[1024,2048]{1,0:T(8,128)(2,1)} %refs_2_.3, bf16[1024,2048]{1,0:T(8,128)(2,1)S(1)} %collective-permute-done.16.refs_3_), custom_call_target="tpu_custom_call" | custom-call | flops 1 | bytes 1 | tf_op jit(solution)/shard_map/mask_tiles/pallas_call | solution.py:131
  16.4 0.0 copy-done
  16.4 0.0 collective-permute-done.13.refs_4_
  16.5 0.0 copy-start.9
  16.5 9.7 %collective-permute-done.14.refs_4_ = bf16[5648,128]{1,0:T(8,128)(2,1)S(1)} collective-permute-done((bf16[5648,128]{1,0:T(8,128)(2,1)S(1)}, bf16[5648,128]{1,0:T(8,128)(2,1)S(1)}, u32[]{:S(2)}, u32[]{:S(2)}) %collective-permute-start.14) | collective-permute-done | bytes 1445920 | tf_op jit(solution)/shard_map/ppermute | solution.py:478
  26.1 0.0 collective-permute-done.15.refs_5_
  26.1 3.4 %collective-permute-start.17 = (bf16[5648,128]{1,0:T(8,128)(2,1)S(1)}, bf16[5648,128]{1,0:T(8,128)(2,1)S(1)}, u32[]{:S(2)}, u32[]{:S(2)}) collective-permute-start(bf16[5648,128]{1,0:T(8,128)(2,1)S(1)} %collective-permute-done.14.refs_4_), channel_id=1, source_target_pairs={{1,5},{3,7},{5,1},{7,3},{8,12},{10,14},{12,8},{14,10},{17,21},{19,... | collective-permute-start | bytes 4337672 | tf_op jit(solution)/shard_map/ppermute | solution.py:478
  29.6 0.8 collective-permute-start.18
  30.3 0.8 collective-permute-start.19
  31.1 6.0 %shard_product.5 = (f32[1024,256]{1,0:T(8,128)}, s16[656,256]{1,0:T(8,128)(2,1)S(1)}, s16[656,256]{1,0:T(8,128)(2,1)S(1)}, f32[8,128]{1,0:T(8,128)S(1)}) custom-call(s32[10]{0:T(128)S(1)} %stack.37.picks_ref, f32[8,128]{1,0:T(8,128)S(1)} %get-tuple-element.101.refs_0_, bf16[1024,2048]{1,0:T(8,128)(2,1)S(1)} %get-tuple-element.102.refs_1_.refs_2_, ...), custom_call_target="tpu_custom_call" | custom-call | flops 1 | bytes 1 | tf_op jit(solution)/shard_map/shard_product/pallas_call | solution.py:219
  37.1 3.0 %collective-permute-start.20 = (s16[656,256]{1,0:T(8,128)(2,1)S(1)}, s16[656,256]{1,0:T(8,128)(2,1)S(1)}, u32[]{:S(2)}, u32[]{:S(2)}) collective-permute-start(s16[656,256]{1,0:T(8,128)(2,1)S(1)} %get-tuple-element.104), channel_id=1, source_target_pairs={{2,0},{3,1},{6,4},{7,5},{10,8},{11,9},{14,12},{15,13},{16,18},{17,... | collective-permute-start | bytes 1007624 | tf_op jit(solution)/shard_map/ppermute | solution.py:478
  40.1 4.6 %collective-permute-done.20 = s16[656,256]{1,0:T(8,128)(2,1)S(1)} collective-permute-done((s16[656,256]{1,0:T(8,128)(2,1)S(1)}, s16[656,256]{1,0:T(8,128)(2,1)S(1)}, u32[]{:S(2)}, u32[]{:S(2)}) %collective-permute-start.20) | collective-permute-done | bytes 335904 | tf_op jit(solution)/shard_map/ppermute | solution.py:478
  44.7 2.4 %collective-permute-done.17.refs_5_ = bf16[5648,128]{1,0:T(8,128)(2,1)S(1)} collective-permute-done((bf16[5648,128]{1,0:T(8,128)(2,1)S(1)}, bf16[5648,128]{1,0:T(8,128)(2,1)S(1)}, u32[]{:S(2)}, u32[]{:S(2)}) %collective-permute-start.17) | collective-permute-done | bytes 1445920 | tf_op jit(solution)/shard_map/ppermute | solution.py:478
  47.1 0.0 collective-permute-done.18.refs_3_
  47.1 0.0 collective-permute-done.19.refs_4_
  47.1 0.8 collective-permute-start.21
  47.9 1.3 %collective-permute-start.22 = (bf16[5648,128]{1,0:T(8,128)(2,1)S(1)}, bf16[5648,128]{1,0:T(8,128)(2,1)S(1)}, u32[]{:S(2)}, u32[]{:S(2)}) collective-permute-start(bf16[5648,128]{1,0:T(8,128)(2,1)S(1)} %collective-permute-done.18.refs_3_), channel_id=1, source_target_pairs={{9,1},{11,3},{13,5},{15,7},{16,24},{18,26},{20,28},{22,30}} | collective-permute-start | bytes 4337672 | tf_op jit(solution)/shard_map/ppermute | solution.py:478
  49.2 0.8 collective-permute-start.23
  50.0 0.8 collective-permute-start.24
  50.7 0.6 shard_product.6
  51.3 0.7 collective-permute-start.25
  52.1 6.0 %shard_product.7 = (f32[1024,256]{1,0:T(8,128)}, s16[1968,256]{1,0:T(8,128)(2,1)S(1)}, f32[8,128]{1,0:T(8,128)S(1)}) custom-call(s32[10]{0:T(128)S(1)} %stack.37.picks_ref, s16[656,256]{1,0:T(8,128)(2,1)S(1)} %get-tuple-element.111.refs_0_, f32[8,128]{1,0:T(8,128)S(1)} %get-tuple-element.112.refs_1_, ...), custom_call_target="tpu_custom_call" | custom-call | flops 1 | bytes 1 | tf_op jit(solution)/shard_map/shard_product/pallas_call | solution.py:219
  58.0 0.0 collective-permute-done.25.refs_3_
  58.1 0.0 collective-permute-done.21.refs_4_
  58.1 12.7 %collective-permute-done.22.refs_6_ = bf16[5648,128]{1,0:T(8,128)(2,1)S(1)} collective-permute-done((bf16[5648,128]{1,0:T(8,128)(2,1)S(1)}, bf16[5648,128]{1,0:T(8,128)(2,1)S(1)}, u32[]{:S(2)}, u32[]{:S(2)}) %collective-permute-start.22) | collective-permute-done | bytes 1445920 | tf_op jit(solution)/shard_map/ppermute | solution.py:478
  70.7 0.0 collective-permute-done.23.refs_3_
  70.7 0.0 collective-permute-done.24.refs_5_
  70.8 2.4 %collective-permute-start.26 = (bf16[5648,128]{1,0:T(8,128)(2,1)S(1)}, bf16[5648,128]{1,0:T(8,128)(2,1)S(1)}, u32[]{:S(2)}, u32[]{:S(2)}) collective-permute-start(bf16[5648,128]{1,0:T(8,128)(2,1)S(1)} %collective-permute-done.22.refs_6_), channel_id=1, source_target_pairs={{1,5},{3,7},{5,1},{7,3},{24,28},{26,30},{28,24},{30,26}} | collective-permute-start | bytes 4337672 | tf_op jit(solution)/shard_map/ppermute | solution.py:478
  73.2 4.4 %collective-permute-start.29 = (s16[1968,256]{1,0:T(8,128)(2,1)S(1)}, s16[1968,256]{1,0:T(8,128)(2,1)}, u32[]{:S(2)}, u32[]{:S(2)}) collective-permute-start(s16[1968,256]{1,0:T(8,128)(2,1)S(1)} %get-tuple-element.131), channel_id=1, source_target_pairs={{2,0},{3,1},{6,4},{7,5},{10,8},{11,9},{14,12},{15,13},{16,18},{17,... | collective-permute-start | bytes 3022856 | tf_op jit(solution)/shard_map/ppermute | solution.py:478
  77.6 4.5 %shard_product.8 = (f32[1024,256]{1,0:T(8,128)S(1)}, s16[1312,256]{1,0:T(8,128)(2,1)S(1)}, f32[8,128]{1,0:T(8,128)S(1)}) custom-call(s32[10]{0:T(128)S(1)} %stack.37.picks_ref, f32[8,128]{1,0:T(8,128)S(1)} %get-tuple-element.116.refs_0_, bf16[1024,2048]{1,0:T(8,128)(2,1)S(1)} %get-tuple-element.102.refs_1_.refs_2_, ...), custom_call_target="tpu_custom_call" | custom-call | flops 1 | bytes 1 | tf_op jit(solution)/shard_map/shard_product/pallas_call | solution.py:219
  82.2 1.3 %collective-permute-start.30 = (s16[1312,256]{1,0:T(8,128)(2,1)S(1)}, s16[1312,256]{1,0:T(8,128)(2,1)S(1)}, u32[]{:S(2)}, u32[]{:S(2)}) collective-permute-start(s16[1312,256]{1,0:T(8,128)(2,1)S(1)} %get-tuple-element.135), channel_id=1, source_target_pairs={{0,2},{1,3},{4,6},{5,7},{8,10},{9,11},{12,14},{13,15},{18,16},{19,... | collective-permute-start | bytes 2015240 | tf_op jit(solution)/shard_map/ppermute | solution.py:478
  83.5 8.2 %collective-permute-done.26.refs_3_ = bf16[5648,128]{1,0:T(8,128)(2,1)S(1)} collective-permute-done((bf16[5648,128]{1,0:T(8,128)(2,1)S(1)}, bf16[5648,128]{1,0:T(8,128)(2,1)S(1)}, u32[]{:S(2)}, u32[]{:S(2)}) %collective-permute-start.26) | collective-permute-done | bytes 1445920 | tf_op jit(solution)/shard_map/ppermute | solution.py:478
  91.7 4.2 %shard_product.9 = (f32[1024,256]{1,0:T(8,128)}, s16[1312,256]{1,0:T(8,128)(2,1)S(1)}, f32[8,128]{1,0:T(8,128)S(1)}) custom-call(s32[10]{0:T(128)S(1)} %stack.37.picks_ref, f32[8,128]{1,0:T(8,128)S(1)} %get-tuple-element.121.refs_0_, bf16[1024,2048]{1,0:T(8,128)(2,1)S(1)} %get-tuple-element.102.refs_1_.refs_2_, ...), custom_call_target="tpu_custom_call" | custom-call | flops 1 | bytes 1 | tf_op jit(solution)/shard_map/shard_product/pallas_call | solution.py:219
  95.9 1.3 %collective-permute-start.31 = (s16[1312,256]{1,0:T(8,128)(2,1)S(1)}, s16[1312,256]{1,0:T(8,128)(2,1)S(1)}, u32[]{:S(2)}, u32[]{:S(2)}) collective-permute-start(s16[1312,256]{1,0:T(8,128)(2,1)S(1)} %get-tuple-element.138), channel_id=1, source_target_pairs={{1,3},{5,7},{26,24},{30,28}} | collective-permute-start | bytes 2015240 | tf_op jit(solution)/shard_map/ppermute | solution.py:478
  97.2 0.1 collective-permute-start.27
  97.3 1.2 %collective-permute-done.27.refs_1_ = f32[8,128]{1,0:T(8,128)S(1)} collective-permute-done((f32[8,128]{1,0:T(8,128)S(1)}, f32[8,128]{1,0:T(8,128)S(1)}, u32[]{:S(2)}, u32[]{:S(2)}) %collective-permute-start.27) | collective-permute-done | bytes 4128 | tf_op jit(solution)/shard_map/ppermute | solution.py:528
  98.5 1.2 %add_coded.2 = (bf16[1024,256]{1,0:T(8,128)(2,1)}, f32[8,128]{1,0:T(8,128)S(1)}) custom-call(f32[8,128]{1,0:T(8,128)S(1)} %get-tuple-element.123.refs_0_, f32[8,128]{1,0:T(8,128)S(1)} %collective-permute-done.27.refs_1_, f32[1024,256]{1,0:T(8,128)S(1)} %get-tuple-element.124.refs_2_, s16[1312,256]{1,0:T(8,128)(2,1)S(1)} %collective-permute-done.25.refs_3_), custom_call_target="tpu_custom_call" | custom-call | flops 1 | bytes 1 | tf_op jit(solution)/shard_map/add_coded/pallas_call | solution.py:315
  99.7 2.7 %collective-permute-start.28 = (f32[8,128]{1,0:T(8,128)S(1)}, f32[8,128]{1,0:T(8,128)S(1)}, u32[]{:S(2)}, u32[]{:S(2)}) collective-permute-start(f32[8,128]{1,0:T(8,128)S(1)} %get-tuple-element.127), channel_id=1, source_target_pairs={{0,2},{2,0},{1,3},{3,1},{4,6},{6,4},{5,7},{7,5},{8,10},{10,8},{9,1... | collective-permute-start | bytes 12296 | tf_op jit(solution)/shard_map/ppermute | solution.py:529
  102.3 0.0 collective-permute-done.30.refs_1_
  102.3 1.2 %add_coded.3 = (bf16[1024,256]{1,0:T(8,128)(2,1)}, f32[8,128]{1,0:T(8,128)}) custom-call(f32[1024,256]{1,0:T(8,128)S(1)} %get-tuple-element.134.refs_0_, s16[1312,256]{1,0:T(8,128)(2,1)S(1)} %collective-permute-done.30.refs_1_), custom_call_target="tpu_custom_call" | custom-call | flops 1 | bytes 1 | tf_op jit(solution)/shard_map/add_coded/pallas_call | solution.py:315
  103.5 5.1 %collective-permute-done.28 = f32[8,128]{1,0:T(8,128)S(1)} collective-permute-done((f32[8,128]{1,0:T(8,128)S(1)}, f32[8,128]{1,0:T(8,128)S(1)}, u32[]{:S(2)}, u32[]{:S(2)}) %collective-permute-start.28) | collective-permute-done | bytes 4128 | tf_op jit(solution)/shard_map/ppermute | solution.py:529
  108.7 0.6 add_reduce_fusion
  109.9 0.0 collective-permute-done.29
  109.9 0.0 collective-permute-done.31
  110.0 0.0 copy-done.4
  110.0 0.0 copy-done.16
  110.0 0.0 copy-done.17
  110.0 3.3 %conditional.1 = (bf16[1024,512]{1,0:T(8,128)(2,1)}) conditional(s32[]{:T(128)} %convert_element_type.32, (s32[2]{0:T(128)S(1)}, f32[1024,256]{1,0:T(8,128)}, s16[656,256]{1,0:T(8,128)(2,1)}, s16[1968,256]{1,0:T(8,128)(2,1)}, f32[1024,256]{1,0:T(8,128)}, /*index=5*/bf16[1024,256]{1,0:T(8,128)(2,1)}, bf16[1024,256]{1,0:T(8,128)(2,1)}, ...), branch_computations={%region_1.2_spmd, %region_2.3_spmd} | conditional | flops 8594653184 | bytes 206655584 | solution.py:539
  110.0 3.0 %lay_out.1 = bf16[1024,512]{1,0:T(8,128)(2,1)} custom-call(s32[2]{0:T(128)S(1)} %get-tuple-element.34.place_ref, f32[1024,256]{1,0:T(8,128)} %get-tuple-element.35.refs_0_, s16[656,256]{1,0:T(8,128)(2,1)} %get-tuple-element.36.refs_1_, s16[1968,256]{1,0:T(8,128)(2,1)} %get-tuple-element.37.refs_2_, f32[1024,256]{1,0:T(8,128)} %get-tuple-element.38.refs_3_, ...), custom_call_target="tpu_custom_call" | custom-call | flops 1 | bytes 1 | tf_op jit(solution)/shard_map/cond/branch_0_fun/lay_out/pallas_call | solution.py:387
  (24 shorter events, 0.0 us)
Async XLA Ops:
  0.0 2.9 %collective-permute-start.11 = (bf16[2048,256]{1,0:T(8,128)(2,1)}, bf16[2048,256]{1,0:T(8,128)(2,1)S(1)}, u32[]{:S(2)}, u32[]{:S(2)}) collective-permute-start(bf16[2048,256]{1,0:T(8,128)(2,1)} %refs_2_.2), channel_id=1, source_target_pairs={{0,1},{1,0},{2,3},{3,2},{4,5},{5,4},{6,7},{7,6},{8,9},{9,8},{10,11... | collective-permute-start | bytes 3145736 | tf_op jit(solution)/shard_map/ppermute | solution.py:494
  0.0 2.9 %collective-permute-start.10 = (s32[2,16]{1,0:T(2,128)}, s32[2,16]{1,0:T(2,128)S(1)}, u32[]{:S(2)}, u32[]{:S(2)}) collective-permute-start(s32[2,16]{1,0:T(2,128)} %bitcast.37), channel_id=1, source_target_pairs={{0,1},{1,0},{2,3},{3,2},{4,5},{5,4},{6,7},{7,6},{8,9},{9,8},{10,11... | collective-permute-start | bytes 392 | tf_op jit(solution)/shard_map/ppermute | solution.py:495
  0.5 4.3 %collective-permute-start.12 = (s32[8,16]{1,0:T(8,128)}, s32[8,16]{1,0:T(8,128)S(1)}, u32[]{:S(2)}, u32[]{:S(2)}) collective-permute-start(s32[8,16]{1,0:T(8,128)} %refs_0_.1), channel_id=1, source_target_pairs={{0,1},{1,0},{2,3},{3,2},{4,5},{5,4},{6,7},{7,6},{8,9},{9,8},{10,11... | collective-permute-start | bytes 1544 | tf_op jit(solution)/shard_map/ppermute | solution.py:496
  4.8 11.6 %copy-start = (bf16[5648,128]{1,0:T(8,128)(2,1)}, bf16[5648,128]{1,0:T(8,128)(2,1)S(1)}, u32[]{:S(2)}) copy-start(bf16[5648,128]{1,0:T(8,128)(2,1)S(1)} %pack_tiles.1.refs_3_) | copy-start | bytes 4337668
  4.8 7.4 %collective-permute-start.16 = (bf16[1024,2048]{1,0:T(8,128)(2,1)}, bf16[1024,2048]{1,0:T(8,128)(2,1)S(1)}, u32[]{:S(2)}, u32[]{:S(2)}) collective-permute-start(bf16[1024,2048]{1,0:T(8,128)(2,1)} %refs_2_.3), channel_id=1, source_target_pairs={{0,1},{1,0},{2,3},{3,2},{4,5},{5,4},{6,7},{7,6},{8,9},{9,8},{10,11... | collective-permute-start | bytes 12582920 | tf_op jit(solution)/shard_map/ppermute | solution.py:500
  5.0 11.4 %collective-permute-start.13 = (bf16[5648,128]{1,0:T(8,128)(2,1)S(1)}, bf16[5648,128]{1,0:T(8,128)(2,1)S(1)}, u32[]{:S(2)}, u32[]{:S(2)}) collective-permute-start(bf16[5648,128]{1,0:T(8,128)(2,1)S(1)} %pack_tiles.1.refs_3_), channel_id=1, source_target_pairs={{0,4},{2,6},{4,0},{6,2},{9,13},{11,15},{13,9},{15,11},{16,20},{18,... | collective-permute-start | bytes 4337672 | tf_op jit(solution)/shard_map/ppermute | solution.py:478
  5.8 20.4 %collective-permute-start.14 = (bf16[5648,128]{1,0:T(8,128)(2,1)S(1)}, bf16[5648,128]{1,0:T(8,128)(2,1)S(1)}, u32[]{:S(2)}, u32[]{:S(2)}) collective-permute-start(bf16[5648,128]{1,0:T(8,128)(2,1)S(1)} %pack_tiles.1.refs_3_), channel_id=1, source_target_pairs={{1,8},{3,10},{5,12},{7,14},{8,1},{10,3},{12,5},{14,7},{17,24},{19,... | collective-permute-start | bytes 4337672 | tf_op jit(solution)/shard_map/ppermute | solution.py:478
  8.1 18.0 %collective-permute-start.15 = (bf16[5648,128]{1,0:T(8,128)(2,1)S(1)}, bf16[5648,128]{1,0:T(8,128)(2,1)S(1)}, u32[]{:S(2)}, u32[]{:S(2)}) collective-permute-start(bf16[5648,128]{1,0:T(8,128)(2,1)S(1)} %pack_tiles.1.refs_3_), channel_id=1, source_target_pairs={{9,17},{11,19},{13,21},{15,23},{16,8},{18,10},{20,12},{22,14}} | collective-permute-start | bytes 4337672 | tf_op jit(solution)/shard_map/ppermute | solution.py:478
  16.5 35.6 %copy-start.9 = (bf16[5648,128]{1,0:T(8,128)(2,1)}, bf16[5648,128]{1,0:T(8,128)(2,1)S(1)}, u32[]{:S(2)}) copy-start(bf16[5648,128]{1,0:T(8,128)(2,1)S(1)} %collective-permute-done.13.refs_4_) | copy-start | bytes 4337668
  26.1 4.9 %copy-start.8 = (bf16[5648,128]{1,0:T(8,128)(2,1)}, bf16[5648,128]{1,0:T(8,128)(2,1)S(1)}, u32[]{:S(2)}) copy-start(bf16[5648,128]{1,0:T(8,128)(2,1)S(1)} %collective-permute-done.14.refs_4_) | copy-start | bytes 4337668
  26.1 10.9 %copy-start.5 = (bf16[5648,128]{1,0:T(8,128)(2,1)}, bf16[5648,128]{1,0:T(8,128)(2,1)S(1)}, u32[]{:S(2)}) copy-start(bf16[5648,128]{1,0:T(8,128)(2,1)S(1)} %collective-permute-done.15.refs_5_) | copy-start | bytes 4337668
  26.1 20.9 %collective-permute-start.17 = (bf16[5648,128]{1,0:T(8,128)(2,1)S(1)}, bf16[5648,128]{1,0:T(8,128)(2,1)S(1)}, u32[]{:S(2)}, u32[]{:S(2)}) collective-permute-start(bf16[5648,128]{1,0:T(8,128)(2,1)S(1)} %collective-permute-done.14.refs_4_), channel_id=1, source_target_pairs={{1,5},{3,7},{5,1},{7,3},{8,12},{10,14},{12,8},{14,10},{17,21},{19,... | collective-permute-start | bytes 4337672 | tf_op jit(solution)/shard_map/ppermute | solution.py:478
  29.6 17.5 %collective-permute-start.18 = (bf16[5648,128]{1,0:T(8,128)(2,1)S(1)}, bf16[5648,128]{1,0:T(8,128)(2,1)S(1)}, u32[]{:S(2)}, u32[]{:S(2)}) collective-permute-start(bf16[5648,128]{1,0:T(8,128)(2,1)S(1)} %collective-permute-done.14.refs_4_), channel_id=1, source_target_pairs={{8,16},{10,18},{12,20},{14,22},{17,9},{19,11},{21,13},{23,15}} | collective-permute-start | bytes 4337672 | tf_op jit(solution)/shard_map/ppermute | solution.py:478
  30.3 16.8 %collective-permute-start.19 = (bf16[5648,128]{1,0:T(8,128)(2,1)S(1)}, bf16[5648,128]{1,0:T(8,128)(2,1)S(1)}, u32[]{:S(2)}, u32[]{:S(2)}) collective-permute-start(bf16[5648,128]{1,0:T(8,128)(2,1)S(1)} %collective-permute-done.15.refs_5_), channel_id=1, source_target_pairs={{8,0},{10,2},{12,4},{14,6},{17,25},{19,27},{21,29},{23,31}} | collective-permute-start | bytes 4337672 | tf_op jit(solution)/shard_map/ppermute | solution.py:478
  37.1 7.6 %collective-permute-start.20 = (s16[656,256]{1,0:T(8,128)(2,1)S(1)}, s16[656,256]{1,0:T(8,128)(2,1)S(1)}, u32[]{:S(2)}, u32[]{:S(2)}) collective-permute-start(s16[656,256]{1,0:T(8,128)(2,1)S(1)} %get-tuple-element.104), channel_id=1, source_target_pairs={{2,0},{3,1},{6,4},{7,5},{10,8},{11,9},{14,12},{15,13},{16,18},{17,... | collective-permute-start | bytes 1007624 | tf_op jit(solution)/shard_map/ppermute | solution.py:478
  44.7 5.2 %copy-start.15 = (s16[656,256]{1,0:T(8,128)(2,1)}, s16[656,256]{1,0:T(8,128)(2,1)S(1)}, u32[]{:S(2)}) copy-start(s16[656,256]{1,0:T(8,128)(2,1)S(1)} %collective-permute-done.20) | copy-start | bytes 1007620
  47.1 5.0 %copy-start.10 = (bf16[5648,128]{1,0:T(8,128)(2,1)}, bf16[5648,128]{1,0:T(8,128)(2,1)S(1)}, u32[]{:S(2)}) copy-start(bf16[5648,128]{1,0:T(8,128)(2,1)S(1)} %collective-permute-done.17.refs_5_) | copy-start | bytes 4337668
  47.1 3.6 %copy-start.6 = (bf16[5648,128]{1,0:T(8,128)(2,1)}, bf16[5648,128]{1,0:T(8,128)(2,1)S(1)}, u32[]{:S(2)}) copy-start(bf16[5648,128]{1,0:T(8,128)(2,1)S(1)} %collective-permute-done.18.refs_3_) | copy-start | bytes 4337668
  47.1 3.6 %copy-start.7 = (bf16[5648,128]{1,0:T(8,128)(2,1)}, bf16[5648,128]{1,0:T(8,128)(2,1)S(1)}, u32[]{:S(2)}) copy-start(bf16[5648,128]{1,0:T(8,128)(2,1)S(1)} %collective-permute-done.19.refs_4_) | copy-start | bytes 4337668
  47.1 10.9 %collective-permute-start.21 = (bf16[5648,128]{1,0:T(8,128)(2,1)S(1)}, bf16[5648,128]{1,0:T(8,128)(2,1)S(1)}, u32[]{:S(2)}, u32[]{:S(2)}) collective-permute-start(bf16[5648,128]{1,0:T(8,128)(2,1)S(1)} %collective-permute-done.19.refs_4_), channel_id=1, source_target_pairs={{0,4},{2,6},{4,0},{6,2},{25,29},{27,31},{29,25},{31,27}} | collective-permute-start | bytes 4337672 | tf_op jit(solution)/shard_map/ppermute | solution.py:478
  47.9 22.9 %collective-permute-start.22 = (bf16[5648,128]{1,0:T(8,128)(2,1)S(1)}, bf16[5648,128]{1,0:T(8,128)(2,1)S(1)}, u32[]{:S(2)}, u32[]{:S(2)}) collective-permute-start(bf16[5648,128]{1,0:T(8,128)(2,1)S(1)} %collective-permute-done.18.refs_3_), channel_id=1, source_target_pairs={{9,1},{11,3},{13,5},{15,7},{16,24},{18,26},{20,28},{22,30}} | collective-permute-start | bytes 4337672 | tf_op jit(solution)/shard_map/ppermute | solution.py:478
  49.2 21.6 %collective-permute-start.23 = (bf16[5648,128]{1,0:T(8,128)(2,1)S(1)}, bf16[5648,128]{1,0:T(8,128)(2,1)S(1)}, u32[]{:S(2)}, u32[]{:S(2)}) collective-permute-start(bf16[5648,128]{1,0:T(8,128)(2,1)S(1)} %collective-permute-done.18.refs_3_), channel_id=1, source_target_pairs={{9,13},{11,15},{13,9},{15,11},{16,20},{18,22},{20,16},{22,18}} | collective-permute-start | bytes 4337672 | tf_op jit(solution)/shard_map/ppermute | solution.py:478
  50.0 20.8 %collective-permute-start.24 = (bf16[5648,128]{1,0:T(8,128)(2,1)S(1)}, bf16[5648,128]{1,0:T(8,128)(2,1)S(1)}, u32[]{:S(2)}, u32[]{:S(2)}) collective-permute-start(bf16[5648,128]{1,0:T(8,128)(2,1)S(1)} %collective-permute-done.13.refs_4_), channel_id=1, source_target_pairs={{9,17},{11,19},{13,21},{15,23},{16,8},{18,10},{20,12},{22,14}} | collective-permute-start | bytes 4337672 | tf_op jit(solution)/shard_map/ppermute | solution.py:478
  51.3 6.7 %collective-permute-start.25 = (s16[1312,256]{1,0:T(8,128)(2,1)S(1)}, s16[1312,256]{1,0:T(8,128)(2,1)S(1)}, u32[]{:S(2)}, u32[]{:S(2)}) collective-permute-start(s16[1312,256]{1,0:T(8,128)(2,1)S(1)} %get-tuple-element.110), channel_id=1, source_target_pairs={{0,2},{4,6},{8,10},{9,11},{12,14},{13,15},{18,16},{19,17},{22,20},... | collective-permute-start | bytes 2015240 | tf_op jit(solution)/shard_map/ppermute | solution.py:478
  58.1 19.6 %copy-start.12 = (bf16[5648,128]{1,0:T(8,128)(2,1)}, bf16[5648,128]{1,0:T(8,128)(2,1)S(1)}, u32[]{:S(2)}) copy-start(bf16[5648,128]{1,0:T(8,128)(2,1)S(1)} %collective-permute-done.21.refs_4_) | copy-start | bytes 4337668
  70.7 6.9 %copy-start.11 = (bf16[5648,128]{1,0:T(8,128)(2,1)}, bf16[5648,128]{1,0:T(8,128)(2,1)S(1)}, u32[]{:S(2)}) copy-start(bf16[5648,128]{1,0:T(8,128)(2,1)S(1)} %collective-permute-done.22.refs_6_) | copy-start | bytes 4337668
  70.7 6.9 %copy-start.13 = (bf16[5648,128]{1,0:T(8,128)(2,1)}, bf16[5648,128]{1,0:T(8,128)(2,1)S(1)}, u32[]{:S(2)}) copy-start(bf16[5648,128]{1,0:T(8,128)(2,1)S(1)} %collective-permute-done.23.refs_3_) | copy-start | bytes 4337668
  70.8 6.9 %copy-start.14 = (bf16[5648,128]{1,0:T(8,128)(2,1)}, bf16[5648,128]{1,0:T(8,128)(2,1)S(1)}, u32[]{:S(2)}) copy-start(bf16[5648,128]{1,0:T(8,128)(2,1)S(1)} %collective-permute-done.24.refs_5_) | copy-start | bytes 4337668
  70.8 20.9 %collective-permute-start.26 = (bf16[5648,128]{1,0:T(8,128)(2,1)S(1)}, bf16[5648,128]{1,0:T(8,128)(2,1)S(1)}, u32[]{:S(2)}, u32[]{:S(2)}) collective-permute-start(bf16[5648,128]{1,0:T(8,128)(2,1)S(1)} %collective-permute-done.22.refs_6_), channel_id=1, source_target_pairs={{1,5},{3,7},{5,1},{7,3},{24,28},{26,30},{28,24},{30,26}} | collective-permute-start | bytes 4337672 | tf_op jit(solution)/shard_map/ppermute | solution.py:478
  73.2 36.7 %collective-permute-start.29 = (s16[1968,256]{1,0:T(8,128)(2,1)S(1)}, s16[1968,256]{1,0:T(8,128)(2,1)}, u32[]{:S(2)}, u32[]{:S(2)}) collective-permute-start(s16[1968,256]{1,0:T(8,128)(2,1)S(1)} %get-tuple-element.131), channel_id=1, source_target_pairs={{2,0},{3,1},{6,4},{7,5},{10,8},{11,9},{14,12},{15,13},{16,18},{17,... | collective-permute-start | bytes 3022856 | tf_op jit(solution)/shard_map/ppermute | solution.py:478
  82.2 20.2 %collective-permute-start.30 = (s16[1312,256]{1,0:T(8,128)(2,1)S(1)}, s16[1312,256]{1,0:T(8,128)(2,1)S(1)}, u32[]{:S(2)}, u32[]{:S(2)}) collective-permute-start(s16[1312,256]{1,0:T(8,128)(2,1)S(1)} %get-tuple-element.135), channel_id=1, source_target_pairs={{0,2},{1,3},{4,6},{5,7},{8,10},{9,11},{12,14},{13,15},{18,16},{19,... | collective-permute-start | bytes 2015240 | tf_op jit(solution)/shard_map/ppermute | solution.py:478
  91.7 18.2 %copy-start.4 = (bf16[2048,256]{1,0:T(8,128)(2,1)S(1)}, bf16[2048,256]{1,0:T(8,128)(2,1)}, u32[]{:S(2)}) copy-start(bf16[2048,256]{1,0:T(8,128)(2,1)} %refs_2_.2) | copy-start | bytes 3145732
  91.7 18.2 %copy-start.16 = (s32[8,16]{1,0:T(8,128)S(1)}, s32[8,16]{1,0:T(8,128)}, u32[]{:S(2)}) copy-start(s32[8,16]{1,0:T(8,128)} %refs_0_.1) | copy-start | bytes 1540
  91.7 18.3 %copy-start.17 = (s32[16,2]{0,1:T(2,128)S(1)}, s32[16,2]{0,1:T(2,128)}, u32[]{:S(2)}) copy-start(s32[16,2]{0,1:T(2,128)} %param.9) | copy-start | bytes 388
  95.9 14.0 %collective-permute-start.31 = (s16[1312,256]{1,0:T(8,128)(2,1)S(1)}, s16[1312,256]{1,0:T(8,128)(2,1)S(1)}, u32[]{:S(2)}, u32[]{:S(2)}) collective-permute-start(s16[1312,256]{1,0:T(8,128)(2,1)S(1)} %get-tuple-element.138), channel_id=1, source_target_pairs={{1,3},{5,7},{26,24},{30,28}} | collective-permute-start | bytes 2015240 | tf_op jit(solution)/shard_map/ppermute | solution.py:478
  97.2 1.2 %collective-permute-start.27 = (f32[8,128]{1,0:T(8,128)S(1)}, f32[8,128]{1,0:T(8,128)S(1)}, u32[]{:S(2)}, u32[]{:S(2)}) collective-permute-start(f32[8,128]{1,0:T(8,128)S(1)} %get-tuple-element.123.refs_0_), channel_id=1, source_target_pairs={{0,1},{1,0},{2,3},{3,2},{4,5},{5,4},{6,7},{7,6},{8,9},{9,8},{10,11... | collective-permute-start | bytes 12296 | tf_op jit(solution)/shard_map/ppermute | solution.py:528
  99.7 9.0 %collective-permute-start.28 = (f32[8,128]{1,0:T(8,128)S(1)}, f32[8,128]{1,0:T(8,128)S(1)}, u32[]{:S(2)}, u32[]{:S(2)}) collective-permute-start(f32[8,128]{1,0:T(8,128)S(1)} %get-tuple-element.127), channel_id=1, source_target_pairs={{0,2},{2,0},{1,3},{3,1},{4,6},{6,4},{5,7},{7,5},{8,10},{10,8},{9,1... | collective-permute-start | bytes 12296 | tf_op jit(solution)/shard_map/ppermute | solution.py:529
